TPU v7x, 32 devices: a whole 2x2x4 slice. The times are simulated.
32 devices in a mesh: gx: 4 (over z), gy: 4 (over x, core), gz: 2 (over y).
Axes of the slice: x: 2, y: 2, z: 4, core: 2. Of those that a mesh axis runs over, the one named last changes fastest.
Arguments:
- schur: float32 [4, 4, 2, 1536, 1536], P('gx', 'gy', 'gz'), as said below
- start_block: float32 [4, 4, 2, 6, 256, 32], P('gx', 'gy', 'gz'), may hold values from -6 to 6
- resid: float32 [4, 4, 2, 1536, 128], P('gx', 'gy', 'gz'), may hold values from -6 to 6
- group_of: int32 [8], replicated, may hold values from 0 to 1, as said below
Outputs:
- correction: float32 [4, 4, 2, 1536, 128], P('gx', 'gy', 'gz')
Inputs may be any that keep to these rules, and one draw needn't show every extreme that they name: Each subdomain's schur is symmetric positive definite. `group_of`: each of the 2 groups has exactly 4 subdomains.
All inputs are finite; a program needn't handle non-finite values.
Results may differ from a plain program's by a relative error of at most 0.00022.
Values sent between devices are 32-bit elements; how exact they have to be, the bound alone decides.
No kernel may reach another device: no remote copies, remote signals or barrier semaphores. Data moves between devices by JAX's collectives and lax.ppermute only.
A program may use at most 128 MiB of HBM per device.

v0:
```python
import jax
import jax.numpy as jnp
from jax import lax
from jax.sharding import PartitionSpec as P

NS_ITERS = 3
SUB_ITERS = 2
GROUP_SIZE = 4


precise = lax.Precision.HIGHEST


def extended(block, sides, width):
    for axis, dim in sides:
        count = lax.axis_size(axis)
        forward = [(i, i + 1) for i in range(count - 1)]
        forward.append((count - 1, 0))
        backward = [(target, source) for source, target in forward]
        low = lax.ppermute(
            lax.slice_in_dim(block, block.shape[dim] - width, None, axis=dim), axis, forward
        )
        high = lax.ppermute(lax.slice_in_dim(block, 0, width, axis=dim), axis, backward)
        block = jnp.concatenate([low, block, high], axis=dim)
    return block


def swap_faces(stack):
    along_x = extended(stack[0:2], (("gx", 0),), 1)
    along_y = extended(stack[2:4], (("gy", 0),), 1)
    along_z = extended(stack[4:6], (("gz", 0),), 1)
    return jnp.stack([along_x[0], along_x[3], along_y[0], along_y[3], along_z[0], along_z[3]])


def newton_inverse(matrices):
    diag_vals = jnp.diagonal(matrices, axis1=1, axis2=2)
    identity = jnp.eye(matrices.shape[1], dtype=jnp.float32)
    inverse = identity[None] / diag_vals[:, None, :]
    for sweep in range(NS_ITERS):
        product = jnp.einsum("fij,fjk->fik", matrices, inverse, precision=precise)
        inverse = 2.0 * inverse - jnp.einsum("fij,fjk->fik", inverse, product, precision=precise)
    return inverse


def right_factor(factor, image):
    return jax.scipy.linalg.solve_triangular(factor, image.T, lower=True).T


def subspace(own, partner, inverse, starts):
    basis = starts
    for sweep in range(SUB_ITERS):
        image = jnp.einsum("fij,fjc->fic", partner, basis, precision=precise)
        image = jnp.einsum("fij,fjc->fic", inverse, image, precision=precise)
        image = jnp.einsum("fij,fjc->fic", own, image, precision=precise)
        gram = jnp.einsum("fic,fid->fcd", image, image, precision=precise)
        factor = jnp.linalg.cholesky(gram)
        basis = jax.vmap(right_factor)(factor, image)
    return basis


def solve_one(matrix, rhs):
    factor = jnp.linalg.cholesky(matrix)
    return jax.scipy.linalg.cho_solve((factor, True), rhs)


def per_device(schur, start_block, resid, group_of):
    matrix_full = schur[0, 0, 0]
    order = matrix_full.shape[0]
    width = order // 6
    starts = start_block[0, 0, 0]
    ncon = starts.shape[2]
    coarse_n = 6 * ncon
    resid_one = resid[0, 0, 0]
    columns = resid_one.shape[1]
    own = jnp.stack(
        [matrix_full[f * width : (f + 1) * width, f * width : (f + 1) * width] for f in range(6)]
    )
    partner = swap_faces(own)
    inverse = newton_inverse(own + partner)
    basis = subspace(own, partner, inverse, starts)
    rows_grouped = matrix_full.reshape(order, 6, width)
    side = jnp.einsum("igj,gjc->igc", rows_grouped, basis, precision=precise).reshape(
        6, width, 6, ncon
    )
    coarse_local = jnp.einsum("fic,figd->fcgd", basis, side, precision=precise).reshape(
        coarse_n, coarse_n
    )
    rhs_local = jnp.einsum(
        "fic,fin->fcn", basis, resid_one.reshape(6, width, columns), precision=precise
    ).reshape(coarse_n, columns)
    linear = lax.axis_index("gy") * lax.axis_size("gz") + lax.axis_index("gz")
    plane = group_of.shape[0]
    groups = plane // GROUP_SIZE
    my_group = group_of[linear]
    picked = (jnp.arange(groups, dtype=jnp.int32) == my_group).astype(jnp.float32)
    total_matrix, total_rhs = lax.psum(
        (picked[:, None, None] * coarse_local[None], picked[:, None, None] * rhs_local[None]),
        ("gy", "gz"),
    )
    matrix = jnp.einsum("g,gab->ab", picked, total_matrix, precision=precise)
    rhs = jnp.einsum("g,gab->ab", picked, total_rhs, precision=precise)
    answer = solve_one(matrix, rhs)
    w_faces = jnp.einsum("fic,fcn->fin", basis, answer.reshape(6, ncon, columns), precision=precise)
    products = jnp.einsum("fij,fjn->fin", own, w_faces, precision=precise)
    partner_y = swap_faces(products)
    correction = jnp.einsum("fij,fjn->fin", inverse, products + partner_y, precision=precise)
    return correction.reshape(order, columns)[None, None, None]


def solution(mesh):
    in_specs = (
        P("gx", "gy", "gz", None, None),
        P("gx", "gy", "gz", None, None, None),
        P("gx", "gy", "gz", None, None),
        P(),
    )
    out_specs = P("gx", "gy", "gz", None, None)
    return jax.shard_map(
        per_device, mesh=mesh, in_specs=in_specs, out_specs=out_specs, check_vma=False
    )
```

profile of v0, /device:TPU:0, one launch (start us, length us, event | category | flops | bytes accessed | tf_op | source)
XLA Modules:
  0.0 303.3 jit_solution(11376283005890711318)
XLA Ops:
  6.5 2.3 slice_bitcast_fusion.1
  8.9 3.0 collective-permute-start
  11.9 2.0 collective-permute-start.1
  13.9 1.8 collective-permute-start.3
  15.7 1.7 collective-permute-start.4
  17.4 1.0 constant_dynamic-update-slice_fusion.5
  18.4 0.7 fusion.14
  19.1 1.0 constant_dynamic-update-slice_fusion.4
  20.1 1.0 constant_dynamic-update-slice_fusion.3
  21.1 1.0 constant_dynamic-update-slice_fusion.2
  22.0 1.0 constant_dynamic-update-slice_fusion.1
  23.0 1.0 constant_dynamic-update-slice_fusion
  24.0 0.7 dynamic_slice.3
  24.7 0.7 fusion.42
  25.4 9.6 %copy.29 = f32[1,1,1,1536,1536]{3,4,2,1,0:T(8,128)} copy(f32[1,1,1,1536,1536]{4,3,2,1,0:T(8,128)} %param.7) | data formatting | bytes 18874368 | tf_op args[0]
  35.3 1.0 constant_dynamic-update-slice_fusion.11
  36.3 1.0 constant_dynamic-update-slice_fusion.10
  37.2 1.0 constant_dynamic-update-slice_fusion.9
  38.2 1.0 constant_dynamic-update-slice_fusion.8
  39.2 1.0 constant_dynamic-update-slice_fusion.7
  40.2 2.6 collective-permute-done.5
  42.8 1.2 copy-done.5
  44.0 1.4 add.57
  45.3 17.5 %copy.23 = f32[6,256,256]{0,2,1:T(8,128)} copy(f32[6,256,256]{2,1,0:T(8,128)} %add.57) | data formatting | bytes 3145728 | tf_op jit(solution)/shard_map/add | solution.py:79
  62.9 2.3 gather_fusion
  65.3 3.1 %fusion = f32[6,256,256]{2,1,0:T(8,128)S(1)} fusion(f32[6,256,256]{2,1,0:T(8,128)} %add.57, f32[6,256]{1,0:T(8,128)S(1)} %copy.24, f32[256,256]{1,0:T(8,128)S(1)} %copy-done.7), kind=kOutput, calls=%fused_computation.4 | convolution fusion | flops 1208352768 | bytes 3414016 | tf_op jit(solution)/shard_map/fij,fjk->fik/dot_general | solution.py:40
  68.4 1.8 multiply_subtract_fusion.2
  70.3 1.7 fusion.46
  72.0 1.8 multiply_subtract_fusion.1
  73.7 1.7 fusion.47
  75.4 1.8 multiply_subtract_fusion
  77.2 1.8 fusion.21
  79.0 1.5 fusion.48
  80.5 1.5 fusion.49
  82.5 17.6 %custom-call.30 = f32[6,32,32]{2,1,0:T(8,128)S(1)} custom-call(f32[6,32,32]{2,1,0:T(8,128)S(1)} %fusion.28), custom_call_target="Cholesky" | custom-call | tf_op jit(solution)/shard_map/jit(cholesky)/cholesky | solution.py:56
  100.3 14.8 %custom-call.31 = f32[6,1,32,32]{2,3,1,0:T(8,128)S(1)} custom-call(f32[6,1,32,32]{3,2,1,0:T(8,128)S(1)} %select_bitcast_fusion.1), custom_call_target="InvertDiagBlocksLowerTriangular" | custom-call | tf_op jit(solution)/shard_map/vmap(jit(_solve_triangular))/triangular_solve | solution.py:46
  115.5 3.1 %fusion.51 = f32[6,256,32]{1,2,0:T(8,128)S(1)} fusion(f32[6,256,256]{2,1,0:T(8,128)} %copy-done.5, f32[6,32,256]{2,1,0:T(8,128)S(1)} %fusion.19), kind=kOutput, calls=%fused_computation.119 | convolution fusion | flops 150994944 | bytes 1966080 | tf_op jit(solution)/shard_map/fij,fjc->fic/dot_general | solution.py:52
  118.6 1.5 fusion.52
  120.1 1.5 fusion.53
  122.1 17.6 %custom-call.32 = f32[6,32,32]{2,1,0:T(8,128)S(1)} custom-call(f32[6,32,32]{2,1,0:T(8,128)S(1)} %fusion.26), custom_call_target="Cholesky" | custom-call | tf_op jit(solution)/shard_map/jit(cholesky)/cholesky | solution.py:56
  139.9 14.8 %custom-call.33 = f32[6,1,32,32]{2,3,1,0:T(8,128)S(1)} custom-call(f32[6,1,32,32]{3,2,1,0:T(8,128)S(1)} %select_bitcast_fusion), custom_call_target="InvertDiagBlocksLowerTriangular" | custom-call | tf_op jit(solution)/shard_map/vmap(jit(_solve_triangular))/triangular_solve | solution.py:46
  155.1 8.3 %fusion.55 = f32[6,32,1536]{2,1,0:T(8,128)S(1)} fusion(f32[6,32,256]{2,1,0:T(8,128)S(1)} %fusion.17, f32[1536,6,256]{0,2,1:T(8,128)} %bitcast.147), kind=kOutput, calls=%fused_computation.123 | convolution fusion | flops 905969664 | bytes 10813440 | tf_op jit(solution)/shard_map/igj,gjc->igc/dot_general | solution.py:82
  163.4 2.8 fusion.3
  167.3 0.8 broadcast_multiply_fusion
  168.2 0.8 broadcast_multiply_fusion.1
  169.0 52.8 %all-reduce.6.cloned.1.call-done = (f32[2,192,128]{2,1,0:T(8,128)}, f32[2,192,192]{2,1,0:T(8,128)}) async-done(((f32[2,192,128]{2,1,0:T(8,128)}, f32[2,192,192]{2,1,0:T(8,128)}), (f32[2,192,128]{2,1,0:T(8,128)}, f32[2,192,192]{2,1,0:T(8,128)})) %all-reduce.6.cloned.1.call-update) | async-done | bytes 491536 | tf_op jit(solution)/shard_map/psum | solution.py:96
  221.8 2.7 fusion.12
  224.7 11.7 %cholesky.79 = f32[128,128]{1,0:T(8,128)S(1)} custom-call(f32[128,128]{1,0:T(8,128)S(1)} %cholesky.189), custom_call_target="Cholesky" | custom-call | tf_op jit(solution)/shard_map/jit(cholesky)/cholesky | solution.py:62
  236.4 9.8 %custom-call.24 = f32[1,128,128]{1,2,0:T(8,128)S(1)} custom-call(f32[1,128,128]{2,1,0:T(8,128)S(1)} %get-tuple-element.42), custom_call_target="InvertDiagBlocksLowerTriangular" | custom-call | tf_op jit(solution)/shard_map/jit(cholesky)/cholesky | solution.py:62
  246.6 5.8 %cholesky.138 = f32[64,64]{1,0:T(8,128)S(1)} custom-call(f32[64,64]{1,0:T(8,128)S(1)} %convolution_subtract_fusion.2), custom_call_target="Cholesky" | custom-call | tf_op jit(solution)/shard_map/jit(cholesky)/cholesky | solution.py:62
  252.5 0.7 compare_reduce_fusion.2
  255.2 19.8 %custom-call.25 = f32[2,128,128]{1,2,0:T(8,128)S(1)} custom-call(f32[2,128,128]{2,1,0:T(8,128)S(1)} %pad_maximum_fusion), custom_call_target="InvertDiagBlocksLowerTriangular" | custom-call | tf_op jit(solution)/shard_map/jit(_cho_solve)/triangular_solve | solution.py:63
  275.1 1.2 fusion.23
  277.8 1.5 fusion.57
  279.3 1.5 fusion.58
  280.9 1.4 collective-permute-start.6
  282.3 2.5 collective-permute-start.7
  284.8 1.7 collective-permute-start.9
  286.5 0.7 collective-permute-start.10
  287.2 1.2 collective-permute-done.6
  288.5 0.8 collective-permute-start.11
  289.6 2.8 collective-permute-done.10
  292.4 1.4 collective-permute-done.11
  293.8 2.4 fusion.6
  (85 shorter events, 6.8 us)
Async XLA Ops:
  6.5 160.3 %copy-start = (f32[1,1,1,1536,128]{4,3,2,1,0:T(8,128)S(1)}, f32[1,1,1,1536,128]{4,3,2,1,0:T(8,128)}, u32[]{:S(2)}) copy-start(f32[1,1,1,1536,128]{4,3,2,1,0:T(8,128)} %param.9) | copy-start | bytes 2359300
  6.5 215.2 %all-reduce.6.cloned.1.call-start = ((), (), s32[]{:S(2)}) async-start(), calls=%async_computation | async-start | bytes 1179648 | tf_op jit(solution)/shard_map/psum | solution.py:96
  8.9 26.1 %collective-permute-start = (f32[1,256,256]{2,1,0:T(8,128)}, f32[1,256,256]{2,1,0:T(8,128)}, u32[]{:S(2)}, u32[]{:S(2)}) collective-permute-start(f32[1,256,256]{2,1,0:T(8,128)} %get-tuple-element.33), channel_id=1, source_target_pairs={{0,8},{8,16},{16,24},{24,0},{1,9},{9,17},{17,25},{25,1},{2,10},{10... | collective-permute-start | bytes 786440 | tf_op jit(solution)/shard_map/ppermute | solution.py:20
  11.9 24.4 %collective-permute-start.1 = (f32[1,256,256]{2,1,0:T(8,128)}, f32[1,256,256]{2,1,0:T(8,128)}, u32[]{:S(2)}, u32[]{:S(2)}) collective-permute-start(f32[1,256,256]{2,1,0:T(8,128)} %get-tuple-element.34), channel_id=1, source_target_pairs={{8,0},{16,8},{24,16},{0,24},{9,1},{17,9},{25,17},{1,25},{10,2},{18... | collective-permute-start | bytes 786440 | tf_op jit(solution)/shard_map/ppermute | solution.py:23
  13.9 23.3 %collective-permute-start.2 = (f32[1,256,256]{2,1,0:T(8,128)S(1)}, f32[1,256,256]{2,1,0:T(8,128)}, u32[]{:S(2)}, u32[]{:S(2)}) collective-permute-start(f32[1,256,256]{2,1,0:T(8,128)S(1)} %get-tuple-element.31), channel_id=1, source_target_pairs={{0,2},{2,4},{4,6},{6,0},{1,3},{3,5},{5,7},{7,1},{8,10},{10,12},{12... | collective-permute-start | bytes 786440 | tf_op jit(solution)/shard_map/ppermute | solution.py:20
  13.9 24.3 %collective-permute-start.3 = (f32[1,256,256]{2,1,0:T(8,128)S(1)}, f32[1,256,256]{2,1,0:T(8,128)}, u32[]{:S(2)}, u32[]{:S(2)}) collective-permute-start(f32[1,256,256]{2,1,0:T(8,128)S(1)} %get-tuple-element.32), channel_id=1, source_target_pairs={{2,0},{4,2},{6,4},{0,6},{3,1},{5,3},{7,5},{1,7},{10,8},{12,10},{14... | collective-permute-start | bytes 786440 | tf_op jit(solution)/shard_map/ppermute | solution.py:23
  15.7 23.5 %collective-permute-start.4 = (f32[1,256,256]{2,1,0:T(8,128)S(1)}, f32[1,256,256]{2,1,0:T(8,128)}, u32[]{:S(2)}, u32[]{:S(2)}) collective-permute-start(f32[1,256,256]{2,1,0:T(8,128)S(1)} %get-tuple-element.30), channel_id=1, source_target_pairs={{0,1},{1,0},{2,3},{3,2},{4,5},{5,4},{6,7},{7,6},{8,9},{9,8},{10,11... | collective-permute-start | bytes 786440 | tf_op jit(solution)/shard_map/ppermute | solution.py:20
  18.4 5.7 %copy-start.10 = (s32[8]{0:T(128)S(1)}, s32[8]{0:T(128)}, u32[]{:S(2)}) copy-start(s32[8]{0:T(128)} %param.10) | copy-start | bytes 100
  35.0 7.8 %collective-permute-start.5 = (f32[1,256,256]{2,1,0:T(8,128)S(1)}, f32[1,256,256]{2,1,0:T(8,128)S(1)}, u32[]{:S(2)}, u32[]{:S(2)}) collective-permute-start(f32[1,256,256]{2,1,0:T(8,128)S(1)} %get-tuple-element.29), channel_id=1, source_target_pairs={{1,0},{0,1},{3,2},{2,3},{5,4},{4,5},{7,6},{6,7},{9,8},{8,9},{11,10... | collective-permute-start | bytes 786440 | tf_op jit(solution)/shard_map/ppermute | solution.py:23
  42.8 1.2 copy-start.5
  45.3 20.0 %copy-start.7 = (f32[256,256]{1,0:T(8,128)S(1)}, f32[256,256]{1,0:T(8,128)}, u32[]{:S(2)}) copy-start(f32[256,256]{1,0:T(8,128)} %fusion.14) | copy-start | bytes 786436
  68.4 1.9 copy-start.1
  75.4 1.8 copy-start.6
  75.4 1.8 copy-start.8
  77.2 3.3 %copy-start.2 = (f32[6,256,256]{2,1,0:T(8,128)}, f32[6,256,256]{2,1,0:T(8,128)S(1)}, u32[]{:S(2)}) copy-start(f32[6,256,256]{2,1,0:T(8,128)S(1)} %multiply_subtract_fusion) | copy-start | bytes 4718596
  115.1 3.5 %copy-start.3 = (f32[6,256,256]{2,1,0:T(8,128)S(1)}, f32[6,256,256]{2,1,0:T(8,128)}, u32[]{:S(2)}) copy-start(f32[6,256,256]{2,1,0:T(8,128)} %copy-done.2) | copy-start | bytes 4718596
  224.5 50.6 %copy-start.9 = (f32[2,192,128]{2,1,0:T(8,128)S(1)}, f32[2,192,128]{2,1,0:T(8,128)}, u32[]{:S(2)}) copy-start(f32[2,192,128]{2,1,0:T(8,128)} %get-tuple-element.27) | copy-start | bytes 589828
  280.8 13.0 %copy-start.4 = (f32[6,256,256]{2,1,0:T(8,128)S(1)}, f32[6,256,256]{2,1,0:T(8,128)}, u32[]{:S(2)}) copy-start(f32[6,256,256]{2,1,0:T(8,128)} %copy-done.2) | copy-start | bytes 4718596
  280.9 7.6 %collective-permute-start.6 = (f32[1,256,128]{2,1,0:T(8,128)S(1)}, f32[1,256,128]{2,1,0:T(8,128)S(1)}, u32[]{:S(2)}, u32[]{:S(2)}) collective-permute-start(f32[1,256,128]{2,1,0:T(8,128)S(1)} %get-tuple-element.40), channel_id=1, source_target_pairs={{0,8},{8,16},{16,24},{24,0},{1,9},{9,17},{17,25},{25,1},{2,10},{10... | collective-permute-start | bytes 393224 | tf_op jit(solution)/shard_map/ppermute | solution.py:20
  282.3 6.9 %collective-permute-start.7 = (f32[1,256,128]{2,1,0:T(8,128)S(1)}, f32[1,256,128]{2,1,0:T(8,128)S(1)}, u32[]{:S(2)}, u32[]{:S(2)}) collective-permute-start(f32[1,256,128]{2,1,0:T(8,128)S(1)} %get-tuple-element.39), channel_id=1, source_target_pairs={{8,0},{16,8},{24,16},{0,24},{9,1},{17,9},{25,17},{1,25},{10,2},{18... | collective-permute-start | bytes 393224 | tf_op jit(solution)/shard_map/ppermute | solution.py:23
  284.8 4.8 %collective-permute-start.8 = (f32[1,256,128]{2,1,0:T(8,128)S(1)}, f32[1,256,128]{2,1,0:T(8,128)S(1)}, u32[]{:S(2)}, u32[]{:S(2)}) collective-permute-start(f32[1,256,128]{2,1,0:T(8,128)S(1)} %get-tuple-element.38), channel_id=1, source_target_pairs={{0,2},{2,4},{4,6},{6,0},{1,3},{3,5},{5,7},{7,1},{8,10},{10,12},{12... | collective-permute-start | bytes 393224 | tf_op jit(solution)/shard_map/ppermute | solution.py:20
  284.8 4.8 %collective-permute-start.9 = (f32[1,256,128]{2,1,0:T(8,128)S(1)}, f32[1,256,128]{2,1,0:T(8,128)S(1)}, u32[]{:S(2)}, u32[]{:S(2)}) collective-permute-start(f32[1,256,128]{2,1,0:T(8,128)S(1)} %get-tuple-element.37), channel_id=1, source_target_pairs={{2,0},{4,2},{6,4},{0,6},{3,1},{5,3},{7,5},{1,7},{10,8},{12,10},{14... | collective-permute-start | bytes 393224 | tf_op jit(solution)/shard_map/ppermute | solution.py:23
  286.5 5.9 %collective-permute-start.10 = (f32[1,256,128]{2,1,0:T(8,128)S(1)}, f32[1,256,128]{2,1,0:T(8,128)S(1)}, u32[]{:S(2)}, u32[]{:S(2)}) collective-permute-start(f32[1,256,128]{2,1,0:T(8,128)S(1)} %get-tuple-element.36), channel_id=1, source_target_pairs={{0,1},{1,0},{2,3},{3,2},{4,5},{5,4},{6,7},{7,6},{8,9},{9,8},{10,11... | collective-permute-start | bytes 393224 | tf_op jit(solution)/shard_map/ppermute | solution.py:20
  288.5 5.3 %collective-permute-start.11 = (f32[1,256,128]{2,1,0:T(8,128)S(1)}, f32[1,256,128]{2,1,0:T(8,128)S(1)}, u32[]{:S(2)}, u32[]{:S(2)}) collective-permute-start(f32[1,256,128]{2,1,0:T(8,128)S(1)} %get-tuple-element.35), channel_id=1, source_target_pairs={{1,0},{0,1},{3,2},{2,3},{5,4},{4,5},{7,6},{6,7},{9,8},{8,9},{11,10... | collective-permute-start | bytes 393224 | tf_op jit(solution)/shard_map/ppermute | solution.py:23
Sparse Core Ops, SparseCore 0:
  169.1 52.6 all-reduce.5
where the time goes:
time: 307 us; the launch traced here: 303 us
  other arithmetic  118 us (38%)
  waiting for transfers between devices  61.1 us (20%)
  matrix products  46.9 us (15%)
  local copies, waits for them, and re-layouts  45.4 us (15%)
  starting transfers between devices  15.9 us (5%)
  between operations  15.6 us (5%)
    psum x1, waiting for transfers between devices, per_device(): lax.psum((picked[:, None, None] * coarse_local[None], picked[:, None, Non...  52.8 us
    another operation x7, other arithmetic, subspace(): factor = jnp.linalg.cholesky(gram)  35.5 us
    another operation x5, other arithmetic, right_factor(): return jax.scipy.linalg.solve_triangular(factor, image.T, lower=True).T  29.7 us
    another operation x7, other arithmetic, solve_one(): factor = jnp.linalg.cholesky(matrix)  28.7 us
    unnamed x38, local copies, waits for them, and re-layouts  20.6 us
    another operation x7, other arithmetic, solve_one(): return jax.scipy.linalg.cho_solve((factor, True), rhs)  20 us
    add x1, local copies, waits for them, and re-layouts, per_device(): inverse = newton_inverse(own + partner)  17.5 us
    ppermute x6, starting transfers between devices, extended(): lax.ppermute(lax.slice_in_dim(block, 0, width, axis=dim), axis, backward)  9.04 us
  transfers between devices with their start and end apart: 13, of which 6 were waited for; matrix products, arithmetic and copies ran while one was open for 7% of the time, Pallas kernels for 0%

commit v1 on v0

v1 whole, which is shorter than its diff:
```python
import functools

import jax
import jax.numpy as jnp
from jax import lax
from jax.experimental import pallas as pl
from jax.experimental.pallas import tpu as pltpu
from jax.sharding import PartitionSpec as P

NS_ITERS = 3
SUB_ITERS = 2
GROUP_SIZE = 4
FACES = 6
AXES = ("gx", "gy", "gz")
LIMIT = 50 * 1024 * 1024

precise = lax.Precision.HIGHEST


def dot(left, right, dims=((1,), (0,))):
    return lax.dot_general(
        left, right, (dims, ((), ())), precision=precise, preferred_element_type=jnp.float32
    )


def iota(shape, dim):
    return lax.broadcasted_iota(jnp.int32, shape, dim)


def ring(axis):
    count = lax.axis_size(axis)
    forward = [(i, (i + 1) % count) for i in range(count)]
    backward = [(target, source) for source, target in forward]
    return forward, backward


def flipped(axis, bit):
    return [(i, i ^ bit) for i in range(lax.axis_size(axis))]


def face_slots(counts):
    slots = []
    arrays = 0
    for count in counts:
        if count == 2:
            slots += [(arrays, 0), (arrays, 1)]
            arrays += 1
        else:
            slots += [(arrays, None), (arrays + 1, None)]
            arrays += 2
    return slots, arrays


def swap(arrays, counts):
    slots, _ = face_slots(counts)
    got = []
    where = []
    for position, axis in enumerate(AXES):
        forward, backward = ring(axis)
        even, odd = slots[2 * position], slots[2 * position + 1]
        if counts[position] == 2:
            where += [(len(got), 1), (len(got), 0)]
            got.append(lax.ppermute(arrays[even[0]], axis, forward))
        else:
            where += [(len(got), None), (len(got) + 1, None)]
            got.append(lax.ppermute(arrays[odd[0]], axis, forward))
            got.append(lax.ppermute(arrays[even[0]], axis, backward))
    return got, where


def pick(refs, slot):
    array, part = slot
    return refs[array][...] if part is None else refs[array][part]


def put(refs, slot, value):
    array, part = slot
    if part is None:
        refs[array][...] = value
    else:
        refs[array][part] = value


def slot_shapes(counts, shape):
    shapes = []
    for count in counts:
        if count == 2:
            shapes.append(jax.ShapeDtypeStruct((2,) + shape, jnp.float32))
        else:
            shapes += [jax.ShapeDtypeStruct(shape, jnp.float32)] * 2
    return shapes


def vmem_specs(count):
    return [pl.BlockSpec(memory_space=pltpu.VMEM)] * count


def pack_kernel(slots, width, schur_ref, *refs):
    outs, blocks, sems = refs[:-2], refs[-2], refs[-1]
    half = width // 2
    copies = []
    for f in range(FACES):
        place = pl.ds(f * width, width)
        copy = pltpu.make_async_copy(schur_ref.at[place, place], blocks.at[f], sems.at[f])
        copy.start()
        copies.append(copy)
    row, col = iota((half, half), 0), iota((half, half), 1)
    for f in range(FACES):
        copies[f].wait()
        first = blocks[f, 0:half, 0:half]
        second = blocks[f, half:width, half:width]
        diag = jnp.sum(jnp.where(row == col, second, 0.0), axis=0, keepdims=True)
        mixed = jnp.where(row >= col, first, second)
        tail = jnp.broadcast_to(diag, (8, half))
        put(outs, slots[f], jnp.concatenate([blocks[f, half:width, 0:half], mixed, tail], axis=0))


def unpack(packed):
    half = packed.shape[1]
    row, col = iota((half, half), 0), iota((half, half), 1)
    low = packed[0:half]
    mixed = packed[half : 2 * half]
    flip = mixed.T
    first = jnp.where(row >= col, mixed, flip)
    second = jnp.where(row < col, mixed, flip)
    second = jnp.where(row == col, packed[2 * half : 2 * half + 1], second)
    return jnp.concatenate(
        [jnp.concatenate([first, low.T], axis=1), jnp.concatenate([low, second], axis=1)], axis=0
    )


def factor_inverses(grams):
    size = grams[0].shape[0]
    strips = size // 8
    state = []
    for gram in grams:
        whole = jnp.concatenate(
            [gram, jnp.where(iota((size, size), 0) == iota((size, size), 1), 1.0, 0.0)], axis=1
        )
        state.append([whole[8 * s : 8 * s + 8] for s in range(strips)])
    below = iota((8, 1), 0)
    for k in range(size):
        strip, line = k // 8, k % 8
        for work in state:
            row = work[strip][line : line + 1]
            scaled = row * (1.0 / row[:, k : k + 1])
            for s in range(strip, strips):
                column = work[s][:, k : k + 1]
                if s == strip:
                    if line == 7:
                        continue
                    column = jnp.where(below > line, column, 0.0)
                work[s] = work[s] - column * scaled
    results = []
    for work in state:
        parts = []
        for s in range(strips):
            place = iota((8, size), 0) + 8 * s == iota((8, size), 1)
            pivot = jnp.sum(jnp.where(place, work[s][:, :size], 0.0), axis=1, keepdims=True)
            parts.append(work[s][:, size:] * lax.rsqrt(pivot))
        results.append(jnp.concatenate(parts, axis=0))
    return results


def main_kernel(where, slots, arrays, width, schur_ref, *refs):
    inputs = refs[:arrays]
    starts_ref, resid_ref = refs[arrays : arrays + 2]
    inverse_ref, payload_ref = refs[arrays + 2 : arrays + 4]
    products = refs[arrays + 4 : -5]
    own_ref, upper_ref, partner_ref, own_sems, upper_sems = refs[-5:]
    ncon = starts_ref.shape[2]
    columns = resid_ref.shape[1]
    copies = []
    for f in range(FACES):
        place = pl.ds(f * width, width)
        copy = pltpu.make_async_copy(schur_ref.at[place, place], own_ref.at[f], own_sems.at[f])
        copy.start()
        copies.append(copy)
    strips = []
    for f in range(FACES - 1):
        rest = (FACES - 1 - f) * width
        copy = pltpu.make_async_copy(
            schur_ref.at[pl.ds(f * width, width), pl.ds((f + 1) * width, rest)],
            upper_ref.at[f, :, pl.ds((f + 1) * width, rest)],
            upper_sems.at[f],
        )
        copy.start()
        strips.append(copy)
    eye = iota((width, width), 0) == iota((width, width), 1)
    for f in range(FACES):
        partner_ref[f] = unpack(pick(inputs, where[f]))
    sums = []
    for f in range(FACES):
        copies[f].wait()
        total = own_ref[f] + partner_ref[f]
        diagonal = jnp.where(eye, total, 0.0)
        across = 1.0 / jnp.sum(diagonal, axis=0, keepdims=True)
        down = 1.0 / jnp.sum(diagonal, axis=1, keepdims=True)
        inverse_ref[f] = jnp.where(eye, 2.0 * across, 0.0) - down * total * across
        sums.append(total)
    for sweep in range(NS_ITERS - 1):
        for f in range(FACES):
            guess = inverse_ref[f]
            inverse_ref[f] = 2.0 * guess - dot(guess, dot(sums[f], guess))
    basis = [starts_ref[f] for f in range(FACES)]
    for sweep in range(SUB_ITERS):
        for f in range(FACES):
            image = dot(own_ref[f], dot(inverse_ref[f], dot(partner_ref[f], basis[f])))
            if sweep < SUB_ITERS - 1:
                image = image * lax.rsqrt(jnp.sum(image * image, axis=0, keepdims=True))
            basis[f] = image
    factors = factor_inverses([dot(b, b, ((0,), (0,))) for b in basis])
    basis = [dot(basis[f], factors[f], ((1,), (1,))) for f in range(FACES)]
    for f in range(FACES - 1):
        strips[f].wait()
    rows = []
    for f in range(FACES):
        product = dot(own_ref[f], basis[f])
        put(products, slots[f], product.T)
        side = [product]
        for g in range(f + 1, FACES):
            side.append(dot(upper_ref[f, :, g * width : (g + 1) * width], basis[g]))
        rows.append(dot(basis[f], jnp.concatenate(side, axis=1), ((0,), (0,))))
    half = FACES * ncon // 2
    gap = jnp.zeros((ncon, ncon), jnp.float32)
    for f in range(FACES // 2):
        payload_ref[f * ncon : (f + 1) * ncon] = jnp.concatenate(
            [rows[f], rows[FACES - 1 - f], gap], axis=1
        )
    for f in range(FACES):
        right = dot(basis[f], resid_ref[f * width : (f + 1) * width], ((0,), (0,)))
        side, place = divmod(f, FACES // 2)
        payload_ref[
            half + place * ncon : half + (place + 1) * ncon, side * columns : (side + 1) * columns
        ] = right


def spread_kernel(where, slots, arrays, *refs):
    mine, theirs = refs[:arrays], refs[arrays : 2 * arrays]
    inverse_ref, out_ref = refs[2 * arrays :]
    for f in range(FACES):
        both = jnp.concatenate([pick(mine, slots[f]), pick(theirs, where[f])], axis=0)
        out_ref[f] = dot(both, inverse_ref[f], ((1,), (1,)))


def solve_kernel(slots, ncon, total_ref, answer_ref, *outs):
    half = FACES * ncon // 2
    columns = answer_ref.shape[1]
    matrix = []
    right = []
    for f in range(FACES):
        if f < FACES // 2:
            line = total_ref[f * ncon : (f + 1) * ncon, 0 : (FACES - f) * ncon]
        else:
            other = FACES - 1 - f
            start = (FACES - other) * ncon
            line = total_ref[other * ncon : (other + 1) * ncon, start : start + (FACES - f) * ncon]
        side, place = divmod(f, FACES // 2)
        matrix.append(line)
        right.append(
            total_ref[
                half + place * ncon : half + (place + 1) * ncon,
                side * columns : (side + 1) * columns,
            ]
        )
    for b in range(FACES):
        (factor,) = factor_inverses([matrix[b][:, 0:ncon]])
        line = dot(factor, matrix[b])
        rhs = dot(factor, right[b])
        for i in range(b + 1, FACES):
            begin = (i - b) * ncon
            lead = line[:, begin : begin + ncon]
            matrix[i] = matrix[i] - dot(lead, line[:, begin:], ((0,), (0,)))
            right[i] = right[i] - dot(lead, rhs, ((0,), (0,)))
        line = dot(factor, line, ((0,), (0,)))
        rhs = dot(factor, rhs, ((0,), (0,)))
        matrix[b], right[b] = line, rhs
        for i in range(b):
            lead = matrix[i][:, (b - i) * ncon : (b - i + 1) * ncon]
            right[i] = right[i] - dot(lead, rhs)
            if b < FACES - 1:
                tail = matrix[i][:, (b - i + 1) * ncon :] - dot(lead, line[:, ncon:])
                matrix[i] = jnp.concatenate([matrix[i][:, : (b - i + 1) * ncon], tail], axis=1)
    for f in range(FACES):
        answer_ref[f * ncon : (f + 1) * ncon] = right[f]
        put(outs, slots[f], right[f])


def last_kernel(where, arrays, ncon, spread_ref, answer_ref, *refs):
    theirs, out_ref = refs[:arrays], refs[arrays]
    width = spread_ref.shape[2]
    for f in range(FACES):
        both = jnp.concatenate(
            [answer_ref[f * ncon : (f + 1) * ncon], pick(theirs, where[f])], axis=0
        )
        out_ref[f * width : (f + 1) * width] = dot(spread_ref[f], both, ((0,), (0,)))


def group_total(payload, group_of):
    rows, planes = lax.axis_size("gy"), lax.axis_size("gz")
    groups = group_of.shape[0] // GROUP_SIZE
    y, z = lax.axis_index("gy"), lax.axis_index("gz")
    mine = group_of[y * planes + z]
    if groups != 2 or rows & (rows - 1) or planes & (planes - 1):
        chosen = jnp.arange(groups, dtype=jnp.int32) == mine
        total = lax.psum(jnp.where(chosen[:, None, None], payload[None], 0.0), ("gy", "gz"))
        return lax.dynamic_index_in_dim(total, mine, 0, keepdims=False)
    core = y & 1
    theirs = group_of[(y ^ 1) * planes + z]
    other = lax.ppermute(payload, "gy", flipped("gy", 1))
    part = jnp.where(mine == core, payload, 0.0) + jnp.where(theirs == core, other, 0.0)
    bit = 2
    while bit < rows:
        part = part + lax.ppermute(part, "gy", flipped("gy", bit))
        bit *= 2
    bit = 1
    while bit < planes:
        part = part + lax.ppermute(part, "gz", flipped("gz", bit))
        bit *= 2
    swapped = lax.ppermute(part, "gy", flipped("gy", 1))
    return jnp.where(mine == core, part, swapped)


def per_device(schur, start_block, resid, group_of):
    matrix = schur[0, 0, 0]
    starts = start_block[0, 0, 0]
    right = resid[0, 0, 0]
    order, columns = right.shape
    width, ncon = starts.shape[1:]
    counts = [lax.axis_size(axis) for axis in AXES]
    slots, arrays = face_slots(counts)
    coarse = FACES * ncon
    params = pltpu.CompilerParams(vmem_limit_bytes=LIMIT)
    anywhere = pl.BlockSpec(memory_space=pl.ANY)

    packed = pl.pallas_call(
        functools.partial(pack_kernel, slots, width),
        out_shape=slot_shapes(counts, (width + 8, width // 2)),
        in_specs=[anywhere],
        out_specs=vmem_specs(arrays),
        scratch_shapes=[
            pltpu.VMEM((FACES, width, width), jnp.float32),
            pltpu.SemaphoreType.DMA((FACES,)),
        ],
        compiler_params=params,
    )(matrix)
    got, where = swap(packed, counts)

    inverse, payload, *products = pl.pallas_call(
        functools.partial(main_kernel, where, slots, arrays, width),
        out_shape=[
            jax.ShapeDtypeStruct((FACES, width, width), jnp.float32),
            jax.ShapeDtypeStruct((coarse, 2 * columns), jnp.float32),
        ]
        + slot_shapes(counts, (ncon, width)),
        in_specs=[anywhere] + vmem_specs(arrays + 2),
        out_specs=vmem_specs(arrays + 2),
        scratch_shapes=[
            pltpu.VMEM((FACES, width, width), jnp.float32),
            pltpu.VMEM((FACES - 1, width, order), jnp.float32),
            pltpu.VMEM((FACES, width, width), jnp.float32),
            pltpu.SemaphoreType.DMA((FACES,)),
            pltpu.SemaphoreType.DMA((FACES - 1,)),
        ],
        compiler_params=params,
    )(matrix, *got, starts, right)

    total = group_total(payload, group_of)
    their_products, _ = swap(products, counts)
    spread = pl.pallas_call(
        functools.partial(spread_kernel, where, slots, arrays),
        out_shape=jax.ShapeDtypeStruct((FACES, 2 * ncon, width), jnp.float32),
        in_specs=vmem_specs(2 * arrays + 1),
        out_specs=pl.BlockSpec(memory_space=pltpu.VMEM),
        compiler_params=params,
    )(*products, *their_products, inverse)

    answer, *answers = pl.pallas_call(
        functools.partial(solve_kernel, slots, ncon),
        out_shape=[jax.ShapeDtypeStruct((coarse, columns), jnp.float32)]
        + slot_shapes(counts, (ncon, columns)),
        in_specs=vmem_specs(1),
        out_specs=vmem_specs(arrays + 1),
        compiler_params=params,
    )(total)
    their_answers, _ = swap(answers, counts)

    correction = pl.pallas_call(
        functools.partial(last_kernel, where, arrays, ncon),
        out_shape=jax.ShapeDtypeStruct((order, columns), jnp.float32),
        in_specs=vmem_specs(2 + arrays),
        out_specs=pl.BlockSpec(memory_space=pltpu.VMEM),
        compiler_params=params,
    )(spread, answer, *their_answers)
    return correction[None, None, None]


def solution(mesh):
    in_specs = (
        P("gx", "gy", "gz", None, None),
        P("gx", "gy", "gz", None, None, None),
        P("gx", "gy", "gz", None, None),
        P(),
    )
    out_specs = P("gx", "gy", "gz", None, None)
    return jax.shard_map(
        per_device, mesh=mesh, in_specs=in_specs, out_specs=out_specs, check_vma=False
    )
```

time: 307 us -> 99.1 us (0.32); the launches traced: 303 us -> 98.9 us
  other arithmetic: 118 us -> 0.11 us
  Pallas kernels: 0 us -> 56 us
  matrix products: 46.9 us -> 0 us
  waiting for transfers between devices: 61.1 us -> 14.6 us
  local copies, waits for them, and re-layouts: 45.4 us -> 2.33 us
  between operations: 15.6 us -> 1.42 us
  starting transfers between devices: 15.9 us -> 24.4 us
    another operation x26 -> x0, other arithmetic: 114 us -> none  [the longest x7 35.5 us: subspace(): factor = jnp.linalg.cholesky(gram)]
    pallas_call x0 -> x5, Pallas kernels: none -> 56 us  [the longest x1 31.3 us: per_device(): pl.pallas_call(functools.partial(main_kernel, where, slots, arrays, width...]
    psum x1 -> x0, waiting for transfers between devices: 52.8 us -> none  [per_device(): lax.psum((picked[:, None, None] * coarse_local[None], picked[:, None, Non...]
    dot_general x22 -> x0, matrix products: 44.4 us -> none  [the longest x1 8.32 us: per_device(): jnp.einsum('igj,gjc->igc', rows_grouped, basis, precision=precise)]
    unnamed x38 -> x9, local copies, waits for them, and re-layouts: 20.6 us -> 1.68 us
    add x1 -> x0, local copies, waits for them, and re-layouts: 17.5 us -> none  [per_device(): inverse = newton_inverse(own + partner)]
    ppermute x12 -> x19, starting transfers between devices: 15.9 us -> 24.4 us  [the longest x6 13.6 us: swap(): got.append(lax.ppermute(arrays[even[0]], axis, backward))]
    ppermute x12 -> x19, waiting for transfers between devices: 8.34 us -> 14.6 us  [the longest x1 5.69 us: group_total(): part = part + lax.ppermute(part, 'gy', flipped('gy', bit))]
  transfers between devices with their start and end apart: 13 -> 19, of which waited for: 6 -> 4; matrix products, arithmetic and copies ran while one was open for 7% -> 1% of each run, Pallas kernels for 0% -> 22%
where the time goes in v1:
time: 99.1 us; the launch traced here: 98.9 us
  Pallas kernels  56 us (57%)
  starting transfers between devices  24.4 us (25%)
  waiting for transfers between devices  14.6 us (15%)
  local copies, waits for them, and re-layouts  2.33 us (2%)
  between operations  1.42 us (1%)
    pallas_call x1, Pallas kernels, per_device(): pl.pallas_call(functools.partial(main_kernel, where, slots, arrays, width...  31.3 us
    pallas_call x1, Pallas kernels, per_device(): pl.pallas_call(functools.partial(solve_kernel, slots, ncon), out_shape=[j...  19.9 us
    ppermute x6, starting transfers between devices, swap(): got.append(lax.ppermute(arrays[even[0]], axis, backward))  13.6 us
    ppermute x1, waiting for transfers between devices, group_total(): part = part + lax.ppermute(part, 'gy', flipped('gy', bit))  5.69 us
    ppermute x1, waiting for transfers between devices, group_total(): part = part + lax.ppermute(part, 'gz', flipped('gz', bit))  5.49 us
    ppermute x3, starting transfers between devices, swap(): got.append(lax.ppermute(arrays[even[0]], axis, forward))  5.13 us
    ppermute x6, starting transfers between devices, swap(): got.append(lax.ppermute(arrays[odd[0]], axis, forward))  3.12 us
    ppermute x6, waiting for transfers between devices, swap(): got.append(lax.ppermute(arrays[odd[0]], axis, forward))  2.48 us
  transfers between devices with their start and end apart: 19, of which 4 were waited for; matrix products, arithmetic and copies ran while one was open for 1% of the time, Pallas kernels for 22%

profile of v1, /device:TPU:0, one launch (start us, length us, event | category | flops | bytes accessed | tf_op | source)
XLA Modules:
  0.0 98.9 jit_solution(14675988350472677625)
XLA Ops:
  0.0 0.0 copy-start.2
  0.0 0.0 copy-start.1
  0.0 0.0 copy-start.3
  0.0 1.5 %shard_map.46 = (f32[264,128]{1,0:T(8,128)S(1)}, f32[264,128]{1,0:T(8,128)S(1)}, f32[264,128]{1,0:T(8,128)S(1)}, f32[264,128]{1,0:T(8,128)S(1)}, f32[2,264,128]{2,1,0:T(8,128)S(1)}) custom-call(f32[1536,1536]{1,0:T(8,128)} %bitcast.8), custom_call_target="tpu_custom_call" | custom-call | tf_op jit(solution)/shard_map/pallas_call | solution.py:336
  1.5 3.0 %collective-permute-start.4 = (f32[2,264,128]{2,1,0:T(8,128)S(1)}, f32[2,264,128]{2,1,0:T(8,128)S(1)}, u32[]{:S(2)}, u32[]{:S(2)}) collective-permute-start(f32[2,264,128]{2,1,0:T(8,128)S(1)} %get-tuple-element.27), channel_id=1, source_target_pairs={{0,1},{1,0},{2,3},{3,2},{4,5},{5,4},{6,7},{7,6},{8,9},{9,8},{10,11... | collective-permute-start | bytes 811016 | tf_op jit(solution)/shard_map/ppermute | solution.py:63
  4.6 1.6 %collective-permute-start = (f32[264,128]{1,0:T(8,128)S(1)}, f32[264,128]{1,0:T(8,128)S(1)}, u32[]{:S(2)}, u32[]{:S(2)}) collective-permute-start(f32[264,128]{1,0:T(8,128)S(1)} %get-tuple-element.23), channel_id=1, source_target_pairs={{0,8},{8,16},{16,24},{24,0},{1,9},{9,17},{17,25},{25,1},{2,10},{10... | collective-permute-start | bytes 405512 | tf_op jit(solution)/shard_map/ppermute | solution.py:66
  6.1 2.2 %collective-permute-start.1 = (f32[264,128]{1,0:T(8,128)S(1)}, f32[264,128]{1,0:T(8,128)S(1)}, u32[]{:S(2)}, u32[]{:S(2)}) collective-permute-start(f32[264,128]{1,0:T(8,128)S(1)} %get-tuple-element.24), channel_id=1, source_target_pairs={{8,0},{16,8},{24,16},{0,24},{9,1},{17,9},{25,17},{1,25},{10,2},{18... | collective-permute-start | bytes 405512 | tf_op jit(solution)/shard_map/ppermute | solution.py:67
  8.4 0.0 collective-permute-start.2
  8.4 1.7 %collective-permute-start.3 = (f32[264,128]{1,0:T(8,128)S(1)}, f32[264,128]{1,0:T(8,128)S(1)}, u32[]{:S(2)}, u32[]{:S(2)}) collective-permute-start(f32[264,128]{1,0:T(8,128)S(1)} %get-tuple-element.26), channel_id=1, source_target_pairs={{2,0},{4,2},{6,4},{0,6},{3,1},{5,3},{7,5},{1,7},{10,8},{12,10},{14... | collective-permute-start | bytes 405512 | tf_op jit(solution)/shard_map/ppermute | solution.py:67
  10.1 0.0 copy-done.2
  10.1 0.3 copy.5
  10.4 2.5 %collective-permute-done.refs_0_ = f32[264,128]{1,0:T(8,128)S(1)} collective-permute-done((f32[264,128]{1,0:T(8,128)S(1)}, f32[264,128]{1,0:T(8,128)S(1)}, u32[]{:S(2)}, u32[]{:S(2)}) %collective-permute-start) | collective-permute-done | bytes 135200 | tf_op jit(solution)/shard_map/ppermute | solution.py:66
  12.9 0.9 collective-permute-done.1.refs_1_
  13.8 0.0 collective-permute-done.2.refs_2_
  13.8 0.0 collective-permute-done.3.refs_3_
  13.8 0.0 collective-permute-done.4.refs_4_
  13.8 0.0 copy-done.1
  13.8 31.3 %shard_map.47 = (f32[6,256,256]{2,1,0:T(8,128)}, f32[192,256]{1,0:T(8,128)S(1)}, f32[32,256]{1,0:T(8,128)S(1)}, f32[32,256]{1,0:T(8,128)S(1)}, f32[32,256]{1,0:T...) custom-call(f32[1536,1536]{1,0:T(8,128)} %bitcast.9, f32[264,128]{1,0:T(8,128)S(1)} %collective-permute-done.refs_0_, ...), custom_call_target="tpu_custom_call" | custom-call | tf_op jit(solution)/shard_map/pallas_call | solution.py:349
  45.1 0.7 collective-permute-start.10
  45.8 0.0 copy-done.3
  45.8 0.7 fusion
  47.7 0.0 collective-permute-done.10
  47.8 1.2 %collective-permute-start.11 = (f32[192,256]{1,0:T(8,128)S(1)}, f32[192,256]{1,0:T(8,128)S(1)}, u32[]{:S(2)}, u32[]{:S(2)}) collective-permute-start(f32[192,256]{1,0:T(8,128)S(1)} %select_add_fusion), channel_id=1, source_target_pairs={{0,4},{2,6},{4,0},{6,2},{1,5},{3,7},{5,1},{7,3},{8,12},{10,14},{12... | collective-permute-start | bytes 589832 | tf_op jit(solution)/shard_map/ppermute | solution.py:314
  49.0 5.7 %collective-permute-done.11 = f32[192,256]{1,0:T(8,128)S(1)} collective-permute-done((f32[192,256]{1,0:T(8,128)S(1)}, f32[192,256]{1,0:T(8,128)S(1)}, u32[]{:S(2)}, u32[]{:S(2)}) %collective-permute-start.11) | collective-permute-done | bytes 196640 | tf_op jit(solution)/shard_map/ppermute | solution.py:314
  54.7 0.6 collective-permute-start.12
  55.3 5.5 %collective-permute-done.12 = f32[192,256]{1,0:T(8,128)S(1)} collective-permute-done((f32[192,256]{1,0:T(8,128)S(1)}, f32[192,256]{1,0:T(8,128)S(1)}, u32[]{:S(2)}, u32[]{:S(2)}) %collective-permute-start.12) | collective-permute-done | bytes 196640 | tf_op jit(solution)/shard_map/ppermute | solution.py:318
  60.8 0.1 collective-permute-start.13
  60.9 1.5 %collective-permute-start.5 = (f32[32,256]{1,0:T(8,128)S(1)}, f32[32,256]{1,0:T(8,128)S(1)}, u32[]{:S(2)}, u32[]{:S(2)}) collective-permute-start(f32[32,256]{1,0:T(8,128)S(1)} %get-tuple-element.29.refs_1_), channel_id=1, source_target_pairs={{0,8},{8,16},{16,24},{24,0},{1,9},{9,17},{17,25},{25,1},{2,10},{10... | collective-permute-start | bytes 98312 | tf_op jit(solution)/shard_map/ppermute | solution.py:66
  62.4 2.3 %collective-permute-start.6 = (f32[32,256]{1,0:T(8,128)S(1)}, f32[32,256]{1,0:T(8,128)S(1)}, u32[]{:S(2)}, u32[]{:S(2)}) collective-permute-start(f32[32,256]{1,0:T(8,128)S(1)} %get-tuple-element.28.refs_0_), channel_id=1, source_target_pairs={{8,0},{16,8},{24,16},{0,24},{9,1},{17,9},{25,17},{1,25},{10,2},{18... | collective-permute-start | bytes 98312 | tf_op jit(solution)/shard_map/ppermute | solution.py:67
  64.8 0.0 collective-permute-start.7
  64.8 1.7 %collective-permute-start.8 = (f32[32,256]{1,0:T(8,128)S(1)}, f32[32,256]{1,0:T(8,128)S(1)}, u32[]{:S(2)}, u32[]{:S(2)}) collective-permute-start(f32[32,256]{1,0:T(8,128)S(1)} %get-tuple-element.30.refs_2_), channel_id=1, source_target_pairs={{2,0},{4,2},{6,4},{0,6},{3,1},{5,3},{7,5},{1,7},{10,8},{12,10},{14... | collective-permute-start | bytes 98312 | tf_op jit(solution)/shard_map/ppermute | solution.py:67
  66.5 0.0 collective-permute-done.13
  66.5 0.5 collective-permute-start.9
  67.1 19.9 %shard_map.49 = (f32[192,128]{1,0:T(8,128)S(1)}, f32[32,128]{1,0:T(8,128)S(1)}, f32[32,128]{1,0:T(8,128)S(1)}, f32[32,128]{1,0:T(8,128)S(1)}, f32[32,128]{1,0:T(8,128)S(1)}, /*index=5*/f32[2,32,128]{2,1,0:T(8,128)S(1)}) custom-call(f32[192,256]{1,0:T(8,128)S(1)} %broadcast_select_fusion.total_ref), custom_call_target="tpu_custom_call" | custom-call | tf_op jit(solution)/shard_map/pallas_call | solution.py:378
  87.0 0.0 collective-permute-done.5.refs_5_
  87.0 1.6 %collective-permute-start.18 = (f32[2,32,128]{2,1,0:T(8,128)S(1)}, f32[2,32,128]{2,1,0:T(8,128)S(1)}, u32[]{:S(2)}, u32[]{:S(2)}) collective-permute-start(f32[2,32,128]{2,1,0:T(8,128)S(1)} %get-tuple-element.40), channel_id=1, source_target_pairs={{0,1},{1,0},{2,3},{3,2},{4,5},{5,4},{6,7},{7,6},{8,9},{9,8},{10,11... | collective-permute-start | bytes 98312 | tf_op jit(solution)/shard_map/ppermute | solution.py:63
  88.6 0.0 collective-permute-done.6.refs_6_
  88.6 0.0 collective-permute-start.14
  88.6 0.0 collective-permute-done.7.refs_7_
  88.6 3.8 %collective-permute-start.15 = (f32[32,128]{1,0:T(8,128)S(1)}, f32[32,128]{1,0:T(8,128)S(1)}, u32[]{:S(2)}, u32[]{:S(2)}) collective-permute-start(f32[32,128]{1,0:T(8,128)S(1)} %get-tuple-element.37), channel_id=1, source_target_pairs={{8,0},{16,8},{24,16},{0,24},{9,1},{17,9},{25,17},{1,25},{10,2},{18... | collective-permute-start | bytes 49160 | tf_op jit(solution)/shard_map/ppermute | solution.py:67
  92.4 0.0 collective-permute-done.8.refs_8_
  92.4 0.0 collective-permute-start.16
  92.4 0.0 collective-permute-done.9.refs_9_
  92.4 1.7 %collective-permute-start.17 = (f32[32,128]{1,0:T(8,128)S(1)}, f32[32,128]{1,0:T(8,128)S(1)}, u32[]{:S(2)}, u32[]{:S(2)}) collective-permute-start(f32[32,128]{1,0:T(8,128)S(1)} %get-tuple-element.39), channel_id=1, source_target_pairs={{2,0},{4,2},{6,4},{0,6},{3,1},{5,3},{7,5},{1,7},{10,8},{12,10},{14... | collective-permute-start | bytes 49160 | tf_op jit(solution)/shard_map/ppermute | solution.py:67
  94.1 0.0 copy-start
  94.2 1.4 %copy-done = f32[6,256,256]{2,1,0:T(8,128)S(1)} copy-done((f32[6,256,256]{2,1,0:T(8,128)S(1)}, f32[6,256,256]{2,1,0:T(8,128)}, u32[]{:S(2)}) %copy-start) | copy-done | bytes 1572888
  95.6 1.6 %shard_map.48.spread_ref = f32[6,64,256]{2,1,0:T(8,128)S(1)} custom-call(f32[32,256]{1,0:T(8,128)S(1)} %get-tuple-element.28.refs_0_, f32[32,256]{1,0:T(8,128)S(1)} %get-tuple-element.29.refs_1_, f32[32,256]{1,0:T(8,128)S(1)} %get-tuple-element.30.refs_2_, f32[32,256]{1,0:T(8,128)S(1)} %get-tuple-element.31.refs_3_, ...), custom_call_target="tpu_custom_call" | custom-call | tf_op jit(solution)/shard_map/pallas_call | solution.py:370
  97.1 0.0 collective-permute-done.14.refs_0_
  97.1 0.0 collective-permute-done.15.refs_1_
  97.1 0.0 collective-permute-done.16.refs_2_
  97.2 0.0 collective-permute-done.17.refs_3_
  97.2 0.0 collective-permute-done.18.refs_4_
  97.2 1.7 %shard_map.50 = f32[1536,128]{1,0:T(8,128)} custom-call(f32[6,64,256]{2,1,0:T(8,128)S(1)} %shard_map.48.spread_ref, f32[192,128]{1,0:T(8,128)S(1)} %get-tuple-element.35.answer_ref, f32[32,128]{1,0:T(8,128)S(1)} %collective-permute-done.14.refs_0_, f32[32,128]{1,0:T(8,128)S(1)} %collective-permute-done.15.refs_1_, ...), custom_call_target="tpu_custom_call" | custom-call | tf_op jit(solution)/shard_map/pallas_call | solution.py:388
  (4 shorter events, 0.1 us)
Async XLA Ops:
  0.0 10.1 %copy-start.2 = (f32[1,1,1,6,256,32]{4,5,3,2,1,0:T(8,128)S(1)}, f32[1,1,1,6,256,32]{4,5,3,2,1,0:T(8,128)}, u32[]{:S(2)}) copy-start(f32[1,1,1,6,256,32]{4,5,3,2,1,0:T(8,128)} %param.5) | copy-start | bytes 589828
  0.0 13.8 %copy-start.1 = (f32[1,1,1,1536,128]{4,3,2,1,0:T(8,128)S(1)}, f32[1,1,1,1536,128]{4,3,2,1,0:T(8,128)}, u32[]{:S(2)}) copy-start(f32[1,1,1,1536,128]{4,3,2,1,0:T(8,128)} %param.6) | copy-start | bytes 2359300
  0.0 45.8 %copy-start.3 = (s32[8]{0:T(128)S(1)}, s32[8]{0:T(128)}, u32[]{:S(2)}) copy-start(s32[8]{0:T(128)} %param.7) | copy-start | bytes 100
  1.5 12.3 %collective-permute-start.4 = (f32[2,264,128]{2,1,0:T(8,128)S(1)}, f32[2,264,128]{2,1,0:T(8,128)S(1)}, u32[]{:S(2)}, u32[]{:S(2)}) collective-permute-start(f32[2,264,128]{2,1,0:T(8,128)S(1)} %get-tuple-element.27), channel_id=1, source_target_pairs={{0,1},{1,0},{2,3},{3,2},{4,5},{5,4},{6,7},{7,6},{8,9},{9,8},{10,11... | collective-permute-start | bytes 811016 | tf_op jit(solution)/shard_map/ppermute | solution.py:63
  4.6 8.3 %collective-permute-start = (f32[264,128]{1,0:T(8,128)S(1)}, f32[264,128]{1,0:T(8,128)S(1)}, u32[]{:S(2)}, u32[]{:S(2)}) collective-permute-start(f32[264,128]{1,0:T(8,128)S(1)} %get-tuple-element.23), channel_id=1, source_target_pairs={{0,8},{8,16},{16,24},{24,0},{1,9},{9,17},{17,25},{25,1},{2,10},{10... | collective-permute-start | bytes 405512 | tf_op jit(solution)/shard_map/ppermute | solution.py:66
  6.1 7.7 %collective-permute-start.1 = (f32[264,128]{1,0:T(8,128)S(1)}, f32[264,128]{1,0:T(8,128)S(1)}, u32[]{:S(2)}, u32[]{:S(2)}) collective-permute-start(f32[264,128]{1,0:T(8,128)S(1)} %get-tuple-element.24), channel_id=1, source_target_pairs={{8,0},{16,8},{24,16},{0,24},{9,1},{17,9},{25,17},{1,25},{10,2},{18... | collective-permute-start | bytes 405512 | tf_op jit(solution)/shard_map/ppermute | solution.py:67
  8.4 5.4 %collective-permute-start.2 = (f32[264,128]{1,0:T(8,128)S(1)}, f32[264,128]{1,0:T(8,128)S(1)}, u32[]{:S(2)}, u32[]{:S(2)}) collective-permute-start(f32[264,128]{1,0:T(8,128)S(1)} %get-tuple-element.25), channel_id=1, source_target_pairs={{0,2},{2,4},{4,6},{6,0},{1,3},{3,5},{5,7},{7,1},{8,10},{10,12},{12... | collective-permute-start | bytes 405512 | tf_op jit(solution)/shard_map/ppermute | solution.py:66
  8.4 5.4 %collective-permute-start.3 = (f32[264,128]{1,0:T(8,128)S(1)}, f32[264,128]{1,0:T(8,128)S(1)}, u32[]{:S(2)}, u32[]{:S(2)}) collective-permute-start(f32[264,128]{1,0:T(8,128)S(1)} %get-tuple-element.26), channel_id=1, source_target_pairs={{2,0},{4,2},{6,4},{0,6},{3,1},{5,3},{7,5},{1,7},{10,8},{12,10},{14... | collective-permute-start | bytes 405512 | tf_op jit(solution)/shard_map/ppermute | solution.py:67
  45.1 2.6 %collective-permute-start.10 = (f32[192,256]{1,0:T(8,128)S(1)}, f32[192,256]{1,0:T(8,128)S(1)}, u32[]{:S(2)}, u32[]{:S(2)}) collective-permute-start(f32[192,256]{1,0:T(8,128)S(1)} %get-tuple-element.34), channel_id=1, source_target_pairs={{0,2},{2,0},{4,6},{6,4},{1,3},{3,1},{5,7},{7,5},{8,10},{10,8},{12,... | collective-permute-start | bytes 589832 | tf_op jit(solution)/shard_map/ppermute | solution.py:310
  47.8 6.9 %collective-permute-start.11 = (f32[192,256]{1,0:T(8,128)S(1)}, f32[192,256]{1,0:T(8,128)S(1)}, u32[]{:S(2)}, u32[]{:S(2)}) collective-permute-start(f32[192,256]{1,0:T(8,128)S(1)} %select_add_fusion), channel_id=1, source_target_pairs={{0,4},{2,6},{4,0},{6,2},{1,5},{3,7},{5,1},{7,3},{8,12},{10,14},{12... | collective-permute-start | bytes 589832 | tf_op jit(solution)/shard_map/ppermute | solution.py:314
  54.7 6.1 %collective-permute-start.12 = (f32[192,256]{1,0:T(8,128)S(1)}, f32[192,256]{1,0:T(8,128)S(1)}, u32[]{:S(2)}, u32[]{:S(2)}) collective-permute-start(f32[192,256]{1,0:T(8,128)S(1)} %add.26), channel_id=1, source_target_pairs={{0,1},{1,0},{2,3},{3,2},{4,5},{5,4},{6,7},{7,6},{8,9},{9,8},{10,11... | collective-permute-start | bytes 589832 | tf_op jit(solution)/shard_map/ppermute | solution.py:318
  60.8 5.7 %collective-permute-start.13 = (f32[192,256]{1,0:T(8,128)S(1)}, f32[192,256]{1,0:T(8,128)S(1)}, u32[]{:S(2)}, u32[]{:S(2)}) collective-permute-start(f32[192,256]{1,0:T(8,128)S(1)} %add.27), channel_id=1, source_target_pairs={{0,2},{2,0},{4,6},{6,4},{1,3},{3,1},{5,7},{7,5},{8,10},{10,8},{12,... | collective-permute-start | bytes 589832 | tf_op jit(solution)/shard_map/ppermute | solution.py:320
  60.9 26.1 %collective-permute-start.5 = (f32[32,256]{1,0:T(8,128)S(1)}, f32[32,256]{1,0:T(8,128)S(1)}, u32[]{:S(2)}, u32[]{:S(2)}) collective-permute-start(f32[32,256]{1,0:T(8,128)S(1)} %get-tuple-element.29.refs_1_), channel_id=1, source_target_pairs={{0,8},{8,16},{16,24},{24,0},{1,9},{9,17},{17,25},{25,1},{2,10},{10... | collective-permute-start | bytes 98312 | tf_op jit(solution)/shard_map/ppermute | solution.py:66
  62.4 26.1 %collective-permute-start.6 = (f32[32,256]{1,0:T(8,128)S(1)}, f32[32,256]{1,0:T(8,128)S(1)}, u32[]{:S(2)}, u32[]{:S(2)}) collective-permute-start(f32[32,256]{1,0:T(8,128)S(1)} %get-tuple-element.28.refs_0_), channel_id=1, source_target_pairs={{8,0},{16,8},{24,16},{0,24},{9,1},{17,9},{25,17},{1,25},{10,2},{18... | collective-permute-start | bytes 98312 | tf_op jit(solution)/shard_map/ppermute | solution.py:67
  64.8 23.8 %collective-permute-start.7 = (f32[32,256]{1,0:T(8,128)S(1)}, f32[32,256]{1,0:T(8,128)S(1)}, u32[]{:S(2)}, u32[]{:S(2)}) collective-permute-start(f32[32,256]{1,0:T(8,128)S(1)} %get-tuple-element.31.refs_3_), channel_id=1, source_target_pairs={{0,2},{2,4},{4,6},{6,0},{1,3},{3,5},{5,7},{7,1},{8,10},{10,12},{12... | collective-permute-start | bytes 98312 | tf_op jit(solution)/shard_map/ppermute | solution.py:66
  64.8 27.6 %collective-permute-start.8 = (f32[32,256]{1,0:T(8,128)S(1)}, f32[32,256]{1,0:T(8,128)S(1)}, u32[]{:S(2)}, u32[]{:S(2)}) collective-permute-start(f32[32,256]{1,0:T(8,128)S(1)} %get-tuple-element.30.refs_2_), channel_id=1, source_target_pairs={{2,0},{4,2},{6,4},{0,6},{3,1},{5,3},{7,5},{1,7},{10,8},{12,10},{14... | collective-permute-start | bytes 98312 | tf_op jit(solution)/shard_map/ppermute | solution.py:67
  66.5 25.9 %collective-permute-start.9 = (f32[2,32,256]{2,1,0:T(8,128)S(1)}, f32[2,32,256]{2,1,0:T(8,128)S(1)}, u32[]{:S(2)}, u32[]{:S(2)}) collective-permute-start(f32[2,32,256]{2,1,0:T(8,128)S(1)} %get-tuple-element.32.refs_4_), channel_id=1, source_target_pairs={{0,1},{1,0},{2,3},{3,2},{4,5},{5,4},{6,7},{7,6},{8,9},{9,8},{10,11... | collective-permute-start | bytes 196616 | tf_op jit(solution)/shard_map/ppermute | solution.py:63
  87.0 10.2 %collective-permute-start.18 = (f32[2,32,128]{2,1,0:T(8,128)S(1)}, f32[2,32,128]{2,1,0:T(8,128)S(1)}, u32[]{:S(2)}, u32[]{:S(2)}) collective-permute-start(f32[2,32,128]{2,1,0:T(8,128)S(1)} %get-tuple-element.40), channel_id=1, source_target_pairs={{0,1},{1,0},{2,3},{3,2},{4,5},{5,4},{6,7},{7,6},{8,9},{9,8},{10,11... | collective-permute-start | bytes 98312 | tf_op jit(solution)/shard_map/ppermute | solution.py:63
  88.6 8.6 %collective-permute-start.14 = (f32[32,128]{1,0:T(8,128)S(1)}, f32[32,128]{1,0:T(8,128)S(1)}, u32[]{:S(2)}, u32[]{:S(2)}) collective-permute-start(f32[32,128]{1,0:T(8,128)S(1)} %get-tuple-element.36), channel_id=1, source_target_pairs={{0,8},{8,16},{16,24},{24,0},{1,9},{9,17},{17,25},{25,1},{2,10},{10... | collective-permute-start | bytes 49160 | tf_op jit(solution)/shard_map/ppermute | solution.py:66
  88.6 8.6 %collective-permute-start.15 = (f32[32,128]{1,0:T(8,128)S(1)}, f32[32,128]{1,0:T(8,128)S(1)}, u32[]{:S(2)}, u32[]{:S(2)}) collective-permute-start(f32[32,128]{1,0:T(8,128)S(1)} %get-tuple-element.37), channel_id=1, source_target_pairs={{8,0},{16,8},{24,16},{0,24},{9,1},{17,9},{25,17},{1,25},{10,2},{18... | collective-permute-start | bytes 49160 | tf_op jit(solution)/shard_map/ppermute | solution.py:67
  92.4 4.8 %collective-permute-start.16 = (f32[32,128]{1,0:T(8,128)S(1)}, f32[32,128]{1,0:T(8,128)S(1)}, u32[]{:S(2)}, u32[]{:S(2)}) collective-permute-start(f32[32,128]{1,0:T(8,128)S(1)} %get-tuple-element.38), channel_id=1, source_target_pairs={{0,2},{2,4},{4,6},{6,0},{1,3},{3,5},{5,7},{7,1},{8,10},{10,12},{12... | collective-permute-start | bytes 49160 | tf_op jit(solution)/shard_map/ppermute | solution.py:66
  92.4 4.8 %collective-permute-start.17 = (f32[32,128]{1,0:T(8,128)S(1)}, f32[32,128]{1,0:T(8,128)S(1)}, u32[]{:S(2)}, u32[]{:S(2)}) collective-permute-start(f32[32,128]{1,0:T(8,128)S(1)} %get-tuple-element.39), channel_id=1, source_target_pairs={{2,0},{4,2},{6,4},{0,6},{3,1},{5,3},{7,5},{1,7},{10,8},{12,10},{14... | collective-permute-start | bytes 49160 | tf_op jit(solution)/shard_map/ppermute | solution.py:67
  94.1 1.4 %copy-start = (f32[6,256,256]{2,1,0:T(8,128)S(1)}, f32[6,256,256]{2,1,0:T(8,128)}, u32[]{:S(2)}) copy-start(f32[6,256,256]{2,1,0:T(8,128)} %get-tuple-element.33.refs_10_) | copy-start | bytes 4718596

commit v2 on v1

v2 whole, which is shorter than its diff:
```python
import functools

import jax
import jax.numpy as jnp
from jax import lax
from jax.experimental import pallas as pl
from jax.experimental.pallas import tpu as pltpu
from jax.sharding import PartitionSpec as P

NS_ITERS = 3
SUB_ITERS = 2
GROUP_SIZE = 4
FACES = 6
BLOCKS = FACES // 2
AXES = ("gx", "gy", "gz")
LIMIT = 56 * 1024 * 1024

precise = lax.Precision.HIGHEST


def dot(left, right, dims=((1,), (0,))):
    return lax.dot_general(
        left, right, (dims, ((), ())), precision=precise, preferred_element_type=jnp.float32
    )


def split(value):
    high = value.astype(jnp.bfloat16)
    return high, (value - high.astype(jnp.float32)).astype(jnp.bfloat16)


def wide(left, right):
    return lax.dot_general(
        jnp.concatenate([left[0], left[0], left[1]], axis=1),
        jnp.concatenate([right[0], right[1], right[0]], axis=0),
        (((1,), (0,)), ((), ())),
        preferred_element_type=jnp.float32,
    )


def stacked(value):
    return jnp.concatenate(split(value), axis=0)


def thin(rows, matrix):
    out = lax.dot_general(
        jnp.concatenate([rows, rows], axis=1),
        jnp.concatenate(matrix, axis=0),
        (((1,), (0,)), ((), ())),
        preferred_element_type=jnp.float32,
    )
    half = rows.shape[0] // 2
    return out[:half] + out[half:]


def iota(shape, dim):
    return lax.broadcasted_iota(jnp.int32, shape, dim)


def ring(axis):
    count = lax.axis_size(axis)
    forward = [(i, (i + 1) % count) for i in range(count)]
    backward = [(target, source) for source, target in forward]
    return forward, backward


def flipped(axis, bit):
    return [(i, i ^ bit) for i in range(lax.axis_size(axis))]


def face_slots(counts):
    slots = []
    arrays = 0
    for count in counts:
        if count == 2:
            slots += [(arrays, 0), (arrays, 1)]
            arrays += 1
        else:
            slots += [(arrays, None), (arrays + 1, None)]
            arrays += 2
    return slots, arrays


def swap(arrays, counts):
    slots, _ = face_slots(counts)
    got = []
    where = []
    for position, axis in enumerate(AXES):
        forward, backward = ring(axis)
        even, odd = slots[2 * position], slots[2 * position + 1]
        if counts[position] == 2:
            where += [(len(got), 1), (len(got), 0)]
            got.append(lax.ppermute(arrays[even[0]], axis, forward))
        else:
            where += [(len(got), None), (len(got) + 1, None)]
            got.append(lax.ppermute(arrays[odd[0]], axis, forward))
            got.append(lax.ppermute(arrays[even[0]], axis, backward))
    return got, where


def pick(refs, slot):
    array, part = slot
    return refs[array][...] if part is None else refs[array][part]


def put(refs, slot, value):
    array, part = slot
    if part is None:
        refs[array][...] = value
    else:
        refs[array][part] = value


def slot_shapes(counts, shape):
    shapes = []
    for count in counts:
        if count == 2:
            shapes.append(jax.ShapeDtypeStruct((2,) + shape, jnp.float32))
        else:
            shapes += [jax.ShapeDtypeStruct(shape, jnp.float32)] * 2
    return shapes


def vmem_specs(count):
    return [pl.BlockSpec(memory_space=pltpu.VMEM)] * count


def pack_kernel(slots, width, schur_ref, starts_ref, *refs):
    outs, blocks, sems = refs[:-2], refs[-2], refs[-1]
    half = width // 2
    copies = []
    for f in range(FACES):
        place = pl.ds(f * width, width)
        copy = pltpu.make_async_copy(schur_ref.at[place, place], blocks.at[f], sems.at[f])
        copy.start()
        copies.append(copy)
    row, col = iota((half, half), 0), iota((half, half), 1)
    for f in range(FACES):
        copies[f].wait()
        first = blocks[f, 0:half, 0:half]
        second = blocks[f, half:width, half:width]
        diag = jnp.sum(jnp.where(row == col, second, 0.0), axis=0, keepdims=True)
        mixed = jnp.where(row >= col, first, second)
        tail = jnp.broadcast_to(diag, (8, half))
        starts = starts_ref[f]
        put(
            outs,
            slots[f],
            jnp.concatenate(
                [blocks[f, half:width, 0:half], mixed, tail, starts[:, :half], starts[:, half:]],
                axis=0,
            ),
        )


def unpack(packed):
    half = packed.shape[1]
    row, col = iota((half, half), 0), iota((half, half), 1)
    low = packed[0:half]
    mixed = packed[half : 2 * half]
    flip = mixed.T
    first = jnp.where(row >= col, mixed, flip)
    second = jnp.where(row < col, mixed, flip)
    second = jnp.where(row == col, packed[2 * half : 2 * half + 1], second)
    return jnp.concatenate(
        [jnp.concatenate([first, low.T], axis=1), jnp.concatenate([low, second], axis=1)], axis=0
    )


def unpack_starts(packed, ncon):
    half = packed.shape[1]
    rows = packed[2 * half + 8 :]
    return jnp.concatenate([rows[:ncon], rows[ncon:]], axis=1)


def factor_inverses(grams, block=8):
    size = grams[0].shape[0]
    strips = size // 8
    lanes = 128
    full = (8, lanes)
    state = []
    for gram in grams:
        parts = [gram, jnp.where(iota((size, size), 0) == iota((size, size), 1), 1.0, 0.0)]
        if 2 * size < lanes:
            parts.append(jnp.zeros((size, lanes - 2 * size), jnp.float32))
        whole = jnp.concatenate(parts, axis=1)
        state.append([whole[8 * s : 8 * s + 8] for s in range(strips)])
    below = iota(full, 0)

    def line_of(strip, line):
        return jnp.broadcast_to(strip[line : line + 1], full)

    for start in range(0, size, block):
        strip, first = start // 8, start % 8
        active = range(strip, strips)
        for work in state:
            cols = [
                {s: jnp.broadcast_to(work[s][:, start + j : start + j + 1], full) for s in active}
                for j in range(block)
            ]
            factors = []

            def eliminate(j, scale, stop):
                line = first + j
                factor = {s: cols[j][s] * scale for s in active}
                factor[strip] = jnp.where(below > line, factor[strip], 0.0)
                for later in range(j + 1, stop):
                    head = line_of(cols[later][strip], line)
                    for s in active:
                        cols[later][s] = cols[later][s] - factor[s] * head
                factors.append(factor)

            for j in range(0, block, 2):
                line = first + j
                corner = line_of(cols[j][strip], line)
                side = line_of(cols[j][strip], line + 1)
                last = line_of(cols[j + 1][strip], line + 1)
                inverse = 1.0 / (corner * last - side * side)
                eliminate(j, 1.0 / corner, block)
                eliminate(j + 1, corner * inverse, block)
            for j in range(block):
                row = line_of(work[strip], first + j)
                for s in active:
                    if s == strip and first + j == 7:
                        continue
                    work[s] = work[s] - factors[j][s] * row
    results = []
    for work in state:
        parts = []
        for s in range(strips):
            place = iota((8, size), 0) + 8 * s == iota((8, size), 1)
            pivot = jnp.sum(jnp.where(place, work[s][:, :size], 0.0), axis=1, keepdims=True)
            parts.append(work[s][:, size : 2 * size] * lax.rsqrt(pivot))
        results.append(jnp.concatenate(parts, axis=0))
    return results


def subspace(before, inverse, after, starts):
    basis = starts
    for sweep in range(SUB_ITERS):
        for matrices in (before, inverse, after):
            for f in range(FACES):
                basis[f] = thin(stacked(basis[f]), (matrices[f, 0], matrices[f, 1]))
        for f in range(FACES):
            norm = jnp.sum(basis[f] * basis[f], axis=1, keepdims=True)
            basis[f] = basis[f] * lax.rsqrt(norm)
    return basis


def main_kernel(where, arrays, width, schur_ref, *refs):
    inputs = refs[:arrays]
    starts_ref, resid_ref = refs[arrays : arrays + 2]
    payload_ref, product_ref, own_out, partner_out, inverse_out = refs[arrays + 2 : arrays + 7]
    own_ref, upper_ref, guess_ref, sum_ref, own_sems, upper_sems = refs[arrays + 7 :]
    ncon = starts_ref.shape[1]
    columns = resid_ref.shape[1]
    copies = []
    for f in range(FACES):
        place = pl.ds(f * width, width)
        copy = pltpu.make_async_copy(schur_ref.at[place, place], own_ref.at[f], own_sems.at[f])
        copy.start()
        copies.append(copy)
    strips = []
    for f in range(FACES - 1):
        rest = (FACES - 1 - f) * width
        copy = pltpu.make_async_copy(
            schur_ref.at[pl.ds(f * width, width), pl.ds((f + 1) * width, rest)],
            upper_ref.at[f, :, pl.ds((f + 1) * width, rest)],
            upper_sems.at[f],
        )
        copy.start()
        strips.append(copy)
    eye = iota((width, width), 0) == iota((width, width), 1)

    def store(ref, f, value):
        ref[f, 0], ref[f, 1] = split(value)

    for f in range(FACES):
        partner = unpack(pick(inputs, where[f]))
        copies[f].wait()
        own = own_ref[f]
        total = own + partner
        store(own_out, f, own)
        store(partner_out, f, partner)
        store(sum_ref, f, total)
        diagonal = jnp.where(eye, total, 0.0)
        across = 1.0 / jnp.sum(diagonal, axis=0, keepdims=True)
        down = 1.0 / jnp.sum(diagonal, axis=1, keepdims=True)
        guess_ref[f] = jnp.where(eye, 2.0 * across, 0.0) - down * total * across
    for sweep in range(NS_ITERS - 1):
        for f in range(FACES):
            guess = guess_ref[f]
            halves = split(guess)
            product = split(wide((sum_ref[f, 0], sum_ref[f, 1]), halves))
            guess = 2.0 * guess - wide(halves, product)
            if sweep < NS_ITERS - 2:
                guess_ref[f] = guess
            else:
                store(inverse_out, f, guess)
    basis = subspace(
        partner_out, inverse_out, own_out, [starts_ref[f] for f in range(FACES)]
    )
    grams = [dot(b, b, ((1,), (1,))) for b in basis]
    for f in range(FACES - 1):
        strips[f].wait()
    sides = []
    rights = []
    for f in range(FACES):
        rows = stacked(basis[f])
        side = {f: thin(rows, (own_out[f, 0], own_out[f, 1]))}
        for g in range(f + 1, FACES):
            side[g] = thin(rows, split(upper_ref[f, :, g * width : (g + 1) * width]))
        sides.append(side)
        rights.append(thin(rows, split(resid_ref[f * width : (f + 1) * width])))
    factors = factor_inverses(grams)
    basis = [dot(factors[f], basis[f]) for f in range(FACES)]
    blocks = []
    for g in range(FACES):
        tall = jnp.concatenate([sides[f][g] for f in range(g + 1)], axis=0)
        blocks.append(dot(tall, basis[g], ((1,), (1,))))
    even, odd, right = [], [], []
    lows = None
    for f in range(FACES):
        product_ref[f] = dot(factors[f], sides[f][f])
        line = [blocks[g][f * ncon : (f + 1) * ncon] for g in range(f, FACES)]
        line = dot(factors[f], jnp.concatenate([rights[f]] + line, axis=1))
        right.append(line[:, :columns])
        line = line[:, columns:]
        if f % 2 == 0:
            even.append(line)
            lows = line[:, ncon : 2 * ncon].T
        else:
            odd += [lows, line]
    payload_ref[...] = jnp.concatenate(
        [
            jnp.concatenate(even + right[0::2], axis=1),
            jnp.concatenate(odd + right[1::2], axis=1),
        ],
        axis=0,
    )


def spread_kernel(where, arrays, *refs):
    inputs = refs[:arrays]
    product_ref, own_ref, partner_ref, inverse_ref, out_ref = refs[arrays:]
    ncon = product_ref.shape[1]
    starts = [unpack_starts(pick(inputs, where[f]), ncon) for f in range(FACES)]
    basis = subspace(own_ref, inverse_ref, partner_ref, starts)
    factors = factor_inverses([dot(b, b, ((1,), (1,))) for b in basis])
    for f in range(FACES):
        theirs = thin(stacked(basis[f]), (partner_ref[f, 0], partner_ref[f, 1]))
        both = jnp.concatenate([product_ref[f], dot(factors[f], theirs)], axis=0)
        high, low = split(thin(stacked(both), (inverse_ref[f, 0], inverse_ref[f, 1])).T)
        out_ref[f] = jnp.concatenate([high, high, low], axis=1)


def factor_kernel(size, terms, *refs):
    total = refs[0][...]
    for term in range(1, terms):
        total = total + refs[term][...]
    scale_ref, out_ref = refs[terms:]
    rows = []
    offset = 0
    for b in range(BLOCKS):
        rows.append(total[:, offset : offset + (BLOCKS - b) * size])
        offset += (BLOCKS - b) * size
    eye = iota((size, size), 0) == iota((size, size), 1)
    downs, acrosses = [], []
    for b in range(BLOCKS):
        diagonal = jnp.where(eye, rows[b][:, :size], 0.0)
        downs.append(lax.rsqrt(jnp.sum(diagonal, axis=1, keepdims=True)))
        acrosses.append(lax.rsqrt(jnp.sum(diagonal, axis=0, keepdims=True)))
    blocks = {}
    for b in range(BLOCKS):
        for c in range(b, BLOCKS):
            block = rows[b][:, (c - b) * size : (c - b + 1) * size]
            blocks[b, c] = downs[b] * block * acrosses[c]
    lower = {}
    for b in range(BLOCKS):
        (inverse,) = factor_inverses([blocks[b, b]])
        upper = {}
        for c in range(b + 1, BLOCKS):
            upper[c] = dot(inverse, blocks[b, c])
        for c in range(b + 1, BLOCKS):
            for d in range(c, BLOCKS):
                blocks[c, d] = blocks[c, d] - dot(upper[c], upper[d], ((0,), (0,)))
        lower[b, b] = inverse
        for c in range(b):
            lower[b, c] = dot(inverse, lower[b, c])
        for later in range(b + 1, BLOCKS):
            for c in range(b + 1):
                term = dot(upper[later], lower[b, c], ((0,), (0,)))
                lower[later, c] = lower[later, c] - term if c < b else -term
    for b in range(BLOCKS):
        line = [lower[b, c] if c <= b else jnp.zeros((size, size), jnp.float32) for c in range(BLOCKS)]
        out_ref[b * size : (b + 1) * size] = jnp.concatenate(line, axis=1)
        scale_ref[b * size : (b + 1) * size] = jnp.broadcast_to(downs[b], (size, 128))


def solve_kernel(size, ncon, terms, scale_ref, factor_ref, *refs):
    total = refs[0][...]
    for term in range(1, terms):
        total = total + refs[term][...]
    answer_ref, even_ref, odd_ref = refs[terms:]
    columns = answer_ref.shape[1]
    right = jnp.concatenate(
        [total[:, b * columns : (b + 1) * columns] for b in range(BLOCKS)], axis=0
    )
    scale = scale_ref[:, 0:1]
    factor = factor_ref[...]
    answer = scale * dot(factor, dot(factor, scale * right), ((0,), (0,)))
    answer_ref[...] = answer
    even_ref[...] = answer[:ncon]
    odd_ref[...] = answer[ncon : 2 * ncon]


def last_product(spread, mine, theirs):
    high, low = split(jnp.concatenate([mine, theirs], axis=0))
    return lax.dot_general(
        spread,
        jnp.concatenate([high, low, high], axis=0),
        (((1,), (0,)), ((), ())),
        preferred_element_type=jnp.float32,
    )


def last_kernel(where, arrays, ncon, spread_ref, answer_ref, *refs):
    theirs, out_ref = refs[:arrays], refs[arrays]
    width = spread_ref.shape[1]
    for f in range(FACES):
        mine = answer_ref[f * ncon : (f + 1) * ncon]
        out_ref[f * width : (f + 1) * width] = last_product(
            spread_ref[f], mine, pick(theirs, where[f])
        )


def last_pair_kernel(
    ncon, flag_ref, spread_ref, here_ref, there_ref, low_ref, high_ref, other_ref, out_ref
):
    width = spread_ref.shape[1]

    def answer(flag, f):
        place = slice(f * ncon, (f + 1) * ncon)
        return jnp.where(flag == 1, here_ref[place], there_ref[place])

    own = flag_ref[0]
    for f in range(FACES):
        if f < 2:
            near = (low_ref, high_ref)[f][...]
            theirs = jnp.where(own == 1, near, other_ref[f * ncon : (f + 1) * ncon])
        else:
            theirs = answer(flag_ref[f], f ^ 1)
        out_ref[f * width : (f + 1) * width] = last_product(spread_ref[f], answer(own, f), theirs)


def pair_sum(value, rows, planes):
    rounds = [("gy", bit) for bit in (2**i for i in range(1, rows.bit_length() - 1))]
    rounds += [("gz", bit) for bit in (2**i for i in range(planes.bit_length() - 1))]
    for axis, bit in rounds[:-1]:
        value = value + lax.ppermute(value, axis, flipped(axis, bit))
    axis, bit = rounds[-1]
    return [value, lax.ppermute(value, axis, flipped(axis, bit))]


def per_device(schur, start_block, resid, group_of):
    matrix = schur[0, 0, 0]
    starts = start_block[0, 0, 0].transpose(0, 2, 1)
    right = resid[0, 0, 0]
    order, columns = right.shape
    ncon, width = starts.shape[1:]
    counts = [lax.axis_size(axis) for axis in AXES]
    slots, arrays = face_slots(counts)
    coarse = FACES * ncon
    size = 2 * ncon
    coarse_lanes = size * BLOCKS * (BLOCKS + 1) // 2
    params = pltpu.CompilerParams(vmem_limit_bytes=LIMIT)
    anywhere = pl.BlockSpec(memory_space=pl.ANY)
    halves = jax.ShapeDtypeStruct((FACES, 2, width, width), jnp.bfloat16)

    def shape(*dims):
        return jax.ShapeDtypeStruct(dims, jnp.float32)

    packed = pl.pallas_call(
        functools.partial(pack_kernel, slots, width),
        out_shape=slot_shapes(counts, (width + 8 + 2 * ncon, width // 2)),
        in_specs=[anywhere] + vmem_specs(1),
        out_specs=vmem_specs(arrays),
        scratch_shapes=[
            pltpu.VMEM((FACES, width, width), jnp.float32),
            pltpu.SemaphoreType.DMA((FACES,)),
        ],
        compiler_params=params,
    )(matrix, starts)
    got, where = swap(packed, counts)

    payload, product, own, partner, inverse = pl.pallas_call(
        functools.partial(main_kernel, where, arrays, width),
        out_shape=[
            shape(size, coarse_lanes + BLOCKS * columns),
            shape(FACES, ncon, width),
            halves,
            halves,
            halves,
        ],
        in_specs=[anywhere] + vmem_specs(arrays + 2),
        out_specs=vmem_specs(5),
        scratch_shapes=[
            pltpu.VMEM((FACES, width, width), jnp.float32),
            pltpu.VMEM((FACES - 1, width, order), jnp.float32),
            pltpu.VMEM((FACES, width, width), jnp.float32),
            pltpu.VMEM((FACES, 2, width, width), jnp.bfloat16),
            pltpu.SemaphoreType.DMA((FACES,)),
            pltpu.SemaphoreType.DMA((FACES - 1,)),
        ],
        compiler_params=params,
    )(matrix, *got, starts, right)

    spread = pl.pallas_call(
        functools.partial(spread_kernel, where, arrays),
        out_shape=jax.ShapeDtypeStruct((FACES, width, 3 * size), jnp.bfloat16),
        in_specs=vmem_specs(arrays + 4),
        out_specs=pl.BlockSpec(memory_space=pltpu.VMEM),
        compiler_params=params,
        cost_estimate=pl.CostEstimate(
            flops=4 * 10**9, bytes_accessed=10 * 2**20, transcendentals=0
        ),
    )(*got, product, own, partner, inverse)

    rows, planes = counts[1], counts[2]
    groups = group_of.shape[0] // GROUP_SIZE
    y, z = lax.axis_index("gy"), lax.axis_index("gz")
    mine = group_of[y * planes + z]
    paired = groups == 2 and rows > 1 and not (rows & (rows - 1) or planes & (planes - 1))
    if paired:
        core = y & 1
        neighbour = group_of[(y ^ 1) * planes + z]
        other = lax.ppermute(payload, "gy", flipped("gy", 1))
        part = jnp.where(mine == core, payload, 0.0) + jnp.where(neighbour == core, other, 0.0)
        matrices = pair_sum(part[:, :coarse_lanes], rows, planes)
        rights = pair_sum(part[:, coarse_lanes:], rows, planes)
    else:
        chosen = jnp.arange(groups, dtype=jnp.int32) == mine
        total = lax.psum(jnp.where(chosen[:, None, None], payload[None], 0.0), ("gy", "gz"))
        total = lax.dynamic_index_in_dim(total, mine, 0, keepdims=False)
        matrices, rights = [total[:, :coarse_lanes]], [total[:, coarse_lanes:]]

    scale, factor = pl.pallas_call(
        functools.partial(factor_kernel, size, len(matrices)),
        out_shape=[shape(coarse, 128), shape(coarse, coarse)],
        in_specs=vmem_specs(len(matrices)),
        out_specs=vmem_specs(2),
        compiler_params=params,
    )(*matrices)
    answer, even, odd = pl.pallas_call(
        functools.partial(solve_kernel, size, ncon, len(rights)),
        out_shape=[shape(coarse, columns), shape(ncon, columns), shape(ncon, columns)],
        in_specs=vmem_specs(2 + len(rights)),
        out_specs=vmem_specs(3),
        compiler_params=params,
    )(scale, factor, *rights)

    result = shape(order, columns)
    out_spec = pl.BlockSpec(memory_space=pltpu.VMEM)
    if paired:
        places = [
            y * planes + z,
            y * planes + z,
            (y + rows - 1) % rows * planes + z,
            (y + 1) % rows * planes + z,
            y * planes + (z + planes - 1) % planes,
            y * planes + (z + 1) % planes,
        ]
        flags = (group_of[jnp.stack(places)] == core).astype(jnp.int32)
        forward, backward = ring("gx")
        low = lax.ppermute(odd, "gx", forward)
        high = lax.ppermute(even, "gx", backward)
        there = lax.ppermute(answer, "gy", flipped("gy", 1))
        others = lax.ppermute(jnp.concatenate([low, high], axis=0), "gy", flipped("gy", 1))
        correction = pl.pallas_call(
            functools.partial(last_pair_kernel, ncon),
            out_shape=result,
            in_specs=[pl.BlockSpec(memory_space=pltpu.SMEM)] + vmem_specs(6),
            out_specs=out_spec,
            compiler_params=params,
        )(flags, spread, answer, there, low, high, others)
    else:
        faces = answer.reshape(FACES, ncon, columns)
        sent = []
        for position, count in enumerate(counts):
            pair = faces[2 * position : 2 * position + 2]
            sent += [pair] if count == 2 else [pair[0], pair[1]]
        their_answers, _ = swap(sent, counts)
        correction = pl.pallas_call(
            functools.partial(last_kernel, where, arrays, ncon),
            out_shape=result,
            in_specs=vmem_specs(2 + arrays),
            out_specs=out_spec,
            compiler_params=params,
        )(spread, answer, *their_answers)
    return correction[None, None, None]


def solution(mesh):
    in_specs = (
        P("gx", "gy", "gz", None, None),
        P("gx", "gy", "gz", None, None, None),
        P("gx", "gy", "gz", None, None),
        P(),
    )
    out_specs = P("gx", "gy", "gz", None, None)
    return jax.shard_map(
        per_device, mesh=mesh, in_specs=in_specs, out_specs=out_specs, check_vma=False
    )
```

time: 99.1 us -> 81.4 us (0.82)
  Pallas kernels: 56 us -> 41.2 us
  starting transfers between devices: 24.4 us -> 16.8 us
  local copies, waits for them, and re-layouts: 2.33 us -> 4.81 us
  other arithmetic: 0.11 us -> 1.59 us
    pallas_call x4 -> x5, Pallas kernels: 54.5 us -> 37.9 us  [the longest x1 14.8 us: per_device(): pl.pallas_call(functools.partial(main_kernel, where, arrays, width), out_...]
    ppermute x6 -> x2, starting transfers between devices: 13.6 us -> 3.99 us  [swap(): got.append(lax.ppermute(arrays[even[0]], axis, backward))]
    ppermute x4 -> x9, starting transfers between devices: 2.54 us -> 8.15 us  [the longest x1 2.68 us: per_device(): high = lax.ppermute(even, 'gx', backward)]
    ppermute x3 -> x1, starting transfers between devices: 5.13 us -> 3.03 us  [swap(): got.append(lax.ppermute(arrays[even[0]], axis, forward))]
    pallas_call x1, Pallas kernels: 1.52 us -> 3.28 us  [per_device(): pl.pallas_call(functools.partial(pack_kernel, slots, width), out_shape=sl...]
    unnamed x9 -> x28, local copies, waits for them, and re-layouts: 1.68 us -> 3.38 us
    ppermute x6 -> x2, starting transfers between devices: 3.12 us -> 1.58 us  [swap(): got.append(lax.ppermute(arrays[odd[0]], axis, forward))]
    ppermute x4 -> x9, waiting for transfers between devices: 11.2 us -> 9.85 us  [the longest x2 4.96 us: pair_sum(): value = value + lax.ppermute(value, axis, flipped(axis, bit))]
  transfers between devices with their start and end apart: 19 -> 14, of which waited for: 4 -> 6; matrix products, arithmetic and copies ran while one was open for 1% -> 2% of each run, Pallas kernels for 22% -> 22%
where the time goes in v2:
time: 81.4 us; the launch traced here: 81 us
  Pallas kernels  41.2 us (51%)
  starting transfers between devices  16.8 us (21%)
  waiting for transfers between devices  15.1 us (19%)
  local copies, waits for them, and re-layouts  4.81 us (6%)
  other arithmetic  1.59 us (2%)
  between operations  1.52 us (2%)
    pallas_call x1, Pallas kernels, per_device(): pl.pallas_call(functools.partial(main_kernel, where, arrays, width), out_...  14.8 us
    pallas_call x1, Pallas kernels, per_device(): pl.pallas_call(functools.partial(spread_kernel, where, arrays), out_shape...  9.14 us
    pallas_call x1, Pallas kernels, per_device(): pl.pallas_call(functools.partial(factor_kernel, size, len(matrices)), out...  8.91 us
    ppermute x2, waiting for transfers between devices, pair_sum(): value = value + lax.ppermute(value, axis, flipped(axis, bit))  4.96 us
    ppermute x2, starting transfers between devices, swap(): got.append(lax.ppermute(arrays[even[0]], axis, backward))  3.99 us
    ppermute x2, waiting for transfers between devices, swap(): got.append(lax.ppermute(arrays[odd[0]], axis, forward))  3.68 us
    ppermute x2, waiting for transfers between devices, pair_sum(): return [value, lax.ppermute(value, axis, flipped(axis, bit))]  3.55 us
    unnamed x28, local copies, waits for them, and re-layouts  3.38 us
  transfers between devices with their start and end apart: 14, of which 6 were waited for; matrix products, arithmetic and copies ran while one was open for 2% of the time, Pallas kernels for 22%

profile of v2, /device:TPU:0, one launch (start us, length us, event | category | flops | bytes accessed | tf_op | source)
XLA Modules:
  0.0 81.0 jit_solution(8904201362977615943)
XLA Ops:
  0.0 3.3 %shard_map.46 = (f32[328,128]{1,0:T(8,128)}, f32[328,128]{1,0:T(8,128)}, f32[328,128]{1,0:T(8,128)}, f32[328,128]{1,0:T(8,128)}, f32[2,328,128]{2,1,0:T(8,128)}) custom-call(f32[1536,1536]{1,0:T(8,128)} %bitcast.14, f32[6,32,256]{2,1,0:T(8,128)} %bitcast.17), custom_call_target="tpu_custom_call" | custom-call | tf_op jit(solution)/shard_map/pallas_call | solution.py:483
  3.3 3.0 %collective-permute-start.4 = (f32[2,328,128]{2,1,0:T(8,128)}, f32[2,328,128]{2,1,0:T(8,128)S(1)}, u32[]{:S(2)}, u32[]{:S(2)}) collective-permute-start(f32[2,328,128]{2,1,0:T(8,128)} %get-tuple-element.24), channel_id=1, source_target_pairs={{0,1},{1,0},{2,3},{3,2},{4,5},{5,4},{6,7},{7,6},{8,9},{9,8},{10,11... | collective-permute-start | bytes 1007624 | tf_op jit(solution)/shard_map/ppermute | solution.py:93
  6.3 1.6 %collective-permute-start = (f32[328,128]{1,0:T(8,128)}, f32[328,128]{1,0:T(8,128)S(1)}, u32[]{:S(2)}, u32[]{:S(2)}) collective-permute-start(f32[328,128]{1,0:T(8,128)} %get-tuple-element.20), channel_id=1, source_target_pairs={{0,8},{8,16},{16,24},{24,0},{1,9},{9,17},{17,25},{25,1},{2,10},{10... | collective-permute-start | bytes 503816 | tf_op jit(solution)/shard_map/ppermute | solution.py:96
  7.9 2.2 %collective-permute-start.1 = (f32[328,128]{1,0:T(8,128)}, f32[328,128]{1,0:T(8,128)S(1)}, u32[]{:S(2)}, u32[]{:S(2)}) collective-permute-start(f32[328,128]{1,0:T(8,128)} %get-tuple-element.21), channel_id=1, source_target_pairs={{8,0},{16,8},{24,16},{0,24},{9,1},{17,9},{25,17},{1,25},{10,2},{18... | collective-permute-start | bytes 503816 | tf_op jit(solution)/shard_map/ppermute | solution.py:97
  10.1 0.0 collective-permute-start.2
  10.1 1.7 %collective-permute-start.3 = (f32[328,128]{1,0:T(8,128)}, f32[328,128]{1,0:T(8,128)S(1)}, u32[]{:S(2)}, u32[]{:S(2)}) collective-permute-start(f32[328,128]{1,0:T(8,128)} %get-tuple-element.23), channel_id=1, source_target_pairs={{2,0},{4,2},{6,4},{0,6},{3,1},{5,3},{7,5},{1,7},{10,8},{12,10},{14... | collective-permute-start | bytes 503816 | tf_op jit(solution)/shard_map/ppermute | solution.py:97
  11.9 3.7 %collective-permute-done.refs_0_ = f32[328,128]{1,0:T(8,128)S(1)} collective-permute-done((f32[328,128]{1,0:T(8,128)}, f32[328,128]{1,0:T(8,128)S(1)}, u32[]{:S(2)}, u32[]{:S(2)}) %collective-permute-start) | collective-permute-done | bytes 167968 | tf_op jit(solution)/shard_map/ppermute | solution.py:96
  15.6 0.0 copy-start.4
  15.6 1.6 %collective-permute-done.1.refs_1_ = f32[328,128]{1,0:T(8,128)S(1)} collective-permute-done((f32[328,128]{1,0:T(8,128)}, f32[328,128]{1,0:T(8,128)S(1)}, u32[]{:S(2)}, u32[]{:S(2)}) %collective-permute-start.1) | collective-permute-done | bytes 167968 | tf_op jit(solution)/shard_map/ppermute | solution.py:97
  17.2 0.0 copy-start.5
  17.2 0.0 collective-permute-done.2.refs_2_
  17.2 0.0 copy-start.6
  17.2 0.0 collective-permute-done.3.refs_3_
  17.2 0.0 copy-start.7
  17.2 0.0 collective-permute-done.4.refs_4_
  17.2 0.0 copy-start.3
  17.2 0.0 copy-done.4
  17.2 0.6 copy-done.5
  17.8 0.1 copy-done.6
  17.9 0.1 copy-done.7
  18.0 0.1 copy-done.3
  18.1 0.0 copy-start
  18.1 14.8 %shard_map.47 = (f32[64,768]{1,0:T(8,128)}, f32[6,32,256]{2,1,0:T(8,128)}, bf16[6,2,256,256]{3,2,1,0:T(8,128)(2,1)}, bf16[6,2,256,256]{3,2,1,0:T(8,128)(2,1)}, bf16[6,2,256,256]{3,2,1,0:T(8,128)(2,1)}) custom-call(f32[1536,1536]{1,0:T(8,128)} %bitcast.15, f32[328,128]{1,0:T(8,128)} %copy-done.4, f32[328,128]{1,0:T(8,128)} %copy-done.5, ...), custom_call_target="tpu_custom_call" | custom-call | tf_op jit(solution)/shard_map/pallas_call | solution.py:496
  32.8 0.1 collective-permute-start.5
  33.0 0.0 copy-done
  33.0 0.7 fusion.2
  35.0 0.1 stack.21
  35.1 0.0 collective-permute-done.5
  35.1 1.0 %select_add_fusion = f32[64,768]{1,0:T(8,128)S(1)} fusion(f32[64,768]{1,0:T(8,128)S(1)} %collective-permute-done.5, f32[64,768]{1,0:T(8,128)} %get-tuple-element.29, pred[]{:T(512)S(6)} %eq.20, pred[]{:T(512)S(6)} %eq.19), kind=kLoop, calls=%fused_computation.1 | loop fusion | flops 147456 | bytes 589826 | tf_op jit(solution)/shard_map/add | solution.py:538
  36.0 1.5 %collective-permute-start.8 = (f32[64,384]{1,0:T(8,128)S(1)}, f32[64,384]{1,0:T(8,128)S(1)}, u32[]{:S(2)}, u32[]{:S(2)}) collective-permute-start(f32[64,384]{1,0:T(8,128)S(1)} %get-tuple-element.37), channel_id=1, source_target_pairs={{0,4},{2,6},{4,0},{6,2},{1,5},{3,7},{5,1},{7,3},{8,12},{10,14},{12... | collective-permute-start | bytes 294920 | tf_op jit(solution)/shard_map/ppermute | solution.py:460
  37.6 0.5 collective-permute-start.6
  38.1 3.5 %collective-permute-done.8 = f32[64,384]{1,0:T(8,128)S(1)} collective-permute-done((f32[64,384]{1,0:T(8,128)S(1)}, f32[64,384]{1,0:T(8,128)S(1)}, u32[]{:S(2)}, u32[]{:S(2)}) %collective-permute-start.8) | collective-permute-done | bytes 98336 | tf_op jit(solution)/shard_map/ppermute | solution.py:460
  41.7 1.4 %collective-permute-done.6 = f32[64,384]{1,0:T(8,128)S(1)} collective-permute-done((f32[64,384]{1,0:T(8,128)S(1)}, f32[64,384]{1,0:T(8,128)S(1)}, u32[]{:S(2)}, u32[]{:S(2)}) %collective-permute-start.6) | collective-permute-done | bytes 98336 | tf_op jit(solution)/shard_map/ppermute | solution.py:460
  43.1 0.0 copy-start.1
  43.1 0.0 copy-start.2
  43.1 0.9 %collective-permute-start.9 = (f32[64,384]{1,0:T(8,128)S(1)}, f32[64,384]{1,0:T(8,128)S(1)}, u32[]{:S(2)}, u32[]{:S(2)}) collective-permute-start(f32[64,384]{1,0:T(8,128)S(1)} %get-tuple-element.35.refs_0_), channel_id=1, source_target_pairs={{0,1},{1,0},{2,3},{3,2},{4,5},{5,4},{6,7},{7,6},{8,9},{9,8},{10,11... | collective-permute-start | bytes 294920 | tf_op jit(solution)/shard_map/ppermute | solution.py:462
  44.0 1.2 %collective-permute-start.7 = (f32[64,384]{1,0:T(8,128)S(1)}, f32[64,384]{1,0:T(8,128)S(1)}, u32[]{:S(2)}, u32[]{:S(2)}) collective-permute-start(f32[64,384]{1,0:T(8,128)S(1)} %get-tuple-element.36.refs_0_), channel_id=1, source_target_pairs={{0,1},{1,0},{2,3},{3,2},{4,5},{5,4},{6,7},{7,6},{8,9},{9,8},{10,11... | collective-permute-start | bytes 294920 | tf_op jit(solution)/shard_map/ppermute | solution.py:462
  45.2 0.6 gather_fusion
  45.9 3.6 %collective-permute-done.7.refs_1_ = f32[64,384]{1,0:T(8,128)S(1)} collective-permute-done((f32[64,384]{1,0:T(8,128)S(1)}, f32[64,384]{1,0:T(8,128)S(1)}, u32[]{:S(2)}, u32[]{:S(2)}) %collective-permute-start.7) | collective-permute-done | bytes 98336 | tf_op jit(solution)/shard_map/ppermute | solution.py:462
  49.4 0.0 copy-done.1
  49.4 0.0 copy-start.8
  49.4 0.7 copy-done.8
  50.1 8.9 %shard_map.49 = (f32[192,128]{1,0:T(8,128)}, f32[192,192]{1,0:T(8,128)}) custom-call(f32[64,384]{1,0:T(8,128)} %copy-done.1, f32[64,384]{1,0:T(8,128)} %copy-done.8), custom_call_target="tpu_custom_call" | custom-call | tf_op jit(solution)/shard_map/pallas_call | solution.py:547
  59.0 0.0 collective-permute-done.9.refs_1_
  59.0 0.0 copy-start.9
  59.0 0.0 copy-done.2
  59.0 0.6 copy-done.9
  59.6 2.7 %shard_map.50 = (f32[192,128]{1,0:T(8,128)}, f32[32,128]{1,0:T(8,128)}, f32[32,128]{1,0:T(8,128)}) custom-call(f32[192,128]{1,0:T(8,128)} %get-tuple-element.30.scale_ref, f32[192,192]{1,0:T(8,128)} %get-tuple-element.31.factor_ref, f32[64,384]{1,0:T(8,128)} %copy-done.2, f32[64,384]{1,0:T(8,128)} %copy-done.9), custom_call_target="tpu_custom_call" | custom-call | tf_op jit(solution)/shard_map/pallas_call | solution.py:554
  62.3 1.1 %collective-permute-start.11 = (f32[32,128]{1,0:T(8,128)}, f32[32,128]{1,0:T(8,128)S(1)}, u32[]{:S(2)}, u32[]{:S(2)}) collective-permute-start(f32[32,128]{1,0:T(8,128)} %get-tuple-element.33), channel_id=1, source_target_pairs={{0,8},{8,16},{16,24},{24,0},{1,9},{9,17},{17,25},{25,1},{2,10},{10... | collective-permute-start | bytes 49160 | tf_op jit(solution)/shard_map/ppermute | solution.py:575
  63.4 2.7 %collective-permute-start.12 = (f32[32,128]{1,0:T(8,128)}, f32[32,128]{1,0:T(8,128)S(1)}, u32[]{:S(2)}, u32[]{:S(2)}) collective-permute-start(f32[32,128]{1,0:T(8,128)} %get-tuple-element.34), channel_id=1, source_target_pairs={{8,0},{16,8},{24,16},{0,24},{9,1},{17,9},{25,17},{1,25},{10,2},{18... | collective-permute-start | bytes 49160 | tf_op jit(solution)/shard_map/ppermute | solution.py:576
  66.1 0.6 compare_convert_fusion.flag_ref
  66.7 0.0 collective-permute-start.10
  66.7 1.3 %collective-permute-done.11.low_ref = f32[32,128]{1,0:T(8,128)S(1)} collective-permute-done((f32[32,128]{1,0:T(8,128)}, f32[32,128]{1,0:T(8,128)S(1)}, u32[]{:S(2)}, u32[]{:S(2)}) %collective-permute-start.11) | collective-permute-done | bytes 16416 | tf_op jit(solution)/shard_map/ppermute | solution.py:575
  68.1 0.0 collective-permute-done.12.high_ref
  68.1 0.1 collective-permute-start.13
  68.1 9.1 %shard_map.48.spread_ref = bf16[6,256,192]{2,1,0:T(8,128)(2,1)} custom-call(f32[328,128]{1,0:T(8,128)} %copy-done.4, f32[328,128]{1,0:T(8,128)} %copy-done.5, f32[328,128]{1,0:T(8,128)} %copy-done.6, f32[328,128]{1,0:T(8,128)} %copy-done.7, f32[2,328,128]{2,1,0:T(8,128)} %copy-done.3, f32[6,32,256]{2,1,0:T(8,128)} %get-tuple-element.25.refs_5_, ...), custom_call_target="tpu_custom_call" | custom-call | flops 4000000000 | bytes 10485760 | tf_op jit(solution)/shard_map/pallas_call | solution.py:518
  77.3 0.0 copy-done.11
  77.3 0.0 copy-done.12
  77.3 0.0 collective-permute-done.13.other_ref
  77.3 0.0 copy-start.13
  77.3 0.0 collective-permute-done.10.there_ref
  77.3 0.6 copy-done.13
  77.9 0.6 copy-done.10
  78.6 2.5 %shard_map.51 = f32[1536,128]{1,0:T(8,128)} custom-call(s32[6]{0:T(128)} %compare_convert_fusion.flag_ref, bf16[6,256,192]{2,1,0:T(8,128)(2,1)} %shard_map.48.spread_ref, f32[192,128]{1,0:T(8,128)} %get-tuple-element.32.here_ref, f32[192,128]{1,0:T(8,128)} %copy-done.10, f32[32,128]{1,0:T(8,128)} %copy-done.11, f32[32,128]{1,0:T(8,128)} %copy-done.12, ...), custom_call_target="tpu_custom_call" | custom-call | tf_op jit(solution)/shard_map/pallas_call | solution.py:579
  (8 shorter events, 0.1 us)
Async XLA Ops:
  3.3 13.9 %collective-permute-start.4 = (f32[2,328,128]{2,1,0:T(8,128)}, f32[2,328,128]{2,1,0:T(8,128)S(1)}, u32[]{:S(2)}, u32[]{:S(2)}) collective-permute-start(f32[2,328,128]{2,1,0:T(8,128)} %get-tuple-element.24), channel_id=1, source_target_pairs={{0,1},{1,0},{2,3},{3,2},{4,5},{5,4},{6,7},{7,6},{8,9},{9,8},{10,11... | collective-permute-start | bytes 1007624 | tf_op jit(solution)/shard_map/ppermute | solution.py:93
  6.3 9.2 %collective-permute-start = (f32[328,128]{1,0:T(8,128)}, f32[328,128]{1,0:T(8,128)S(1)}, u32[]{:S(2)}, u32[]{:S(2)}) collective-permute-start(f32[328,128]{1,0:T(8,128)} %get-tuple-element.20), channel_id=1, source_target_pairs={{0,8},{8,16},{16,24},{24,0},{1,9},{9,17},{17,25},{25,1},{2,10},{10... | collective-permute-start | bytes 503816 | tf_op jit(solution)/shard_map/ppermute | solution.py:96
  7.9 9.3 %collective-permute-start.1 = (f32[328,128]{1,0:T(8,128)}, f32[328,128]{1,0:T(8,128)S(1)}, u32[]{:S(2)}, u32[]{:S(2)}) collective-permute-start(f32[328,128]{1,0:T(8,128)} %get-tuple-element.21), channel_id=1, source_target_pairs={{8,0},{16,8},{24,16},{0,24},{9,1},{17,9},{25,17},{1,25},{10,2},{18... | collective-permute-start | bytes 503816 | tf_op jit(solution)/shard_map/ppermute | solution.py:97
  10.1 7.0 %collective-permute-start.2 = (f32[328,128]{1,0:T(8,128)}, f32[328,128]{1,0:T(8,128)S(1)}, u32[]{:S(2)}, u32[]{:S(2)}) collective-permute-start(f32[328,128]{1,0:T(8,128)} %get-tuple-element.22), channel_id=1, source_target_pairs={{0,2},{2,4},{4,6},{6,0},{1,3},{3,5},{5,7},{7,1},{8,10},{10,12},{12... | collective-permute-start | bytes 503816 | tf_op jit(solution)/shard_map/ppermute | solution.py:96
  10.1 7.0 %collective-permute-start.3 = (f32[328,128]{1,0:T(8,128)}, f32[328,128]{1,0:T(8,128)S(1)}, u32[]{:S(2)}, u32[]{:S(2)}) collective-permute-start(f32[328,128]{1,0:T(8,128)} %get-tuple-element.23), channel_id=1, source_target_pairs={{2,0},{4,2},{6,4},{0,6},{3,1},{5,3},{7,5},{1,7},{10,8},{12,10},{14... | collective-permute-start | bytes 503816 | tf_op jit(solution)/shard_map/ppermute | solution.py:97
  15.6 1.7 %copy-start.4 = (f32[328,128]{1,0:T(8,128)}, f32[328,128]{1,0:T(8,128)S(1)}, u32[]{:S(2)}) copy-start(f32[328,128]{1,0:T(8,128)S(1)} %collective-permute-done.refs_0_) | copy-start | bytes 503812
  17.2 0.7 copy-start.5
  17.2 0.7 copy-start.6
  17.2 0.8 copy-start.7
  17.2 0.9 %copy-start.3 = (f32[2,328,128]{2,1,0:T(8,128)}, f32[2,328,128]{2,1,0:T(8,128)S(1)}, u32[]{:S(2)}) copy-start(f32[2,328,128]{2,1,0:T(8,128)S(1)} %collective-permute-done.4.refs_4_) | copy-start | bytes 1007620
  18.1 14.9 %copy-start = (s32[8]{0:T(128)S(1)}, s32[8]{0:T(128)}, u32[]{:S(2)}) copy-start(s32[8]{0:T(128)} %param.7) | copy-start | bytes 100
  32.8 2.2 %collective-permute-start.5 = (f32[64,768]{1,0:T(8,128)}, f32[64,768]{1,0:T(8,128)S(1)}, u32[]{:S(2)}, u32[]{:S(2)}) collective-permute-start(f32[64,768]{1,0:T(8,128)} %get-tuple-element.29), channel_id=1, source_target_pairs={{0,2},{2,0},{4,6},{6,4},{1,3},{3,1},{5,7},{7,5},{8,10},{10,8},{12,... | collective-permute-start | bytes 589832 | tf_op jit(solution)/shard_map/ppermute | solution.py:537
  36.0 5.6 %collective-permute-start.8 = (f32[64,384]{1,0:T(8,128)S(1)}, f32[64,384]{1,0:T(8,128)S(1)}, u32[]{:S(2)}, u32[]{:S(2)}) collective-permute-start(f32[64,384]{1,0:T(8,128)S(1)} %get-tuple-element.37), channel_id=1, source_target_pairs={{0,4},{2,6},{4,0},{6,2},{1,5},{3,7},{5,1},{7,3},{8,12},{10,14},{12... | collective-permute-start | bytes 294920 | tf_op jit(solution)/shard_map/ppermute | solution.py:460
  37.6 5.5 %collective-permute-start.6 = (f32[64,384]{1,0:T(8,128)S(1)}, f32[64,384]{1,0:T(8,128)S(1)}, u32[]{:S(2)}, u32[]{:S(2)}) collective-permute-start(f32[64,384]{1,0:T(8,128)S(1)} %get-tuple-element.38), channel_id=1, source_target_pairs={{0,4},{2,6},{4,0},{6,2},{1,5},{3,7},{5,1},{7,3},{8,12},{10,14},{12... | collective-permute-start | bytes 294920 | tf_op jit(solution)/shard_map/ppermute | solution.py:460
  43.1 6.3 %copy-start.1 = (f32[64,384]{1,0:T(8,128)}, f32[64,384]{1,0:T(8,128)S(1)}, u32[]{:S(2)}) copy-start(f32[64,384]{1,0:T(8,128)S(1)} %get-tuple-element.36.refs_0_) | copy-start | bytes 294916
  43.1 15.9 %copy-start.2 = (f32[64,384]{1,0:T(8,128)}, f32[64,384]{1,0:T(8,128)S(1)}, u32[]{:S(2)}) copy-start(f32[64,384]{1,0:T(8,128)S(1)} %get-tuple-element.35.refs_0_) | copy-start | bytes 294916
  43.1 15.9 %collective-permute-start.9 = (f32[64,384]{1,0:T(8,128)S(1)}, f32[64,384]{1,0:T(8,128)S(1)}, u32[]{:S(2)}, u32[]{:S(2)}) collective-permute-start(f32[64,384]{1,0:T(8,128)S(1)} %get-tuple-element.35.refs_0_), channel_id=1, source_target_pairs={{0,1},{1,0},{2,3},{3,2},{4,5},{5,4},{6,7},{7,6},{8,9},{9,8},{10,11... | collective-permute-start | bytes 294920 | tf_op jit(solution)/shard_map/ppermute | solution.py:462
  44.0 5.4 %collective-permute-start.7 = (f32[64,384]{1,0:T(8,128)S(1)}, f32[64,384]{1,0:T(8,128)S(1)}, u32[]{:S(2)}, u32[]{:S(2)}) collective-permute-start(f32[64,384]{1,0:T(8,128)S(1)} %get-tuple-element.36.refs_0_), channel_id=1, source_target_pairs={{0,1},{1,0},{2,3},{3,2},{4,5},{5,4},{6,7},{7,6},{8,9},{9,8},{10,11... | collective-permute-start | bytes 294920 | tf_op jit(solution)/shard_map/ppermute | solution.py:462
  49.4 0.7 copy-start.8
  59.0 0.6 copy-start.9
  62.3 5.7 %collective-permute-start.11 = (f32[32,128]{1,0:T(8,128)}, f32[32,128]{1,0:T(8,128)S(1)}, u32[]{:S(2)}, u32[]{:S(2)}) collective-permute-start(f32[32,128]{1,0:T(8,128)} %get-tuple-element.33), channel_id=1, source_target_pairs={{0,8},{8,16},{16,24},{24,0},{1,9},{9,17},{17,25},{25,1},{2,10},{10... | collective-permute-start | bytes 49160 | tf_op jit(solution)/shard_map/ppermute | solution.py:575
  63.4 4.6 %collective-permute-start.12 = (f32[32,128]{1,0:T(8,128)}, f32[32,128]{1,0:T(8,128)S(1)}, u32[]{:S(2)}, u32[]{:S(2)}) collective-permute-start(f32[32,128]{1,0:T(8,128)} %get-tuple-element.34), channel_id=1, source_target_pairs={{8,0},{16,8},{24,16},{0,24},{9,1},{17,9},{25,17},{1,25},{10,2},{18... | collective-permute-start | bytes 49160 | tf_op jit(solution)/shard_map/ppermute | solution.py:576
  66.7 10.6 %collective-permute-start.10 = (f32[192,128]{1,0:T(8,128)}, f32[192,128]{1,0:T(8,128)S(1)}, u32[]{:S(2)}, u32[]{:S(2)}) collective-permute-start(f32[192,128]{1,0:T(8,128)} %get-tuple-element.32.here_ref), channel_id=1, source_target_pairs={{0,2},{2,0},{4,6},{6,4},{1,3},{3,1},{5,7},{7,5},{8,10},{10,8},{12,... | collective-permute-start | bytes 294920 | tf_op jit(solution)/shard_map/ppermute | solution.py:577
  68.1 9.2 %copy-start.11 = (f32[32,128]{1,0:T(8,128)}, f32[32,128]{1,0:T(8,128)S(1)}, u32[]{:S(2)}) copy-start(f32[32,128]{1,0:T(8,128)S(1)} %collective-permute-done.11.low_ref) | copy-start | bytes 49156
  68.1 9.2 %copy-start.12 = (f32[32,128]{1,0:T(8,128)}, f32[32,128]{1,0:T(8,128)S(1)}, u32[]{:S(2)}) copy-start(f32[32,128]{1,0:T(8,128)S(1)} %collective-permute-done.12.high_ref) | copy-start | bytes 49156
  68.1 9.2 %collective-permute-start.13 = (f32[64,128]{1,0:T(8,128)S(1)}, f32[64,128]{1,0:T(8,128)S(1)}, u32[]{:S(2)}, u32[]{:S(2)}) collective-permute-start(f32[64,128]{1,0:T(8,128)S(1)} %pad_maximum_fusion), channel_id=1, source_target_pairs={{0,2},{2,0},{4,6},{6,4},{1,3},{3,1},{5,7},{7,5},{8,10},{10,8},{12,... | collective-permute-start | bytes 98312 | tf_op jit(solution)/shard_map/ppermute | solution.py:578
  77.3 0.6 copy-start.13
  77.9 0.6 copy-start.10

commit v3 on v2

v3 whole, which is shorter than its diff:
```python
import functools

import jax
import jax.numpy as jnp
from jax import lax
from jax.experimental import pallas as pl
from jax.experimental.pallas import tpu as pltpu
from jax.sharding import PartitionSpec as P

NS_ITERS = 3
SUB_ITERS = 2
GROUP_SIZE = 4
FACES = 6
BLOCKS = FACES // 2
AXES = ("gx", "gy", "gz")
MIB = 1024 * 1024

precise = lax.Precision.HIGHEST


def dot(left, right, dims=((1,), (0,))):
    return lax.dot_general(
        left, right, (dims, ((), ())), precision=precise, preferred_element_type=jnp.float32
    )


def split(value):
    high = value.astype(jnp.bfloat16)
    return high, (value - high.astype(jnp.float32)).astype(jnp.bfloat16)


def wide(left, right):
    return lax.dot_general(
        jnp.concatenate([left[0], left[0], left[1]], axis=1),
        jnp.concatenate([right[0], right[1], right[0]], axis=0),
        (((1,), (0,)), ((), ())),
        preferred_element_type=jnp.float32,
    )


def stacked(value):
    return jnp.concatenate(split(value), axis=0)


def thin(rows, matrix):
    out = lax.dot_general(
        jnp.concatenate([rows, rows], axis=1),
        jnp.concatenate(matrix, axis=0),
        (((1,), (0,)), ((), ())),
        preferred_element_type=jnp.float32,
    )
    half = rows.shape[0] // 2
    return out[:half] + out[half:]


def iota(shape, dim):
    return lax.broadcasted_iota(jnp.int32, shape, dim)


def ring(axis):
    count = lax.axis_size(axis)
    forward = [(i, (i + 1) % count) for i in range(count)]
    backward = [(target, source) for source, target in forward]
    return forward, backward


def flipped(axis, bit):
    return [(i, i ^ bit) for i in range(lax.axis_size(axis))]


def face_slots(counts):
    slots = []
    arrays = 0
    for count in counts:
        if count == 2:
            slots += [(arrays, 0), (arrays, 1)]
            arrays += 1
        else:
            slots += [(arrays, None), (arrays + 1, None)]
            arrays += 2
    return slots, arrays


def swap(arrays, counts):
    slots, _ = face_slots(counts)
    got = []
    where = []
    for position, axis in enumerate(AXES):
        forward, backward = ring(axis)
        even, odd = slots[2 * position], slots[2 * position + 1]
        if counts[position] == 2:
            where += [(len(got), 1), (len(got), 0)]
            got.append(lax.ppermute(arrays[even[0]], axis, forward))
        else:
            where += [(len(got), None), (len(got) + 1, None)]
            got.append(lax.ppermute(arrays[odd[0]], axis, forward))
            got.append(lax.ppermute(arrays[even[0]], axis, backward))
    return got, where


def pick(refs, slot):
    array, part = slot
    return refs[array][...] if part is None else refs[array][part]


def put(refs, slot, value):
    array, part = slot
    if part is None:
        refs[array][...] = value
    else:
        refs[array][part] = value


def slot_shapes(counts, shape):
    shapes = []
    for count in counts:
        if count == 2:
            shapes.append(jax.ShapeDtypeStruct((2,) + shape, jnp.float32))
        else:
            shapes += [jax.ShapeDtypeStruct(shape, jnp.float32)] * 2
    return shapes


def vmem_specs(count):
    return [pl.BlockSpec(memory_space=pltpu.VMEM)] * count


def pack_kernel(slots, width, schur_ref, starts_ref, *refs):
    outs, blocks, starts, sems, start_sem = refs[:-4], refs[-4], refs[-3], refs[-2], refs[-1]
    half = width // 2
    copies = []
    for f in range(FACES):
        place = pl.ds(f * width, width)
        copy = pltpu.make_async_copy(schur_ref.at[place, place], blocks.at[f], sems.at[f])
        copy.start()
        copies.append(copy)
    start_copy = pltpu.make_async_copy(starts_ref, starts, start_sem)
    start_copy.start()
    row, col = iota((half, half), 0), iota((half, half), 1)
    start_copy.wait()
    for f in range(FACES):
        copies[f].wait()
        first = blocks[f, 0:half, 0:half]
        second = blocks[f, half:width, half:width]
        diag = jnp.sum(jnp.where(row == col, second, 0.0), axis=0, keepdims=True)
        mixed = jnp.where(row >= col, first, second)
        tail = jnp.broadcast_to(diag, (8, half))
        start = starts[f]
        put(
            outs,
            slots[f],
            jnp.concatenate(
                [blocks[f, half:width, 0:half], mixed, tail, start[:, :half], start[:, half:]],
                axis=0,
            ),
        )


def unpack(packed):
    half = packed.shape[1]
    row, col = iota((half, half), 0), iota((half, half), 1)
    low = packed[0:half]
    mixed = packed[half : 2 * half]
    flip = mixed.T
    first = jnp.where(row >= col, mixed, flip)
    second = jnp.where(row < col, mixed, flip)
    second = jnp.where(row == col, packed[2 * half : 2 * half + 1], second)
    return jnp.concatenate(
        [jnp.concatenate([first, low.T], axis=1), jnp.concatenate([low, second], axis=1)], axis=0
    )


def unpack_starts(packed, ncon):
    half = packed.shape[1]
    rows = packed[2 * half + 8 :]
    return jnp.concatenate([rows[:ncon], rows[ncon:]], axis=1)


def factor_inverses(grams, block=8):
    size = grams[0].shape[0]
    strips = size // 8
    lanes = 128
    full = (8, lanes)
    state = []
    for gram in grams:
        parts = [gram, jnp.where(iota((size, size), 0) == iota((size, size), 1), 1.0, 0.0)]
        if 2 * size < lanes:
            parts.append(jnp.zeros((size, lanes - 2 * size), jnp.float32))
        whole = jnp.concatenate(parts, axis=1)
        state.append([whole[8 * s : 8 * s + 8] for s in range(strips)])
    below = iota(full, 0)

    def line_of(strip, line):
        return jnp.broadcast_to(strip[line : line + 1], full)

    for start in range(0, size, block):
        strip, first = start // 8, start % 8
        active = range(strip, strips)
        for work in state:
            cols = [
                {s: jnp.broadcast_to(work[s][:, start + j : start + j + 1], full) for s in active}
                for j in range(block)
            ]
            factors = []

            def eliminate(j, scale, stop):
                line = first + j
                factor = {s: cols[j][s] * scale for s in active}
                factor[strip] = jnp.where(below > line, factor[strip], 0.0)
                for later in range(j + 1, stop):
                    head = line_of(cols[later][strip], line)
                    for s in active:
                        cols[later][s] = cols[later][s] - factor[s] * head
                factors.append(factor)

            for j in range(0, block, 2):
                line = first + j
                corner = line_of(cols[j][strip], line)
                side = line_of(cols[j][strip], line + 1)
                last = line_of(cols[j + 1][strip], line + 1)
                inverse = 1.0 / (corner * last - side * side)
                eliminate(j, 1.0 / corner, block)
                eliminate(j + 1, corner * inverse, block)
            for j in range(block):
                row = line_of(work[strip], first + j)
                for s in active:
                    if s == strip and first + j == 7:
                        continue
                    work[s] = work[s] - factors[j][s] * row
    results = []
    for work in state:
        parts = []
        for s in range(strips):
            place = iota((8, size), 0) + 8 * s == iota((8, size), 1)
            pivot = jnp.sum(jnp.where(place, work[s][:, :size], 0.0), axis=1, keepdims=True)
            parts.append(work[s][:, size : 2 * size] * lax.rsqrt(pivot))
        results.append(jnp.concatenate(parts, axis=0))
    return results


def store(ref, f, value):
    ref[f, 0], ref[f, 1] = split(value)


def load(ref, f):
    return ref[f, 0], ref[f, 1]


def begin(packed, copies, own_ref, own_out, partner_out, sum_ref):
    width = own_ref.shape[1]
    eye = iota((width, width), 0) == iota((width, width), 1)
    guesses = []
    for f in range(len(packed)):
        partner = unpack(packed[f])
        copies[f].wait()
        own = own_ref[f]
        total = own + partner
        store(own_out, f, own)
        store(partner_out, f, partner)
        store(sum_ref, f, total)
        diagonal = jnp.where(eye, total, 0.0)
        across = 1.0 / jnp.sum(diagonal, axis=0, keepdims=True)
        down = 1.0 / jnp.sum(diagonal, axis=1, keepdims=True)
        guesses.append(jnp.where(eye, 2.0 * across, 0.0) - down * total * across)
    return guesses


def newton(guesses, sum_ref):
    results = []
    for f, guess in enumerate(guesses):
        halves = split(guess)
        product = split(wide(load(sum_ref, f), halves))
        results.append(2.0 * guess - wide(halves, product))
    return results


def unit_rows(basis):
    return [b * lax.rsqrt(jnp.sum(b * b, axis=1, keepdims=True)) for b in basis]


def sweep_basis(before, inverse, after, basis):
    for matrices in (before, inverse, after):
        basis = [thin(stacked(b), matrix) for b, matrix in zip(basis, matrices)]
    return unit_rows(basis)


def copy_own(schur_ref, faces, width, own_ref, sems):
    copies = []
    for i, f in enumerate(faces):
        place = pl.ds(f * width, width)
        copy = pltpu.make_async_copy(schur_ref.at[place, place], own_ref.at[i], sems.at[i])
        copy.start()
        copies.append(copy)
    return copies


def early_kernel(faces, where, arrays, width, schur_ref, *refs):
    inputs = refs[:arrays]
    starts_ref = refs[arrays]
    basis_out, own_out, partner_out, inverse_out = refs[arrays + 1 : arrays + 5]
    own_ref, sum_ref, own_sems = refs[arrays + 5 :]
    count = len(faces)
    copies = copy_own(schur_ref, faces, width, own_ref, own_sems)
    packed = [pick(inputs, slot) for slot in where]
    guesses = begin(packed, copies, own_ref, own_out, partner_out, sum_ref)
    for sweep in range(NS_ITERS - 1):
        guesses = newton(guesses, sum_ref)
    for i in range(count):
        store(inverse_out, i, guesses[i])
    basis = [starts_ref[f] for f in faces]
    matrices = [[load(ref, i) for i in range(count)] for ref in (partner_out, inverse_out, own_out)]
    for sweep in range(SUB_ITERS):
        basis = sweep_basis(*matrices, basis)
    for i in range(count):
        basis_out[i] = basis[i]


def main_kernel(early, late, where, arrays, width, schur_ref, *refs):
    inputs = refs[:arrays]
    starts_ref, resid_ref, early_basis, early_own = refs[arrays : arrays + 4]
    payload_ref, product_ref, own_out, partner_out, inverse_out = refs[arrays + 4 : arrays + 9]
    own_ref, upper_ref, sum_ref, own_sems, upper_sems = refs[arrays + 9 :]
    ncon = starts_ref.shape[1]
    columns = resid_ref.shape[1]
    copies = copy_own(schur_ref, late, width, own_ref, own_sems)
    strips = {}
    for f in [*early, *late]:
        rest = (FACES - 1 - f) * width
        if not rest:
            continue
        strips[f] = pltpu.make_async_copy(
            schur_ref.at[pl.ds(f * width, width), pl.ds((f + 1) * width, rest)],
            upper_ref.at[f, :, pl.ds((f + 1) * width, rest)],
            upper_sems.at[f],
        )
        strips[f].start()
    sides = {}
    rights = {}
    grams = {}

    def project(f, basis, own):
        rows = stacked(basis)
        grams[f] = dot(basis, basis, ((1,), (1,)))
        side = {f: thin(rows, own)}
        for g in range(f + 1, FACES):
            side[g] = thin(rows, split(upper_ref[f, :, g * width : (g + 1) * width]))
        sides[f] = side
        rights[f] = thin(rows, split(resid_ref[f * width : (f + 1) * width]))

    packed = [pick(inputs, slot) for slot in where]
    guesses = begin(packed, copies, own_ref, own_out, partner_out, sum_ref)
    for f in early:
        if f in strips:
            strips[f].wait()
    vectors = {f: early_basis[i] for i, f in enumerate(early)}
    pending = [(f, vectors[f], load(early_own, i)) for i, f in enumerate(early)]
    for sweep in range(NS_ITERS - 1):
        guesses = newton(guesses, sum_ref)
        if pending:
            project(*pending.pop(0))
    for i in range(len(late)):
        store(inverse_out, i, guesses[i])
    basis = [starts_ref[f] for f in late]
    matrices = [
        [load(ref, i) for i in range(len(late))] for ref in (partner_out, inverse_out, own_out)
    ]
    for sweep in range(SUB_ITERS):
        basis = sweep_basis(*matrices, basis)
        if pending:
            project(*pending.pop(0))
    for item in pending:
        project(*item)
    for f in late:
        if f in strips:
            strips[f].wait()
    for i, f in enumerate(late):
        vectors[f] = basis[i]
        project(f, basis[i], load(own_out, i))
    factors = factor_inverses([grams[f] for f in range(FACES)])
    basis = [dot(factors[f], vectors[f]) for f in range(FACES)]
    blocks = []
    for g in range(FACES):
        tall = jnp.concatenate([sides[f][g] for f in range(g + 1)], axis=0)
        blocks.append(dot(tall, basis[g], ((1,), (1,))))
    even, odd, right = [], [], []
    lows = None
    for f in range(FACES):
        product_ref[f] = dot(factors[f], sides[f][f])
        line = [blocks[g][f * ncon : (f + 1) * ncon] for g in range(f, FACES)]
        line = dot(factors[f], jnp.concatenate([rights[f]] + line, axis=1))
        right.append(line[:, :columns])
        line = line[:, columns:]
        if f % 2 == 0:
            even.append(line)
            lows = line[:, ncon : 2 * ncon].T
        else:
            odd += [lows, line]
    payload_ref[...] = jnp.concatenate(
        [
            jnp.concatenate(even + right[0::2], axis=1),
            jnp.concatenate(odd + right[1::2], axis=1),
        ],
        axis=0,
    )


def find(faces, refs, f):
    for group, ref in zip(faces, refs):
        if f in group:
            return load(ref, list(group).index(f))


def theirs_kernel(faces, where, arrays, ncon, *refs):
    inputs = refs[:arrays]
    own_refs, partner_refs, inverse_refs = (refs[arrays + i : arrays + i + 2] for i in (0, 2, 4))
    basis_out = refs[arrays + 6]
    basis = [unpack_starts(pick(inputs, where[f]), ncon) for f in range(FACES)]
    matrices = [
        [find(faces, group, f) for f in range(FACES)]
        for group in (own_refs, inverse_refs, partner_refs)
    ]
    for sweep in range(SUB_ITERS):
        basis = sweep_basis(*matrices, basis)
    for f in range(FACES):
        basis_out[f] = basis[f]


def spread_kernel(faces, unread, basis_ref, product_ref, *refs):
    partner_refs, inverse_refs, out_ref = refs[0:2], refs[2:4], refs[4]
    basis = [basis_ref[f] for f in range(FACES)]
    factors = factor_inverses([dot(b, b, ((1,), (1,))) for b in basis])
    for f in range(FACES):
        product = thin(stacked(basis[f]), find(faces, partner_refs, f))
        both = jnp.concatenate([product_ref[f], dot(factors[f], product)], axis=0)
        high, low = split(thin(stacked(both), find(faces, inverse_refs, f)).T)
        out_ref[f] = jnp.concatenate([high, high, low], axis=1)


def member(group_ref, planes, dy=0, dz=0):
    y, z = lax.axis_index("gy"), lax.axis_index("gz")
    rows = lax.axis_size("gy")
    return group_ref[lax.rem(y + dy + rows, rows) * planes + lax.rem(z + dz + planes, planes)]


def choose_kernel(planes, group_ref, here_ref, there_ref, out_ref):
    core = lax.rem(lax.axis_index("gy"), 2)
    mine = member(group_ref, planes) == core
    other = member(group_ref, planes, dy=1 - 2 * core) == core
    out_ref[...] = jnp.where(mine, here_ref[...], 0.0) + jnp.where(other, there_ref[...], 0.0)


def add_kernel(first_ref, second_ref, unread, out_ref):
    out_ref[...] = first_ref[...] + second_ref[...]


def solve_kernel(size, ncon, terms, *refs):
    total = refs[0][...]
    for term in range(1, terms):
        total = total + refs[term][...]
    answer_ref, even_ref, odd_ref = refs[-3:]
    columns = answer_ref.shape[1]
    lines = []
    offset = 0
    for b in range(BLOCKS):
        lines.append(total[:, offset : offset + (BLOCKS - b) * size])
        offset += (BLOCKS - b) * size
    eye = iota((size, size), 0) == iota((size, size), 1)
    downs, acrosses = [], []
    for b in range(BLOCKS):
        diagonal = jnp.where(eye, lines[b][:, :size], 0.0)
        downs.append(lax.rsqrt(jnp.sum(diagonal, axis=1, keepdims=True)))
        acrosses.append(lax.rsqrt(jnp.sum(diagonal, axis=0, keepdims=True)))
    blocks = {}
    rights = []
    for b in range(BLOCKS):
        for c in range(b, BLOCKS):
            block = lines[b][:, (c - b) * size : (c - b + 1) * size]
            blocks[b, c] = downs[b] * block * acrosses[c]
        start = offset + b * columns
        rights.append(downs[b] * total[:, start : start + columns])
    for b in range(BLOCKS):
        (inverse,) = factor_inverses([blocks[b, b]])
        later = range(b + 1, BLOCKS)
        row = dot(inverse, jnp.concatenate([rights[b]] + [blocks[b, c] for c in later], axis=1))
        upper = {c: row[:, columns + (c - b - 1) * size : columns + (c - b) * size] for c in later}
        for c in later:
            for d in range(c, BLOCKS):
                blocks[c, d] = blocks[c, d] - dot(upper[c], upper[d], ((0,), (0,)))
            rights[c] = rights[c] - dot(upper[c], row[:, :columns], ((0,), (0,)))
        row = dot(inverse, row, ((0,), (0,)))
        rights[b] = row[:, :columns]
        for c in later:
            blocks[b, c] = row[:, columns + (c - b - 1) * size : columns + (c - b) * size]
        for i in range(b):
            for c in later:
                blocks[i, c] = blocks[i, c] - dot(blocks[i, b], blocks[b, c])
            rights[i] = rights[i] - dot(blocks[i, b], rights[b])
    answer = [downs[b] * rights[b] for b in range(BLOCKS)]
    answer_ref[...] = jnp.concatenate(answer, axis=0)
    even_ref[...] = answer[0][:ncon]
    odd_ref[...] = answer[0][ncon : 2 * ncon]


def last_product(spread, mine, theirs):
    high, low = split(jnp.concatenate([mine, theirs], axis=0))
    return lax.dot_general(
        spread,
        jnp.concatenate([high, low, high], axis=0),
        (((1,), (0,)), ((), ())),
        preferred_element_type=jnp.float32,
    )


def last_faces(spread_ref, pairs, out_ref, result, sems):
    width = spread_ref.shape[1]
    copies = []
    for f, (mine, theirs) in enumerate(pairs):
        place = pl.ds(f * width, width)
        result[f * width : (f + 1) * width] = last_product(spread_ref[f], mine, theirs)
        copy = pltpu.make_async_copy(result.at[place], out_ref.at[place], sems.at[f])
        copy.start()
        copies.append(copy)
    for copy in copies:
        copy.wait()


def last_kernel(where, arrays, ncon, spread_ref, answer_ref, *refs):
    theirs = refs[:arrays]
    pairs = [
        (answer_ref[f * ncon : (f + 1) * ncon], pick(theirs, where[f])) for f in range(FACES)
    ]
    last_faces(spread_ref, pairs, *refs[arrays:])


def last_pair_kernel(
    ncon, planes, group_ref, spread_ref, here_ref, there_ref, low_ref, high_ref, other_ref, *refs
):
    core = lax.rem(lax.axis_index("gy"), 2)

    def answer(group, f):
        place = slice(f * ncon, (f + 1) * ncon)
        return jnp.where(group == core, here_ref[place], there_ref[place])

    own = member(group_ref, planes)
    shifts = [(0, 0), (0, 0), (-1, 0), (1, 0), (0, -1), (0, 1)]
    pairs = []
    for f, (dy, dz) in enumerate(shifts):
        if f < 2:
            near = (low_ref, high_ref)[f][...]
            theirs = jnp.where(own == core, near, other_ref[f * ncon : (f + 1) * ncon])
        else:
            theirs = answer(member(group_ref, planes, dy, dz), f ^ 1)
        pairs.append((answer(own, f), theirs))
    last_faces(spread_ref, pairs, *refs)


def sum_rounds(rows, planes):
    rounds = [("gy", 2**i) for i in range(1, rows.bit_length() - 1)]
    return rounds + [("gz", 2**i) for i in range(planes.bit_length() - 1)]


def per_device(schur, start_block, resid, group_of):
    matrix = schur[0, 0, 0]
    starts = start_block[0, 0, 0].transpose(0, 2, 1)
    right = resid[0, 0, 0]
    order, columns = right.shape
    ncon, width = starts.shape[1:]
    counts = [lax.axis_size(axis) for axis in AXES]
    slots, arrays = face_slots(counts)
    coarse = FACES * ncon
    size = 2 * ncon
    lanes = size * BLOCKS * (BLOCKS + 1) // 2 + BLOCKS * columns
    anywhere = pl.BlockSpec(memory_space=pl.ANY)
    scalars = pl.BlockSpec(memory_space=pltpu.SMEM)
    early, late = (2, 3, 4, 5), (0, 1)
    faces = (early, late)

    def shape(*dims):
        return jax.ShapeDtypeStruct(dims, jnp.float32)

    def halves(count):
        return jax.ShapeDtypeStruct((count, 2, width, width), jnp.bfloat16)

    def params(mib):
        return pltpu.CompilerParams(vmem_limit_bytes=mib * MIB)

    packed = pl.pallas_call(
        functools.partial(pack_kernel, slots, width),
        out_shape=slot_shapes(counts, (width + 8 + 2 * ncon, width // 2)),
        in_specs=[anywhere, anywhere],
        out_specs=vmem_specs(arrays),
        scratch_shapes=[
            pltpu.VMEM((FACES, width, width), jnp.float32),
            pltpu.VMEM((FACES, ncon, width), jnp.float32),
            pltpu.SemaphoreType.DMA((FACES,)),
            pltpu.SemaphoreType.DMA,
        ],
        compiler_params=params(12),
    )(matrix, starts)
    got, where = swap(packed, counts)
    ahead = slots[2][0]
    got_late, got_early = got[:ahead], got[ahead:]
    where_early = [(where[f][0] - ahead, where[f][1]) for f in early]
    where_late = [where[f] for f in late]

    early_basis, early_own, early_partner, early_inverse = pl.pallas_call(
        functools.partial(early_kernel, early, where_early, len(got_early), width),
        out_shape=[shape(len(early), ncon, width)] + [halves(len(early))] * 3,
        in_specs=[anywhere] + vmem_specs(len(got_early) + 1),
        out_specs=vmem_specs(4),
        scratch_shapes=[
            pltpu.VMEM((len(early), width, width), jnp.float32),
            pltpu.VMEM((len(early), 2, width, width), jnp.bfloat16),
            pltpu.SemaphoreType.DMA((len(early),)),
        ],
        compiler_params=params(24),
    )(matrix, *got_early, starts)

    payload, product, late_own, late_partner, late_inverse = pl.pallas_call(
        functools.partial(main_kernel, early, late, where_late, len(got_late), width),
        out_shape=[shape(size, lanes), shape(FACES, ncon, width)] + [halves(len(late))] * 3,
        in_specs=[anywhere] + vmem_specs(len(got_late) + 4),
        out_specs=vmem_specs(5),
        scratch_shapes=[
            pltpu.VMEM((len(late), width, width), jnp.float32),
            pltpu.VMEM((FACES - 1, width, order), jnp.float32),
            pltpu.VMEM((len(late), 2, width, width), jnp.bfloat16),
            pltpu.SemaphoreType.DMA((len(late),)),
            pltpu.SemaphoreType.DMA((FACES - 1,)),
        ],
        compiler_params=params(32),
    )(matrix, *got_late, starts, right, early_basis, early_own)

    owns = [early_own, late_own]
    partners = [early_partner, late_partner]
    inverses = [early_inverse, late_inverse]
    theirs = pl.pallas_call(
        functools.partial(theirs_kernel, faces, where, arrays, ncon),
        out_shape=shape(FACES, ncon, width),
        in_specs=vmem_specs(arrays + 6),
        out_specs=vmem_specs(1)[0],
        compiler_params=params(20),
        cost_estimate=pl.CostEstimate(
            flops=4 * 10**9, bytes_accessed=10 * 2**20, transcendentals=0
        ),
    )(*got, *owns, *partners, *inverses)

    def spread_of(token):
        return pl.pallas_call(
            functools.partial(spread_kernel, faces),
            out_shape=jax.ShapeDtypeStruct((FACES, width, 3 * size), jnp.bfloat16),
            in_specs=[anywhere] + vmem_specs(6),
            out_specs=vmem_specs(1)[0],
            compiler_params=params(20),
            cost_estimate=pl.CostEstimate(
                flops=4 * 10**9, bytes_accessed=10 * 2**20, transcendentals=0
            ),
        )(token, theirs, product, *partners, *inverses)

    def solve(terms, unread):
        return pl.pallas_call(
            functools.partial(solve_kernel, size, ncon, len(terms)),
            out_shape=[shape(coarse, columns), shape(ncon, columns), shape(ncon, columns)],
            in_specs=vmem_specs(len(terms)) + [anywhere] * len(unread),
            out_specs=vmem_specs(3),
            compiler_params=params(12),
        )(*terms, *unread)

    rows, planes = counts[1], counts[2]
    groups = group_of.shape[0] // GROUP_SIZE
    result_scratch = [
        pltpu.VMEM((order, columns), jnp.float32),
        pltpu.SemaphoreType.DMA((FACES,)),
    ]
    if groups == 2 and rows > 1 and not (rows & (rows - 1) or planes & (planes - 1)):
        other = lax.ppermute(payload, "gy", flipped("gy", 1))
        part = pl.pallas_call(
            functools.partial(choose_kernel, planes),
            out_shape=shape(size, lanes),
            in_specs=[scalars] + vmem_specs(2),
            out_specs=vmem_specs(1)[0],
            compiler_params=params(8),
        )(group_of, payload, other)
        rounds = sum_rounds(rows, planes)
        spread = None
        for axis, bit in rounds[:-1]:
            moved = lax.ppermute(part, axis, flipped(axis, bit))
            part = pl.pallas_call(
                add_kernel,
                out_shape=shape(size, lanes),
                in_specs=vmem_specs(2) + [anywhere],
                out_specs=vmem_specs(1)[0],
                compiler_params=params(8),
            )(part, moved, theirs)
        axis, bit = rounds[-1]
        moved = lax.ppermute(part, axis, flipped(axis, bit))
        spread = spread_of(part)
        answer, even, odd = solve([part, moved], [spread])
        there = lax.ppermute(answer, "gy", flipped("gy", 1))
        forward, backward = ring("gx")
        low = lax.ppermute(odd, "gx", forward)
        high = lax.ppermute(even, "gx", backward)
        others = lax.ppermute(jnp.concatenate([low, high], axis=0), "gy", flipped("gy", 1))
        correction = pl.pallas_call(
            functools.partial(last_pair_kernel, ncon, planes),
            out_shape=shape(order, columns),
            in_specs=[scalars] + vmem_specs(6),
            out_specs=anywhere,
            scratch_shapes=result_scratch,
            compiler_params=params(8),
        )(group_of, spread, answer, there, low, high, others)
    else:
        y, z = lax.axis_index("gy"), lax.axis_index("gz")
        mine = group_of[y * planes + z]
        chosen = jnp.arange(groups, dtype=jnp.int32) == mine
        total = lax.psum(jnp.where(chosen[:, None, None], payload[None], 0.0), ("gy", "gz"))
        total = lax.dynamic_index_in_dim(total, mine, 0, keepdims=False)
        spread = spread_of(payload)
        answer, _, _ = solve([total], [])
        blocks = answer.reshape(FACES, ncon, columns)
        sent = []
        for position, count in enumerate(counts):
            pair = blocks[2 * position : 2 * position + 2]
            sent += [pair] if count == 2 else [pair[0], pair[1]]
        their_answers, _ = swap(sent, counts)
        correction = pl.pallas_call(
            functools.partial(last_kernel, where, arrays, ncon),
            out_shape=shape(order, columns),
            in_specs=vmem_specs(2 + arrays),
            out_specs=anywhere,
            scratch_shapes=result_scratch,
            compiler_params=params(8),
        )(spread, answer, *their_answers)
    return correction[None, None, None]


def solution(mesh):
    in_specs = (
        P("gx", "gy", "gz", None, None),
        P("gx", "gy", "gz", None, None, None),
        P("gx", "gy", "gz", None, None),
        P(),
    )
    out_specs = P("gx", "gy", "gz", None, None)
    return jax.shard_map(
        per_device, mesh=mesh, in_specs=in_specs, out_specs=out_specs, check_vma=False
    )
```

time: 81.4 us -> 60.6 us (0.74)
  Pallas kernels: 41.2 us -> 28.1 us
  waiting for transfers between devices: 15.1 us -> 12.5 us
  starting transfers between devices: 16.8 us -> 14.9 us
  other arithmetic: 1.59 us -> 0.01 us
  between operations: 1.52 us -> 0.27 us
    pallas_call x5 -> x8, Pallas kernels: 37.9 us -> 27.5 us  [the longest x1 7.73 us: per_device(): pl.pallas_call(functools.partial(main_kernel, early, late, where_late, le...]
    ppermute x2, waiting for transfers between devices: 3.68 us -> 0.01 us  [swap(): got.append(lax.ppermute(arrays[odd[0]], axis, forward))]
    ppermute x4 -> x2, waiting for transfers between devices: 8.51 us -> 5.24 us  [per_device(): moved = lax.ppermute(part, axis, flipped(axis, bit))]
    pallas_call x1, Pallas kernels: 3.28 us -> 0.61 us  [per_device(): pl.pallas_call(functools.partial(pack_kernel, slots, width), out_shape=sl...]
    ppermute x1, waiting for transfers between devices: 0.01 us -> 2.29 us  [swap(): got.append(lax.ppermute(arrays[even[0]], axis, forward))]
    ppermute x4 -> x2, starting transfers between devices: 4.18 us -> 2.37 us  [per_device(): moved = lax.ppermute(part, axis, flipped(axis, bit))]
    ppermute x1, waiting for transfers between devices: 0.01 us -> 1.43 us  [per_device(): other = lax.ppermute(payload, 'gy', flipped('gy', 1))]
    unnamed x28 -> x12, local copies, waits for them, and re-layouts: 3.38 us -> 4.62 us
  transfers between devices with their start and end apart: 14 -> 12, of which waited for: 6 -> 7; matrix products, arithmetic and copies ran while one was open for 2% -> 0% of each run, Pallas kernels for 22% -> 16%
where the time goes in v3:
time: 60.6 us; the launch traced here: 60.5 us
  Pallas kernels  28.1 us (46%)
  starting transfers between devices  14.9 us (25%)
  waiting for transfers between devices  12.5 us (21%)
  local copies, waits for them, and re-layouts  4.62 us (8%)
    pallas_call x1, Pallas kernels, per_device(): pl.pallas_call(functools.partial(main_kernel, early, late, where_late, le...  7.73 us
    pallas_call x1, Pallas kernels, solve(): pl.pallas_call(functools.partial(solve_kernel, size, ncon, len(terms)), o...  7.72 us
    ppermute x2, waiting for transfers between devices, per_device(): moved = lax.ppermute(part, axis, flipped(axis, bit))  5.24 us
    unnamed x12, local copies, waits for them, and re-layouts  4.62 us
    pallas_call x1, Pallas kernels, per_device(): pl.pallas_call(functools.partial(early_kernel, early, where_early, len(go...  4.16 us
    ppermute x2, starting transfers between devices, swap(): got.append(lax.ppermute(arrays[even[0]], axis, backward))  3.99 us
    pallas_call x1, Pallas kernels, spread_of(): pl.pallas_call(functools.partial(spread_kernel, faces), out_shape=jax.Sha...  3.7 us
    ppermute x1, starting transfers between devices, swap(): got.append(lax.ppermute(arrays[even[0]], axis, forward))  3.03 us
  transfers between devices with their start and end apart: 12, of which 7 were waited for; matrix products, arithmetic and copies ran while one was open for 0% of the time, Pallas kernels for 16%

profile of v3, /device:TPU:0, one launch (start us, length us, event | category | flops | bytes accessed | tf_op | source)
XLA Modules:
  0.0 60.5 jit_solution(3086984373149533161)
XLA Ops:
  0.0 0.0 copy-start
  0.0 3.7 %copy-done = f32[1,1,1,1536,1536]{4,3,2,1,0:T(8,128)S(1)} copy-done((f32[1,1,1,1536,1536]{4,3,2,1,0:T(8,128)S(1)}, f32[1,1,1,1536,1536]{4,3,2,1,0:T(8,128)}, u32[]{:S(2)}) %copy-start) | copy-done | bytes 9437208
  3.7 0.0 copy-start.2
  3.7 0.9 %copy-done.2 = f32[1,1,1,6,256,32]{4,5,3,2,1,0:T(8,128)S(1)} copy-done((f32[1,1,1,6,256,32]{4,5,3,2,1,0:T(8,128)S(1)}, f32[1,1,1,6,256,32]{4,5,3,2,1,0:T(8,128)}, u32[]{:S(2)}) %copy-start.2) | copy-done | bytes 196632
  4.6 0.0 copy-start.1
  4.6 0.0 copy-start.3
  4.6 0.0 copy-start.4
  4.6 0.6 %shard_map.46 = (f32[328,128]{1,0:T(8,128)S(1)}, f32[328,128]{1,0:T(8,128)S(1)}, f32[328,128]{1,0:T(8,128)S(1)}, f32[328,128]{1,0:T(8,128)S(1)}, f32[2,328,128]{2,1,0:T(8,128)S(1)}) custom-call(f32[1536,1536]{1,0:T(8,128)S(1)} %bitcast.6, f32[6,32,256]{2,1,0:T(8,128)S(1)} %bitcast.9), custom_call_target="tpu_custom_call" | custom-call | tf_op jit(solution)/shard_map/pallas_call | solution.py:587
  5.2 3.0 %collective-permute-start.4 = (f32[2,328,128]{2,1,0:T(8,128)S(1)}, f32[2,328,128]{2,1,0:T(8,128)S(1)}, u32[]{:S(2)}, u32[]{:S(2)}) collective-permute-start(f32[2,328,128]{2,1,0:T(8,128)S(1)} %get-tuple-element.26), channel_id=1, source_target_pairs={{0,1},{1,0},{2,3},{3,2},{4,5},{5,4},{6,7},{7,6},{8,9},{9,8},{10,11... | collective-permute-start | bytes 1007624 | tf_op jit(solution)/shard_map/ppermute | solution.py:93
  8.3 0.0 collective-permute-start.2
  8.3 1.7 %collective-permute-start.3 = (f32[328,128]{1,0:T(8,128)S(1)}, f32[328,128]{1,0:T(8,128)S(1)}, u32[]{:S(2)}, u32[]{:S(2)}) collective-permute-start(f32[328,128]{1,0:T(8,128)S(1)} %get-tuple-element.25), channel_id=1, source_target_pairs={{2,0},{4,2},{6,4},{0,6},{3,1},{5,3},{7,5},{1,7},{10,8},{12,10},{14... | collective-permute-start | bytes 503816 | tf_op jit(solution)/shard_map/ppermute | solution.py:97
  10.0 1.6 %collective-permute-start = (f32[328,128]{1,0:T(8,128)S(1)}, f32[328,128]{1,0:T(8,128)S(1)}, u32[]{:S(2)}, u32[]{:S(2)}) collective-permute-start(f32[328,128]{1,0:T(8,128)S(1)} %get-tuple-element.22), channel_id=1, source_target_pairs={{0,8},{8,16},{16,24},{24,0},{1,9},{9,17},{17,25},{25,1},{2,10},{10... | collective-permute-start | bytes 503816 | tf_op jit(solution)/shard_map/ppermute | solution.py:96
  11.6 0.0 copy-start.5
  11.6 2.2 %collective-permute-start.1 = (f32[328,128]{1,0:T(8,128)S(1)}, f32[328,128]{1,0:T(8,128)S(1)}, u32[]{:S(2)}, u32[]{:S(2)}) collective-permute-start(f32[328,128]{1,0:T(8,128)S(1)} %get-tuple-element.23), channel_id=1, source_target_pairs={{8,0},{16,8},{24,16},{0,24},{9,1},{17,9},{25,17},{1,25},{10,2},{18... | collective-permute-start | bytes 503816 | tf_op jit(solution)/shard_map/ppermute | solution.py:97
  13.8 0.0 collective-permute-done.2.refs_0_.refs_2_
  13.8 0.0 collective-permute-done.3.refs_1_.refs_3_
  13.9 2.3 %collective-permute-done.4.refs_2_.refs_4_ = f32[2,328,128]{2,1,0:T(8,128)S(1)} collective-permute-done((f32[2,328,128]{2,1,0:T(8,128)S(1)}, f32[2,328,128]{2,1,0:T(8,128)S(1)}, u32[]{:S(2)}, u32[]{:S(2)}) %collective-permute-start.4) | collective-permute-done | bytes 335904 | tf_op jit(solution)/shard_map/ppermute | solution.py:93
  16.1 0.0 copy-done.1
  16.1 0.0 copy-done.3
  16.2 4.2 %shard_map.47 = (f32[4,32,256]{2,1,0:T(8,128)S(1)}, bf16[4,2,256,256]{3,2,1,0:T(8,128)(2,1)S(1)}, bf16[4,2,256,256]{3,2,1,0:T(8,128)(2,1)S(1)}, bf16[4,2,256,256]{3,2,1,0:T(8,128)(2,1)S(1)}) custom-call(f32[1536,1536]{1,0:T(8,128)S(1)} %bitcast.7, f32[328,128]{1,0:T(8,128)S(1)} %collective-permute-done.2.refs_0_.refs_2_, ...), custom_call_target="tpu_custom_call" | custom-call | tf_op jit(solution)/shard_map/pallas_call | solution.py:606
  20.3 0.0 collective-permute-done.refs_0_
  20.3 0.6 %collective-permute-done.1.refs_1_ = f32[328,128]{1,0:T(8,128)S(1)} collective-permute-done((f32[328,128]{1,0:T(8,128)S(1)}, f32[328,128]{1,0:T(8,128)S(1)}, u32[]{:S(2)}, u32[]{:S(2)}) %collective-permute-start.1) | collective-permute-done | bytes 167968 | tf_op jit(solution)/shard_map/ppermute | solution.py:97
  21.0 0.0 copy-done.4
  21.0 7.7 %shard_map.48 = (f32[64,768]{1,0:T(8,128)S(1)}, f32[6,32,256]{2,1,0:T(8,128)S(1)}, bf16[2,2,256,256]{3,2,1,0:T(8,128)(2,1)S(1)}, bf16[2,2,256,256]{3,2,1,0:T(8,128)(2,1)S(1)}, bf16[2,2,256,256]{3,2,1,0:T(8,128)(2,1)S(1)}) custom-call(f32[1536,1536]{1,0:T(8,128)S(1)} %bitcast.8, f32[328,128]{1,0:T(8,128)S(1)} %collective-permute-done.refs_0_, ...), custom_call_target="tpu_custom_call" | custom-call | tf_op jit(solution)/shard_map/pallas_call | solution.py:619
  28.7 0.1 collective-permute-start.5
  28.8 1.4 %collective-permute-done.5.there_ref = f32[64,768]{1,0:T(8,128)S(1)} collective-permute-done((f32[64,768]{1,0:T(8,128)S(1)}, f32[64,768]{1,0:T(8,128)S(1)}, u32[]{:S(2)}, u32[]{:S(2)}) %collective-permute-start.5) | collective-permute-done | bytes 196640 | tf_op jit(solution)/shard_map/ppermute | solution.py:676
  30.2 0.0 copy-done.5
  30.2 0.6 shard_map.49.first_ref
  30.8 1.2 %collective-permute-start.6 = (f32[64,768]{1,0:T(8,128)S(1)}, f32[64,768]{1,0:T(8,128)S(1)}, u32[]{:S(2)}, u32[]{:S(2)}) collective-permute-start(f32[64,768]{1,0:T(8,128)S(1)} %shard_map.49.first_ref), channel_id=1, source_target_pairs={{0,4},{2,6},{4,0},{6,2},{1,5},{3,7},{5,1},{7,3},{8,12},{10,14},{12... | collective-permute-start | bytes 589832 | tf_op jit(solution)/shard_map/ppermute | solution.py:687
  32.0 1.9 %shard_map.50.unread.basis_ref = f32[6,32,256]{2,1,0:T(8,128)S(1)} custom-call(f32[328,128]{1,0:T(8,128)S(1)} %collective-permute-done.refs_0_, f32[328,128]{1,0:T(8,128)S(1)} %collective-permute-done.1.refs_1_, f32[328,128]{1,0:T(8,128)S(1)} %collective-permute-done.2.refs_0_.refs_2_, f32[328,128]{1,0:T(8,128)S(1)} %collective-permute-done.3.refs_1_.refs_3_, ...), custom_call_target="tpu_custom_call" | custom-call | flops 4000000000 | bytes 10485760 | tf_op jit(solution)/shard_map/pallas_call | solution.py:637
  33.9 4.0 %collective-permute-done.6.second_ref = f32[64,768]{1,0:T(8,128)S(1)} collective-permute-done((f32[64,768]{1,0:T(8,128)S(1)}, f32[64,768]{1,0:T(8,128)S(1)}, u32[]{:S(2)}, u32[]{:S(2)}) %collective-permute-start.6) | collective-permute-done | bytes 196640 | tf_op jit(solution)/shard_map/ppermute | solution.py:687
  37.9 1.2 %collective-permute-start.7 = (f32[64,768]{1,0:T(8,128)S(1)}, f32[64,768]{1,0:T(8,128)S(1)}, u32[]{:S(2)}, u32[]{:S(2)}) collective-permute-start(f32[64,768]{1,0:T(8,128)S(1)} %shard_map.51.unread.refs_0_), channel_id=1, source_target_pairs={{0,1},{1,0},{2,3},{3,2},{4,5},{5,4},{6,7},{7,6},{8,9},{9,8},{10,11... | collective-permute-start | bytes 589832 | tf_op jit(solution)/shard_map/ppermute | solution.py:696
  39.0 3.7 %shard_map.52.refs_2_.spread_ref = bf16[6,256,192]{2,1,0:T(8,128)(2,1)S(1)} custom-call(f32[64,768]{1,0:T(8,128)S(1)} %shard_map.51.unread.refs_0_, f32[6,32,256]{2,1,0:T(8,128)S(1)} %shard_map.50.unread.basis_ref, f32[6,32,256]{2,1,0:T(8,128)S(1)} %get-tuple-element.35.product_ref, bf16[4,2,256,256]{3,2,1,0:T(8,128)(2,1)S(1)} %get-tuple-element.31.refs_7_.refs_0_, ...), custom_call_target="tpu_custom_call" | custom-call | flops 4000000000 | bytes 10485760 | tf_op jit(solution)/shard_map/pallas_call | solution.py:649
  42.8 1.3 %collective-permute-done.7.refs_1_ = f32[64,768]{1,0:T(8,128)S(1)} collective-permute-done((f32[64,768]{1,0:T(8,128)S(1)}, f32[64,768]{1,0:T(8,128)S(1)}, u32[]{:S(2)}, u32[]{:S(2)}) %collective-permute-start.7) | collective-permute-done | bytes 196640 | tf_op jit(solution)/shard_map/ppermute | solution.py:696
  44.0 7.7 %shard_map.53 = (f32[192,128]{1,0:T(8,128)S(1)}, f32[32,128]{1,0:T(8,128)S(1)}, f32[32,128]{1,0:T(8,128)S(1)}) custom-call(f32[64,768]{1,0:T(8,128)S(1)} %shard_map.51.unread.refs_0_, f32[64,768]{1,0:T(8,128)S(1)} %collective-permute-done.7.refs_1_, bf16[6,256,192]{2,1,0:T(8,128)(2,1)S(1)} %shard_map.52.refs_2_.spread_ref), custom_call_target="tpu_custom_call" | custom-call | tf_op jit(solution)/shard_map/pallas_call | solution.py:661
  51.8 1.2 %collective-permute-start.9 = (f32[32,128]{1,0:T(8,128)S(1)}, f32[32,128]{1,0:T(8,128)S(1)}, u32[]{:S(2)}, u32[]{:S(2)}) collective-permute-start(f32[32,128]{1,0:T(8,128)S(1)} %get-tuple-element.37), channel_id=1, source_target_pairs={{0,8},{8,16},{16,24},{24,0},{1,9},{9,17},{17,25},{25,1},{2,10},{10... | collective-permute-start | bytes 49160 | tf_op jit(solution)/shard_map/ppermute | solution.py:701
  53.0 2.6 %collective-permute-start.10 = (f32[32,128]{1,0:T(8,128)S(1)}, f32[32,128]{1,0:T(8,128)S(1)}, u32[]{:S(2)}, u32[]{:S(2)}) collective-permute-start(f32[32,128]{1,0:T(8,128)S(1)} %get-tuple-element.38), channel_id=1, source_target_pairs={{8,0},{16,8},{24,16},{0,24},{9,1},{17,9},{25,17},{1,25},{10,2},{18... | collective-permute-start | bytes 49160 | tf_op jit(solution)/shard_map/ppermute | solution.py:702
  55.6 0.0 collective-permute-start.8
  55.6 1.7 %collective-permute-done.9.low_ref = f32[32,128]{1,0:T(8,128)S(1)} collective-permute-done((f32[32,128]{1,0:T(8,128)S(1)}, f32[32,128]{1,0:T(8,128)S(1)}, u32[]{:S(2)}, u32[]{:S(2)}) %collective-permute-start.9) | collective-permute-done | bytes 16416 | tf_op jit(solution)/shard_map/ppermute | solution.py:701
  57.3 0.0 collective-permute-done.10.high_ref
  57.4 0.0 collective-permute-start.11
  57.4 1.2 %collective-permute-done.11.other_ref = f32[64,128]{1,0:T(8,128)S(1)} collective-permute-done((f32[64,128]{1,0:T(8,128)S(1)}, f32[64,128]{1,0:T(8,128)S(1)}, u32[]{:S(2)}, u32[]{:S(2)}) %collective-permute-start.11) | collective-permute-done | bytes 32800 | tf_op jit(solution)/shard_map/ppermute | solution.py:703
  58.6 0.0 collective-permute-done.8.there_ref
  58.6 1.7 %shard_map.54 = f32[1536,128]{1,0:T(8,128)} custom-call(s32[8]{0:T(128)S(1)} %copy-done.5, bf16[6,256,192]{2,1,0:T(8,128)(2,1)S(1)} %shard_map.52.refs_2_.spread_ref, f32[192,128]{1,0:T(8,128)S(1)} %get-tuple-element.36.here_ref, f32[192,128]{1,0:T(8,128)S(1)} %collective-permute-done.8.there_ref, f32[32,128]{1,0:T(8,128)S(1)} %collective-permute-done.9.low_ref, ...), custom_call_target="tpu_custom_call" | custom-call | tf_op jit(solution)/shard_map/pallas_call | solution.py:704
  (2 shorter events, 0.0 us)
Async XLA Ops:
  0.0 3.7 %copy-start = (f32[1,1,1,1536,1536]{4,3,2,1,0:T(8,128)S(1)}, f32[1,1,1,1536,1536]{4,3,2,1,0:T(8,128)}, u32[]{:S(2)}) copy-start(f32[1,1,1,1536,1536]{4,3,2,1,0:T(8,128)} %param.4) | copy-start | bytes 28311556
  3.7 0.9 %copy-start.2 = (f32[1,1,1,6,256,32]{4,5,3,2,1,0:T(8,128)S(1)}, f32[1,1,1,6,256,32]{4,5,3,2,1,0:T(8,128)}, u32[]{:S(2)}) copy-start(f32[1,1,1,6,256,32]{4,5,3,2,1,0:T(8,128)} %param.5) | copy-start | bytes 589828
  4.6 11.5 %copy-start.1 = (f32[1,1,1,1536,1536]{4,3,2,1,0:T(8,128)S(1)}, f32[1,1,1,1536,1536]{4,3,2,1,0:T(8,128)}, u32[]{:S(2)}) copy-start(f32[1,1,1,1536,1536]{4,3,2,1,0:T(8,128)} %param.4) | copy-start | bytes 28311556
  4.6 11.5 %copy-start.3 = (f32[1,1,1,6,256,32]{4,5,3,2,1,0:T(8,128)S(1)}, f32[1,1,1,6,256,32]{4,5,3,2,1,0:T(8,128)}, u32[]{:S(2)}) copy-start(f32[1,1,1,6,256,32]{4,5,3,2,1,0:T(8,128)} %param.5) | copy-start | bytes 589828
  4.6 16.4 %copy-start.4 = (f32[1,1,1,1536,128]{4,3,2,1,0:T(8,128)S(1)}, f32[1,1,1,1536,128]{4,3,2,1,0:T(8,128)}, u32[]{:S(2)}) copy-start(f32[1,1,1,1536,128]{4,3,2,1,0:T(8,128)} %param.6) | copy-start | bytes 2359300
  5.2 10.9 %collective-permute-start.4 = (f32[2,328,128]{2,1,0:T(8,128)S(1)}, f32[2,328,128]{2,1,0:T(8,128)S(1)}, u32[]{:S(2)}, u32[]{:S(2)}) collective-permute-start(f32[2,328,128]{2,1,0:T(8,128)S(1)} %get-tuple-element.26), channel_id=1, source_target_pairs={{0,1},{1,0},{2,3},{3,2},{4,5},{5,4},{6,7},{7,6},{8,9},{9,8},{10,11... | collective-permute-start | bytes 1007624 | tf_op jit(solution)/shard_map/ppermute | solution.py:93
  8.3 5.6 %collective-permute-start.2 = (f32[328,128]{1,0:T(8,128)S(1)}, f32[328,128]{1,0:T(8,128)S(1)}, u32[]{:S(2)}, u32[]{:S(2)}) collective-permute-start(f32[328,128]{1,0:T(8,128)S(1)} %get-tuple-element.24), channel_id=1, source_target_pairs={{0,2},{2,4},{4,6},{6,0},{1,3},{3,5},{5,7},{7,1},{8,10},{10,12},{12... | collective-permute-start | bytes 503816 | tf_op jit(solution)/shard_map/ppermute | solution.py:96
  8.3 5.6 %collective-permute-start.3 = (f32[328,128]{1,0:T(8,128)S(1)}, f32[328,128]{1,0:T(8,128)S(1)}, u32[]{:S(2)}, u32[]{:S(2)}) collective-permute-start(f32[328,128]{1,0:T(8,128)S(1)} %get-tuple-element.25), channel_id=1, source_target_pairs={{2,0},{4,2},{6,4},{0,6},{3,1},{5,3},{7,5},{1,7},{10,8},{12,10},{14... | collective-permute-start | bytes 503816 | tf_op jit(solution)/shard_map/ppermute | solution.py:97
  10.0 10.3 %collective-permute-start = (f32[328,128]{1,0:T(8,128)S(1)}, f32[328,128]{1,0:T(8,128)S(1)}, u32[]{:S(2)}, u32[]{:S(2)}) collective-permute-start(f32[328,128]{1,0:T(8,128)S(1)} %get-tuple-element.22), channel_id=1, source_target_pairs={{0,8},{8,16},{16,24},{24,0},{1,9},{9,17},{17,25},{25,1},{2,10},{10... | collective-permute-start | bytes 503816 | tf_op jit(solution)/shard_map/ppermute | solution.py:96
  11.6 18.6 %copy-start.5 = (s32[8]{0:T(128)S(1)}, s32[8]{0:T(128)}, u32[]{:S(2)}) copy-start(s32[8]{0:T(128)} %group_ref.3) | copy-start | bytes 100
  11.6 9.4 %collective-permute-start.1 = (f32[328,128]{1,0:T(8,128)S(1)}, f32[328,128]{1,0:T(8,128)S(1)}, u32[]{:S(2)}, u32[]{:S(2)}) collective-permute-start(f32[328,128]{1,0:T(8,128)S(1)} %get-tuple-element.23), channel_id=1, source_target_pairs={{8,0},{16,8},{24,16},{0,24},{9,1},{17,9},{25,17},{1,25},{10,2},{18... | collective-permute-start | bytes 503816 | tf_op jit(solution)/shard_map/ppermute | solution.py:97
  28.7 1.5 %collective-permute-start.5 = (f32[64,768]{1,0:T(8,128)S(1)}, f32[64,768]{1,0:T(8,128)S(1)}, u32[]{:S(2)}, u32[]{:S(2)}) collective-permute-start(f32[64,768]{1,0:T(8,128)S(1)} %get-tuple-element.29.here_ref), channel_id=1, source_target_pairs={{0,2},{2,0},{4,6},{6,4},{1,3},{3,1},{5,7},{7,5},{8,10},{10,8},{12,... | collective-permute-start | bytes 589832 | tf_op jit(solution)/shard_map/ppermute | solution.py:676
  30.8 7.0 %collective-permute-start.6 = (f32[64,768]{1,0:T(8,128)S(1)}, f32[64,768]{1,0:T(8,128)S(1)}, u32[]{:S(2)}, u32[]{:S(2)}) collective-permute-start(f32[64,768]{1,0:T(8,128)S(1)} %shard_map.49.first_ref), channel_id=1, source_target_pairs={{0,4},{2,6},{4,0},{6,2},{1,5},{3,7},{5,1},{7,3},{8,12},{10,14},{12... | collective-permute-start | bytes 589832 | tf_op jit(solution)/shard_map/ppermute | solution.py:687
  37.9 6.2 %collective-permute-start.7 = (f32[64,768]{1,0:T(8,128)S(1)}, f32[64,768]{1,0:T(8,128)S(1)}, u32[]{:S(2)}, u32[]{:S(2)}) collective-permute-start(f32[64,768]{1,0:T(8,128)S(1)} %shard_map.51.unread.refs_0_), channel_id=1, source_target_pairs={{0,1},{1,0},{2,3},{3,2},{4,5},{5,4},{6,7},{7,6},{8,9},{9,8},{10,11... | collective-permute-start | bytes 589832 | tf_op jit(solution)/shard_map/ppermute | solution.py:696
  51.8 5.6 %collective-permute-start.9 = (f32[32,128]{1,0:T(8,128)S(1)}, f32[32,128]{1,0:T(8,128)S(1)}, u32[]{:S(2)}, u32[]{:S(2)}) collective-permute-start(f32[32,128]{1,0:T(8,128)S(1)} %get-tuple-element.37), channel_id=1, source_target_pairs={{0,8},{8,16},{16,24},{24,0},{1,9},{9,17},{17,25},{25,1},{2,10},{10... | collective-permute-start | bytes 49160 | tf_op jit(solution)/shard_map/ppermute | solution.py:701
  53.0 4.4 %collective-permute-start.10 = (f32[32,128]{1,0:T(8,128)S(1)}, f32[32,128]{1,0:T(8,128)S(1)}, u32[]{:S(2)}, u32[]{:S(2)}) collective-permute-start(f32[32,128]{1,0:T(8,128)S(1)} %get-tuple-element.38), channel_id=1, source_target_pairs={{8,0},{16,8},{24,16},{0,24},{9,1},{17,9},{25,17},{1,25},{10,2},{18... | collective-permute-start | bytes 49160 | tf_op jit(solution)/shard_map/ppermute | solution.py:702
  55.6 2.9 %collective-permute-start.8 = (f32[192,128]{1,0:T(8,128)S(1)}, f32[192,128]{1,0:T(8,128)S(1)}, u32[]{:S(2)}, u32[]{:S(2)}) collective-permute-start(f32[192,128]{1,0:T(8,128)S(1)} %get-tuple-element.36.here_ref), channel_id=1, source_target_pairs={{0,2},{2,0},{4,6},{6,4},{1,3},{3,1},{5,7},{7,5},{8,10},{10,8},{12,... | collective-permute-start | bytes 294920 | tf_op jit(solution)/shard_map/ppermute | solution.py:699
  57.4 1.2 %collective-permute-start.11 = (f32[64,128]{1,0:T(8,128)S(1)}, f32[64,128]{1,0:T(8,128)S(1)}, u32[]{:S(2)}, u32[]{:S(2)}) collective-permute-start(f32[64,128]{1,0:T(8,128)S(1)} %pad_maximum_fusion), channel_id=1, source_target_pairs={{0,2},{2,0},{4,6},{6,4},{1,3},{3,1},{5,7},{7,5},{8,10},{10,8},{12,... | collective-permute-start | bytes 98312 | tf_op jit(solution)/shard_map/ppermute | solution.py:703

commit v4 on v3

v4 whole, which is shorter than its diff:
```python
import functools

import jax
import jax.numpy as jnp
from jax import lax
from jax.experimental import pallas as pl
from jax.experimental.pallas import tpu as pltpu
from jax.sharding import PartitionSpec as P

NS_ITERS = 3
SUB_ITERS = 2
GROUP_SIZE = 4
FACES = 6
BLOCKS = FACES // 2
AXES = ("gx", "gy", "gz")
MIB = 1024 * 1024

precise = lax.Precision.HIGHEST


def dot(left, right, dims=((1,), (0,))):
    return lax.dot_general(
        left, right, (dims, ((), ())), precision=precise, preferred_element_type=jnp.float32
    )


def split(value):
    high = value.astype(jnp.bfloat16)
    return high, (value - high.astype(jnp.float32)).astype(jnp.bfloat16)


def wide(left, right):
    return lax.dot_general(
        jnp.concatenate([left[0], left[0], left[1]], axis=1),
        jnp.concatenate([right[0], right[1], right[0]], axis=0),
        (((1,), (0,)), ((), ())),
        preferred_element_type=jnp.float32,
    )


def stacked(value):
    return jnp.concatenate(split(value), axis=0)


def thin(rows, matrix):
    out = lax.dot_general(
        jnp.concatenate([rows, rows], axis=1),
        jnp.concatenate(matrix, axis=0),
        (((1,), (0,)), ((), ())),
        preferred_element_type=jnp.float32,
    )
    half = rows.shape[0] // 2
    return out[:half] + out[half:]


def iota(shape, dim):
    return lax.broadcasted_iota(jnp.int32, shape, dim)


def flipped(axis, bit):
    return [(i, i ^ bit) for i in range(lax.axis_size(axis))]


def outer_pairs(axis):
    count = lax.axis_size(axis)
    return [(i, (i + 1 if i % 2 else i - 1) % count) for i in range(count)]


def face_arrays(count):
    return 1 if count == 2 else 2


def exchange(arrays, axis):
    if lax.axis_size(axis) == 2:
        return [lax.ppermute(arrays[0], axis, flipped(axis, 1))]
    return [
        lax.ppermute(arrays[0], axis, flipped(axis, 1)),
        lax.ppermute(arrays[1], axis, outer_pairs(axis)),
    ]


def is_even(axis):
    return lax.rem(lax.axis_index(axis), 2) == 0


def send(refs, axis, even, odd):
    if lax.axis_size(axis) == 2:
        refs[0][0] = even
        refs[0][1] = odd
    else:
        upward = is_even(axis)
        refs[0][...] = jnp.where(upward, odd, even)
        refs[1][...] = jnp.where(upward, even, odd)


def receive(refs, axis):
    if lax.axis_size(axis) == 2:
        return refs[0][1], refs[0][0]
    upward = is_even(axis)
    first, second = refs[0][...], refs[1][...]
    return jnp.where(upward, second, first), jnp.where(upward, first, second)


def face_shapes(count, shape):
    if count == 2:
        return [jax.ShapeDtypeStruct((2,) + shape, jnp.float32)]
    return [jax.ShapeDtypeStruct(shape, jnp.float32)] * 2


def vmem_specs(count):
    return [pl.BlockSpec(memory_space=pltpu.VMEM)] * count


def pack_kernel(counts, width, schur_ref, starts_ref, *refs):
    outs, blocks = refs[:-4], refs[-4]
    starts, sems, start_sem = refs[-3:]
    half = width // 2
    copies = []
    for f in range(FACES):
        place = pl.ds(f * width, width)
        copy = pltpu.make_async_copy(schur_ref.at[place, place], blocks.at[f], sems.at[f])
        copy.start()
        copies.append(copy)
    start_copy = pltpu.make_async_copy(starts_ref, starts, start_sem)
    start_copy.start()
    row, col = iota((half, half), 0), iota((half, half), 1)
    start_copy.wait()

    def pack(f):
        copies[f].wait()
        first = blocks[f, 0:half, 0:half]
        second = blocks[f, half:width, half:width]
        diag = jnp.sum(jnp.where(row == col, second, 0.0), axis=0, keepdims=True)
        mixed = jnp.where(row >= col, first, second)
        tail = jnp.broadcast_to(diag, (8, half))
        start = starts[f]
        return jnp.concatenate(
            [blocks[f, half:width, 0:half], mixed, tail, start[:, :half], start[:, half:]], axis=0
        )

    done = 0
    for position, axis in enumerate(AXES):
        number = face_arrays(counts[position])
        send(outs[done : done + number], axis, pack(2 * position), pack(2 * position + 1))
        done += number


def unpack(packed):
    half = packed.shape[1]
    row, col = iota((half, half), 0), iota((half, half), 1)
    low = packed[0:half]
    mixed = packed[half : 2 * half]
    flip = mixed.T
    first = jnp.where(row >= col, mixed, flip)
    second = jnp.where(row < col, mixed, flip)
    second = jnp.where(row == col, packed[2 * half : 2 * half + 1], second)
    return jnp.concatenate(
        [jnp.concatenate([first, low.T], axis=1), jnp.concatenate([low, second], axis=1)], axis=0
    )


def unpack_starts(packed, ncon):
    half = packed.shape[1]
    rows = packed[2 * half + 8 :]
    return jnp.concatenate([rows[:ncon], rows[ncon:]], axis=1)


def factor_inverses(grams, block=8, invert=False):
    size = grams[0].shape[0]
    strips = size // 8
    lanes = 128
    full = (8, lanes)
    state = []
    for gram in grams:
        parts = [gram, jnp.where(iota((size, size), 0) == iota((size, size), 1), 1.0, 0.0)]
        if 2 * size < lanes:
            parts.append(jnp.zeros((size, lanes - 2 * size), jnp.float32))
        whole = jnp.concatenate(parts, axis=1)
        state.append([whole[8 * s : 8 * s + 8] for s in range(strips)])
    below = iota(full, 0)

    def line_of(strip, line):
        return jnp.broadcast_to(strip[line : line + 1], full)

    for start in range(0, size, block):
        strip, first = start // 8, start % 8
        active = range(0 if invert else strip, strips)
        for work in state:
            cols = [
                {s: jnp.broadcast_to(work[s][:, start + j : start + j + 1], full) for s in active}
                for j in range(block)
            ]
            factors = []

            def eliminate(j, scale, stop):
                line = first + j
                factor = {s: cols[j][s] * scale for s in active}
                hit = below != line if invert else below > line
                factor[strip] = jnp.where(hit, factor[strip], 0.0)
                for later in range(j + 1, stop):
                    head = line_of(cols[later][strip], line)
                    for s in active:
                        cols[later][s] = cols[later][s] - factor[s] * head
                factors.append(factor)

            for j in range(0, block, 2):
                line = first + j
                corner = line_of(cols[j][strip], line)
                side = line_of(cols[j][strip], line + 1)
                last = line_of(cols[j + 1][strip], line + 1)
                inverse = 1.0 / (corner * last - side * side)
                eliminate(j, 1.0 / corner, block)
                eliminate(j + 1, corner * inverse, block)
            for j in range(block):
                row = line_of(work[strip], first + j)
                for s in active:
                    if s == strip and first + j == 7 and not invert:
                        continue
                    work[s] = work[s] - factors[j][s] * row
    results = []
    for work in state:
        parts = []
        for s in range(strips):
            place = iota((8, size), 0) + 8 * s == iota((8, size), 1)
            pivot = jnp.sum(jnp.where(place, work[s][:, :size], 0.0), axis=1, keepdims=True)
            scale = 1.0 / pivot if invert else lax.rsqrt(pivot)
            parts.append(work[s][:, size : 2 * size] * scale)
        results.append(jnp.concatenate(parts, axis=0))
    return results


def member(group_ref, planes, dy=0, dz=0):
    y, z = lax.axis_index("gy"), lax.axis_index("gz")
    rows = lax.axis_size("gy")
    return group_ref[lax.rem(y + dy + rows, rows) * planes + lax.rem(z + dz + planes, planes)]


def store(ref, f, value):
    ref[f, 0], ref[f, 1] = split(value)


def load(ref, f):
    return ref[f, 0], ref[f, 1]


def upper_index(f, g):
    return sum(FACES - 1 - i for i in range(f)) + g - f - 1


def halves_kernel(planes, schur_ref, group_ref, own_ref, own_out, upper_out, flag_out, *scratch):
    upper_ref, sems = scratch
    width = own_ref.shape[1]
    strips = []
    for f in range(FACES - 1):
        rest = (FACES - 1 - f) * width
        copy = pltpu.make_async_copy(
            schur_ref.at[pl.ds(f * width, width), pl.ds((f + 1) * width, rest)],
            upper_ref.at[f, :, pl.ds((f + 1) * width, rest)],
            sems.at[f],
        )
        copy.start()
        strips.append(copy)
    core = lax.rem(lax.axis_index("gy"), 2)
    near = [(0, 0), (1 - 2 * core, 0), (-1, 0), (1, 0), (0, -1), (0, 1)]
    row = iota(flag_out.shape, 0)
    flags = jnp.zeros(flag_out.shape, jnp.float32)
    for i, (dy, dz) in enumerate(near):
        hit = member(group_ref, planes, dy, dz) == core
        flags = jnp.where(row == i, jnp.where(hit, 1.0, 0.0), flags)
    flag_out[...] = flags
    for f in range(FACES):
        store(own_out, f, own_ref[f])
    for f in range(FACES - 1):
        strips[f].wait()
        for g in range(f + 1, FACES):
            store(upper_out, upper_index(f, g), upper_ref[f, :, g * width : (g + 1) * width])


def begin(packed, owns, partner_out, sum_ref):
    width = owns[0].shape[1]
    eye = iota((width, width), 0) == iota((width, width), 1)
    guesses = []
    for f in range(len(packed)):
        partner = unpack(packed[f])
        total = owns[f] + partner
        store(partner_out, f, partner)
        store(sum_ref, f, total)
        diagonal = jnp.where(eye, total, 0.0)
        across = 1.0 / jnp.sum(diagonal, axis=0, keepdims=True)
        down = 1.0 / jnp.sum(diagonal, axis=1, keepdims=True)
        guesses.append(jnp.where(eye, 2.0 * across, 0.0) - down * total * across)
    return guesses


def newton(guesses, sum_ref):
    results = []
    for f, guess in enumerate(guesses):
        halves = split(guess)
        product = split(wide(load(sum_ref, f), halves))
        results.append(2.0 * guess - wide(halves, product))
    return results


def unit_rows(basis):
    return [b * lax.rsqrt(jnp.sum(b * b, axis=1, keepdims=True)) for b in basis]


def sweep_basis(before, inverse, after, basis):
    for matrices in (before, inverse, after):
        basis = [thin(stacked(b), matrix) for b, matrix in zip(basis, matrices)]
    return unit_rows(basis)


def early_kernel(axes, faces, *refs):
    arrays = len(refs) - 7
    inputs = refs[:arrays]
    own_ref, halves_ref, starts_ref, basis_out, partner_out, inverse_out, sum_ref = refs[arrays:]
    count = len(faces)
    packed = []
    done = 0
    for axis in axes:
        number = face_arrays(lax.axis_size(axis))
        packed += receive(inputs[done : done + number], axis)
        done += number
    guesses = begin(packed, [own_ref[f] for f in faces], partner_out, sum_ref)
    for sweep in range(NS_ITERS - 1):
        guesses = newton(guesses, sum_ref)
    for i in range(count):
        store(inverse_out, i, guesses[i])
    basis = [starts_ref[f] for f in faces]
    matrices = [
        [load(partner_out, i) for i in range(count)],
        [load(inverse_out, i) for i in range(count)],
        [load(halves_ref, f) for f in faces],
    ]
    for sweep in range(SUB_ITERS):
        basis = sweep_basis(*matrices, basis)
    for i in range(count):
        basis_out[i] = basis[i]


def main_kernel(axes, early, late, *refs):
    arrays = len(refs) - 11
    inputs = refs[:arrays]
    own_ref, halves_ref, upper_ref, starts_ref, resid_ref, early_basis = refs[arrays : arrays + 6]
    payload_ref, product_ref, partner_out, inverse_out, sum_ref = refs[arrays + 6 :]
    ncon, width = starts_ref.shape[1:]
    columns = resid_ref.shape[1]
    sides = {}
    rights = {}
    grams = {}
    vectors = {}
    count = len(late)

    def project(f, basis):
        vectors[f] = basis
        rows = stacked(basis)
        grams[f] = dot(basis, basis, ((1,), (1,)))
        side = {f: thin(rows, load(halves_ref, f))}
        for g in range(f + 1, FACES):
            side[g] = thin(rows, load(upper_ref, upper_index(f, g)))
        sides[f] = side
        rights[f] = thin(rows, split(resid_ref[f * width : (f + 1) * width]))

    packed = []
    done = 0
    for axis in axes:
        number = face_arrays(lax.axis_size(axis))
        packed += receive(inputs[done : done + number], axis)
        done += number
    guesses = begin(packed, [own_ref[f] for f in late], partner_out, sum_ref)
    pending = [(f, early_basis[i]) for i, f in enumerate(early)]
    for sweep in range(NS_ITERS - 1):
        guesses = newton(guesses, sum_ref)
        if pending:
            project(*pending.pop(0))
    for i in range(count):
        store(inverse_out, i, guesses[i])
    basis = [starts_ref[f] for f in late]
    matrices = [
        [load(partner_out, i) for i in range(count)],
        [load(inverse_out, i) for i in range(count)],
        [load(halves_ref, f) for f in late],
    ]
    for sweep in range(SUB_ITERS):
        basis = sweep_basis(*matrices, basis)
        if pending:
            project(*pending.pop(0))
    for item in pending:
        project(*item)
    for i, f in enumerate(late):
        project(f, basis[i])
    factors = factor_inverses([grams[f] for f in range(FACES)])
    blocks = []
    for g in range(FACES):
        tall = jnp.concatenate([sides[f][g] for f in range(g + 1)], axis=0)
        blocks.append(dot(dot(tall, vectors[g], ((1,), (1,))), factors[g], ((1,), (1,))))
    even, odd, right = [], [], []
    lows = None
    for f in range(FACES):
        product_ref[f] = dot(factors[f], sides[f][f])
        line = [blocks[g][f * ncon : (f + 1) * ncon] for g in range(f, FACES)]
        line = dot(factors[f], jnp.concatenate([rights[f]] + line, axis=1))
        right.append(line[:, :columns])
        line = line[:, columns:]
        if f % 2 == 0:
            even.append(line)
            lows = line[:, ncon : 2 * ncon].T
        else:
            odd += [lows, line]
    payload_ref[...] = jnp.concatenate(
        [
            jnp.concatenate(even + right[0::2], axis=1),
            jnp.concatenate(odd + right[1::2], axis=1),
        ],
        axis=0,
    )


def find(faces, refs, f):
    for group, ref in zip(faces, refs):
        if f in group:
            return load(ref, list(group).index(f))


def theirs_kernel(faces, ncon, *refs):
    arrays = len(refs) - 7
    inputs = refs[:arrays]
    own_ref, partner_refs, inverse_refs = refs[arrays], refs[-6:-4], refs[-4:-2]
    basis_out, product_out = refs[-2:]
    basis = []
    done = 0
    for axis in AXES:
        number = face_arrays(lax.axis_size(axis))
        packed = receive(inputs[done : done + number], axis)
        basis += [unpack_starts(part, ncon) for part in packed]
        done += number
    matrices = [
        [load(own_ref, f) for f in range(FACES)],
        [find(faces, inverse_refs, f) for f in range(FACES)],
        [find(faces, partner_refs, f) for f in range(FACES)],
    ]
    for sweep in range(SUB_ITERS):
        basis = sweep_basis(*matrices, basis)
    for f in range(FACES):
        basis_out[f] = basis[f]
        product_out[f] = thin(stacked(basis[f]), matrices[2][f])


def spread_kernel(faces, unread, basis_ref, theirs_ref, product_ref, *refs):
    inverse_refs, out_ref = refs[0:2], refs[2]
    basis = [basis_ref[f] for f in range(FACES)]
    factors = factor_inverses([dot(b, b, ((1,), (1,))) for b in basis])
    for f in range(FACES):
        both = jnp.concatenate([product_ref[f], dot(factors[f], theirs_ref[f])], axis=0)
        high, low = split(thin(stacked(both), find(faces, inverse_refs, f)).T)
        out_ref[f] = jnp.concatenate([high, high, low], axis=1)


def choose_kernel(flag_ref, here_ref, there_ref, matrix_ref, right_ref):
    mine = flag_ref[0:1, 0:1] > 0.5
    other = flag_ref[1:2, 0:1] > 0.5
    total = jnp.where(mine, here_ref[...], 0.0) + jnp.where(other, there_ref[...], 0.0)
    lanes = matrix_ref.shape[1]
    matrix_ref[...] = total[:, :lanes]
    right_ref[...] = total[:, lanes:]


def add_kernel(first_ref, second_ref, third_ref, fourth_ref, unread, matrix_ref, right_ref):
    matrix_ref[...] = first_ref[...] + second_ref[...]
    right_ref[...] = third_ref[...] + fourth_ref[...]


def solve_kernel(size, ncon, terms, *refs):
    matrix, right = refs[0][...], refs[terms][...]
    for term in range(1, terms):
        matrix = matrix + refs[term][...]
        right = right + refs[terms + term][...]
    answer_ref, sent = refs[2 * terms + 1], refs[2 * terms + 2 :]
    columns = answer_ref.shape[1]
    lines = []
    offset = 0
    for b in range(BLOCKS):
        lines.append(matrix[:, offset : offset + (BLOCKS - b) * size])
        offset += (BLOCKS - b) * size
    eye = iota((size, size), 0) == iota((size, size), 1)
    downs, acrosses = [], []
    for b in range(BLOCKS):
        diagonal = jnp.where(eye, lines[b][:, :size], 0.0)
        downs.append(lax.rsqrt(jnp.sum(diagonal, axis=1, keepdims=True)))
        acrosses.append(lax.rsqrt(jnp.sum(diagonal, axis=0, keepdims=True)))
    blocks = {}
    rights = []
    for b in range(BLOCKS):
        for c in range(b, BLOCKS):
            block = lines[b][:, (c - b) * size : (c - b + 1) * size]
            blocks[b, c] = downs[b] * block * acrosses[c]
            if c > b:
                blocks[c, b] = blocks[b, c].T
        rights.append(downs[b] * right[:, b * columns : (b + 1) * columns])
    for b in range(BLOCKS):
        (inverse,) = factor_inverses([blocks[b, b]], invert=True)
        later = range(b + 1, BLOCKS)
        row = dot(inverse, jnp.concatenate([rights[b]] + [blocks[b, c] for c in later], axis=1))
        rights[b] = row[:, :columns]
        for c in later:
            start = columns + (c - b - 1) * size
            blocks[b, c] = row[:, start : start + size]
        for i in range(BLOCKS):
            if i == b:
                continue
            change = dot(blocks[i, b], row)
            rights[i] = rights[i] - change[:, :columns]
            for c in later:
                start = columns + (c - b - 1) * size
                blocks[i, c] = blocks[i, c] - change[:, start : start + size]
    answer = [downs[b] * rights[b] for b in range(BLOCKS)]
    answer_ref[...] = jnp.concatenate(answer, axis=0)
    if sent:
        send(sent, AXES[0], answer[0][:ncon], answer[0][ncon : 2 * ncon])


def last_product(spread, mine, theirs):
    high, low = split(jnp.concatenate([mine, theirs], axis=0))
    return lax.dot_general(
        spread,
        jnp.concatenate([high, low, high], axis=0),
        (((1,), (0,)), ((), ())),
        preferred_element_type=jnp.float32,
    )


def last_faces(spread_ref, pairs, out_ref, result, sems):
    width = spread_ref.shape[1]
    copies = []
    for f, (mine, theirs) in pairs.items():
        place = pl.ds(f * width, width)
        result[f * width : (f + 1) * width] = last_product(spread_ref[f], mine, theirs)
        copy = pltpu.make_async_copy(result.at[place], out_ref.at[place], sems.at[f])
        copy.start()
        copies.append(copy)
    for copy in copies:
        copy.wait()


def last_kernel(ncon, spread_ref, answer_ref, *refs):
    inputs, rest = refs[:-3], refs[-3:]
    pairs = {}
    done = 0
    for position, axis in enumerate(AXES):
        number = face_arrays(lax.axis_size(axis))
        near = receive(inputs[done : done + number], axis)
        done += number
        for f, theirs in zip((2 * position, 2 * position + 1), near):
            pairs[f] = (answer_ref[f * ncon : (f + 1) * ncon], theirs)
    last_faces(spread_ref, pairs, *rest)


def last_near_kernel(ncon, flag_ref, spread_ref, here_ref, there_ref, *refs):
    def answer(flag, f):
        place = slice(f * ncon, (f + 1) * ncon)
        hit = flag_ref[flag : flag + 1, 0:1] > 0.5
        return jnp.where(hit, here_ref[place], there_ref[place])

    pairs = {f: (answer(0, f), answer(f, f ^ 1)) for f in range(2, FACES)}
    last_faces(spread_ref, pairs, *refs)


def last_far_kernel(ncon, flag_ref, spread_ref, here_ref, there_ref, *refs):
    arrays = (len(refs) - 4) // 2
    same, other = refs[:arrays], refs[arrays : 2 * arrays]
    hit = flag_ref[0:1, 0:1] > 0.5
    pairs = {}
    for f, near, far in zip((0, 1), receive(same, AXES[0]), receive(other, AXES[0])):
        place = slice(f * ncon, (f + 1) * ncon)
        mine = jnp.where(hit, here_ref[place], there_ref[place])
        pairs[f] = (mine, jnp.where(hit, near, far))
    last_faces(spread_ref, pairs, *refs[2 * arrays + 1 :])


def sum_rounds(rows, planes):
    rounds = [("gy", 2**i) for i in range(1, rows.bit_length() - 1)]
    return rounds + [("gz", 2**i) for i in range(planes.bit_length() - 1)]


def per_device(schur, start_block, resid, group_of):
    matrix = schur[0, 0, 0]
    matrix = pltpu.with_memory_space_constraint(matrix, pltpu.HBM)
    starts = start_block[0, 0, 0].transpose(0, 2, 1)
    right = resid[0, 0, 0]
    order, columns = right.shape
    ncon, width = starts.shape[1:]
    counts = [lax.axis_size(axis) for axis in AXES]
    arrays = sum(face_arrays(count) for count in counts)
    coarse = FACES * ncon
    size = 2 * ncon
    lanes = size * BLOCKS * (BLOCKS + 1) // 2
    uppers = FACES * (FACES - 1) // 2
    anywhere = pl.BlockSpec(memory_space=pl.ANY)
    main_memory = pl.BlockSpec(memory_space=pltpu.HBM)
    scalars = pl.BlockSpec(memory_space=pltpu.SMEM)
    early, late = (2, 3), (0, 1, 4, 5)
    faces = (early, late)
    planes = counts[2]

    def shape(*dims):
        return jax.ShapeDtypeStruct(dims, jnp.float32)

    def halves(count):
        return jax.ShapeDtypeStruct((count, 2, width, width), jnp.bfloat16)

    def params(mib):
        return pltpu.CompilerParams(vmem_limit_bytes=mib * MIB)

    def cost(us):
        return pl.CostEstimate(flops=us * 10**9, bytes_accessed=2**20, transcendentals=0)

    *packed, own = pl.pallas_call(
        functools.partial(pack_kernel, counts, width),
        out_shape=[
            part
            for count in counts
            for part in face_shapes(count, (width + 8 + 2 * ncon, width // 2))
        ]
        + [shape(FACES, width, width)],
        in_specs=[main_memory, main_memory],
        out_specs=vmem_specs(arrays + 1),
        scratch_shapes=[
            pltpu.VMEM((FACES, ncon, width), jnp.float32),
            pltpu.SemaphoreType.DMA((FACES,)),
            pltpu.SemaphoreType.DMA,
        ],
        compiler_params=params(12),
    )(matrix, pltpu.with_memory_space_constraint(starts, pltpu.HBM))
    got = []
    for axis in AXES:
        number = face_arrays(lax.axis_size(axis))
        got.append(exchange(packed[:number], axis))
        packed = packed[number:]

    own_halves, upper_halves, flags = pl.pallas_call(
        functools.partial(halves_kernel, planes),
        out_shape=[halves(FACES), halves(uppers), shape(8, 128)],
        in_specs=[main_memory, scalars] + vmem_specs(1),
        out_specs=vmem_specs(3),
        scratch_shapes=[
            pltpu.VMEM((FACES - 1, width, order), jnp.float32),
            pltpu.SemaphoreType.DMA((FACES - 1,)),
        ],
        compiler_params=params(24),
        cost_estimate=cost(2),
    )(matrix, group_of, own)

    early_basis, early_partner, early_inverse = pl.pallas_call(
        functools.partial(early_kernel, AXES[1:2], early),
        out_shape=[shape(len(early), ncon, width)] + [halves(len(early))] * 2,
        in_specs=vmem_specs(len(got[1]) + 3),
        out_specs=vmem_specs(3),
        scratch_shapes=[pltpu.VMEM((len(early), 2, width, width), jnp.bfloat16)],
        compiler_params=params(16),
        cost_estimate=cost(2),
    )(*got[1], own, own_halves, starts)

    payload, product, late_partner, late_inverse = pl.pallas_call(
        functools.partial(main_kernel, (AXES[0], AXES[2]), early, late),
        out_shape=[shape(size, lanes + BLOCKS * columns), shape(FACES, ncon, width)]
        + [halves(len(late))] * 2,
        in_specs=vmem_specs(len(got[0]) + len(got[2]) + 6),
        out_specs=vmem_specs(4),
        scratch_shapes=[pltpu.VMEM((len(late), 2, width, width), jnp.bfloat16)],
        compiler_params=params(24),
        cost_estimate=cost(8),
    )(*got[0], *got[2], own, own_halves, upper_halves, starts, right, early_basis)

    partners = [early_partner, late_partner]
    inverses = [early_inverse, late_inverse]
    their_basis, their_product = pl.pallas_call(
        functools.partial(theirs_kernel, faces, ncon),
        out_shape=[shape(FACES, ncon, width)] * 2,
        in_specs=vmem_specs(arrays + 5),
        out_specs=vmem_specs(2),
        compiler_params=params(16),
        cost_estimate=cost(2),
    )(*got[0], *got[1], *got[2], own_halves, *partners, *inverses)

    def spread_of(token):
        return pl.pallas_call(
            functools.partial(spread_kernel, faces),
            out_shape=jax.ShapeDtypeStruct((FACES, width, 3 * size), jnp.bfloat16),
            in_specs=[anywhere] + vmem_specs(5),
            out_specs=vmem_specs(1)[0],
            compiler_params=params(16),
            cost_estimate=cost(3),
        )(token, their_basis, their_product, product, *inverses)

    def solve(matrices, rights, token, sent):
        return pl.pallas_call(
            functools.partial(solve_kernel, size, ncon, len(matrices)),
            out_shape=[shape(coarse, columns)] + sent,
            in_specs=vmem_specs(2 * len(matrices)) + [anywhere],
            out_specs=vmem_specs(1 + len(sent)),
            compiler_params=params(12),
            cost_estimate=cost(7),
        )(*matrices, *rights, token)

    result = dict(
        out_shape=shape(order, columns),
        out_specs=main_memory,
        scratch_shapes=[
            pltpu.VMEM((order, columns), jnp.float32),
            pltpu.SemaphoreType.DMA((FACES,)),
        ],
        compiler_params=params(8),
        cost_estimate=cost(1),
    )
    rows = counts[1]
    groups = group_of.shape[0] // GROUP_SIZE
    if groups == 2 and rows > 1 and not (rows & (rows - 1) or planes & (planes - 1)):
        other = lax.ppermute(payload, "gy", flipped("gy", 1))
        pair_shape = [shape(size, lanes), shape(size, BLOCKS * columns)]
        left, rest = pl.pallas_call(
            choose_kernel,
            out_shape=pair_shape,
            in_specs=vmem_specs(3),
            out_specs=vmem_specs(2),
            compiler_params=params(8),
        )(flags, payload, other)
        rounds = sum_rounds(rows, planes)
        for step in range(len(rounds)):
            axis, bit = rounds[step]
            left_moved = lax.ppermute(left, axis, flipped(axis, bit))
            axis, bit = rounds[-1 - step]
            rest_moved = lax.ppermute(rest, axis, flipped(axis, bit))
            if step == len(rounds) - 1:
                break
            left, rest = pl.pallas_call(
                add_kernel,
                out_shape=pair_shape,
                in_specs=vmem_specs(4) + [anywhere],
                out_specs=vmem_specs(2),
                compiler_params=params(8),
            )(left, left_moved, rest, rest_moved, their_basis)
        spread = spread_of(left)
        answer, *sent = solve(
            [left, left_moved],
            [rest, rest_moved],
            spread,
            face_shapes(counts[0], (ncon, columns)),
        )
        there = lax.ppermute(answer, "gy", flipped("gy", 1))
        same = exchange(sent, AXES[0])
        across = lax.ppermute(jnp.concatenate(same, axis=0), "gy", flipped("gy", 1))
        cut = across.shape[0] // len(same)
        across = [across[i * cut : (i + 1) * cut] for i in range(len(same))]
        correction = pl.pallas_call(
            functools.partial(last_near_kernel, ncon),
            in_specs=vmem_specs(4),
            **result,
        )(flags, spread, answer, there)
        correction = pl.pallas_call(
            functools.partial(last_far_kernel, ncon),
            in_specs=vmem_specs(4 + 2 * len(same)) + [main_memory],
            input_output_aliases={4 + 2 * len(same): 0},
            **result,
        )(flags, spread, answer, there, *same, *across, correction)
    else:
        y, z = lax.axis_index("gy"), lax.axis_index("gz")
        mine = group_of[y * planes + z]
        chosen = jnp.arange(groups, dtype=jnp.int32) == mine
        total = lax.psum(jnp.where(chosen[:, None, None], payload[None], 0.0), ("gy", "gz"))
        total = lax.dynamic_index_in_dim(total, mine, 0, keepdims=False)
        spread = spread_of(payload)
        (answer,) = solve([total[:, :lanes]], [total[:, lanes:]], spread, [])
        blocks = answer.reshape(FACES, ncon, columns)
        near = []
        for position, axis in enumerate(AXES):
            even, odd = blocks[2 * position], blocks[2 * position + 1]
            if counts[position] == 2:
                sent = [jnp.stack([even, odd])]
            else:
                upward = is_even(axis)
                sent = [jnp.where(upward, odd, even), jnp.where(upward, even, odd)]
            near += exchange(sent, axis)
        correction = pl.pallas_call(
            functools.partial(last_kernel, ncon),
            in_specs=vmem_specs(2 + arrays),
            **result,
        )(spread, answer, *near)
    return correction[None, None, None]


def solution(mesh):
    in_specs = (
        P("gx", "gy", "gz", None, None),
        P("gx", "gy", "gz", None, None, None),
        P("gx", "gy", "gz", None, None),
        P(),
    )
    out_specs = P("gx", "gy", "gz", None, None)
    return jax.shard_map(
        per_device, mesh=mesh, in_specs=in_specs, out_specs=out_specs, check_vma=False
    )
```

time: 60.6 us -> 59.5 us (0.982)
  local copies, waits for them, and re-layouts: 4.62 us -> 0.02 us
  Pallas kernels: 28.1 us -> 32.3 us
  waiting for transfers between devices: 12.5 us -> 10.6 us
  starting transfers between devices: 14.9 us -> 16.1 us
    pallas_call x8 -> x10, Pallas kernels: 24.4 us -> 29.3 us  [the longest x1 8.89 us: per_device(): pl.pallas_call(functools.partial(main_kernel, (AXES[0], AXES[2]), early,...]
    unnamed x12 -> x6, local copies, waits for them, and re-layouts: 4.62 us -> 0.01 us
    ppermute x10 -> x12, waiting for transfers between devices: 11.1 us -> 8.97 us  [the longest x1 2.57 us: exchange(): return [lax.ppermute(arrays[0], axis, flipped(axis, 1))]]
    pallas_call x1, Pallas kernels: 3.7 us -> 2.95 us  [spread_of(): pl.pallas_call(functools.partial(spread_kernel, faces), out_shape=jax.Sha...]
    ppermute x10 -> x12, starting transfers between devices: 14.8 us -> 15.5 us  [the longest x3 4.98 us: exchange(): lax.ppermute(arrays[1], axis, outer_pairs(axis))]
  transfers between devices with their start and end apart: 12 -> 14, of which waited for: 7 -> 10; matrix products, arithmetic and copies ran while one was open for 0% -> 0% of each run, Pallas kernels for 16% -> 18%
where the time goes in v4:
time: 59.5 us; the launch traced here: 59.3 us
  Pallas kernels  32.3 us (54%)
  starting transfers between devices  16.1 us (27%)
  waiting for transfers between devices  10.6 us (18%)
    pallas_call x1, Pallas kernels, per_device(): pl.pallas_call(functools.partial(main_kernel, (AXES[0], AXES[2]), early,...  8.89 us
    pallas_call x1, Pallas kernels, solve(): pl.pallas_call(functools.partial(solve_kernel, size, ncon, len(matrices))...  8.7 us
    ppermute x3, starting transfers between devices, exchange(): lax.ppermute(arrays[1], axis, outer_pairs(axis))  4.98 us
    ppermute x3, starting transfers between devices, exchange(): lax.ppermute(arrays[0], axis, flipped(axis, 1))  3.83 us
    ppermute x2, starting transfers between devices, per_device(): rest_moved = lax.ppermute(rest, axis, flipped(axis, bit))  3.08 us
    pallas_call x1, Pallas kernels, spread_of(): pl.pallas_call(functools.partial(spread_kernel, faces), out_shape=jax.Sha...  2.95 us
    pallas_call x1, Pallas kernels, per_device(): pl.pallas_call(functools.partial(early_kernel, AXES[1:2], early), out_sha...  2.86 us
    pallas_call x1, Pallas kernels, per_device(): pl.pallas_call(functools.partial(halves_kernel, planes), out_shape=[halve...  2.7 us
  transfers between devices with their start and end apart: 14, of which 10 were waited for; matrix products, arithmetic and copies ran while one was open for 0% of the time, Pallas kernels for 18%

profile of v4, /device:TPU:0, one launch (start us, length us, event | category | flops | bytes accessed | tf_op | source)
XLA Modules:
  0.0 59.3 jit_solution(11493758666055780533)
XLA Ops:
  0.0 0.0 copy-start.1
  0.0 1.7 %shard_map.46 = (f32[328,128]{1,0:T(8,128)S(1)}, f32[328,128]{1,0:T(8,128)S(1)}, f32[328,128]{1,0:T(8,128)S(1)}, f32[328,128]{1,0:T(8,128)S(1)}, f32[2,328,128]{2,1,0:T(8,128)S(1)}, /*index=5*/f32[6,256,256]{2,1,0:T(8,128)S(1)}) custom-call(f32[1536,1536]{1,0:T(8,128)} %bitcast.10, f32[6,32,256]{2,1,0:T(8,128)} %bitcast.6), custom_call_target="tpu_custom_call" | custom-call | tf_op jit(solution)/shard_map/pallas_call | solution.py:618
  1.7 3.1 %collective-permute-start = (f32[328,128]{1,0:T(8,128)S(1)}, f32[328,128]{1,0:T(8,128)S(1)}, u32[]{:S(2)}, u32[]{:S(2)}) collective-permute-start(f32[328,128]{1,0:T(8,128)S(1)} %get-tuple-element.32), channel_id=1, source_target_pairs={{0,8},{8,0},{16,24},{24,16},{1,9},{9,1},{17,25},{25,17},{2,10},{10... | collective-permute-start | bytes 503816 | tf_op jit(solution)/shard_map/ppermute | solution.py:77
  4.8 2.5 %collective-permute-start.1 = (f32[328,128]{1,0:T(8,128)S(1)}, f32[328,128]{1,0:T(8,128)S(1)}, u32[]{:S(2)}, u32[]{:S(2)}) collective-permute-start(f32[328,128]{1,0:T(8,128)S(1)} %get-tuple-element.33), channel_id=1, source_target_pairs={{0,24},{8,16},{16,8},{24,0},{1,25},{9,17},{17,9},{25,1},{2,26},{10... | collective-permute-start | bytes 503816 | tf_op jit(solution)/shard_map/ppermute | solution.py:78
  7.3 0.0 collective-permute-start.3
  7.3 1.6 %collective-permute-start.4 = (f32[328,128]{1,0:T(8,128)S(1)}, f32[328,128]{1,0:T(8,128)S(1)}, u32[]{:S(2)}, u32[]{:S(2)}) collective-permute-start(f32[328,128]{1,0:T(8,128)S(1)} %get-tuple-element.38), channel_id=1, source_target_pairs={{0,6},{2,4},{4,2},{6,0},{1,7},{3,5},{5,3},{7,1},{8,14},{10,12},{12... | collective-permute-start | bytes 503816 | tf_op jit(solution)/shard_map/ppermute | solution.py:78
  8.9 1.5 %collective-permute-start.2 = (f32[2,328,128]{2,1,0:T(8,128)S(1)}, f32[2,328,128]{2,1,0:T(8,128)S(1)}, u32[]{:S(2)}, u32[]{:S(2)}) collective-permute-start(f32[2,328,128]{2,1,0:T(8,128)S(1)} %get-tuple-element.34), channel_id=1, source_target_pairs={{0,1},{1,0},{2,3},{3,2},{4,5},{5,4},{6,7},{7,6},{8,9},{9,8},{10,11... | collective-permute-start | bytes 1007624 | tf_op jit(solution)/shard_map/ppermute | solution.py:75
  10.4 0.0 copy-done.1
  10.4 0.0 copy-start
  10.4 2.7 %shard_map.47 = (bf16[6,2,256,256]{3,2,1,0:T(8,128)(2,1)S(1)}, bf16[15,2,256,256]{3,2,1,0:T(8,128)(2,1)S(1)}, f32[8,128]{1,0:T(8,128)S(1)}) custom-call(f32[1536,1536]{1,0:T(8,128)} %bitcast.11, s32[8]{0:T(128)S(1)} %copy-done.1, f32[6,256,256]{2,1,0:T(8,128)S(1)} %get-tuple-element.30.own_ref.refs_2_.refs_3_), custom_call_target="tpu_custom_call" | custom-call | flops 2000000000 | bytes 1048576 | tf_op jit(solution)/shard_map/pallas_call | solution.py:641
  13.1 0.0 copy-start.2
  13.1 0.0 collective-permute-done.3.refs_0_.refs_2_
  13.1 0.1 collective-permute-done.4.refs_1_.refs_3_
  13.2 0.0 copy-done
  13.2 2.9 %shard_map.48 = (f32[2,32,256]{2,1,0:T(8,128)S(1)}, bf16[2,2,256,256]{3,2,1,0:T(8,128)(2,1)S(1)}, bf16[2,2,256,256]{3,2,1,0:T(8,128)(2,1)S(1)}) custom-call(f32[328,128]{1,0:T(8,128)S(1)} %collective-permute-done.3.refs_0_.refs_2_, f32[328,128]{1,0:T(8,128)S(1)} %collective-permute-done.4.refs_1_.refs_3_, ...), custom_call_target="tpu_custom_call" | custom-call | flops 2000000000 | bytes 1048576 | tf_op jit(solution)/shard_map/pallas_call | solution.py:654
  16.1 0.0 collective-permute-done.refs_0_
  16.1 0.0 collective-permute-done.1.refs_1_
  16.1 2.6 %collective-permute-done.2.refs_2_.refs_4_ = f32[2,328,128]{2,1,0:T(8,128)S(1)} collective-permute-done((f32[2,328,128]{2,1,0:T(8,128)S(1)}, f32[2,328,128]{2,1,0:T(8,128)S(1)}, u32[]{:S(2)}, u32[]{:S(2)}) %collective-permute-start.2) | collective-permute-done | bytes 335904 | tf_op jit(solution)/shard_map/ppermute | solution.py:75
  18.7 0.0 copy-done.2
  18.7 8.9 %shard_map.49 = (f32[64,768]{1,0:T(8,128)S(1)}, f32[6,32,256]{2,1,0:T(8,128)S(1)}, bf16[4,2,256,256]{3,2,1,0:T(8,128)(2,1)S(1)}, bf16[4,2,256,256]{3,2,1,0:T(8,128)(2,1)S(1)}) custom-call(f32[328,128]{1,0:T(8,128)S(1)} %collective-permute-done.refs_0_, f32[328,128]{1,0:T(8,128)S(1)} %collective-permute-done.1.refs_1_, ...), custom_call_target="tpu_custom_call" | custom-call | flops 8000000000 | bytes 1048576 | tf_op jit(solution)/shard_map/pallas_call | solution.py:664
  27.6 0.1 collective-permute-start.5
  27.7 1.4 %collective-permute-done.5.there_ref = f32[64,768]{1,0:T(8,128)S(1)} collective-permute-done((f32[64,768]{1,0:T(8,128)S(1)}, f32[64,768]{1,0:T(8,128)S(1)}, u32[]{:S(2)}, u32[]{:S(2)}) %collective-permute-start.5) | collective-permute-done | bytes 196640 | tf_op jit(solution)/shard_map/ppermute | solution.py:719
  29.1 0.1 shard_map.50
  29.2 0.6 %collective-permute-start.6 = (f32[64,384]{1,0:T(8,128)S(1)}, f32[64,384]{1,0:T(8,128)S(1)}, u32[]{:S(2)}, u32[]{:S(2)}) collective-permute-start(f32[64,384]{1,0:T(8,128)S(1)} %get-tuple-element.41.first_ref), channel_id=1, source_target_pairs={{0,4},{2,6},{4,0},{6,2},{1,5},{3,7},{5,1},{7,3},{8,12},{10,14},{12... | collective-permute-start | bytes 294920 | tf_op jit(solution)/shard_map/ppermute | solution.py:731
  29.8 1.5 %collective-permute-start.7 = (f32[64,384]{1,0:T(8,128)S(1)}, f32[64,384]{1,0:T(8,128)S(1)}, u32[]{:S(2)}, u32[]{:S(2)}) collective-permute-start(f32[64,384]{1,0:T(8,128)S(1)} %get-tuple-element.42.third_ref), channel_id=1, source_target_pairs={{0,1},{1,0},{2,3},{3,2},{4,5},{5,4},{6,7},{7,6},{8,9},{9,8},{10,11... | collective-permute-start | bytes 294920 | tf_op jit(solution)/shard_map/ppermute | solution.py:733
  31.3 2.2 %shard_map.51 = (f32[6,32,256]{2,1,0:T(8,128)S(1)}, f32[6,32,256]{2,1,0:T(8,128)S(1)}) custom-call(f32[328,128]{1,0:T(8,128)S(1)} %collective-permute-done.refs_0_, f32[328,128]{1,0:T(8,128)S(1)} %collective-permute-done.1.refs_1_, f32[328,128]{1,0:T(8,128)S(1)} %collective-permute-done.3.refs_0_.refs_2_, ...), custom_call_target="tpu_custom_call" | custom-call | flops 2000000000 | bytes 1048576 | tf_op jit(solution)/shard_map/pallas_call | solution.py:677
  33.5 0.5 collective-permute-done.6.second_ref
  34.1 0.3 collective-permute-done.7.fourth_ref
  34.4 1.6 %collective-permute-start.9 = (f32[64,384]{1,0:T(8,128)S(1)}, f32[64,384]{1,0:T(8,128)S(1)}, u32[]{:S(2)}, u32[]{:S(2)}) collective-permute-start(f32[64,384]{1,0:T(8,128)S(1)} %get-tuple-element.51.refs_2_), channel_id=1, source_target_pairs={{0,4},{2,6},{4,0},{6,2},{1,5},{3,7},{5,1},{7,3},{8,12},{10,14},{12... | collective-permute-start | bytes 294920 | tf_op jit(solution)/shard_map/ppermute | solution.py:733
  36.0 1.5 %collective-permute-start.8 = (f32[64,384]{1,0:T(8,128)S(1)}, f32[64,384]{1,0:T(8,128)S(1)}, u32[]{:S(2)}, u32[]{:S(2)}) collective-permute-start(f32[64,384]{1,0:T(8,128)S(1)} %get-tuple-element.48.unread.refs_0_), channel_id=1, source_target_pairs={{0,1},{1,0},{2,3},{3,2},{4,5},{5,4},{6,7},{7,6},{8,9},{9,8},{10,11... | collective-permute-start | bytes 294920 | tf_op jit(solution)/shard_map/ppermute | solution.py:731
  37.5 3.0 %shard_map.53.refs_4_.spread_ref = bf16[6,256,192]{2,1,0:T(8,128)(2,1)S(1)} custom-call(f32[64,384]{1,0:T(8,128)S(1)} %get-tuple-element.48.unread.refs_0_, f32[6,32,256]{2,1,0:T(8,128)S(1)} %get-tuple-element.47.unread.basis_ref, f32[6,32,256]{2,1,0:T(8,128)S(1)} %get-tuple-element.49.theirs_ref, f32[6,32,256]{2,1,0:T(8,128)S(1)} %get-tuple-element.50.product_ref, ...), custom_call_target="tpu_custom_call" | custom-call | flops 3000000000 | bytes 1048576 | tf_op jit(solution)/shard_map/pallas_call | solution.py:687
  40.4 0.0 collective-permute-done.9.refs_3_
  40.5 0.1 collective-permute-done.8.refs_1_
  40.6 8.7 %shard_map.54 = (f32[192,128]{1,0:T(8,128)S(1)}, f32[32,128]{1,0:T(8,128)S(1)}, f32[32,128]{1,0:T(8,128)S(1)}) custom-call(f32[64,384]{1,0:T(8,128)S(1)} %get-tuple-element.48.unread.refs_0_, f32[64,384]{1,0:T(8,128)S(1)} %collective-permute-done.8.refs_1_, f32[64,384]{1,0:T(8,128)S(1)} %get-tuple-element.51.refs_2_, ...), custom_call_target="tpu_custom_call" | custom-call | flops 7000000000 | bytes 1048576 | tf_op jit(solution)/shard_map/pallas_call | solution.py:697
  49.3 0.7 %collective-permute-start.11 = (f32[32,128]{1,0:T(8,128)S(1)}, f32[32,128]{1,0:T(8,128)S(1)}, u32[]{:S(2)}, u32[]{:S(2)}) collective-permute-start(f32[32,128]{1,0:T(8,128)S(1)} %get-tuple-element.53), channel_id=1, source_target_pairs={{0,8},{8,0},{16,24},{24,16},{1,9},{9,1},{17,25},{25,17},{2,10},{10... | collective-permute-start | bytes 49160 | tf_op jit(solution)/shard_map/ppermute | solution.py:77
  50.0 0.9 %collective-permute-start.12 = (f32[32,128]{1,0:T(8,128)S(1)}, f32[32,128]{1,0:T(8,128)S(1)}, u32[]{:S(2)}, u32[]{:S(2)}) collective-permute-start(f32[32,128]{1,0:T(8,128)S(1)} %get-tuple-element.54), channel_id=1, source_target_pairs={{0,24},{8,16},{16,8},{24,0},{1,25},{9,17},{17,9},{25,1},{2,26},{10... | collective-permute-start | bytes 49160 | tf_op jit(solution)/shard_map/ppermute | solution.py:78
  50.9 2.2 %collective-permute-done.11.refs_0_ = f32[32,128]{1,0:T(8,128)S(1)} collective-permute-done((f32[32,128]{1,0:T(8,128)S(1)}, f32[32,128]{1,0:T(8,128)S(1)}, u32[]{:S(2)}, u32[]{:S(2)}) %collective-permute-start.11) | collective-permute-done | bytes 16416 | tf_op jit(solution)/shard_map/ppermute | solution.py:77
  53.1 2.5 %collective-permute-done.12.refs_1_ = f32[32,128]{1,0:T(8,128)S(1)} collective-permute-done((f32[32,128]{1,0:T(8,128)S(1)}, f32[32,128]{1,0:T(8,128)S(1)}, u32[]{:S(2)}, u32[]{:S(2)}) %collective-permute-start.12) | collective-permute-done | bytes 16416 | tf_op jit(solution)/shard_map/ppermute | solution.py:78
  55.6 0.0 collective-permute-start.13
  55.6 0.5 collective-permute-start.10
  56.1 0.7 %collective-permute-done.13 = f32[64,128]{1,0:T(8,128)S(1)} collective-permute-done((f32[64,128]{1,0:T(8,128)S(1)}, f32[64,128]{1,0:T(8,128)S(1)}, u32[]{:S(2)}, u32[]{:S(2)}) %collective-permute-start.13) | collective-permute-done | bytes 32800 | tf_op jit(solution)/shard_map/ppermute | solution.py:752
  56.8 0.2 collective-permute-done.10.there_ref
  57.0 1.1 %shard_map.55.refs_4_ = f32[1536,128]{1,0:T(8,128)} custom-call(f32[8,128]{1,0:T(8,128)S(1)} %get-tuple-element.31.flag_ref, bf16[6,256,192]{2,1,0:T(8,128)(2,1)S(1)} %shard_map.53.refs_4_.spread_ref, f32[192,128]{1,0:T(8,128)S(1)} %get-tuple-element.52.here_ref, f32[192,128]{1,0:T(8,128)S(1)} %collective-permute-done.10.there_ref), custom_call_target="tpu_custom_call" | custom-call | flops 1000000000 | bytes 1048576 | tf_op jit(solution)/shard_map/pallas_call | solution.py:755
  58.1 1.0 %shard_map.56 = f32[1536,128]{1,0:T(8,128)} custom-call(f32[8,128]{1,0:T(8,128)S(1)} %get-tuple-element.31.flag_ref, bf16[6,256,192]{2,1,0:T(8,128)(2,1)S(1)} %shard_map.53.refs_4_.spread_ref, f32[192,128]{1,0:T(8,128)S(1)} %get-tuple-element.52.here_ref, f32[192,128]{1,0:T(8,128)S(1)} %collective-permute-done.10.there_ref, ...), custom_call_target="tpu_custom_call", output_to_operand_aliasing={{}: (8, {})} | custom-call | flops 1000000000 | bytes 1048576 | tf_op jit(solution)/shard_map/pallas_call | solution.py:760
  (3 shorter events, 0.0 us)
Async XLA Ops:
  0.0 10.4 %copy-start.1 = (s32[8]{0:T(128)S(1)}, s32[8]{0:T(128)}, u32[]{:S(2)}) copy-start(s32[8]{0:T(128)} %group_ref.1) | copy-start | bytes 100
  1.7 14.4 %collective-permute-start = (f32[328,128]{1,0:T(8,128)S(1)}, f32[328,128]{1,0:T(8,128)S(1)}, u32[]{:S(2)}, u32[]{:S(2)}) collective-permute-start(f32[328,128]{1,0:T(8,128)S(1)} %get-tuple-element.32), channel_id=1, source_target_pairs={{0,8},{8,0},{16,24},{24,16},{1,9},{9,1},{17,25},{25,17},{2,10},{10... | collective-permute-start | bytes 503816 | tf_op jit(solution)/shard_map/ppermute | solution.py:77
  4.8 11.3 %collective-permute-start.1 = (f32[328,128]{1,0:T(8,128)S(1)}, f32[328,128]{1,0:T(8,128)S(1)}, u32[]{:S(2)}, u32[]{:S(2)}) collective-permute-start(f32[328,128]{1,0:T(8,128)S(1)} %get-tuple-element.33), channel_id=1, source_target_pairs={{0,24},{8,16},{16,8},{24,0},{1,25},{9,17},{17,9},{25,1},{2,26},{10... | collective-permute-start | bytes 503816 | tf_op jit(solution)/shard_map/ppermute | solution.py:78
  7.3 5.8 %collective-permute-start.3 = (f32[328,128]{1,0:T(8,128)S(1)}, f32[328,128]{1,0:T(8,128)S(1)}, u32[]{:S(2)}, u32[]{:S(2)}) collective-permute-start(f32[328,128]{1,0:T(8,128)S(1)} %get-tuple-element.37), channel_id=1, source_target_pairs={{0,2},{2,0},{4,6},{6,4},{1,3},{3,1},{5,7},{7,5},{8,10},{10,8},{12,... | collective-permute-start | bytes 503816 | tf_op jit(solution)/shard_map/ppermute | solution.py:77
  7.3 5.9 %collective-permute-start.4 = (f32[328,128]{1,0:T(8,128)S(1)}, f32[328,128]{1,0:T(8,128)S(1)}, u32[]{:S(2)}, u32[]{:S(2)}) collective-permute-start(f32[328,128]{1,0:T(8,128)S(1)} %get-tuple-element.38), channel_id=1, source_target_pairs={{0,6},{2,4},{4,2},{6,0},{1,7},{3,5},{5,3},{7,1},{8,14},{10,12},{12... | collective-permute-start | bytes 503816 | tf_op jit(solution)/shard_map/ppermute | solution.py:78
  8.9 9.8 %collective-permute-start.2 = (f32[2,328,128]{2,1,0:T(8,128)S(1)}, f32[2,328,128]{2,1,0:T(8,128)S(1)}, u32[]{:S(2)}, u32[]{:S(2)}) collective-permute-start(f32[2,328,128]{2,1,0:T(8,128)S(1)} %get-tuple-element.34), channel_id=1, source_target_pairs={{0,1},{1,0},{2,3},{3,2},{4,5},{5,4},{6,7},{7,6},{8,9},{9,8},{10,11... | collective-permute-start | bytes 1007624 | tf_op jit(solution)/shard_map/ppermute | solution.py:75
  10.4 2.8 %copy-start = (f32[1,1,1,6,256,32]{4,5,3,2,1,0:T(8,128)S(1)}, f32[1,1,1,6,256,32]{4,5,3,2,1,0:T(8,128)}, u32[]{:S(2)}) copy-start(f32[1,1,1,6,256,32]{4,5,3,2,1,0:T(8,128)} %param.5) | copy-start | bytes 589828
  13.1 5.6 %copy-start.2 = (f32[1,1,1,1536,128]{4,3,2,1,0:T(8,128)S(1)}, f32[1,1,1,1536,128]{4,3,2,1,0:T(8,128)}, u32[]{:S(2)}) copy-start(f32[1,1,1,1536,128]{4,3,2,1,0:T(8,128)} %param.6) | copy-start | bytes 2359300
  27.6 1.5 %collective-permute-start.5 = (f32[64,768]{1,0:T(8,128)S(1)}, f32[64,768]{1,0:T(8,128)S(1)}, u32[]{:S(2)}, u32[]{:S(2)}) collective-permute-start(f32[64,768]{1,0:T(8,128)S(1)} %get-tuple-element.40.here_ref), channel_id=1, source_target_pairs={{0,2},{2,0},{4,6},{6,4},{1,3},{3,1},{5,7},{7,5},{8,10},{10,8},{12,... | collective-permute-start | bytes 589832 | tf_op jit(solution)/shard_map/ppermute | solution.py:719
  29.2 4.9 %collective-permute-start.6 = (f32[64,384]{1,0:T(8,128)S(1)}, f32[64,384]{1,0:T(8,128)S(1)}, u32[]{:S(2)}, u32[]{:S(2)}) collective-permute-start(f32[64,384]{1,0:T(8,128)S(1)} %get-tuple-element.41.first_ref), channel_id=1, source_target_pairs={{0,4},{2,6},{4,0},{6,2},{1,5},{3,7},{5,1},{7,3},{8,12},{10,14},{12... | collective-permute-start | bytes 294920 | tf_op jit(solution)/shard_map/ppermute | solution.py:731
  29.8 4.6 %collective-permute-start.7 = (f32[64,384]{1,0:T(8,128)S(1)}, f32[64,384]{1,0:T(8,128)S(1)}, u32[]{:S(2)}, u32[]{:S(2)}) collective-permute-start(f32[64,384]{1,0:T(8,128)S(1)} %get-tuple-element.42.third_ref), channel_id=1, source_target_pairs={{0,1},{1,0},{2,3},{3,2},{4,5},{5,4},{6,7},{7,6},{8,9},{9,8},{10,11... | collective-permute-start | bytes 294920 | tf_op jit(solution)/shard_map/ppermute | solution.py:733
  34.4 6.0 %collective-permute-start.9 = (f32[64,384]{1,0:T(8,128)S(1)}, f32[64,384]{1,0:T(8,128)S(1)}, u32[]{:S(2)}, u32[]{:S(2)}) collective-permute-start(f32[64,384]{1,0:T(8,128)S(1)} %get-tuple-element.51.refs_2_), channel_id=1, source_target_pairs={{0,4},{2,6},{4,0},{6,2},{1,5},{3,7},{5,1},{7,3},{8,12},{10,14},{12... | collective-permute-start | bytes 294920 | tf_op jit(solution)/shard_map/ppermute | solution.py:733
  36.0 4.6 %collective-permute-start.8 = (f32[64,384]{1,0:T(8,128)S(1)}, f32[64,384]{1,0:T(8,128)S(1)}, u32[]{:S(2)}, u32[]{:S(2)}) collective-permute-start(f32[64,384]{1,0:T(8,128)S(1)} %get-tuple-element.48.unread.refs_0_), channel_id=1, source_target_pairs={{0,1},{1,0},{2,3},{3,2},{4,5},{5,4},{6,7},{7,6},{8,9},{9,8},{10,11... | collective-permute-start | bytes 294920 | tf_op jit(solution)/shard_map/ppermute | solution.py:731
  49.3 3.8 %collective-permute-start.11 = (f32[32,128]{1,0:T(8,128)S(1)}, f32[32,128]{1,0:T(8,128)S(1)}, u32[]{:S(2)}, u32[]{:S(2)}) collective-permute-start(f32[32,128]{1,0:T(8,128)S(1)} %get-tuple-element.53), channel_id=1, source_target_pairs={{0,8},{8,0},{16,24},{24,16},{1,9},{9,1},{17,25},{25,17},{2,10},{10... | collective-permute-start | bytes 49160 | tf_op jit(solution)/shard_map/ppermute | solution.py:77
  50.0 5.5 %collective-permute-start.12 = (f32[32,128]{1,0:T(8,128)S(1)}, f32[32,128]{1,0:T(8,128)S(1)}, u32[]{:S(2)}, u32[]{:S(2)}) collective-permute-start(f32[32,128]{1,0:T(8,128)S(1)} %get-tuple-element.54), channel_id=1, source_target_pairs={{0,24},{8,16},{16,8},{24,0},{1,25},{9,17},{17,9},{25,1},{2,26},{10... | collective-permute-start | bytes 49160 | tf_op jit(solution)/shard_map/ppermute | solution.py:78
  55.6 1.2 %collective-permute-start.13 = (f32[64,128]{1,0:T(8,128)S(1)}, f32[64,128]{1,0:T(8,128)S(1)}, u32[]{:S(2)}, u32[]{:S(2)}) collective-permute-start(f32[64,128]{1,0:T(8,128)S(1)} %pad_maximum_fusion), channel_id=1, source_target_pairs={{0,2},{2,0},{4,6},{6,4},{1,3},{3,1},{5,7},{7,5},{8,10},{10,8},{12,... | collective-permute-start | bytes 98312 | tf_op jit(solution)/shard_map/ppermute | solution.py:752
  55.6 1.5 %collective-permute-start.10 = (f32[192,128]{1,0:T(8,128)S(1)}, f32[192,128]{1,0:T(8,128)S(1)}, u32[]{:S(2)}, u32[]{:S(2)}) collective-permute-start(f32[192,128]{1,0:T(8,128)S(1)} %get-tuple-element.52.here_ref), channel_id=1, source_target_pairs={{0,2},{2,0},{4,6},{6,4},{1,3},{3,1},{5,7},{7,5},{8,10},{10,8},{12,... | collective-permute-start | bytes 294920 | tf_op jit(solution)/shard_map/ppermute | solution.py:750

commit v5 on v4

--- a/solution.py
+++ b/solution.py
@@ -74,8 +74,8 @@
     if lax.axis_size(axis) == 2:
         return [lax.ppermute(arrays[0], axis, flipped(axis, 1))]
     return [
-        lax.ppermute(arrays[0], axis, flipped(axis, 1)),
-        lax.ppermute(arrays[1], axis, outer_pairs(axis)),
+        lax.ppermute(arrays[0], axis, outer_pairs(axis)),
+        lax.ppermute(arrays[1], axis, flipped(axis, 1)),
     ]
 
 
@@ -89,8 +89,8 @@
         refs[0][1] = odd
     else:
         upward = is_even(axis)
-        refs[0][...] = jnp.where(upward, odd, even)
-        refs[1][...] = jnp.where(upward, even, odd)
+        refs[0][...] = jnp.where(upward, even, odd)
+        refs[1][...] = jnp.where(upward, odd, even)
 
 
 def receive(refs, axis):
@@ -98,7 +98,7 @@
         return refs[0][1], refs[0][0]
     upward = is_even(axis)
     first, second = refs[0][...], refs[1][...]
-    return jnp.where(upward, second, first), jnp.where(upward, first, second)
+    return jnp.where(upward, first, second), jnp.where(upward, second, first)
 
 
 def face_shapes(count, shape):
@@ -165,7 +165,7 @@
     return jnp.concatenate([rows[:ncon], rows[ncon:]], axis=1)
 
 
-def factor_inverses(grams, block=8, invert=False):
+def factor_inverses(grams, block=8):
     size = grams[0].shape[0]
     strips = size // 8
     lanes = 128
@@ -184,7 +184,7 @@
 
     for start in range(0, size, block):
         strip, first = start // 8, start % 8
-        active = range(0 if invert else strip, strips)
+        active = range(strip, strips)
         for work in state:
             cols = [
                 {s: jnp.broadcast_to(work[s][:, start + j : start + j + 1], full) for s in active}
@@ -195,8 +195,7 @@
             def eliminate(j, scale, stop):
                 line = first + j
                 factor = {s: cols[j][s] * scale for s in active}
-                hit = below != line if invert else below > line
-                factor[strip] = jnp.where(hit, factor[strip], 0.0)
+                factor[strip] = jnp.where(below > line, factor[strip], 0.0)
                 for later in range(j + 1, stop):
                     head = line_of(cols[later][strip], line)
                     for s in active:
@@ -214,7 +213,7 @@
             for j in range(block):
                 row = line_of(work[strip], first + j)
                 for s in active:
-                    if s == strip and first + j == 7 and not invert:
+                    if s == strip and first + j == 7:
                         continue
                     work[s] = work[s] - factors[j][s] * row
     results = []
@@ -223,8 +222,7 @@
         for s in range(strips):
             place = iota((8, size), 0) + 8 * s == iota((8, size), 1)
             pivot = jnp.sum(jnp.where(place, work[s][:, :size], 0.0), axis=1, keepdims=True)
-            scale = 1.0 / pivot if invert else lax.rsqrt(pivot)
-            parts.append(work[s][:, size : 2 * size] * scale)
+            parts.append(work[s][:, size : 2 * size] * lax.rsqrt(pivot))
         results.append(jnp.concatenate(parts, axis=0))
     return results
 
@@ -471,12 +469,12 @@
     right_ref[...] = third_ref[...] + fourth_ref[...]
 
 
-def solve_kernel(size, ncon, terms, *refs):
+def solve_kernel(size, terms, *refs):
     matrix, right = refs[0][...], refs[terms][...]
     for term in range(1, terms):
         matrix = matrix + refs[term][...]
         right = right + refs[terms + term][...]
-    answer_ref, sent = refs[2 * terms + 1], refs[2 * terms + 2 :]
+    answer_ref = refs[2 * terms + 1]
     columns = answer_ref.shape[1]
     lines = []
     offset = 0
@@ -495,29 +493,33 @@
         for c in range(b, BLOCKS):
             block = lines[b][:, (c - b) * size : (c - b + 1) * size]
             blocks[b, c] = downs[b] * block * acrosses[c]
-            if c > b:
-                blocks[c, b] = blocks[b, c].T
         rights.append(downs[b] * right[:, b * columns : (b + 1) * columns])
     for b in range(BLOCKS):
-        (inverse,) = factor_inverses([blocks[b, b]], invert=True)
+        (inverse,) = factor_inverses([blocks[b, b]])
         later = range(b + 1, BLOCKS)
         row = dot(inverse, jnp.concatenate([rights[b]] + [blocks[b, c] for c in later], axis=1))
+        upper = {c: row[:, columns + (c - b - 1) * size : columns + (c - b) * size] for c in later}
+        for c in later:
+            for d in range(c, BLOCKS):
+                blocks[c, d] = blocks[c, d] - dot(upper[c], upper[d], ((0,), (0,)))
+            rights[c] = rights[c] - dot(upper[c], row[:, :columns], ((0,), (0,)))
+        row = dot(inverse, row, ((0,), (0,)))
         rights[b] = row[:, :columns]
         for c in later:
-            start = columns + (c - b - 1) * size
-            blocks[b, c] = row[:, start : start + size]
-        for i in range(BLOCKS):
-            if i == b:
-                continue
-            change = dot(blocks[i, b], row)
-            rights[i] = rights[i] - change[:, :columns]
+            blocks[b, c] = row[:, columns + (c - b - 1) * size : columns + (c - b) * size]
+        for i in range(b):
             for c in later:
-                start = columns + (c - b - 1) * size
-                blocks[i, c] = blocks[i, c] - change[:, start : start + size]
+                blocks[i, c] = blocks[i, c] - dot(blocks[i, b], blocks[b, c])
+            rights[i] = rights[i] - dot(blocks[i, b], rights[b])
     answer = [downs[b] * rights[b] for b in range(BLOCKS)]
     answer_ref[...] = jnp.concatenate(answer, axis=0)
-    if sent:
-        send(sent, AXES[0], answer[0][:ncon], answer[0][ncon : 2 * ncon])
+
+
+def rows_kernel(ncon, flag_ref, here_ref, there_ref, *refs):
+    hit = flag_ref[0:1, 0:1] > 0.5
+    rows = jnp.where(hit, here_ref[: 2 * ncon], there_ref[: 2 * ncon])
+    refs[-1][...] = rows
+    send(refs[:-1], AXES[0], rows[:ncon], rows[ncon:])
 
 
 def last_product(spread, mine, theirs):
@@ -566,16 +568,10 @@
     last_faces(spread_ref, pairs, *refs)
 
 
-def last_far_kernel(ncon, flag_ref, spread_ref, here_ref, there_ref, *refs):
-    arrays = (len(refs) - 4) // 2
-    same, other = refs[:arrays], refs[arrays : 2 * arrays]
-    hit = flag_ref[0:1, 0:1] > 0.5
-    pairs = {}
-    for f, near, far in zip((0, 1), receive(same, AXES[0]), receive(other, AXES[0])):
-        place = slice(f * ncon, (f + 1) * ncon)
-        mine = jnp.where(hit, here_ref[place], there_ref[place])
-        pairs[f] = (mine, jnp.where(hit, near, far))
-    last_faces(spread_ref, pairs, *refs[2 * arrays + 1 :])
+def last_far_kernel(ncon, spread_ref, rows_ref, *refs):
+    theirs = receive(refs[:-4], AXES[0])
+    pairs = {f: (rows_ref[f * ncon : (f + 1) * ncon], theirs[f]) for f in (0, 1)}
+    last_faces(spread_ref, pairs, *refs[-3:])
 
 
 def sum_rounds(rows, planes):
@@ -599,7 +595,7 @@
     anywhere = pl.BlockSpec(memory_space=pl.ANY)
     main_memory = pl.BlockSpec(memory_space=pltpu.HBM)
     scalars = pl.BlockSpec(memory_space=pltpu.SMEM)
-    early, late = (2, 3), (0, 1, 4, 5)
+    early, late = (4, 5), (0, 1, 2, 3)
     faces = (early, late)
     planes = counts[2]
 
@@ -632,11 +628,10 @@
         ],
         compiler_params=params(12),
     )(matrix, pltpu.with_memory_space_constraint(starts, pltpu.HBM))
-    got = []
-    for axis in AXES:
-        number = face_arrays(lax.axis_size(axis))
-        got.append(exchange(packed[:number], axis))
-        packed = packed[number:]
+    ends = [sum(face_arrays(count) for count in counts[:position]) for position in range(4)]
+    got = {}
+    for position in (2, 0, 1):
+        got[position] = exchange(packed[ends[position] : ends[position + 1]], AXES[position])
 
     own_halves, upper_halves, flags = pl.pallas_call(
         functools.partial(halves_kernel, planes),
@@ -652,25 +647,25 @@
     )(matrix, group_of, own)
 
     early_basis, early_partner, early_inverse = pl.pallas_call(
-        functools.partial(early_kernel, AXES[1:2], early),
+        functools.partial(early_kernel, AXES[2:3], early),
         out_shape=[shape(len(early), ncon, width)] + [halves(len(early))] * 2,
-        in_specs=vmem_specs(len(got[1]) + 3),
+        in_specs=vmem_specs(len(got[2]) + 3),
         out_specs=vmem_specs(3),
         scratch_shapes=[pltpu.VMEM((len(early), 2, width, width), jnp.bfloat16)],
         compiler_params=params(16),
         cost_estimate=cost(2),
-    )(*got[1], own, own_halves, starts)
+    )(*got[2], own, own_halves, starts)
 
     payload, product, late_partner, late_inverse = pl.pallas_call(
-        functools.partial(main_kernel, (AXES[0], AXES[2]), early, late),
+        functools.partial(main_kernel, (AXES[0], AXES[1]), early, late),
         out_shape=[shape(size, lanes + BLOCKS * columns), shape(FACES, ncon, width)]
         + [halves(len(late))] * 2,
-        in_specs=vmem_specs(len(got[0]) + len(got[2]) + 6),
+        in_specs=vmem_specs(len(got[0]) + len(got[1]) + 6),
         out_specs=vmem_specs(4),
         scratch_shapes=[pltpu.VMEM((len(late), 2, width, width), jnp.bfloat16)],
         compiler_params=params(24),
         cost_estimate=cost(8),
-    )(*got[0], *got[2], own, own_halves, upper_halves, starts, right, early_basis)
+    )(*got[0], *got[1], own, own_halves, upper_halves, starts, right, early_basis)
 
     partners = [early_partner, late_partner]
     inverses = [early_inverse, late_inverse]
@@ -693,12 +688,12 @@
             cost_estimate=cost(3),
         )(token, their_basis, their_product, product, *inverses)
 
-    def solve(matrices, rights, token, sent):
+    def solve(matrices, rights, token):
         return pl.pallas_call(
-            functools.partial(solve_kernel, size, ncon, len(matrices)),
-            out_shape=[shape(coarse, columns)] + sent,
+            functools.partial(solve_kernel, size, len(matrices)),
+            out_shape=shape(coarse, columns),
             in_specs=vmem_specs(2 * len(matrices)) + [anywhere],
-            out_specs=vmem_specs(1 + len(sent)),
+            out_specs=vmem_specs(1)[0],
             compiler_params=params(12),
             cost_estimate=cost(7),
         )(*matrices, *rights, token)
@@ -741,17 +736,16 @@
                 compiler_params=params(8),
             )(left, left_moved, rest, rest_moved, their_basis)
         spread = spread_of(left)
-        answer, *sent = solve(
-            [left, left_moved],
-            [rest, rest_moved],
-            spread,
-            face_shapes(counts[0], (ncon, columns)),
-        )
+        answer = solve([left, left_moved], [rest, rest_moved], spread)
         there = lax.ppermute(answer, "gy", flipped("gy", 1))
-        same = exchange(sent, AXES[0])
-        across = lax.ppermute(jnp.concatenate(same, axis=0), "gy", flipped("gy", 1))
-        cut = across.shape[0] // len(same)
-        across = [across[i * cut : (i + 1) * cut] for i in range(len(same))]
+        *sent, mine = pl.pallas_call(
+            functools.partial(rows_kernel, ncon),
+            out_shape=face_shapes(counts[0], (ncon, columns)) + [shape(size, columns)],
+            in_specs=vmem_specs(3),
+            out_specs=vmem_specs(face_arrays(counts[0]) + 1),
+            compiler_params=params(8),
+        )(flags, answer, there)
+        across = exchange(sent, AXES[0])
         correction = pl.pallas_call(
             functools.partial(last_near_kernel, ncon),
             in_specs=vmem_specs(4),
@@ -759,10 +753,10 @@
         )(flags, spread, answer, there)
         correction = pl.pallas_call(
             functools.partial(last_far_kernel, ncon),
-            in_specs=vmem_specs(4 + 2 * len(same)) + [main_memory],
-            input_output_aliases={4 + 2 * len(same): 0},
+            in_specs=vmem_specs(2 + len(across)) + [main_memory],
+            input_output_aliases={2 + len(across): 0},
             **result,
-        )(flags, spread, answer, there, *same, *across, correction)
+        )(spread, mine, *across, correction)
     else:
         y, z = lax.axis_index("gy"), lax.axis_index("gz")
         mine = group_of[y * planes + z]
@@ -770,7 +764,7 @@
         total = lax.psum(jnp.where(chosen[:, None, None], payload[None], 0.0), ("gy", "gz"))
         total = lax.dynamic_index_in_dim(total, mine, 0, keepdims=False)
         spread = spread_of(payload)
-        (answer,) = solve([total[:, :lanes]], [total[:, lanes:]], spread, [])
+        answer = solve([total[:, :lanes]], [total[:, lanes:]], spread)
         blocks = answer.reshape(FACES, ncon, columns)
         near = []
         for position, axis in enumerate(AXES):
@@ -779,7 +773,7 @@
                 sent = [jnp.stack([even, odd])]
             else:
                 upward = is_even(axis)
-                sent = [jnp.where(upward, odd, even), jnp.where(upward, even, odd)]
+                sent = [jnp.where(upward, even, odd), jnp.where(upward, odd, even)]
             near += exchange(sent, axis)
         correction = pl.pallas_call(
             functools.partial(last_kernel, ncon),

time: 59.5 us -> 55.3 us (0.929)
  waiting for transfers between devices: 10.6 us -> 7.44 us
  Pallas kernels: 32.3 us -> 30.9 us
    ppermute x1, waiting for transfers between devices: 2.57 us -> 0.01 us  [exchange(): return [lax.ppermute(arrays[0], axis, flipped(axis, 1))]]
    ppermute x7 -> x6, waiting for transfers between devices: 5.42 us -> 3.12 us  [the longest x3 1.99 us: exchange(): lax.ppermute(arrays[1], axis, flipped(axis, 1))]
    ppermute x1, starting transfers between devices: 1.52 us -> 3.03 us  [exchange(): return [lax.ppermute(arrays[0], axis, flipped(axis, 1))]]
    ppermute x2, starting transfers between devices: 3.08 us -> 1.83 us  [per_device(): rest_moved = lax.ppermute(rest, axis, flipped(axis, bit))]
    pallas_call x3 -> x4, Pallas kernels: 20.5 us -> 19.3 us  [the longest x1 8.87 us: per_device(): pl.pallas_call(functools.partial(main_kernel, (AXES[0], AXES[1]), early,...]
    ppermute x1, waiting for transfers between devices: 0.24 us -> 1.29 us  [per_device(): there = lax.ppermute(answer, 'gy', flipped('gy', 1))]
    ppermute x2, waiting for transfers between devices: 0.31 us -> 1.12 us  [per_device(): rest_moved = lax.ppermute(rest, axis, flipped(axis, bit))]
    ppermute x2, starting transfers between devices: 2.11 us -> 2.76 us  [per_device(): left_moved = lax.ppermute(left, axis, flipped(axis, bit))]
  transfers between devices with their start and end apart: 14 -> 13, of which waited for: 10 -> 8; matrix products, arithmetic and copies ran while one was open for 0% -> 0% of each run, Pallas kernels for 18% -> 21%
where the time goes in v5:
time: 55.3 us; the launch traced here: 55.1 us
  Pallas kernels  30.9 us (56%)
  starting transfers between devices  16.3 us (29%)
  waiting for transfers between devices  7.44 us (13%)
    pallas_call x1, Pallas kernels, per_device(): pl.pallas_call(functools.partial(main_kernel, (AXES[0], AXES[1]), early,...  8.87 us
    pallas_call x1, Pallas kernels, solve(): pl.pallas_call(functools.partial(solve_kernel, size, len(matrices)), out_...  7.51 us
    ppermute x3, starting transfers between devices, exchange(): lax.ppermute(arrays[0], axis, outer_pairs(axis))  7.34 us
    ppermute x1, starting transfers between devices, exchange(): return [lax.ppermute(arrays[0], axis, flipped(axis, 1))]  3.03 us
    pallas_call x1, Pallas kernels, spread_of(): pl.pallas_call(functools.partial(spread_kernel, faces), out_shape=jax.Sha...  2.96 us
    pallas_call x1, Pallas kernels, per_device(): pl.pallas_call(functools.partial(early_kernel, AXES[2:3], early), out_sha...  2.85 us
    ppermute x2, starting transfers between devices, per_device(): left_moved = lax.ppermute(left, axis, flipped(axis, bit))  2.76 us
    pallas_call x1, Pallas kernels, per_device(): pl.pallas_call(functools.partial(halves_kernel, planes), out_shape=[halve...  2.7 us
  transfers between devices with their start and end apart: 13, of which 8 were waited for; matrix products, arithmetic and copies ran while one was open for 0% of the time, Pallas kernels for 21%

profile of v5, /device:TPU:0, one launch (start us, length us, event | category | flops | bytes accessed | tf_op | source)
XLA Modules:
  0.0 55.1 jit_solution(16611572943056040353)
XLA Ops:
  0.0 0.0 copy-start.1
  0.0 1.7 %shard_map.46 = (f32[328,128]{1,0:T(8,128)S(1)}, f32[328,128]{1,0:T(8,128)S(1)}, f32[328,128]{1,0:T(8,128)S(1)}, f32[328,128]{1,0:T(8,128)S(1)}, f32[2,328,128]{2,1,0:T(8,128)S(1)}, /*index=5*/f32[6,256,256]{2,1,0:T(8,128)S(1)}) custom-call(f32[1536,1536]{1,0:T(8,128)} %bitcast.10, f32[6,32,256]{2,1,0:T(8,128)} %bitcast.6), custom_call_target="tpu_custom_call" | custom-call | tf_op jit(solution)/shard_map/pallas_call | solution.py:614
  1.7 3.0 %collective-permute-start.4 = (f32[2,328,128]{2,1,0:T(8,128)S(1)}, f32[2,328,128]{2,1,0:T(8,128)S(1)}, u32[]{:S(2)}, u32[]{:S(2)}) collective-permute-start(f32[2,328,128]{2,1,0:T(8,128)S(1)} %get-tuple-element.38), channel_id=1, source_target_pairs={{0,1},{1,0},{2,3},{3,2},{4,5},{5,4},{6,7},{7,6},{8,9},{9,8},{10,11... | collective-permute-start | bytes 1007624 | tf_op jit(solution)/shard_map/ppermute | solution.py:75
  4.7 3.6 %collective-permute-start = (f32[328,128]{1,0:T(8,128)S(1)}, f32[328,128]{1,0:T(8,128)S(1)}, u32[]{:S(2)}, u32[]{:S(2)}) collective-permute-start(f32[328,128]{1,0:T(8,128)S(1)} %get-tuple-element.32), channel_id=1, source_target_pairs={{0,24},{8,16},{16,8},{24,0},{1,25},{9,17},{17,9},{25,1},{2,26},{10... | collective-permute-start | bytes 503816 | tf_op jit(solution)/shard_map/ppermute | solution.py:77
  8.3 0.0 collective-permute-start.1
  8.4 0.4 collective-permute-start.2
  8.7 1.2 %collective-permute-start.3 = (f32[328,128]{1,0:T(8,128)S(1)}, f32[328,128]{1,0:T(8,128)S(1)}, u32[]{:S(2)}, u32[]{:S(2)}) collective-permute-start(f32[328,128]{1,0:T(8,128)S(1)} %get-tuple-element.35), channel_id=1, source_target_pairs={{0,2},{2,0},{4,6},{6,4},{1,3},{3,1},{5,7},{7,5},{8,10},{10,8},{12,... | collective-permute-start | bytes 503816 | tf_op jit(solution)/shard_map/ppermute | solution.py:78
  10.0 0.0 copy-done.1
  10.0 0.0 copy-start
  10.0 2.7 %shard_map.47 = (bf16[6,2,256,256]{3,2,1,0:T(8,128)(2,1)S(1)}, bf16[15,2,256,256]{3,2,1,0:T(8,128)(2,1)S(1)}, f32[8,128]{1,0:T(8,128)S(1)}) custom-call(f32[1536,1536]{1,0:T(8,128)} %bitcast.11, s32[8]{0:T(128)S(1)} %copy-done.1, f32[6,256,256]{2,1,0:T(8,128)S(1)} %get-tuple-element.30.own_ref.refs_1_.refs_4_), custom_call_target="tpu_custom_call" | custom-call | flops 2000000000 | bytes 1048576 | tf_op jit(solution)/shard_map/pallas_call | solution.py:636
  12.7 0.0 copy-start.2
  12.7 0.0 collective-permute-done.4.refs_0_.refs_4_
  12.7 0.0 copy-done
  12.7 2.8 %shard_map.48 = (f32[2,32,256]{2,1,0:T(8,128)S(1)}, bf16[2,2,256,256]{3,2,1,0:T(8,128)(2,1)S(1)}, bf16[2,2,256,256]{3,2,1,0:T(8,128)(2,1)S(1)}) custom-call(f32[2,328,128]{2,1,0:T(8,128)S(1)} %collective-permute-done.4.refs_0_.refs_4_, f32[6,256,256]{2,1,0:T(8,128)S(1)} %get-tuple-element.30.own_ref.refs_1_.refs_4_, ...), custom_call_target="tpu_custom_call" | custom-call | flops 2000000000 | bytes 1048576 | tf_op jit(solution)/shard_map/pallas_call | solution.py:649
  15.6 0.0 collective-permute-done.refs_0_
  15.6 0.5 collective-permute-done.1.refs_1_
  16.1 0.0 collective-permute-done.2.refs_2_
  16.1 0.0 collective-permute-done.3.refs_3_
  16.1 0.0 copy-done.2
  16.1 8.9 %shard_map.49 = (f32[64,768]{1,0:T(8,128)S(1)}, f32[6,32,256]{2,1,0:T(8,128)S(1)}, bf16[4,2,256,256]{3,2,1,0:T(8,128)(2,1)S(1)}, bf16[4,2,256,256]{3,2,1,0:T(8,128)(2,1)S(1)}) custom-call(f32[328,128]{1,0:T(8,128)S(1)} %collective-permute-done.refs_0_, f32[328,128]{1,0:T(8,128)S(1)} %collective-permute-done.1.refs_1_, ...), custom_call_target="tpu_custom_call" | custom-call | flops 8000000000 | bytes 1048576 | tf_op jit(solution)/shard_map/pallas_call | solution.py:659
  24.9 0.1 collective-permute-start.5
  25.0 1.4 %collective-permute-done.5.there_ref = f32[64,768]{1,0:T(8,128)S(1)} collective-permute-done((f32[64,768]{1,0:T(8,128)S(1)}, f32[64,768]{1,0:T(8,128)S(1)}, u32[]{:S(2)}, u32[]{:S(2)}) %collective-permute-start.5) | collective-permute-done | bytes 196640 | tf_op jit(solution)/shard_map/ppermute | solution.py:714
  26.4 0.1 shard_map.50
  26.5 1.5 %collective-permute-start.6 = (f32[64,384]{1,0:T(8,128)S(1)}, f32[64,384]{1,0:T(8,128)S(1)}, u32[]{:S(2)}, u32[]{:S(2)}) collective-permute-start(f32[64,384]{1,0:T(8,128)S(1)} %get-tuple-element.41.first_ref), channel_id=1, source_target_pairs={{0,4},{2,6},{4,0},{6,2},{1,5},{3,7},{5,1},{7,3},{8,12},{10,14},{12... | collective-permute-start | bytes 294920 | tf_op jit(solution)/shard_map/ppermute | solution.py:726
  28.1 1.2 %collective-permute-start.7 = (f32[64,384]{1,0:T(8,128)S(1)}, f32[64,384]{1,0:T(8,128)S(1)}, u32[]{:S(2)}, u32[]{:S(2)}) collective-permute-start(f32[64,384]{1,0:T(8,128)S(1)} %get-tuple-element.42.third_ref), channel_id=1, source_target_pairs={{0,1},{1,0},{2,3},{3,2},{4,5},{5,4},{6,7},{7,6},{8,9},{9,8},{10,11... | collective-permute-start | bytes 294920 | tf_op jit(solution)/shard_map/ppermute | solution.py:728
  29.3 2.1 %shard_map.51 = (f32[6,32,256]{2,1,0:T(8,128)S(1)}, f32[6,32,256]{2,1,0:T(8,128)S(1)}) custom-call(f32[328,128]{1,0:T(8,128)S(1)} %collective-permute-done.refs_0_, f32[328,128]{1,0:T(8,128)S(1)} %collective-permute-done.1.refs_1_, f32[328,128]{1,0:T(8,128)S(1)} %collective-permute-done.2.refs_2_, f32[328,128]{1,0:T(8,128)S(1)} %collective-permute-done.3.refs_3_, ...), custom_call_target="tpu_custom_call" | custom-call | flops 2000000000 | bytes 1048576 | tf_op jit(solution)/shard_map/pallas_call | solution.py:672
  31.4 0.1 collective-permute-done.6.second_ref
  31.6 1.1 %collective-permute-done.7.fourth_ref = f32[64,384]{1,0:T(8,128)S(1)} collective-permute-done((f32[64,384]{1,0:T(8,128)S(1)}, f32[64,384]{1,0:T(8,128)S(1)}, u32[]{:S(2)}, u32[]{:S(2)}) %collective-permute-start.7) | collective-permute-done | bytes 98336 | tf_op jit(solution)/shard_map/ppermute | solution.py:728
  32.7 0.6 %collective-permute-start.9 = (f32[64,384]{1,0:T(8,128)S(1)}, f32[64,384]{1,0:T(8,128)S(1)}, u32[]{:S(2)}, u32[]{:S(2)}) collective-permute-start(f32[64,384]{1,0:T(8,128)S(1)} %get-tuple-element.51.refs_2_), channel_id=1, source_target_pairs={{0,4},{2,6},{4,0},{6,2},{1,5},{3,7},{5,1},{7,3},{8,12},{10,14},{12... | collective-permute-start | bytes 294920 | tf_op jit(solution)/shard_map/ppermute | solution.py:728
  33.3 1.2 %collective-permute-start.8 = (f32[64,384]{1,0:T(8,128)S(1)}, f32[64,384]{1,0:T(8,128)S(1)}, u32[]{:S(2)}, u32[]{:S(2)}) collective-permute-start(f32[64,384]{1,0:T(8,128)S(1)} %get-tuple-element.48.unread.refs_0_), channel_id=1, source_target_pairs={{0,1},{1,0},{2,3},{3,2},{4,5},{5,4},{6,7},{7,6},{8,9},{9,8},{10,11... | collective-permute-start | bytes 294920 | tf_op jit(solution)/shard_map/ppermute | solution.py:726
  34.5 3.0 %shard_map.53.refs_4_.spread_ref = bf16[6,256,192]{2,1,0:T(8,128)(2,1)S(1)} custom-call(f32[64,384]{1,0:T(8,128)S(1)} %get-tuple-element.48.unread.refs_0_, f32[6,32,256]{2,1,0:T(8,128)S(1)} %get-tuple-element.47.unread.basis_ref, f32[6,32,256]{2,1,0:T(8,128)S(1)} %get-tuple-element.49.theirs_ref, f32[6,32,256]{2,1,0:T(8,128)S(1)} %get-tuple-element.50.product_ref, ...), custom_call_target="tpu_custom_call" | custom-call | flops 3000000000 | bytes 1048576 | tf_op jit(solution)/shard_map/pallas_call | solution.py:682
  37.5 0.0 collective-permute-done.9.refs_3_
  37.5 0.4 collective-permute-done.8.refs_1_
  37.9 7.5 %shard_map.54.here_ref = f32[192,128]{1,0:T(8,128)S(1)} custom-call(f32[64,384]{1,0:T(8,128)S(1)} %get-tuple-element.48.unread.refs_0_, f32[64,384]{1,0:T(8,128)S(1)} %collective-permute-done.8.refs_1_, f32[64,384]{1,0:T(8,128)S(1)} %get-tuple-element.51.refs_2_, f32[64,384]{1,0:T(8,128)S(1)} %collective-permute-done.9.refs_3_, ...), custom_call_target="tpu_custom_call" | custom-call | flops 7000000000 | bytes 1048576 | tf_op jit(solution)/shard_map/pallas_call | solution.py:692
  45.5 0.1 collective-permute-start.10
  45.5 1.3 %collective-permute-done.10.there_ref = f32[192,128]{1,0:T(8,128)S(1)} collective-permute-done((f32[192,128]{1,0:T(8,128)S(1)}, f32[192,128]{1,0:T(8,128)S(1)}, u32[]{:S(2)}, u32[]{:S(2)}) %collective-permute-start.10) | collective-permute-done | bytes 98336 | tf_op jit(solution)/shard_map/ppermute | solution.py:740
  46.9 3.4 %collective-permute-start.11 = (f32[32,128]{1,0:T(8,128)S(1)}, f32[32,128]{1,0:T(8,128)S(1)}, u32[]{:S(2)}, u32[]{:S(2)}) collective-permute-start(f32[32,128]{1,0:T(8,128)S(1)} %get-tuple-element.53), channel_id=1, source_target_pairs={{0,24},{8,16},{16,8},{24,0},{1,25},{9,17},{17,9},{25,1},{2,26},{10... | collective-permute-start | bytes 49160 | tf_op jit(solution)/shard_map/ppermute | solution.py:77
  50.3 0.0 collective-permute-start.12
  50.3 1.1 %shard_map.56.refs_2_ = f32[1536,128]{1,0:T(8,128)} custom-call(f32[8,128]{1,0:T(8,128)S(1)} %get-tuple-element.31.flag_ref, bf16[6,256,192]{2,1,0:T(8,128)(2,1)S(1)} %shard_map.53.refs_4_.spread_ref, f32[192,128]{1,0:T(8,128)S(1)} %shard_map.54.here_ref, f32[192,128]{1,0:T(8,128)S(1)} %collective-permute-done.10.there_ref), custom_call_target="tpu_custom_call" | custom-call | flops 1000000000 | bytes 1048576 | tf_op jit(solution)/shard_map/pallas_call | solution.py:749
  51.4 1.1 %collective-permute-done.11.refs_0_ = f32[32,128]{1,0:T(8,128)S(1)} collective-permute-done((f32[32,128]{1,0:T(8,128)S(1)}, f32[32,128]{1,0:T(8,128)S(1)}, u32[]{:S(2)}, u32[]{:S(2)}) %collective-permute-start.11) | collective-permute-done | bytes 16416 | tf_op jit(solution)/shard_map/ppermute | solution.py:77
  52.5 1.5 %collective-permute-done.12.refs_1_ = f32[32,128]{1,0:T(8,128)S(1)} collective-permute-done((f32[32,128]{1,0:T(8,128)S(1)}, f32[32,128]{1,0:T(8,128)S(1)}, u32[]{:S(2)}, u32[]{:S(2)}) %collective-permute-start.12) | collective-permute-done | bytes 16416 | tf_op jit(solution)/shard_map/ppermute | solution.py:78
  54.0 1.0 %shard_map.57 = f32[1536,128]{1,0:T(8,128)} custom-call(bf16[6,256,192]{2,1,0:T(8,128)(2,1)S(1)} %shard_map.53.refs_4_.spread_ref, f32[64,128]{1,0:T(8,128)S(1)} %get-tuple-element.52.rows_ref, f32[32,128]{1,0:T(8,128)S(1)} %collective-permute-done.11.refs_0_, f32[32,128]{1,0:T(8,128)S(1)} %collective-permute-done.12.refs_1_, ...), custom_call_target="tpu_custom_call", output_to_operand_aliasing={{}: (4, {})} | custom-call | flops 1000000000 | bytes 1048576 | tf_op jit(solution)/shard_map/pallas_call | solution.py:754
  (2 shorter events, 0.1 us)
Async XLA Ops:
  0.0 10.0 %copy-start.1 = (s32[8]{0:T(128)S(1)}, s32[8]{0:T(128)}, u32[]{:S(2)}) copy-start(s32[8]{0:T(128)} %group_ref.1) | copy-start | bytes 100
  1.7 11.0 %collective-permute-start.4 = (f32[2,328,128]{2,1,0:T(8,128)S(1)}, f32[2,328,128]{2,1,0:T(8,128)S(1)}, u32[]{:S(2)}, u32[]{:S(2)}) collective-permute-start(f32[2,328,128]{2,1,0:T(8,128)S(1)} %get-tuple-element.38), channel_id=1, source_target_pairs={{0,1},{1,0},{2,3},{3,2},{4,5},{5,4},{6,7},{7,6},{8,9},{9,8},{10,11... | collective-permute-start | bytes 1007624 | tf_op jit(solution)/shard_map/ppermute | solution.py:75
  4.7 10.8 %collective-permute-start = (f32[328,128]{1,0:T(8,128)S(1)}, f32[328,128]{1,0:T(8,128)S(1)}, u32[]{:S(2)}, u32[]{:S(2)}) collective-permute-start(f32[328,128]{1,0:T(8,128)S(1)} %get-tuple-element.32), channel_id=1, source_target_pairs={{0,24},{8,16},{16,8},{24,0},{1,25},{9,17},{17,9},{25,1},{2,26},{10... | collective-permute-start | bytes 503816 | tf_op jit(solution)/shard_map/ppermute | solution.py:77
  8.3 7.7 %collective-permute-start.1 = (f32[328,128]{1,0:T(8,128)S(1)}, f32[328,128]{1,0:T(8,128)S(1)}, u32[]{:S(2)}, u32[]{:S(2)}) collective-permute-start(f32[328,128]{1,0:T(8,128)S(1)} %get-tuple-element.33), channel_id=1, source_target_pairs={{0,8},{8,0},{16,24},{24,16},{1,9},{9,1},{17,25},{25,17},{2,10},{10... | collective-permute-start | bytes 503816 | tf_op jit(solution)/shard_map/ppermute | solution.py:78
  8.4 7.7 %collective-permute-start.2 = (f32[328,128]{1,0:T(8,128)S(1)}, f32[328,128]{1,0:T(8,128)S(1)}, u32[]{:S(2)}, u32[]{:S(2)}) collective-permute-start(f32[328,128]{1,0:T(8,128)S(1)} %get-tuple-element.34), channel_id=1, source_target_pairs={{0,6},{2,4},{4,2},{6,0},{1,7},{3,5},{5,3},{7,1},{8,14},{10,12},{12... | collective-permute-start | bytes 503816 | tf_op jit(solution)/shard_map/ppermute | solution.py:77
  8.7 7.3 %collective-permute-start.3 = (f32[328,128]{1,0:T(8,128)S(1)}, f32[328,128]{1,0:T(8,128)S(1)}, u32[]{:S(2)}, u32[]{:S(2)}) collective-permute-start(f32[328,128]{1,0:T(8,128)S(1)} %get-tuple-element.35), channel_id=1, source_target_pairs={{0,2},{2,0},{4,6},{6,4},{1,3},{3,1},{5,7},{7,5},{8,10},{10,8},{12,... | collective-permute-start | bytes 503816 | tf_op jit(solution)/shard_map/ppermute | solution.py:78
  10.0 2.7 %copy-start = (f32[1,1,1,6,256,32]{4,5,3,2,1,0:T(8,128)S(1)}, f32[1,1,1,6,256,32]{4,5,3,2,1,0:T(8,128)}, u32[]{:S(2)}) copy-start(f32[1,1,1,6,256,32]{4,5,3,2,1,0:T(8,128)} %param.5) | copy-start | bytes 589828
  12.7 3.4 %copy-start.2 = (f32[1,1,1,1536,128]{4,3,2,1,0:T(8,128)S(1)}, f32[1,1,1,1536,128]{4,3,2,1,0:T(8,128)}, u32[]{:S(2)}) copy-start(f32[1,1,1,1536,128]{4,3,2,1,0:T(8,128)} %param.6) | copy-start | bytes 2359300
  24.9 1.5 %collective-permute-start.5 = (f32[64,768]{1,0:T(8,128)S(1)}, f32[64,768]{1,0:T(8,128)S(1)}, u32[]{:S(2)}, u32[]{:S(2)}) collective-permute-start(f32[64,768]{1,0:T(8,128)S(1)} %get-tuple-element.40.here_ref), channel_id=1, source_target_pairs={{0,2},{2,0},{4,6},{6,4},{1,3},{3,1},{5,7},{7,5},{8,10},{10,8},{12,... | collective-permute-start | bytes 589832 | tf_op jit(solution)/shard_map/ppermute | solution.py:714
  26.5 4.9 %collective-permute-start.6 = (f32[64,384]{1,0:T(8,128)S(1)}, f32[64,384]{1,0:T(8,128)S(1)}, u32[]{:S(2)}, u32[]{:S(2)}) collective-permute-start(f32[64,384]{1,0:T(8,128)S(1)} %get-tuple-element.41.first_ref), channel_id=1, source_target_pairs={{0,4},{2,6},{4,0},{6,2},{1,5},{3,7},{5,1},{7,3},{8,12},{10,14},{12... | collective-permute-start | bytes 294920 | tf_op jit(solution)/shard_map/ppermute | solution.py:726
  28.1 4.6 %collective-permute-start.7 = (f32[64,384]{1,0:T(8,128)S(1)}, f32[64,384]{1,0:T(8,128)S(1)}, u32[]{:S(2)}, u32[]{:S(2)}) collective-permute-start(f32[64,384]{1,0:T(8,128)S(1)} %get-tuple-element.42.third_ref), channel_id=1, source_target_pairs={{0,1},{1,0},{2,3},{3,2},{4,5},{5,4},{6,7},{7,6},{8,9},{9,8},{10,11... | collective-permute-start | bytes 294920 | tf_op jit(solution)/shard_map/ppermute | solution.py:728
  32.7 4.8 %collective-permute-start.9 = (f32[64,384]{1,0:T(8,128)S(1)}, f32[64,384]{1,0:T(8,128)S(1)}, u32[]{:S(2)}, u32[]{:S(2)}) collective-permute-start(f32[64,384]{1,0:T(8,128)S(1)} %get-tuple-element.51.refs_2_), channel_id=1, source_target_pairs={{0,4},{2,6},{4,0},{6,2},{1,5},{3,7},{5,1},{7,3},{8,12},{10,14},{12... | collective-permute-start | bytes 294920 | tf_op jit(solution)/shard_map/ppermute | solution.py:728
  33.3 4.6 %collective-permute-start.8 = (f32[64,384]{1,0:T(8,128)S(1)}, f32[64,384]{1,0:T(8,128)S(1)}, u32[]{:S(2)}, u32[]{:S(2)}) collective-permute-start(f32[64,384]{1,0:T(8,128)S(1)} %get-tuple-element.48.unread.refs_0_), channel_id=1, source_target_pairs={{0,1},{1,0},{2,3},{3,2},{4,5},{5,4},{6,7},{7,6},{8,9},{9,8},{10,11... | collective-permute-start | bytes 294920 | tf_op jit(solution)/shard_map/ppermute | solution.py:726
  45.5 1.4 %collective-permute-start.10 = (f32[192,128]{1,0:T(8,128)S(1)}, f32[192,128]{1,0:T(8,128)S(1)}, u32[]{:S(2)}, u32[]{:S(2)}) collective-permute-start(f32[192,128]{1,0:T(8,128)S(1)} %shard_map.54.here_ref), channel_id=1, source_target_pairs={{0,2},{2,0},{4,6},{6,4},{1,3},{3,1},{5,7},{7,5},{8,10},{10,8},{12,... | collective-permute-start | bytes 294920 | tf_op jit(solution)/shard_map/ppermute | solution.py:740
  46.9 5.6 %collective-permute-start.11 = (f32[32,128]{1,0:T(8,128)S(1)}, f32[32,128]{1,0:T(8,128)S(1)}, u32[]{:S(2)}, u32[]{:S(2)}) collective-permute-start(f32[32,128]{1,0:T(8,128)S(1)} %get-tuple-element.53), channel_id=1, source_target_pairs={{0,24},{8,16},{16,8},{24,0},{1,25},{9,17},{17,9},{25,1},{2,26},{10... | collective-permute-start | bytes 49160 | tf_op jit(solution)/shard_map/ppermute | solution.py:77
  50.3 3.7 %collective-permute-start.12 = (f32[32,128]{1,0:T(8,128)S(1)}, f32[32,128]{1,0:T(8,128)S(1)}, u32[]{:S(2)}, u32[]{:S(2)}) collective-permute-start(f32[32,128]{1,0:T(8,128)S(1)} %get-tuple-element.54), channel_id=1, source_target_pairs={{0,8},{8,0},{16,24},{24,16},{1,9},{9,1},{17,25},{25,17},{2,10},{10... | collective-permute-start | bytes 49160 | tf_op jit(solution)/shard_map/ppermute | solution.py:78

commit v6 on v5

--- a/solution.py
+++ b/solution.py
@@ -121,7 +121,7 @@
         copy = pltpu.make_async_copy(schur_ref.at[place, place], blocks.at[f], sems.at[f])
         copy.start()
         copies.append(copy)
-    start_copy = pltpu.make_async_copy(starts_ref, starts, start_sem)
+    start_copy = pltpu.make_async_copy(starts_ref.at[pl.ds(0, 4)], starts, start_sem)
     start_copy.start()
     row, col = iota((half, half), 0), iota((half, half), 1)
     start_copy.wait()
@@ -133,10 +133,10 @@
         diag = jnp.sum(jnp.where(row == col, second, 0.0), axis=0, keepdims=True)
         mixed = jnp.where(row >= col, first, second)
         tail = jnp.broadcast_to(diag, (8, half))
-        start = starts[f]
-        return jnp.concatenate(
-            [blocks[f, half:width, 0:half], mixed, tail, start[:, :half], start[:, half:]], axis=0
-        )
+        parts = [blocks[f, half:width, 0:half], mixed, tail]
+        if f < 4:
+            parts += [starts[f, :, :half], starts[f, :, half:]]
+        return jnp.concatenate(parts, axis=0)
 
     done = 0
     for position, axis in enumerate(AXES):
@@ -393,10 +393,11 @@
     for g in range(FACES):
         tall = jnp.concatenate([sides[f][g] for f in range(g + 1)], axis=0)
         blocks.append(dot(dot(tall, vectors[g], ((1,), (1,))), factors[g], ((1,), (1,))))
-    even, odd, right = [], [], []
+    even, odd, right, products = [], [], [], []
     lows = None
     for f in range(FACES):
-        product_ref[f] = dot(factors[f], sides[f][f])
+        products.append(dot(factors[f], sides[f][f]))
+        product_ref[f] = products[f]
         line = [blocks[g][f * ncon : (f + 1) * ncon] for g in range(f, FACES)]
         line = dot(factors[f], jnp.concatenate([rights[f]] + line, axis=1))
         right.append(line[:, :columns])
@@ -406,13 +407,26 @@
             lows = line[:, ncon : 2 * ncon].T
         else:
             odd += [lows, line]
+    upward = is_even("gy")
+    inner = jnp.where(upward, products[3], products[2])
+    outer = jnp.where(upward, products[2], products[3])
+    whole = [
+        jnp.concatenate(even + right[0::2], axis=1),
+        jnp.concatenate(odd + right[1::2], axis=1),
+    ]
     payload_ref[...] = jnp.concatenate(
-        [
-            jnp.concatenate(even + right[0::2], axis=1),
-            jnp.concatenate(odd + right[1::2], axis=1),
-        ],
-        axis=0,
+        [jnp.concatenate(whole, axis=0), fold(inner), fold(outer)], axis=1
     )
+
+
+def fold(product):
+    half = product.shape[1] // 2
+    return jnp.concatenate([product[:, :half], product[:, half:]], axis=0)
+
+
+def unfold(rows):
+    half = rows.shape[0] // 2
+    return jnp.concatenate([rows[:half], rows[half:]], axis=1)
 
 
 def find(faces, refs, f):
@@ -421,61 +435,54 @@
             return load(ref, list(group).index(f))
 
 
-def theirs_kernel(faces, ncon, *refs):
-    arrays = len(refs) - 7
-    inputs = refs[:arrays]
-    own_ref, partner_refs, inverse_refs = refs[arrays], refs[-6:-4], refs[-4:-2]
-    basis_out, product_out = refs[-2:]
-    basis = []
-    done = 0
-    for axis in AXES:
-        number = face_arrays(lax.axis_size(axis))
-        packed = receive(inputs[done : done + number], axis)
-        basis += [unpack_starts(part, ncon) for part in packed]
-        done += number
+def spread_kernel(faces, ncon, unread, *refs):
+    packed = receive(refs[:-7], AXES[0])
+    own_ref, product_ref = refs[-7:-5]
+    partner_refs, inverse_refs, out_ref = refs[-5:-3], refs[-3:-1], refs[-1]
+    basis = [unpack_starts(part, ncon) for part in packed]
     matrices = [
-        [load(own_ref, f) for f in range(FACES)],
-        [find(faces, inverse_refs, f) for f in range(FACES)],
-        [find(faces, partner_refs, f) for f in range(FACES)],
+        [load(own_ref, f) for f in range(2)],
+        [find(faces, inverse_refs, f) for f in range(2)],
+        [find(faces, partner_refs, f) for f in range(2)],
     ]
     for sweep in range(SUB_ITERS):
         basis = sweep_basis(*matrices, basis)
-    for f in range(FACES):
-        basis_out[f] = basis[f]
-        product_out[f] = thin(stacked(basis[f]), matrices[2][f])
-
-
-def spread_kernel(faces, unread, basis_ref, theirs_ref, product_ref, *refs):
-    inverse_refs, out_ref = refs[0:2], refs[2]
-    basis = [basis_ref[f] for f in range(FACES)]
     factors = factor_inverses([dot(b, b, ((1,), (1,))) for b in basis])
-    for f in range(FACES):
-        both = jnp.concatenate([product_ref[f], dot(factors[f], theirs_ref[f])], axis=0)
-        high, low = split(thin(stacked(both), find(faces, inverse_refs, f)).T)
+    for f in range(2):
+        theirs = dot(factors[f], thin(stacked(basis[f]), matrices[2][f]))
+        both = jnp.concatenate([product_ref[f], theirs], axis=0)
+        high, low = split(thin(stacked(both), matrices[1][f]).T)
         out_ref[f] = jnp.concatenate([high, high, low], axis=1)
 
 
-def choose_kernel(flag_ref, here_ref, there_ref, matrix_ref, right_ref):
+def choose_kernel(flag_ref, here_ref, there_ref, product_ref, matrix_ref, right_ref):
     mine = flag_ref[0:1, 0:1] > 0.5
     other = flag_ref[1:2, 0:1] > 0.5
-    total = jnp.where(mine, here_ref[...], 0.0) + jnp.where(other, there_ref[...], 0.0)
-    lanes = matrix_ref.shape[1]
-    matrix_ref[...] = total[:, :lanes]
-    right_ref[...] = total[:, lanes:]
-
-
-def add_kernel(first_ref, second_ref, third_ref, fourth_ref, unread, matrix_ref, right_ref):
-    matrix_ref[...] = first_ref[...] + second_ref[...]
-    right_ref[...] = third_ref[...] + fourth_ref[...]
-
-
-def solve_kernel(size, terms, *refs):
-    matrix, right = refs[0][...], refs[terms][...]
+    half = product_ref.shape[2] // 2
+    lanes, wide_lanes = matrix_ref.shape[1] - half, here_ref.shape[1] - 2 * half
+    here, there = here_ref[:, :wide_lanes], there_ref[:, :wide_lanes]
+    total = jnp.where(mine, here, 0.0) + jnp.where(other, there, 0.0)
+    outer = there_ref[:, wide_lanes + half :]
+    matrix_ref[...] = jnp.concatenate([total[:, :lanes], outer], axis=1)
+    right_ref[...] = jnp.concatenate([total[:, lanes:], fold(product_ref[4])], axis=1)
+
+
+def add_kernel(first_ref, second_ref, third_ref, fourth_ref, product_ref, unread, *refs):
+    matrix_ref, right_ref = refs
+    half = product_ref.shape[2] // 2
+    lanes, right_lanes = matrix_ref.shape[1] - half, right_ref.shape[1]
+    total = first_ref[:, :lanes] + second_ref[:, :lanes]
+    matrix_ref[...] = jnp.concatenate([total, fold(product_ref[5])], axis=1)
+    right_ref[...] = third_ref[:, :right_lanes] + fourth_ref[:, :right_lanes]
+
+
+def solve_kernel(size, terms, columns, *refs):
+    lanes = size * BLOCKS * (BLOCKS + 1) // 2
+    matrix, right = refs[0][:, :lanes], refs[terms][...]
     for term in range(1, terms):
-        matrix = matrix + refs[term][...]
+        matrix = matrix + refs[term][:, :lanes]
         right = right + refs[terms + term][...]
-    answer_ref = refs[2 * terms + 1]
-    columns = answer_ref.shape[1]
+    answer_ref = refs[-1]
     lines = []
     offset = 0
     for b in range(BLOCKS):
@@ -493,16 +500,22 @@
         for c in range(b, BLOCKS):
             block = lines[b][:, (c - b) * size : (c - b + 1) * size]
             blocks[b, c] = downs[b] * block * acrosses[c]
+            if c > b:
+                blocks[c, b] = blocks[b, c].T
         rights.append(downs[b] * right[:, b * columns : (b + 1) * columns])
     for b in range(BLOCKS):
         (inverse,) = factor_inverses([blocks[b, b]])
         later = range(b + 1, BLOCKS)
         row = dot(inverse, jnp.concatenate([rights[b]] + [blocks[b, c] for c in later], axis=1))
-        upper = {c: row[:, columns + (c - b - 1) * size : columns + (c - b) * size] for c in later}
-        for c in later:
-            for d in range(c, BLOCKS):
-                blocks[c, d] = blocks[c, d] - dot(upper[c], upper[d], ((0,), (0,)))
-            rights[c] = rights[c] - dot(upper[c], row[:, :columns], ((0,), (0,)))
+        if later:
+            column = jnp.concatenate([blocks[c, b] for c in later], axis=0)
+            change = dot(dot(column, inverse, ((1,), (1,))), row)
+        for i, c in enumerate(later):
+            part = change[i * size : (i + 1) * size]
+            rights[c] = rights[c] - part[:, :columns]
+            for j, d in enumerate(later):
+                start = columns + j * size
+                blocks[c, d] = blocks[c, d] - part[:, start : start + size]
         row = dot(inverse, row, ((0,), (0,)))
         rights[b] = row[:, :columns]
         for c in later:
@@ -532,12 +545,17 @@
     )
 
 
-def last_faces(spread_ref, pairs, out_ref, result, sems):
-    width = spread_ref.shape[1]
+def through(inverse, mine, theirs, my_answer, their_answer):
+    high, low = split(jnp.concatenate([mine, theirs], axis=0).T)
+    spread = jnp.concatenate([high, high, low], axis=1)
+    return wide(inverse, split(last_product(spread, my_answer, their_answer)))
+
+
+def last_faces(values, width, out_ref, result, sems):
     copies = []
-    for f, (mine, theirs) in pairs.items():
+    for f, value in values.items():
         place = pl.ds(f * width, width)
-        result[f * width : (f + 1) * width] = last_product(spread_ref[f], mine, theirs)
+        result[f * width : (f + 1) * width] = value()
         copy = pltpu.make_async_copy(result.at[place], out_ref.at[place], sems.at[f])
         copy.start()
         copies.append(copy)
@@ -545,38 +563,81 @@
         copy.wait()
 
 
-def last_kernel(ncon, spread_ref, answer_ref, *refs):
+def last_plain_kernel(faces, product_ref, early_inverse, late_inverse, answer_ref, *refs):
     inputs, rest = refs[:-3], refs[-3:]
-    pairs = {}
+    ncon, width = product_ref.shape[1:]
+    values = {}
     done = 0
-    for position, axis in enumerate(AXES):
+    near = []
+    for axis in AXES[1:] * 2:
         number = face_arrays(lax.axis_size(axis))
-        near = receive(inputs[done : done + number], axis)
+        near += receive(inputs[done : done + number], axis)
         done += number
-        for f, theirs in zip((2 * position, 2 * position + 1), near):
-            pairs[f] = (answer_ref[f * ncon : (f + 1) * ncon], theirs)
-    last_faces(spread_ref, pairs, *rest)
-
-
-def last_near_kernel(ncon, flag_ref, spread_ref, here_ref, there_ref, *refs):
+    for f in range(2, FACES):
+        values[f] = functools.partial(
+            through,
+            find(faces, (early_inverse, late_inverse), f),
+            product_ref[f],
+            near[f - 2],
+            answer_ref[f * ncon : (f + 1) * ncon],
+            near[f + 2],
+        )
+    last_faces(values, width, *rest)
+
+
+def last_near_kernel(
+    faces,
+    columns,
+    flag_ref,
+    product_ref,
+    early_inverse,
+    late_inverse,
+    there_ref,
+    matrix_ref,
+    right_ref,
+    matrix_last,
+    here_answer,
+    there_answer,
+    *refs,
+):
+    ncon, width = product_ref.shape[1:]
+    half = width // 2
+    lanes = matrix_ref.shape[1] - half
+    inner = unfold(there_ref[:, lanes + BLOCKS * columns : lanes + BLOCKS * columns + half])
+    outer = unfold(matrix_ref[:, lanes:])
+    upward = is_even("gy")
+    theirs = {
+        2: jnp.where(upward, outer, inner),
+        3: jnp.where(upward, inner, outer),
+        4: unfold(matrix_last[:, lanes:]),
+        5: unfold(right_ref[:, BLOCKS * columns :]),
+    }
+
     def answer(flag, f):
         place = slice(f * ncon, (f + 1) * ncon)
         hit = flag_ref[flag : flag + 1, 0:1] > 0.5
-        return jnp.where(hit, here_ref[place], there_ref[place])
-
-    pairs = {f: (answer(0, f), answer(f, f ^ 1)) for f in range(2, FACES)}
-    last_faces(spread_ref, pairs, *refs)
+        return jnp.where(hit, here_answer[place], there_answer[place])
+
+    values = {}
+    for f in range(2, FACES):
+        values[f] = functools.partial(
+            through,
+            find(faces, (early_inverse, late_inverse), f),
+            product_ref[f],
+            theirs[f],
+            answer(0, f),
+            answer(f, f ^ 1),
+        )
+    last_faces(values, width, *refs)
 
 
 def last_far_kernel(ncon, spread_ref, rows_ref, *refs):
     theirs = receive(refs[:-4], AXES[0])
-    pairs = {f: (rows_ref[f * ncon : (f + 1) * ncon], theirs[f]) for f in (0, 1)}
-    last_faces(spread_ref, pairs, *refs[-3:])
-
-
-def sum_rounds(rows, planes):
-    rounds = [("gy", 2**i) for i in range(1, rows.bit_length() - 1)]
-    return rounds + [("gz", 2**i) for i in range(planes.bit_length() - 1)]
+    values = {}
+    for f in range(2):
+        mine = rows_ref[f * ncon : (f + 1) * ncon]
+        values[f] = functools.partial(last_product, spread_ref[f], mine, theirs[f])
+    last_faces(values, spread_ref.shape[1], *refs[-3:])
 
 
 def per_device(schur, start_block, resid, group_of):
@@ -590,7 +651,9 @@
     arrays = sum(face_arrays(count) for count in counts)
     coarse = FACES * ncon
     size = 2 * ncon
+    half = width // 2
     lanes = size * BLOCKS * (BLOCKS + 1) // 2
+    right_lanes = BLOCKS * columns
     uppers = FACES * (FACES - 1) // 2
     anywhere = pl.BlockSpec(memory_space=pl.ANY)
     main_memory = pl.BlockSpec(memory_space=pltpu.HBM)
@@ -613,16 +676,14 @@
 
     *packed, own = pl.pallas_call(
         functools.partial(pack_kernel, counts, width),
-        out_shape=[
-            part
-            for count in counts
-            for part in face_shapes(count, (width + 8 + 2 * ncon, width // 2))
-        ]
+        out_shape=face_shapes(counts[0], (width + 8 + 2 * ncon, half))
+        + face_shapes(counts[1], (width + 8 + 2 * ncon, half))
+        + face_shapes(counts[2], (width + 8, half))
         + [shape(FACES, width, width)],
         in_specs=[main_memory, main_memory],
         out_specs=vmem_specs(arrays + 1),
         scratch_shapes=[
-            pltpu.VMEM((FACES, ncon, width), jnp.float32),
+            pltpu.VMEM((4, ncon, width), jnp.float32),
             pltpu.SemaphoreType.DMA((FACES,)),
             pltpu.SemaphoreType.DMA,
         ],
@@ -658,7 +719,7 @@
 
     payload, product, late_partner, late_inverse = pl.pallas_call(
         functools.partial(main_kernel, (AXES[0], AXES[1]), early, late),
-        out_shape=[shape(size, lanes + BLOCKS * columns), shape(FACES, ncon, width)]
+        out_shape=[shape(size, lanes + right_lanes + 2 * half), shape(FACES, ncon, width)]
         + [halves(len(late))] * 2,
         in_specs=vmem_specs(len(got[0]) + len(got[1]) + 6),
         out_specs=vmem_specs(4),
@@ -669,34 +730,25 @@
 
     partners = [early_partner, late_partner]
     inverses = [early_inverse, late_inverse]
-    their_basis, their_product = pl.pallas_call(
-        functools.partial(theirs_kernel, faces, ncon),
-        out_shape=[shape(FACES, ncon, width)] * 2,
-        in_specs=vmem_specs(arrays + 5),
-        out_specs=vmem_specs(2),
-        compiler_params=params(16),
-        cost_estimate=cost(2),
-    )(*got[0], *got[1], *got[2], own_halves, *partners, *inverses)
-
     def spread_of(token):
         return pl.pallas_call(
-            functools.partial(spread_kernel, faces),
-            out_shape=jax.ShapeDtypeStruct((FACES, width, 3 * size), jnp.bfloat16),
-            in_specs=[anywhere] + vmem_specs(5),
+            functools.partial(spread_kernel, faces, ncon),
+            out_shape=jax.ShapeDtypeStruct((2, width, 3 * size), jnp.bfloat16),
+            in_specs=[anywhere] + vmem_specs(len(got[0]) + 6),
             out_specs=vmem_specs(1)[0],
             compiler_params=params(16),
             cost_estimate=cost(3),
-        )(token, their_basis, their_product, product, *inverses)
-
-    def solve(matrices, rights, token):
+        )(token, *got[0], own_halves, product, *partners, *inverses)
+
+    def solve(matrices, rights):
         return pl.pallas_call(
-            functools.partial(solve_kernel, size, len(matrices)),
+            functools.partial(solve_kernel, size, len(matrices), columns),
             out_shape=shape(coarse, columns),
-            in_specs=vmem_specs(2 * len(matrices)) + [anywhere],
+            in_specs=vmem_specs(2 * len(matrices)),
             out_specs=vmem_specs(1)[0],
             compiler_params=params(12),
             cost_estimate=cost(7),
-        )(*matrices, *rights, token)
+        )(*matrices, *rights)
 
     result = dict(
         out_shape=shape(order, columns),
@@ -705,39 +757,34 @@
             pltpu.VMEM((order, columns), jnp.float32),
             pltpu.SemaphoreType.DMA((FACES,)),
         ],
-        compiler_params=params(8),
+        compiler_params=params(12),
         cost_estimate=cost(1),
     )
-    rows = counts[1]
     groups = group_of.shape[0] // GROUP_SIZE
-    if groups == 2 and rows > 1 and not (rows & (rows - 1) or planes & (planes - 1)):
-        other = lax.ppermute(payload, "gy", flipped("gy", 1))
-        pair_shape = [shape(size, lanes), shape(size, BLOCKS * columns)]
+    if groups == 2 and counts[1] == 4 and planes == 2:
+        core_swap, chip_x, chip_y = flipped("gy", 1), flipped("gy", 2), flipped("gz", 1)
+        other = lax.ppermute(payload, "gy", core_swap)
         left, rest = pl.pallas_call(
             choose_kernel,
-            out_shape=pair_shape,
-            in_specs=vmem_specs(3),
+            out_shape=[shape(size, lanes + half), shape(size, right_lanes + half)],
+            in_specs=vmem_specs(4),
             out_specs=vmem_specs(2),
             compiler_params=params(8),
-        )(flags, payload, other)
-        rounds = sum_rounds(rows, planes)
-        for step in range(len(rounds)):
-            axis, bit = rounds[step]
-            left_moved = lax.ppermute(left, axis, flipped(axis, bit))
-            axis, bit = rounds[-1 - step]
-            rest_moved = lax.ppermute(rest, axis, flipped(axis, bit))
-            if step == len(rounds) - 1:
-                break
-            left, rest = pl.pallas_call(
-                add_kernel,
-                out_shape=pair_shape,
-                in_specs=vmem_specs(4) + [anywhere],
-                out_specs=vmem_specs(2),
-                compiler_params=params(8),
-            )(left, left_moved, rest, rest_moved, their_basis)
+        )(flags, payload, other, product)
+        left_moved = lax.ppermute(left, "gy", chip_x)
+        rest_moved = lax.ppermute(rest, "gz", chip_y)
         spread = spread_of(left)
-        answer = solve([left, left_moved], [rest, rest_moved], spread)
-        there = lax.ppermute(answer, "gy", flipped("gy", 1))
+        left_last, rest_last = pl.pallas_call(
+            add_kernel,
+            out_shape=[shape(size, lanes + half), shape(size, right_lanes)],
+            in_specs=vmem_specs(5) + [anywhere],
+            out_specs=vmem_specs(2),
+            compiler_params=params(8),
+        )(left, left_moved, rest, rest_moved, product, spread)
+        left_other = lax.ppermute(left_last, "gz", chip_y)
+        rest_other = lax.ppermute(rest_last, "gy", chip_x)
+        answer = solve([left_last, left_other], [rest_last, rest_other])
+        there = lax.ppermute(answer, "gy", core_swap)
         *sent, mine = pl.pallas_call(
             functools.partial(rows_kernel, ncon),
             out_shape=face_shapes(counts[0], (ncon, columns)) + [shape(size, columns)],
@@ -747,39 +794,46 @@
         )(flags, answer, there)
         across = exchange(sent, AXES[0])
         correction = pl.pallas_call(
-            functools.partial(last_near_kernel, ncon),
-            in_specs=vmem_specs(4),
+            functools.partial(last_near_kernel, faces, columns),
+            in_specs=vmem_specs(10),
             **result,
-        )(flags, spread, answer, there)
-        correction = pl.pallas_call(
-            functools.partial(last_far_kernel, ncon),
-            in_specs=vmem_specs(2 + len(across)) + [main_memory],
-            input_output_aliases={2 + len(across): 0},
-            **result,
-        )(spread, mine, *across, correction)
+        )(
+            flags, product, *inverses, other, left_moved, rest_moved, left_other, answer, there
+        )
     else:
         y, z = lax.axis_index("gy"), lax.axis_index("gz")
-        mine = group_of[y * planes + z]
-        chosen = jnp.arange(groups, dtype=jnp.int32) == mine
-        total = lax.psum(jnp.where(chosen[:, None, None], payload[None], 0.0), ("gy", "gz"))
-        total = lax.dynamic_index_in_dim(total, mine, 0, keepdims=False)
+        member_of = group_of[y * planes + z]
+        chosen = jnp.arange(groups, dtype=jnp.int32) == member_of
+        part = payload[:, : lanes + right_lanes]
+        total = lax.psum(jnp.where(chosen[:, None, None], part[None], 0.0), ("gy", "gz"))
+        total = lax.dynamic_index_in_dim(total, member_of, 0, keepdims=False)
         spread = spread_of(payload)
-        answer = solve([total[:, :lanes]], [total[:, lanes:]], spread)
+        answer = solve([total[:, :lanes]], [total[:, lanes:]])
+
+        def from_near(faces_of, axis):
+            even, odd = faces_of
+            if lax.axis_size(axis) == 2:
+                return exchange([jnp.stack([even, odd])], axis)
+            upward = is_even(axis)
+            return exchange([jnp.where(upward, even, odd), jnp.where(upward, odd, even)], axis)
+
         blocks = answer.reshape(FACES, ncon, columns)
         near = []
-        for position, axis in enumerate(AXES):
-            even, odd = blocks[2 * position], blocks[2 * position + 1]
-            if counts[position] == 2:
-                sent = [jnp.stack([even, odd])]
-            else:
-                upward = is_even(axis)
-                sent = [jnp.where(upward, even, odd), jnp.where(upward, odd, even)]
-            near += exchange(sent, axis)
+        for parts in (product, blocks):
+            near += from_near(parts[2:4], AXES[1]) + from_near(parts[4:6], AXES[2])
+        mine = answer[:size]
+        across = from_near(blocks[:2], AXES[0])
         correction = pl.pallas_call(
-            functools.partial(last_kernel, ncon),
-            in_specs=vmem_specs(2 + arrays),
+            functools.partial(last_plain_kernel, faces),
+            in_specs=vmem_specs(4 + len(near)),
             **result,
-        )(spread, answer, *near)
+        )(product, *inverses, answer, *near)
+    correction = pl.pallas_call(
+        functools.partial(last_far_kernel, ncon),
+        in_specs=vmem_specs(2 + len(across)) + [main_memory],
+        input_output_aliases={2 + len(across): 0},
+        **result,
+    )(spread, mine, *across, correction)
     return correction[None, None, None]
 
 

time: 55.3 us -> 54.7 us (0.989)
  waiting for transfers between devices: 7.44 us -> 8.53 us
  starting transfers between devices: 16.3 us -> 15.5 us
  Pallas kernels: 30.9 us -> 30.2 us
    ppermute x6, waiting for transfers between devices: 4.31 us -> 6.51 us  [the longest x1 3.13 us: per_device(): rest_other = lax.ppermute(rest_last, 'gy', chip_x)]
    ppermute x3, starting transfers between devices: 7.34 us -> 5.95 us  [exchange(): lax.ppermute(arrays[0], axis, outer_pairs(axis))]
    ppermute x3, waiting for transfers between devices: 1.99 us -> 0.65 us  [exchange(): lax.ppermute(arrays[1], axis, flipped(axis, 1))]
    pallas_call x7 -> x6, Pallas kernels: 15.4 us -> 14.8 us  [the longest x1 7.57 us: solve(): pl.pallas_call(functools.partial(solve_kernel, size, len(matrices), colum...]
  transfers between devices with their start and end apart: 13 -> 13, of which waited for: 8 -> 8; matrix products, arithmetic and copies ran while one was open for 0% -> 0% of each run, Pallas kernels for 21% -> 20%
where the time goes in v6:
time: 54.7 us; the launch traced here: 54.6 us
  Pallas kernels  30.2 us (55%)
  starting transfers between devices  15.5 us (28%)
  waiting for transfers between devices  8.53 us (16%)
    pallas_call x1, Pallas kernels, per_device(): pl.pallas_call(functools.partial(main_kernel, (AXES[0], AXES[1]), early,...  8.86 us
    pallas_call x1, Pallas kernels, solve(): pl.pallas_call(functools.partial(solve_kernel, size, len(matrices), colum...  7.57 us
    ppermute x3, starting transfers between devices, exchange(): lax.ppermute(arrays[0], axis, outer_pairs(axis))  5.95 us
    pallas_call x1, Pallas kernels, spread_of(): pl.pallas_call(functools.partial(spread_kernel, faces, ncon), out_shape=j...  3.19 us
    ppermute x1, waiting for transfers between devices, per_device(): rest_other = lax.ppermute(rest_last, 'gy', chip_x)  3.13 us
    ppermute x1, starting transfers between devices, exchange(): return [lax.ppermute(arrays[0], axis, flipped(axis, 1))]  3.03 us
    pallas_call x1, Pallas kernels, per_device(): pl.pallas_call(functools.partial(early_kernel, AXES[2:3], early), out_sha...  2.86 us
    pallas_call x1, Pallas kernels, per_device(): pl.pallas_call(functools.partial(halves_kernel, planes), out_shape=[halve...  2.7 us
  transfers between devices with their start and end apart: 13, of which 8 were waited for; matrix products, arithmetic and copies ran while one was open for 0% of the time, Pallas kernels for 20%

profile of v6, /device:TPU:0, one launch (start us, length us, event | category | flops | bytes accessed | tf_op | source)
XLA Modules:
  0.0 54.6 jit_solution(10435394094042105448)
XLA Ops:
  0.0 0.0 copy-start.1
  0.0 1.7 %shard_map.46 = (f32[328,128]{1,0:T(8,128)S(1)}, f32[328,128]{1,0:T(8,128)S(1)}, f32[328,128]{1,0:T(8,128)S(1)}, f32[328,128]{1,0:T(8,128)S(1)}, f32[2,264,128]{2,1,0:T(8,128)S(1)}, /*index=5*/f32[6,256,256]{2,1,0:T(8,128)S(1)}) custom-call(f32[1536,1536]{1,0:T(8,128)} %bitcast.10, f32[6,32,256]{2,1,0:T(8,128)} %bitcast.6), custom_call_target="tpu_custom_call" | custom-call | tf_op jit(solution)/shard_map/pallas_call | solution.py:677
  1.7 3.0 %collective-permute-start.4 = (f32[2,264,128]{2,1,0:T(8,128)S(1)}, f32[2,264,128]{2,1,0:T(8,128)S(1)}, u32[]{:S(2)}, u32[]{:S(2)}) collective-permute-start(f32[2,264,128]{2,1,0:T(8,128)S(1)} %get-tuple-element.36), channel_id=1, source_target_pairs={{0,1},{1,0},{2,3},{3,2},{4,5},{5,4},{6,7},{7,6},{8,9},{9,8},{10,11... | collective-permute-start | bytes 811016 | tf_op jit(solution)/shard_map/ppermute | solution.py:75
  4.7 3.6 %collective-permute-start = (f32[328,128]{1,0:T(8,128)S(1)}, f32[328,128]{1,0:T(8,128)S(1)}, u32[]{:S(2)}, u32[]{:S(2)}) collective-permute-start(f32[328,128]{1,0:T(8,128)S(1)} %get-tuple-element.30), channel_id=1, source_target_pairs={{0,24},{8,16},{16,8},{24,0},{1,25},{9,17},{17,9},{25,1},{2,26},{10... | collective-permute-start | bytes 503816 | tf_op jit(solution)/shard_map/ppermute | solution.py:77
  8.3 0.0 collective-permute-start.1
  8.3 0.4 collective-permute-start.2
  8.7 1.2 %collective-permute-start.3 = (f32[328,128]{1,0:T(8,128)S(1)}, f32[328,128]{1,0:T(8,128)S(1)}, u32[]{:S(2)}, u32[]{:S(2)}) collective-permute-start(f32[328,128]{1,0:T(8,128)S(1)} %get-tuple-element.33), channel_id=1, source_target_pairs={{0,2},{2,0},{4,6},{6,4},{1,3},{3,1},{5,7},{7,5},{8,10},{10,8},{12,... | collective-permute-start | bytes 503816 | tf_op jit(solution)/shard_map/ppermute | solution.py:78
  9.9 0.0 copy-done.1
  9.9 0.0 copy-start
  9.9 2.7 %shard_map.47 = (bf16[6,2,256,256]{3,2,1,0:T(8,128)(2,1)S(1)}, bf16[15,2,256,256]{3,2,1,0:T(8,128)(2,1)S(1)}, f32[8,128]{1,0:T(8,128)S(1)}) custom-call(f32[1536,1536]{1,0:T(8,128)} %bitcast.11, s32[8]{0:T(128)S(1)} %copy-done.1, f32[6,256,256]{2,1,0:T(8,128)S(1)} %get-tuple-element.28.own_ref.refs_1_.refs_4_), custom_call_target="tpu_custom_call" | custom-call | flops 2000000000 | bytes 1048576 | tf_op jit(solution)/shard_map/pallas_call | solution.py:697
  12.6 0.0 copy-start.2
  12.7 0.0 collective-permute-done.4.refs_0_
  12.7 0.0 copy-done
  12.7 2.9 %shard_map.48 = (f32[2,32,256]{2,1,0:T(8,128)S(1)}, bf16[2,2,256,256]{3,2,1,0:T(8,128)(2,1)S(1)}, bf16[2,2,256,256]{3,2,1,0:T(8,128)(2,1)S(1)}) custom-call(f32[2,264,128]{2,1,0:T(8,128)S(1)} %collective-permute-done.4.refs_0_, f32[6,256,256]{2,1,0:T(8,128)S(1)} %get-tuple-element.28.own_ref.refs_1_.refs_4_, ...), custom_call_target="tpu_custom_call" | custom-call | flops 2000000000 | bytes 1048576 | tf_op jit(solution)/shard_map/pallas_call | solution.py:710
  15.5 0.0 collective-permute-done.refs_0_
  15.6 0.5 collective-permute-done.1.refs_1_
  16.0 0.0 collective-permute-done.2.refs_2_
  16.0 0.0 collective-permute-done.3.refs_3_
  16.0 0.0 copy-done.2
  16.0 8.9 %shard_map.49 = (f32[64,1024]{1,0:T(8,128)S(1)}, f32[6,32,256]{2,1,0:T(8,128)S(1)}, bf16[4,2,256,256]{3,2,1,0:T(8,128)(2,1)S(1)}, bf16[4,2,256,256]{3,2,1,0:T(8,128)(2,1)S(1)}) custom-call(f32[328,128]{1,0:T(8,128)S(1)} %collective-permute-done.refs_0_, f32[328,128]{1,0:T(8,128)S(1)} %collective-permute-done.1.refs_1_, ...), custom_call_target="tpu_custom_call" | custom-call | flops 8000000000 | bytes 1048576 | tf_op jit(solution)/shard_map/pallas_call | solution.py:720
  24.9 0.1 collective-permute-start.5
  25.0 1.5 %collective-permute-done.5.there_ref = f32[64,1024]{1,0:T(8,128)S(1)} collective-permute-done((f32[64,1024]{1,0:T(8,128)S(1)}, f32[64,1024]{1,0:T(8,128)S(1)}, u32[]{:S(2)}, u32[]{:S(2)}) %collective-permute-start.5) | collective-permute-done | bytes 262176 | tf_op jit(solution)/shard_map/ppermute | solution.py:766
  26.5 0.1 shard_map.50
  26.6 0.6 %collective-permute-start.7 = (f32[64,512]{1,0:T(8,128)S(1)}, f32[64,512]{1,0:T(8,128)S(1)}, u32[]{:S(2)}, u32[]{:S(2)}) collective-permute-start(f32[64,512]{1,0:T(8,128)S(1)} %get-tuple-element.45.third_ref), channel_id=1, source_target_pairs={{0,1},{1,0},{2,3},{3,2},{4,5},{5,4},{6,7},{7,6},{8,9},{9,8},{10,11... | collective-permute-start | bytes 393224 | tf_op jit(solution)/shard_map/ppermute | solution.py:775
  27.2 1.5 %collective-permute-start.6 = (f32[64,512]{1,0:T(8,128)S(1)}, f32[64,512]{1,0:T(8,128)S(1)}, u32[]{:S(2)}, u32[]{:S(2)}) collective-permute-start(f32[64,512]{1,0:T(8,128)S(1)} %get-tuple-element.40.unread.first_ref), channel_id=1, source_target_pairs={{0,4},{2,6},{4,0},{6,2},{1,5},{3,7},{5,1},{7,3},{8,12},{10,14},{12... | collective-permute-start | bytes 393224 | tf_op jit(solution)/shard_map/ppermute | solution.py:774
  28.7 3.2 %shard_map.51.unread.spread_ref = bf16[2,256,192]{2,1,0:T(8,128)(2,1)S(1)} custom-call(f32[64,512]{1,0:T(8,128)S(1)} %get-tuple-element.40.unread.first_ref, f32[328,128]{1,0:T(8,128)S(1)} %collective-permute-done.refs_0_, f32[328,128]{1,0:T(8,128)S(1)} %collective-permute-done.1.refs_1_, bf16[6,2,256,256]{3,2,1,0:T(8,128)(2,1)S(1)} %get-tuple-element.34.refs_2_.refs_5_, ...), custom_call_target="tpu_custom_call" | custom-call | flops 3000000000 | bytes 1048576 | tf_op jit(solution)/shard_map/pallas_call | solution.py:734
  31.9 0.3 collective-permute-done.7.fourth_ref.right_ref
  32.2 0.2 collective-permute-done.6.second_ref.matrix_ref
  32.5 1.6 %collective-permute-start.8 = (f32[64,512]{1,0:T(8,128)S(1)}, f32[64,512]{1,0:T(8,128)S(1)}, u32[]{:S(2)}, u32[]{:S(2)}) collective-permute-start(f32[64,512]{1,0:T(8,128)S(1)} %get-tuple-element.46.refs_0_), channel_id=1, source_target_pairs={{0,1},{1,0},{2,3},{3,2},{4,5},{5,4},{6,7},{7,6},{8,9},{9,8},{10,11... | collective-permute-start | bytes 393224 | tf_op jit(solution)/shard_map/ppermute | solution.py:784
  34.0 1.5 %collective-permute-start.9 = (f32[64,384]{1,0:T(8,128)S(1)}, f32[64,384]{1,0:T(8,128)S(1)}, u32[]{:S(2)}, u32[]{:S(2)}) collective-permute-start(f32[64,384]{1,0:T(8,128)S(1)} %get-tuple-element.47.refs_2_), channel_id=1, source_target_pairs={{0,4},{2,6},{4,0},{6,2},{1,5},{3,7},{5,1},{7,3},{8,12},{10,14},{12... | collective-permute-start | bytes 294920 | tf_op jit(solution)/shard_map/ppermute | solution.py:785
  35.5 3.1 %collective-permute-done.9.refs_3_ = f32[64,384]{1,0:T(8,128)S(1)} collective-permute-done((f32[64,384]{1,0:T(8,128)S(1)}, f32[64,384]{1,0:T(8,128)S(1)}, u32[]{:S(2)}, u32[]{:S(2)}) %collective-permute-start.9) | collective-permute-done | bytes 98336 | tf_op jit(solution)/shard_map/ppermute | solution.py:785
  38.7 0.0 collective-permute-done.8.refs_1_.matrix_last
  38.7 7.6 %shard_map.53.here_ref.here_answer = f32[192,128]{1,0:T(8,128)S(1)} custom-call(f32[64,512]{1,0:T(8,128)S(1)} %get-tuple-element.46.refs_0_, f32[64,512]{1,0:T(8,128)S(1)} %collective-permute-done.8.refs_1_.matrix_last, f32[64,384]{1,0:T(8,128)S(1)} %get-tuple-element.47.refs_2_, f32[64,384]{1,0:T(8,128)S(1)} %collective-permute-done.9.refs_3_), custom_call_target="tpu_custom_call" | custom-call | flops 7000000000 | bytes 1048576 | tf_op jit(solution)/shard_map/pallas_call | solution.py:744
  46.2 0.1 collective-permute-start.10
  46.3 1.3 %collective-permute-done.10.there_ref.there_answer = f32[192,128]{1,0:T(8,128)S(1)} collective-permute-done((f32[192,128]{1,0:T(8,128)S(1)}, f32[192,128]{1,0:T(8,128)S(1)}, u32[]{:S(2)}, u32[]{:S(2)}) %collective-permute-start.10) | collective-permute-done | bytes 98336 | tf_op jit(solution)/shard_map/ppermute | solution.py:787
  47.7 2.0 %collective-permute-start.11 = (f32[32,128]{1,0:T(8,128)S(1)}, f32[32,128]{1,0:T(8,128)S(1)}, u32[]{:S(2)}, u32[]{:S(2)}) collective-permute-start(f32[32,128]{1,0:T(8,128)S(1)} %get-tuple-element.49), channel_id=1, source_target_pairs={{0,24},{8,16},{16,8},{24,0},{1,25},{9,17},{17,9},{25,1},{2,26},{10... | collective-permute-start | bytes 49160 | tf_op jit(solution)/shard_map/ppermute | solution.py:77
  49.6 0.0 collective-permute-start.12
  49.6 2.3 %shard_map.55.refs_2_ = f32[1536,128]{1,0:T(8,128)} custom-call(f32[8,128]{1,0:T(8,128)S(1)} %get-tuple-element.29.flag_ref, f32[6,32,256]{2,1,0:T(8,128)S(1)} %get-tuple-element.39.product_ref.refs_3_, bf16[2,2,256,256]{3,2,1,0:T(8,128)(2,1)S(1)} %get-tuple-element.43.refs_6_.early_inverse, ...), custom_call_target="tpu_custom_call" | custom-call | flops 1000000000 | bytes 1048576 | tf_op jit(solution)/shard_map/pallas_call | solution.py:796
  51.9 1.4 %collective-permute-done.11.refs_0_ = f32[32,128]{1,0:T(8,128)S(1)} collective-permute-done((f32[32,128]{1,0:T(8,128)S(1)}, f32[32,128]{1,0:T(8,128)S(1)}, u32[]{:S(2)}, u32[]{:S(2)}) %collective-permute-start.11) | collective-permute-done | bytes 16416 | tf_op jit(solution)/shard_map/ppermute | solution.py:77
  53.3 0.2 collective-permute-done.12.refs_1_
  53.4 1.0 %shard_map.56 = f32[1536,128]{1,0:T(8,128)} custom-call(bf16[2,256,192]{2,1,0:T(8,128)(2,1)S(1)} %shard_map.51.unread.spread_ref, f32[64,128]{1,0:T(8,128)S(1)} %get-tuple-element.48.rows_ref, f32[32,128]{1,0:T(8,128)S(1)} %collective-permute-done.11.refs_0_, f32[32,128]{1,0:T(8,128)S(1)} %collective-permute-done.12.refs_1_, ...), custom_call_target="tpu_custom_call", output_to_operand_aliasing={{}: (4, {})} | custom-call | flops 1000000000 | bytes 1048576 | tf_op jit(solution)/shard_map/pallas_call | solution.py:831
  (2 shorter events, 0.1 us)
Async XLA Ops:
  0.0 9.9 %copy-start.1 = (s32[8]{0:T(128)S(1)}, s32[8]{0:T(128)}, u32[]{:S(2)}) copy-start(s32[8]{0:T(128)} %group_ref.1) | copy-start | bytes 100
  1.7 11.0 %collective-permute-start.4 = (f32[2,264,128]{2,1,0:T(8,128)S(1)}, f32[2,264,128]{2,1,0:T(8,128)S(1)}, u32[]{:S(2)}, u32[]{:S(2)}) collective-permute-start(f32[2,264,128]{2,1,0:T(8,128)S(1)} %get-tuple-element.36), channel_id=1, source_target_pairs={{0,1},{1,0},{2,3},{3,2},{4,5},{5,4},{6,7},{7,6},{8,9},{9,8},{10,11... | collective-permute-start | bytes 811016 | tf_op jit(solution)/shard_map/ppermute | solution.py:75
  4.7 10.8 %collective-permute-start = (f32[328,128]{1,0:T(8,128)S(1)}, f32[328,128]{1,0:T(8,128)S(1)}, u32[]{:S(2)}, u32[]{:S(2)}) collective-permute-start(f32[328,128]{1,0:T(8,128)S(1)} %get-tuple-element.30), channel_id=1, source_target_pairs={{0,24},{8,16},{16,8},{24,0},{1,25},{9,17},{17,9},{25,1},{2,26},{10... | collective-permute-start | bytes 503816 | tf_op jit(solution)/shard_map/ppermute | solution.py:77
  8.3 7.7 %collective-permute-start.1 = (f32[328,128]{1,0:T(8,128)S(1)}, f32[328,128]{1,0:T(8,128)S(1)}, u32[]{:S(2)}, u32[]{:S(2)}) collective-permute-start(f32[328,128]{1,0:T(8,128)S(1)} %get-tuple-element.31), channel_id=1, source_target_pairs={{0,8},{8,0},{16,24},{24,16},{1,9},{9,1},{17,25},{25,17},{2,10},{10... | collective-permute-start | bytes 503816 | tf_op jit(solution)/shard_map/ppermute | solution.py:78
  8.3 7.7 %collective-permute-start.2 = (f32[328,128]{1,0:T(8,128)S(1)}, f32[328,128]{1,0:T(8,128)S(1)}, u32[]{:S(2)}, u32[]{:S(2)}) collective-permute-start(f32[328,128]{1,0:T(8,128)S(1)} %get-tuple-element.32), channel_id=1, source_target_pairs={{0,6},{2,4},{4,2},{6,0},{1,7},{3,5},{5,3},{7,1},{8,14},{10,12},{12... | collective-permute-start | bytes 503816 | tf_op jit(solution)/shard_map/ppermute | solution.py:77
  8.7 7.3 %collective-permute-start.3 = (f32[328,128]{1,0:T(8,128)S(1)}, f32[328,128]{1,0:T(8,128)S(1)}, u32[]{:S(2)}, u32[]{:S(2)}) collective-permute-start(f32[328,128]{1,0:T(8,128)S(1)} %get-tuple-element.33), channel_id=1, source_target_pairs={{0,2},{2,0},{4,6},{6,4},{1,3},{3,1},{5,7},{7,5},{8,10},{10,8},{12,... | collective-permute-start | bytes 503816 | tf_op jit(solution)/shard_map/ppermute | solution.py:78
  9.9 2.7 %copy-start = (f32[1,1,1,6,256,32]{4,5,3,2,1,0:T(8,128)S(1)}, f32[1,1,1,6,256,32]{4,5,3,2,1,0:T(8,128)}, u32[]{:S(2)}) copy-start(f32[1,1,1,6,256,32]{4,5,3,2,1,0:T(8,128)} %param.5) | copy-start | bytes 589828
  12.6 3.4 %copy-start.2 = (f32[1,1,1,1536,128]{4,3,2,1,0:T(8,128)S(1)}, f32[1,1,1,1536,128]{4,3,2,1,0:T(8,128)}, u32[]{:S(2)}) copy-start(f32[1,1,1,1536,128]{4,3,2,1,0:T(8,128)} %param.6) | copy-start | bytes 2359300
  24.9 1.6 %collective-permute-start.5 = (f32[64,1024]{1,0:T(8,128)S(1)}, f32[64,1024]{1,0:T(8,128)S(1)}, u32[]{:S(2)}, u32[]{:S(2)}) collective-permute-start(f32[64,1024]{1,0:T(8,128)S(1)} %get-tuple-element.38.here_ref), channel_id=1, source_target_pairs={{0,2},{2,0},{4,6},{6,4},{1,3},{3,1},{5,7},{7,5},{8,10},{10,8},{12,... | collective-permute-start | bytes 786440 | tf_op jit(solution)/shard_map/ppermute | solution.py:766
  26.6 5.6 %collective-permute-start.7 = (f32[64,512]{1,0:T(8,128)S(1)}, f32[64,512]{1,0:T(8,128)S(1)}, u32[]{:S(2)}, u32[]{:S(2)}) collective-permute-start(f32[64,512]{1,0:T(8,128)S(1)} %get-tuple-element.45.third_ref), channel_id=1, source_target_pairs={{0,1},{1,0},{2,3},{3,2},{4,5},{5,4},{6,7},{7,6},{8,9},{9,8},{10,11... | collective-permute-start | bytes 393224 | tf_op jit(solution)/shard_map/ppermute | solution.py:775
  27.2 5.3 %collective-permute-start.6 = (f32[64,512]{1,0:T(8,128)S(1)}, f32[64,512]{1,0:T(8,128)S(1)}, u32[]{:S(2)}, u32[]{:S(2)}) collective-permute-start(f32[64,512]{1,0:T(8,128)S(1)} %get-tuple-element.40.unread.first_ref), channel_id=1, source_target_pairs={{0,4},{2,6},{4,0},{6,2},{1,5},{3,7},{5,1},{7,3},{8,12},{10,14},{12... | collective-permute-start | bytes 393224 | tf_op jit(solution)/shard_map/ppermute | solution.py:774
  32.5 6.2 %collective-permute-start.8 = (f32[64,512]{1,0:T(8,128)S(1)}, f32[64,512]{1,0:T(8,128)S(1)}, u32[]{:S(2)}, u32[]{:S(2)}) collective-permute-start(f32[64,512]{1,0:T(8,128)S(1)} %get-tuple-element.46.refs_0_), channel_id=1, source_target_pairs={{0,1},{1,0},{2,3},{3,2},{4,5},{5,4},{6,7},{7,6},{8,9},{9,8},{10,11... | collective-permute-start | bytes 393224 | tf_op jit(solution)/shard_map/ppermute | solution.py:784
  34.0 4.6 %collective-permute-start.9 = (f32[64,384]{1,0:T(8,128)S(1)}, f32[64,384]{1,0:T(8,128)S(1)}, u32[]{:S(2)}, u32[]{:S(2)}) collective-permute-start(f32[64,384]{1,0:T(8,128)S(1)} %get-tuple-element.47.refs_2_), channel_id=1, source_target_pairs={{0,4},{2,6},{4,0},{6,2},{1,5},{3,7},{5,1},{7,3},{8,12},{10,14},{12... | collective-permute-start | bytes 294920 | tf_op jit(solution)/shard_map/ppermute | solution.py:785
  46.2 1.4 %collective-permute-start.10 = (f32[192,128]{1,0:T(8,128)S(1)}, f32[192,128]{1,0:T(8,128)S(1)}, u32[]{:S(2)}, u32[]{:S(2)}) collective-permute-start(f32[192,128]{1,0:T(8,128)S(1)} %shard_map.53.here_ref.here_answer), channel_id=1, source_target_pairs={{0,2},{2,0},{4,6},{6,4},{1,3},{3,1},{5,7},{7,5},{8,10},{10,8},{12,... | collective-permute-start | bytes 294920 | tf_op jit(solution)/shard_map/ppermute | solution.py:787
  47.7 5.6 %collective-permute-start.11 = (f32[32,128]{1,0:T(8,128)S(1)}, f32[32,128]{1,0:T(8,128)S(1)}, u32[]{:S(2)}, u32[]{:S(2)}) collective-permute-start(f32[32,128]{1,0:T(8,128)S(1)} %get-tuple-element.49), channel_id=1, source_target_pairs={{0,24},{8,16},{16,8},{24,0},{1,25},{9,17},{17,9},{25,1},{2,26},{10... | collective-permute-start | bytes 49160 | tf_op jit(solution)/shard_map/ppermute | solution.py:77
  49.6 3.8 %collective-permute-start.12 = (f32[32,128]{1,0:T(8,128)S(1)}, f32[32,128]{1,0:T(8,128)S(1)}, u32[]{:S(2)}, u32[]{:S(2)}) collective-permute-start(f32[32,128]{1,0:T(8,128)S(1)} %get-tuple-element.50), channel_id=1, source_target_pairs={{0,8},{8,0},{16,24},{24,16},{1,9},{9,1},{17,25},{25,17},{2,10},{10... | collective-permute-start | bytes 49160 | tf_op jit(solution)/shard_map/ppermute | solution.py:78

commit v7 on v6

--- a/solution.py
+++ b/solution.py
@@ -111,9 +111,8 @@
     return [pl.BlockSpec(memory_space=pltpu.VMEM)] * count
 
 
-def pack_kernel(counts, width, schur_ref, starts_ref, *refs):
-    outs, blocks = refs[:-4], refs[-4]
-    starts, sems, start_sem = refs[-3:]
+def pack_kernel(counts, width, schur_ref, *refs):
+    outs, blocks, sems = refs[:-2], refs[-2], refs[-1]
     half = width // 2
     copies = []
     for f in range(FACES):
@@ -121,10 +120,7 @@
         copy = pltpu.make_async_copy(schur_ref.at[place, place], blocks.at[f], sems.at[f])
         copy.start()
         copies.append(copy)
-    start_copy = pltpu.make_async_copy(starts_ref.at[pl.ds(0, 4)], starts, start_sem)
-    start_copy.start()
     row, col = iota((half, half), 0), iota((half, half), 1)
-    start_copy.wait()
 
     def pack(f):
         copies[f].wait()
@@ -133,10 +129,7 @@
         diag = jnp.sum(jnp.where(row == col, second, 0.0), axis=0, keepdims=True)
         mixed = jnp.where(row >= col, first, second)
         tail = jnp.broadcast_to(diag, (8, half))
-        parts = [blocks[f, half:width, 0:half], mixed, tail]
-        if f < 4:
-            parts += [starts[f, :, :half], starts[f, :, half:]]
-        return jnp.concatenate(parts, axis=0)
+        return jnp.concatenate([blocks[f, half:width, 0:half], mixed, tail], axis=0)
 
     done = 0
     for position, axis in enumerate(AXES):
@@ -157,12 +150,6 @@
     return jnp.concatenate(
         [jnp.concatenate([first, low.T], axis=1), jnp.concatenate([low, second], axis=1)], axis=0
     )
-
-
-def unpack_starts(packed, ncon):
-    half = packed.shape[1]
-    rows = packed[2 * half + 8 :]
-    return jnp.concatenate([rows[:ncon], rows[ncon:]], axis=1)
 
 
 def factor_inverses(grams, block=8):
@@ -435,27 +422,36 @@
             return load(ref, list(group).index(f))
 
 
-def spread_kernel(faces, ncon, unread, *refs):
-    packed = receive(refs[:-7], AXES[0])
-    own_ref, product_ref = refs[-7:-5]
-    partner_refs, inverse_refs, out_ref = refs[-5:-3], refs[-3:-1], refs[-1]
-    basis = [unpack_starts(part, ncon) for part in packed]
-    matrices = [
-        [load(own_ref, f) for f in range(2)],
-        [find(faces, inverse_refs, f) for f in range(2)],
-        [find(faces, partner_refs, f) for f in range(2)],
-    ]
-    for sweep in range(SUB_ITERS):
-        basis = sweep_basis(*matrices, basis)
-    factors = factor_inverses([dot(b, b, ((1,), (1,))) for b in basis])
-    for f in range(2):
-        theirs = dot(factors[f], thin(stacked(basis[f]), matrices[2][f]))
-        both = jnp.concatenate([product_ref[f], theirs], axis=0)
-        high, low = split(thin(stacked(both), matrices[1][f]).T)
-        out_ref[f] = jnp.concatenate([high, high, low], axis=1)
-
-
-def choose_kernel(flag_ref, here_ref, there_ref, product_ref, matrix_ref, right_ref):
+def spread_pair(mine, theirs, inverse):
+    high, low = split(thin(stacked(jnp.concatenate([mine, theirs], axis=0)), inverse).T)
+    return jnp.concatenate([high, high, low], axis=1)
+
+
+def their_y_products(there_ref, matrix_ref, start):
+    half = (there_ref.shape[1] - start) // 2
+    inner = unfold(there_ref[:, start : start + half])
+    outer = unfold(matrix_ref[:, matrix_ref.shape[1] - half :])
+    upward = is_even("gy")
+    return jnp.where(upward, outer, inner), jnp.where(upward, inner, outer)
+
+
+def spread_kernel(faces, start, unread, product_ref, early_inverse, late_inverse, *refs):
+    out_ref = refs[-1]
+    inverses = (early_inverse, late_inverse)
+    ready = refs[:-1]
+    if start:
+        ready, (there_ref, matrix_ref, right_ref) = refs[:-4], refs[-4:-1]
+    theirs = list(receive(ready, AXES[0]))
+    if start:
+        theirs += their_y_products(there_ref, matrix_ref, start)
+        half = product_ref.shape[2] // 2
+        theirs.append(unfold(right_ref[:, right_ref.shape[1] - half :]))
+    for i, product in enumerate(theirs):
+        f = i if i < 4 else FACES - 1
+        out_ref[i] = spread_pair(product_ref[f], product, find(faces, inverses, f))
+
+
+def choose_kernel(flag_ref, here_ref, there_ref, product_ref, matrix_ref, right_ref, *sent):
     mine = flag_ref[0:1, 0:1] > 0.5
     other = flag_ref[1:2, 0:1] > 0.5
     half = product_ref.shape[2] // 2
@@ -465,10 +461,11 @@
     outer = there_ref[:, wide_lanes + half :]
     matrix_ref[...] = jnp.concatenate([total[:, :lanes], outer], axis=1)
     right_ref[...] = jnp.concatenate([total[:, lanes:], fold(product_ref[4])], axis=1)
-
-
-def add_kernel(first_ref, second_ref, third_ref, fourth_ref, product_ref, unread, *refs):
-    matrix_ref, right_ref = refs
+    send(sent, AXES[0], product_ref[0], product_ref[1])
+
+
+def add_kernel(first_ref, second_ref, third_ref, fourth_ref, product_ref, *refs):
+    matrix_ref, right_ref = refs[-2:]
     half = product_ref.shape[2] // 2
     lanes, right_lanes = matrix_ref.shape[1] - half, right_ref.shape[1]
     total = first_ref[:, :lanes] + second_ref[:, :lanes]
@@ -586,32 +583,11 @@
 
 
 def last_near_kernel(
-    faces,
-    columns,
-    flag_ref,
-    product_ref,
-    early_inverse,
-    late_inverse,
-    there_ref,
-    matrix_ref,
-    right_ref,
-    matrix_last,
-    here_answer,
-    there_answer,
-    *refs,
+    faces, flag_ref, product_ref, early_inverse, late_inverse, matrix_ref, spread_ref, *refs
 ):
+    here_answer, there_answer = refs[:2]
     ncon, width = product_ref.shape[1:]
     half = width // 2
-    lanes = matrix_ref.shape[1] - half
-    inner = unfold(there_ref[:, lanes + BLOCKS * columns : lanes + BLOCKS * columns + half])
-    outer = unfold(matrix_ref[:, lanes:])
-    upward = is_even("gy")
-    theirs = {
-        2: jnp.where(upward, outer, inner),
-        3: jnp.where(upward, inner, outer),
-        4: unfold(matrix_last[:, lanes:]),
-        5: unfold(right_ref[:, BLOCKS * columns :]),
-    }
 
     def answer(flag, f):
         place = slice(f * ncon, (f + 1) * ncon)
@@ -619,16 +595,19 @@
         return jnp.where(hit, here_answer[place], there_answer[place])
 
     values = {}
-    for f in range(2, FACES):
+    for f in (2, 3, 5):
         values[f] = functools.partial(
-            through,
-            find(faces, (early_inverse, late_inverse), f),
-            product_ref[f],
-            theirs[f],
-            answer(0, f),
-            answer(f, f ^ 1),
+            last_product, spread_ref[min(f, 4)], answer(0, f), answer(f, f ^ 1)
         )
-    last_faces(values, width, *refs)
+    values[4] = functools.partial(
+        through,
+        find(faces, (early_inverse, late_inverse), 4),
+        product_ref[4],
+        unfold(matrix_ref[:, matrix_ref.shape[1] - half :]),
+        answer(0, 4),
+        answer(4, 5),
+    )
+    last_faces(values, width, *refs[2:])
 
 
 def last_far_kernel(ncon, spread_ref, rows_ref, *refs):
@@ -658,7 +637,7 @@
     anywhere = pl.BlockSpec(memory_space=pl.ANY)
     main_memory = pl.BlockSpec(memory_space=pltpu.HBM)
     scalars = pl.BlockSpec(memory_space=pltpu.SMEM)
-    early, late = (4, 5), (0, 1, 2, 3)
+    early, late = (2, 3), (0, 1, 4, 5)
     faces = (early, late)
     planes = counts[2]
 
@@ -676,19 +655,13 @@
 
     *packed, own = pl.pallas_call(
         functools.partial(pack_kernel, counts, width),
-        out_shape=face_shapes(counts[0], (width + 8 + 2 * ncon, half))
-        + face_shapes(counts[1], (width + 8 + 2 * ncon, half))
-        + face_shapes(counts[2], (width + 8, half))
+        out_shape=[part for count in counts for part in face_shapes(count, (width + 8, half))]
         + [shape(FACES, width, width)],
-        in_specs=[main_memory, main_memory],
+        in_specs=[main_memory],
         out_specs=vmem_specs(arrays + 1),
-        scratch_shapes=[
-            pltpu.VMEM((4, ncon, width), jnp.float32),
-            pltpu.SemaphoreType.DMA((FACES,)),
-            pltpu.SemaphoreType.DMA,
-        ],
+        scratch_shapes=[pltpu.SemaphoreType.DMA((FACES,))],
         compiler_params=params(12),
-    )(matrix, pltpu.with_memory_space_constraint(starts, pltpu.HBM))
+    )(matrix)
     ends = [sum(face_arrays(count) for count in counts[:position]) for position in range(4)]
     got = {}
     for position in (2, 0, 1):
@@ -708,47 +681,46 @@
     )(matrix, group_of, own)
 
     early_basis, early_partner, early_inverse = pl.pallas_call(
-        functools.partial(early_kernel, AXES[2:3], early),
+        functools.partial(early_kernel, AXES[1:2], early),
         out_shape=[shape(len(early), ncon, width)] + [halves(len(early))] * 2,
-        in_specs=vmem_specs(len(got[2]) + 3),
+        in_specs=vmem_specs(len(got[1]) + 3),
         out_specs=vmem_specs(3),
         scratch_shapes=[pltpu.VMEM((len(early), 2, width, width), jnp.bfloat16)],
         compiler_params=params(16),
         cost_estimate=cost(2),
-    )(*got[2], own, own_halves, starts)
+    )(*got[1], own, own_halves, starts)
 
     payload, product, late_partner, late_inverse = pl.pallas_call(
-        functools.partial(main_kernel, (AXES[0], AXES[1]), early, late),
+        functools.partial(main_kernel, (AXES[0], AXES[2]), early, late),
         out_shape=[shape(size, lanes + right_lanes + 2 * half), shape(FACES, ncon, width)]
         + [halves(len(late))] * 2,
-        in_specs=vmem_specs(len(got[0]) + len(got[1]) + 6),
+        in_specs=vmem_specs(len(got[0]) + len(got[2]) + 6),
         out_specs=vmem_specs(4),
         scratch_shapes=[pltpu.VMEM((len(late), 2, width, width), jnp.bfloat16)],
         compiler_params=params(24),
         cost_estimate=cost(8),
-    )(*got[0], *got[1], own, own_halves, upper_halves, starts, right, early_basis)
-
-    partners = [early_partner, late_partner]
+    )(*got[0], *got[2], own, own_halves, upper_halves, starts, right, early_basis)
+
     inverses = [early_inverse, late_inverse]
-    def spread_of(token):
+    def spread_of(token, theirs, start, *more):
         return pl.pallas_call(
-            functools.partial(spread_kernel, faces, ncon),
-            out_shape=jax.ShapeDtypeStruct((2, width, 3 * size), jnp.bfloat16),
-            in_specs=[anywhere] + vmem_specs(len(got[0]) + 6),
+            functools.partial(spread_kernel, faces, start),
+            out_shape=jax.ShapeDtypeStruct((5 if start else 2, width, 3 * size), jnp.bfloat16),
+            in_specs=[anywhere] + vmem_specs(3 + len(theirs) + len(more)),
             out_specs=vmem_specs(1)[0],
             compiler_params=params(16),
             cost_estimate=cost(3),
-        )(token, *got[0], own_halves, product, *partners, *inverses)
-
-    def solve(matrices, rights):
+        )(token, product, *inverses, *theirs, *more)
+
+    def solve(matrices, rights, unread):
         return pl.pallas_call(
             functools.partial(solve_kernel, size, len(matrices), columns),
             out_shape=shape(coarse, columns),
-            in_specs=vmem_specs(2 * len(matrices)),
+            in_specs=vmem_specs(2 * len(matrices)) + [anywhere],
             out_specs=vmem_specs(1)[0],
             compiler_params=params(12),
             cost_estimate=cost(7),
-        )(*matrices, *rights)
+        )(*matrices, *rights, unread)
 
     result = dict(
         out_shape=shape(order, columns),
@@ -764,26 +736,30 @@
     if groups == 2 and counts[1] == 4 and planes == 2:
         core_swap, chip_x, chip_y = flipped("gy", 1), flipped("gy", 2), flipped("gz", 1)
         other = lax.ppermute(payload, "gy", core_swap)
-        left, rest = pl.pallas_call(
+        left, rest, *sent = pl.pallas_call(
             choose_kernel,
-            out_shape=[shape(size, lanes + half), shape(size, right_lanes + half)],
+            out_shape=[shape(size, lanes + half), shape(size, right_lanes + half)]
+            + face_shapes(counts[0], (ncon, width)),
             in_specs=vmem_specs(4),
-            out_specs=vmem_specs(2),
+            out_specs=vmem_specs(2 + face_arrays(counts[0])),
             compiler_params=params(8),
         )(flags, payload, other, product)
         left_moved = lax.ppermute(left, "gy", chip_x)
         rest_moved = lax.ppermute(rest, "gz", chip_y)
-        spread = spread_of(left)
+        theirs = exchange(sent, AXES[0])
         left_last, rest_last = pl.pallas_call(
             add_kernel,
             out_shape=[shape(size, lanes + half), shape(size, right_lanes)],
-            in_specs=vmem_specs(5) + [anywhere],
+            in_specs=vmem_specs(5) + [anywhere] * len(theirs),
             out_specs=vmem_specs(2),
             compiler_params=params(8),
-        )(left, left_moved, rest, rest_moved, product, spread)
+        )(left, left_moved, rest, rest_moved, product, *theirs)
         left_other = lax.ppermute(left_last, "gz", chip_y)
         rest_other = lax.ppermute(rest_last, "gy", chip_x)
-        answer = solve([left_last, left_other], [rest_last, rest_other])
+        spread = spread_of(
+            left_last, theirs, lanes + right_lanes, other, left_moved, rest_moved
+        )
+        answer = solve([left_last, left_other], [rest_last, rest_other], spread)
         there = lax.ppermute(answer, "gy", core_swap)
         *sent, mine = pl.pallas_call(
             functools.partial(rows_kernel, ncon),
@@ -794,12 +770,10 @@
         )(flags, answer, there)
         across = exchange(sent, AXES[0])
         correction = pl.pallas_call(
-            functools.partial(last_near_kernel, faces, columns),
-            in_specs=vmem_specs(10),
+            functools.partial(last_near_kernel, faces),
+            in_specs=vmem_specs(8),
             **result,
-        )(
-            flags, product, *inverses, other, left_moved, rest_moved, left_other, answer, there
-        )
+        )(flags, product, *inverses, left_other, spread, answer, there)
     else:
         y, z = lax.axis_index("gy"), lax.axis_index("gz")
         member_of = group_of[y * planes + z]
@@ -807,8 +781,7 @@
         part = payload[:, : lanes + right_lanes]
         total = lax.psum(jnp.where(chosen[:, None, None], part[None], 0.0), ("gy", "gz"))
         total = lax.dynamic_index_in_dim(total, member_of, 0, keepdims=False)
-        spread = spread_of(payload)
-        answer = solve([total[:, :lanes]], [total[:, lanes:]])
+        answer = solve([total[:, :lanes]], [total[:, lanes:]], product)
 
         def from_near(faces_of, axis):
             even, odd = faces_of
@@ -823,6 +796,7 @@
             near += from_near(parts[2:4], AXES[1]) + from_near(parts[4:6], AXES[2])
         mine = answer[:size]
         across = from_near(blocks[:2], AXES[0])
+        spread = spread_of(payload, from_near(product[:2], AXES[0]), 0)
         correction = pl.pallas_call(
             functools.partial(last_plain_kernel, faces),
             in_specs=vmem_specs(4 + len(near)),

time: 54.7 us -> 57.9 us (1.059)
  waiting for transfers between devices: 8.53 us -> 13.1 us
  Pallas kernels: 30.2 us -> 27.5 us
  starting transfers between devices: 15.5 us -> 16.8 us
    ppermute x3 -> x4, waiting for transfers between devices: 1.36 us -> 5.64 us  [exchange(): lax.ppermute(arrays[0], axis, outer_pairs(axis))]
    pallas_call x5, Pallas kernels: 18.9 us -> 15.9 us  [the longest x1 8.9 us: per_device(): pl.pallas_call(functools.partial(main_kernel, (AXES[0], AXES[2]), early,...]
    ppermute x3 -> x4, starting transfers between devices: 5.95 us -> 8.67 us  [exchange(): lax.ppermute(arrays[0], axis, outer_pairs(axis))]
    ppermute x1, waiting for transfers between devices: 0.01 us -> 1.79 us  [per_device(): left_other = lax.ppermute(left_last, 'gz', chip_y)]
    ppermute x1, starting transfers between devices: 3.03 us -> 1.52 us  [exchange(): return [lax.ppermute(arrays[0], axis, flipped(axis, 1))]]
    ppermute x1, waiting for transfers between devices: 3.13 us -> 1.98 us  [per_device(): rest_other = lax.ppermute(rest_last, 'gy', chip_x)]
    ppermute x3 -> x4, starting transfers between devices: 1.24 us -> 2.31 us  [exchange(): lax.ppermute(arrays[1], axis, flipped(axis, 1))]
    ppermute x1, starting transfers between devices: 1.58 us -> 0.51 us  [per_device(): left_other = lax.ppermute(left_last, 'gz', chip_y)]
  transfers between devices with their start and end apart: 13 -> 15, of which waited for: 8 -> 8; matrix products, arithmetic and copies ran while one was open for 0% -> 0% of each run, Pallas kernels for 20% -> 14%
where the time goes in v7:
time: 57.9 us; the launch traced here: 57.7 us
  Pallas kernels  27.5 us (47%)
  starting transfers between devices  16.8 us (29%)
  waiting for transfers between devices  13.1 us (23%)
    pallas_call x1, Pallas kernels, per_device(): pl.pallas_call(functools.partial(main_kernel, (AXES[0], AXES[2]), early,...  8.9 us
    ppermute x4, starting transfers between devices, exchange(): lax.ppermute(arrays[0], axis, outer_pairs(axis))  8.67 us
    pallas_call x1, Pallas kernels, solve(): pl.pallas_call(functools.partial(solve_kernel, size, len(matrices), colum...  7.74 us
    ppermute x4, waiting for transfers between devices, exchange(): lax.ppermute(arrays[0], axis, outer_pairs(axis))  5.64 us
    pallas_call x1, Pallas kernels, per_device(): pl.pallas_call(functools.partial(early_kernel, AXES[1:2], early), out_sha...  3.45 us
    pallas_call x1, Pallas kernels, per_device(): pl.pallas_call(functools.partial(halves_kernel, planes), out_shape=[halve...  2.7 us
    ppermute x4, starting transfers between devices, exchange(): lax.ppermute(arrays[1], axis, flipped(axis, 1))  2.31 us
    ppermute x1, waiting for transfers between devices, per_device(): rest_other = lax.ppermute(rest_last, 'gy', chip_x)  1.98 us
  transfers between devices with their start and end apart: 15, of which 8 were waited for; matrix products, arithmetic and copies ran while one was open for 0% of the time, Pallas kernels for 14%

profile of v7, /device:TPU:0, one launch (start us, length us, event | category | flops | bytes accessed | tf_op | source)
XLA Modules:
  0.0 57.7 jit_solution(6507281515154140534)
XLA Ops:
  0.0 0.0 copy-start
  0.0 1.5 %shard_map.46 = (f32[264,128]{1,0:T(8,128)S(1)}, f32[264,128]{1,0:T(8,128)S(1)}, f32[264,128]{1,0:T(8,128)S(1)}, f32[264,128]{1,0:T(8,128)S(1)}, f32[2,264,128]{2,1,0:T(8,128)S(1)}, /*index=5*/f32[6,256,256]{2,1,0:T(8,128)S(1)}) custom-call(f32[1536,1536]{1,0:T(8,128)} %bitcast.9), custom_call_target="tpu_custom_call" | custom-call | tf_op jit(solution)/shard_map/pallas_call | solution.py:656
  1.5 5.1 %collective-permute-start = (f32[264,128]{1,0:T(8,128)S(1)}, f32[264,128]{1,0:T(8,128)S(1)}, u32[]{:S(2)}, u32[]{:S(2)}) collective-permute-start(f32[264,128]{1,0:T(8,128)S(1)} %get-tuple-element.30), channel_id=1, source_target_pairs={{0,24},{8,16},{16,8},{24,0},{1,25},{9,17},{17,9},{25,1},{2,26},{10... | collective-permute-start | bytes 405512 | tf_op jit(solution)/shard_map/ppermute | solution.py:77
  6.6 0.0 collective-permute-start.1
  6.6 0.7 %collective-permute-start.3 = (f32[264,128]{1,0:T(8,128)S(1)}, f32[264,128]{1,0:T(8,128)S(1)}, u32[]{:S(2)}, u32[]{:S(2)}) collective-permute-start(f32[264,128]{1,0:T(8,128)S(1)} %get-tuple-element.35), channel_id=1, source_target_pairs={{0,6},{2,4},{4,2},{6,0},{1,7},{3,5},{5,3},{7,1},{8,14},{10,12},{12... | collective-permute-start | bytes 405512 | tf_op jit(solution)/shard_map/ppermute | solution.py:77
  7.2 1.0 %collective-permute-start.4 = (f32[264,128]{1,0:T(8,128)S(1)}, f32[264,128]{1,0:T(8,128)S(1)}, u32[]{:S(2)}, u32[]{:S(2)}) collective-permute-start(f32[264,128]{1,0:T(8,128)S(1)} %get-tuple-element.36), channel_id=1, source_target_pairs={{0,2},{2,0},{4,6},{6,4},{1,3},{3,1},{5,7},{7,5},{8,10},{10,8},{12,... | collective-permute-start | bytes 405512 | tf_op jit(solution)/shard_map/ppermute | solution.py:78
  8.2 1.5 %collective-permute-start.2 = (f32[2,264,128]{2,1,0:T(8,128)S(1)}, f32[2,264,128]{2,1,0:T(8,128)S(1)}, u32[]{:S(2)}, u32[]{:S(2)}) collective-permute-start(f32[2,264,128]{2,1,0:T(8,128)S(1)} %get-tuple-element.32), channel_id=1, source_target_pairs={{0,1},{1,0},{2,3},{3,2},{4,5},{5,4},{6,7},{7,6},{8,9},{9,8},{10,11... | collective-permute-start | bytes 811016 | tf_op jit(solution)/shard_map/ppermute | solution.py:75
  9.7 0.0 copy-done
  9.7 0.0 copy-start.2
  9.7 2.7 %shard_map.47 = (bf16[6,2,256,256]{3,2,1,0:T(8,128)(2,1)S(1)}, bf16[15,2,256,256]{3,2,1,0:T(8,128)(2,1)S(1)}, f32[8,128]{1,0:T(8,128)S(1)}) custom-call(f32[1536,1536]{1,0:T(8,128)} %bitcast.10, s32[8]{0:T(128)S(1)} %copy-done, f32[6,256,256]{2,1,0:T(8,128)S(1)} %get-tuple-element.28.own_ref.refs_2_.refs_3_), custom_call_target="tpu_custom_call" | custom-call | flops 2000000000 | bytes 1048576 | tf_op jit(solution)/shard_map/pallas_call | solution.py:670
  12.4 0.0 copy-start.1
  12.4 0.0 collective-permute-done.3.refs_0_
  12.4 0.0 collective-permute-done.4.refs_1_
  12.5 0.0 copy-done.2
  12.5 3.5 %shard_map.48 = (f32[2,32,256]{2,1,0:T(8,128)S(1)}, bf16[2,2,256,256]{3,2,1,0:T(8,128)(2,1)}, bf16[2,2,256,256]{3,2,1,0:T(8,128)(2,1)S(1)}) custom-call(f32[264,128]{1,0:T(8,128)S(1)} %collective-permute-done.3.refs_0_, f32[264,128]{1,0:T(8,128)S(1)} %collective-permute-done.4.refs_1_, f32[6,256,256]{2,1,0:T(8,128)S(1)} %get-tuple-element.28.own_ref.refs_2_.refs_3_, ...), custom_call_target="tpu_custom_call" | custom-call | flops 2000000000 | bytes 1048576 | tf_op jit(solution)/shard_map/pallas_call | solution.py:683
  15.9 0.0 collective-permute-done.refs_0_
  15.9 0.0 collective-permute-done.1.refs_1_
  15.9 0.7 %collective-permute-done.2.refs_2_ = f32[2,264,128]{2,1,0:T(8,128)S(1)} collective-permute-done((f32[2,264,128]{2,1,0:T(8,128)S(1)}, f32[2,264,128]{2,1,0:T(8,128)S(1)}, u32[]{:S(2)}, u32[]{:S(2)}) %collective-permute-start.2) | collective-permute-done | bytes 270368 | tf_op jit(solution)/shard_map/ppermute | solution.py:75
  16.6 0.0 copy-done.1
  16.6 8.9 %shard_map.49 = (f32[64,1024]{1,0:T(8,128)S(1)}, f32[6,32,256]{2,1,0:T(8,128)S(1)}, bf16[4,2,256,256]{3,2,1,0:T(8,128)(2,1)}, bf16[4,2,256,256]{3,2,1,0:T(8,128)(2,1)S(1)}) custom-call(f32[264,128]{1,0:T(8,128)S(1)} %collective-permute-done.refs_0_, f32[264,128]{1,0:T(8,128)S(1)} %collective-permute-done.1.refs_1_, ...), custom_call_target="tpu_custom_call" | custom-call | flops 8000000000 | bytes 1048576 | tf_op jit(solution)/shard_map/pallas_call | solution.py:693
  25.5 0.1 collective-permute-start.5
  25.6 1.5 %collective-permute-done.5.there_ref.refs_2_ = f32[64,1024]{1,0:T(8,128)S(1)} collective-permute-done((f32[64,1024]{1,0:T(8,128)S(1)}, f32[64,1024]{1,0:T(8,128)S(1)}, u32[]{:S(2)}, u32[]{:S(2)}) %collective-permute-start.5) | collective-permute-done | bytes 262176 | tf_op jit(solution)/shard_map/ppermute | solution.py:738
  27.1 0.1 shard_map.50
  27.2 0.7 %collective-permute-start.6 = (f32[64,512]{1,0:T(8,128)S(1)}, f32[64,512]{1,0:T(8,128)S(1)}, u32[]{:S(2)}, u32[]{:S(2)}) collective-permute-start(f32[64,512]{1,0:T(8,128)S(1)} %get-tuple-element.40.first_ref), channel_id=1, source_target_pairs={{0,4},{2,6},{4,0},{6,2},{1,5},{3,7},{5,1},{7,3},{8,12},{10,14},{12... | collective-permute-start | bytes 393224 | tf_op jit(solution)/shard_map/ppermute | solution.py:747
  27.8 1.5 %collective-permute-start.7 = (f32[64,512]{1,0:T(8,128)S(1)}, f32[64,512]{1,0:T(8,128)S(1)}, u32[]{:S(2)}, u32[]{:S(2)}) collective-permute-start(f32[64,512]{1,0:T(8,128)S(1)} %get-tuple-element.41.third_ref), channel_id=1, source_target_pairs={{0,1},{1,0},{2,3},{3,2},{4,5},{5,4},{6,7},{7,6},{8,9},{9,8},{10,11... | collective-permute-start | bytes 393224 | tf_op jit(solution)/shard_map/ppermute | solution.py:748
  29.4 0.8 %collective-permute-start.8 = (f32[32,256]{1,0:T(8,128)S(1)}, f32[32,256]{1,0:T(8,128)S(1)}, u32[]{:S(2)}, u32[]{:S(2)}) collective-permute-start(f32[32,256]{1,0:T(8,128)S(1)} %get-tuple-element.42), channel_id=1, source_target_pairs={{0,24},{8,16},{16,8},{24,0},{1,25},{9,17},{17,9},{25,1},{2,26},{10... | collective-permute-start | bytes 98312 | tf_op jit(solution)/shard_map/ppermute | solution.py:77
  30.2 1.1 %collective-permute-start.9 = (f32[32,256]{1,0:T(8,128)S(1)}, f32[32,256]{1,0:T(8,128)S(1)}, u32[]{:S(2)}, u32[]{:S(2)}) collective-permute-start(f32[32,256]{1,0:T(8,128)S(1)} %get-tuple-element.43), channel_id=1, source_target_pairs={{0,8},{8,0},{16,24},{24,16},{1,9},{9,1},{17,25},{25,17},{2,10},{10... | collective-permute-start | bytes 98312 | tf_op jit(solution)/shard_map/ppermute | solution.py:78
  31.3 3.7 %collective-permute-done.8.refs_0_ = f32[32,256]{1,0:T(8,128)S(1)} collective-permute-done((f32[32,256]{1,0:T(8,128)S(1)}, f32[32,256]{1,0:T(8,128)S(1)}, u32[]{:S(2)}, u32[]{:S(2)}) %collective-permute-start.8) | collective-permute-done | bytes 32800 | tf_op jit(solution)/shard_map/ppermute | solution.py:77
  35.1 0.0 collective-permute-done.9.refs_1_
  35.1 0.0 collective-permute-done.6.second_ref.refs_3_
  35.1 0.0 collective-permute-done.7.fourth_ref.refs_4_
  35.1 1.5 %collective-permute-start.11 = (f32[64,384]{1,0:T(8,128)S(1)}, f32[64,384]{1,0:T(8,128)S(1)}, u32[]{:S(2)}, u32[]{:S(2)}) collective-permute-start(f32[64,384]{1,0:T(8,128)S(1)} %get-tuple-element.47.refs_2_), channel_id=1, source_target_pairs={{0,4},{2,6},{4,0},{6,2},{1,5},{3,7},{5,1},{7,3},{8,12},{10,14},{12... | collective-permute-start | bytes 294920 | tf_op jit(solution)/shard_map/ppermute | solution.py:758
  36.6 0.5 collective-permute-start.10
  37.1 0.7 %shard_map.52.refs_4_.spread_ref = bf16[5,256,192]{2,1,0:T(8,128)(2,1)S(1)} custom-call(f32[64,512]{1,0:T(8,128)S(1)} %get-tuple-element.44.unread.refs_0_, f32[6,32,256]{2,1,0:T(8,128)S(1)} %get-tuple-element.39.product_ref, bf16[2,2,256,256]{3,2,1,0:T(8,128)(2,1)S(1)} %get-tuple-element.45.early_inverse, ...), custom_call_target="tpu_custom_call" | custom-call | flops 3000000000 | bytes 1048576 | tf_op jit(solution)/shard_map/pallas_call | solution.py:706
  37.8 2.0 %collective-permute-done.11.refs_3_ = f32[64,384]{1,0:T(8,128)S(1)} collective-permute-done((f32[64,384]{1,0:T(8,128)S(1)}, f32[64,384]{1,0:T(8,128)S(1)}, u32[]{:S(2)}, u32[]{:S(2)}) %collective-permute-start.11) | collective-permute-done | bytes 98336 | tf_op jit(solution)/shard_map/ppermute | solution.py:758
  39.8 1.8 %collective-permute-done.10.refs_1_.matrix_ref = f32[64,512]{1,0:T(8,128)S(1)} collective-permute-done((f32[64,512]{1,0:T(8,128)S(1)}, f32[64,512]{1,0:T(8,128)S(1)}, u32[]{:S(2)}, u32[]{:S(2)}) %collective-permute-start.10) | collective-permute-done | bytes 131104 | tf_op jit(solution)/shard_map/ppermute | solution.py:757
  41.6 7.7 %shard_map.53.here_ref.refs_0_ = f32[192,128]{1,0:T(8,128)S(1)} custom-call(f32[64,512]{1,0:T(8,128)S(1)} %get-tuple-element.44.unread.refs_0_, f32[64,512]{1,0:T(8,128)S(1)} %collective-permute-done.10.refs_1_.matrix_ref, f32[64,384]{1,0:T(8,128)S(1)} %get-tuple-element.47.refs_2_, f32[64,384]{1,0:T(8,128)S(1)} %collective-permute-done.11.refs_3_, ...), custom_call_target="tpu_custom_call" | custom-call | flops 7000000000 | bytes 1048576 | tf_op jit(solution)/shard_map/pallas_call | solution.py:716
  49.4 0.1 collective-permute-start.12
  49.4 1.3 %collective-permute-done.12.there_ref.refs_1_ = f32[192,128]{1,0:T(8,128)S(1)} collective-permute-done((f32[192,128]{1,0:T(8,128)S(1)}, f32[192,128]{1,0:T(8,128)S(1)}, u32[]{:S(2)}, u32[]{:S(2)}) %collective-permute-start.12) | collective-permute-done | bytes 98336 | tf_op jit(solution)/shard_map/ppermute | solution.py:763
  50.8 2.1 %collective-permute-start.13 = (f32[32,128]{1,0:T(8,128)S(1)}, f32[32,128]{1,0:T(8,128)S(1)}, u32[]{:S(2)}, u32[]{:S(2)}) collective-permute-start(f32[32,128]{1,0:T(8,128)S(1)} %get-tuple-element.49), channel_id=1, source_target_pairs={{0,24},{8,16},{16,8},{24,0},{1,25},{9,17},{17,9},{25,1},{2,26},{10... | collective-permute-start | bytes 49160 | tf_op jit(solution)/shard_map/ppermute | solution.py:77
  52.8 0.2 collective-permute-start.14
  53.1 1.4 %shard_map.55.refs_2_ = f32[1536,128]{1,0:T(8,128)} custom-call(f32[8,128]{1,0:T(8,128)S(1)} %get-tuple-element.29.flag_ref, f32[6,32,256]{2,1,0:T(8,128)S(1)} %get-tuple-element.39.product_ref, bf16[2,2,256,256]{3,2,1,0:T(8,128)(2,1)S(1)} %get-tuple-element.45.early_inverse, bf16[4,2,256,256]{3,2,1,0:T(8,128)(2,1)S(1)} %get-tuple-element.46.late_inverse, ...), custom_call_target="tpu_custom_call" | custom-call | flops 1000000000 | bytes 1048576 | tf_op jit(solution)/shard_map/pallas_call | solution.py:772
  54.5 1.9 %collective-permute-done.13.refs_0_ = f32[32,128]{1,0:T(8,128)S(1)} collective-permute-done((f32[32,128]{1,0:T(8,128)S(1)}, f32[32,128]{1,0:T(8,128)S(1)}, u32[]{:S(2)}, u32[]{:S(2)}) %collective-permute-start.13) | collective-permute-done | bytes 16416 | tf_op jit(solution)/shard_map/ppermute | solution.py:77
  56.4 0.2 collective-permute-done.14.refs_1_
  56.6 1.0 %shard_map.56 = f32[1536,128]{1,0:T(8,128)} custom-call(bf16[5,256,192]{2,1,0:T(8,128)(2,1)S(1)} %shard_map.52.refs_4_.spread_ref, f32[64,128]{1,0:T(8,128)S(1)} %get-tuple-element.48.rows_ref, f32[32,128]{1,0:T(8,128)S(1)} %collective-permute-done.13.refs_0_, f32[32,128]{1,0:T(8,128)S(1)} %collective-permute-done.14.refs_1_, ...), custom_call_target="tpu_custom_call", output_to_operand_aliasing={{}: (4, {})} | custom-call | flops 1000000000 | bytes 1048576 | tf_op jit(solution)/shard_map/pallas_call | solution.py:805
  (2 shorter events, 0.1 us)
Async XLA Ops:
  0.0 9.7 %copy-start = (s32[8]{0:T(128)S(1)}, s32[8]{0:T(128)}, u32[]{:S(2)}) copy-start(s32[8]{0:T(128)} %group_ref.1) | copy-start | bytes 100
  1.5 14.5 %collective-permute-start = (f32[264,128]{1,0:T(8,128)S(1)}, f32[264,128]{1,0:T(8,128)S(1)}, u32[]{:S(2)}, u32[]{:S(2)}) collective-permute-start(f32[264,128]{1,0:T(8,128)S(1)} %get-tuple-element.30), channel_id=1, source_target_pairs={{0,24},{8,16},{16,8},{24,0},{1,25},{9,17},{17,9},{25,1},{2,26},{10... | collective-permute-start | bytes 405512 | tf_op jit(solution)/shard_map/ppermute | solution.py:77
  6.6 9.3 %collective-permute-start.1 = (f32[264,128]{1,0:T(8,128)S(1)}, f32[264,128]{1,0:T(8,128)S(1)}, u32[]{:S(2)}, u32[]{:S(2)}) collective-permute-start(f32[264,128]{1,0:T(8,128)S(1)} %get-tuple-element.31), channel_id=1, source_target_pairs={{0,8},{8,0},{16,24},{24,16},{1,9},{9,1},{17,25},{25,17},{2,10},{10... | collective-permute-start | bytes 405512 | tf_op jit(solution)/shard_map/ppermute | solution.py:78
  6.6 5.9 %collective-permute-start.3 = (f32[264,128]{1,0:T(8,128)S(1)}, f32[264,128]{1,0:T(8,128)S(1)}, u32[]{:S(2)}, u32[]{:S(2)}) collective-permute-start(f32[264,128]{1,0:T(8,128)S(1)} %get-tuple-element.35), channel_id=1, source_target_pairs={{0,6},{2,4},{4,2},{6,0},{1,7},{3,5},{5,3},{7,1},{8,14},{10,12},{12... | collective-permute-start | bytes 405512 | tf_op jit(solution)/shard_map/ppermute | solution.py:77
  7.2 5.2 %collective-permute-start.4 = (f32[264,128]{1,0:T(8,128)S(1)}, f32[264,128]{1,0:T(8,128)S(1)}, u32[]{:S(2)}, u32[]{:S(2)}) collective-permute-start(f32[264,128]{1,0:T(8,128)S(1)} %get-tuple-element.36), channel_id=1, source_target_pairs={{0,2},{2,0},{4,6},{6,4},{1,3},{3,1},{5,7},{7,5},{8,10},{10,8},{12,... | collective-permute-start | bytes 405512 | tf_op jit(solution)/shard_map/ppermute | solution.py:78
  8.2 8.4 %collective-permute-start.2 = (f32[2,264,128]{2,1,0:T(8,128)S(1)}, f32[2,264,128]{2,1,0:T(8,128)S(1)}, u32[]{:S(2)}, u32[]{:S(2)}) collective-permute-start(f32[2,264,128]{2,1,0:T(8,128)S(1)} %get-tuple-element.32), channel_id=1, source_target_pairs={{0,1},{1,0},{2,3},{3,2},{4,5},{5,4},{6,7},{7,6},{8,9},{9,8},{10,11... | collective-permute-start | bytes 811016 | tf_op jit(solution)/shard_map/ppermute | solution.py:75
  9.7 2.7 %copy-start.2 = (f32[1,1,1,6,256,32]{4,5,3,2,1,0:T(8,128)S(1)}, f32[1,1,1,6,256,32]{4,5,3,2,1,0:T(8,128)}, u32[]{:S(2)}) copy-start(f32[1,1,1,6,256,32]{4,5,3,2,1,0:T(8,128)} %param.5) | copy-start | bytes 589828
  12.4 4.2 %copy-start.1 = (f32[1,1,1,1536,128]{4,3,2,1,0:T(8,128)S(1)}, f32[1,1,1,1536,128]{4,3,2,1,0:T(8,128)}, u32[]{:S(2)}) copy-start(f32[1,1,1,1536,128]{4,3,2,1,0:T(8,128)} %param.6) | copy-start | bytes 2359300
  25.5 1.6 %collective-permute-start.5 = (f32[64,1024]{1,0:T(8,128)S(1)}, f32[64,1024]{1,0:T(8,128)S(1)}, u32[]{:S(2)}, u32[]{:S(2)}) collective-permute-start(f32[64,1024]{1,0:T(8,128)S(1)} %get-tuple-element.38.here_ref), channel_id=1, source_target_pairs={{0,2},{2,0},{4,6},{6,4},{1,3},{3,1},{5,7},{7,5},{8,10},{10,8},{12,... | collective-permute-start | bytes 786440 | tf_op jit(solution)/shard_map/ppermute | solution.py:738
  27.2 7.9 %collective-permute-start.6 = (f32[64,512]{1,0:T(8,128)S(1)}, f32[64,512]{1,0:T(8,128)S(1)}, u32[]{:S(2)}, u32[]{:S(2)}) collective-permute-start(f32[64,512]{1,0:T(8,128)S(1)} %get-tuple-element.40.first_ref), channel_id=1, source_target_pairs={{0,4},{2,6},{4,0},{6,2},{1,5},{3,7},{5,1},{7,3},{8,12},{10,14},{12... | collective-permute-start | bytes 393224 | tf_op jit(solution)/shard_map/ppermute | solution.py:747
  27.8 7.2 %collective-permute-start.7 = (f32[64,512]{1,0:T(8,128)S(1)}, f32[64,512]{1,0:T(8,128)S(1)}, u32[]{:S(2)}, u32[]{:S(2)}) collective-permute-start(f32[64,512]{1,0:T(8,128)S(1)} %get-tuple-element.41.third_ref), channel_id=1, source_target_pairs={{0,1},{1,0},{2,3},{3,2},{4,5},{5,4},{6,7},{7,6},{8,9},{9,8},{10,11... | collective-permute-start | bytes 393224 | tf_op jit(solution)/shard_map/ppermute | solution.py:748
  29.4 5.7 %collective-permute-start.8 = (f32[32,256]{1,0:T(8,128)S(1)}, f32[32,256]{1,0:T(8,128)S(1)}, u32[]{:S(2)}, u32[]{:S(2)}) collective-permute-start(f32[32,256]{1,0:T(8,128)S(1)} %get-tuple-element.42), channel_id=1, source_target_pairs={{0,24},{8,16},{16,8},{24,0},{1,25},{9,17},{17,9},{25,1},{2,26},{10... | collective-permute-start | bytes 98312 | tf_op jit(solution)/shard_map/ppermute | solution.py:77
  30.2 4.9 %collective-permute-start.9 = (f32[32,256]{1,0:T(8,128)S(1)}, f32[32,256]{1,0:T(8,128)S(1)}, u32[]{:S(2)}, u32[]{:S(2)}) collective-permute-start(f32[32,256]{1,0:T(8,128)S(1)} %get-tuple-element.43), channel_id=1, source_target_pairs={{0,8},{8,0},{16,24},{24,16},{1,9},{9,1},{17,25},{25,17},{2,10},{10... | collective-permute-start | bytes 98312 | tf_op jit(solution)/shard_map/ppermute | solution.py:78
  35.1 4.7 %collective-permute-start.11 = (f32[64,384]{1,0:T(8,128)S(1)}, f32[64,384]{1,0:T(8,128)S(1)}, u32[]{:S(2)}, u32[]{:S(2)}) collective-permute-start(f32[64,384]{1,0:T(8,128)S(1)} %get-tuple-element.47.refs_2_), channel_id=1, source_target_pairs={{0,4},{2,6},{4,0},{6,2},{1,5},{3,7},{5,1},{7,3},{8,12},{10,14},{12... | collective-permute-start | bytes 294920 | tf_op jit(solution)/shard_map/ppermute | solution.py:758
  36.6 5.0 %collective-permute-start.10 = (f32[64,512]{1,0:T(8,128)S(1)}, f32[64,512]{1,0:T(8,128)S(1)}, u32[]{:S(2)}, u32[]{:S(2)}) collective-permute-start(f32[64,512]{1,0:T(8,128)S(1)} %get-tuple-element.44.unread.refs_0_), channel_id=1, source_target_pairs={{0,1},{1,0},{2,3},{3,2},{4,5},{5,4},{6,7},{7,6},{8,9},{9,8},{10,11... | collective-permute-start | bytes 393224 | tf_op jit(solution)/shard_map/ppermute | solution.py:757
  49.4 1.4 %collective-permute-start.12 = (f32[192,128]{1,0:T(8,128)S(1)}, f32[192,128]{1,0:T(8,128)S(1)}, u32[]{:S(2)}, u32[]{:S(2)}) collective-permute-start(f32[192,128]{1,0:T(8,128)S(1)} %shard_map.53.here_ref.refs_0_), channel_id=1, source_target_pairs={{0,2},{2,0},{4,6},{6,4},{1,3},{3,1},{5,7},{7,5},{8,10},{10,8},{12,... | collective-permute-start | bytes 294920 | tf_op jit(solution)/shard_map/ppermute | solution.py:763
  50.8 5.6 %collective-permute-start.13 = (f32[32,128]{1,0:T(8,128)S(1)}, f32[32,128]{1,0:T(8,128)S(1)}, u32[]{:S(2)}, u32[]{:S(2)}) collective-permute-start(f32[32,128]{1,0:T(8,128)S(1)} %get-tuple-element.49), channel_id=1, source_target_pairs={{0,24},{8,16},{16,8},{24,0},{1,25},{9,17},{17,9},{25,1},{2,26},{10... | collective-permute-start | bytes 49160 | tf_op jit(solution)/shard_map/ppermute | solution.py:77
  52.8 3.7 %collective-permute-start.14 = (f32[32,128]{1,0:T(8,128)S(1)}, f32[32,128]{1,0:T(8,128)S(1)}, u32[]{:S(2)}, u32[]{:S(2)}) collective-permute-start(f32[32,128]{1,0:T(8,128)S(1)} %get-tuple-element.50), channel_id=1, source_target_pairs={{0,8},{8,0},{16,24},{24,16},{1,9},{9,1},{17,25},{25,17},{2,10},{10... | collective-permute-start | bytes 49160 | tf_op jit(solution)/shard_map/ppermute | solution.py:78

commit v8 on v7

--- a/solution.py
+++ b/solution.py
@@ -74,8 +74,8 @@
     if lax.axis_size(axis) == 2:
         return [lax.ppermute(arrays[0], axis, flipped(axis, 1))]
     return [
-        lax.ppermute(arrays[0], axis, outer_pairs(axis)),
-        lax.ppermute(arrays[1], axis, flipped(axis, 1)),
+        lax.ppermute(arrays[0], axis, flipped(axis, 1)),
+        lax.ppermute(arrays[1], axis, outer_pairs(axis)),
     ]
 
 
@@ -89,8 +89,8 @@
         refs[0][1] = odd
     else:
         upward = is_even(axis)
-        refs[0][...] = jnp.where(upward, even, odd)
-        refs[1][...] = jnp.where(upward, odd, even)
+        refs[0][...] = jnp.where(upward, odd, even)
+        refs[1][...] = jnp.where(upward, even, odd)
 
 
 def receive(refs, axis):
@@ -98,7 +98,7 @@
         return refs[0][1], refs[0][0]
     upward = is_even(axis)
     first, second = refs[0][...], refs[1][...]
-    return jnp.where(upward, first, second), jnp.where(upward, second, first)
+    return jnp.where(upward, second, first), jnp.where(upward, first, second)
 
 
 def face_shapes(count, shape):
@@ -261,14 +261,14 @@
             store(upper_out, upper_index(f, g), upper_ref[f, :, g * width : (g + 1) * width])
 
 
-def begin(packed, owns, partner_out, sum_ref):
+def begin(packed, owns, partner_ref, sum_ref):
     width = owns[0].shape[1]
     eye = iota((width, width), 0) == iota((width, width), 1)
     guesses = []
     for f in range(len(packed)):
         partner = unpack(packed[f])
         total = owns[f] + partner
-        store(partner_out, f, partner)
+        store(partner_ref, f, partner)
         store(sum_ref, f, total)
         diagonal = jnp.where(eye, total, 0.0)
         across = 1.0 / jnp.sum(diagonal, axis=0, keepdims=True)
@@ -299,7 +299,7 @@
 def early_kernel(axes, faces, *refs):
     arrays = len(refs) - 7
     inputs = refs[:arrays]
-    own_ref, halves_ref, starts_ref, basis_out, partner_out, inverse_out, sum_ref = refs[arrays:]
+    own_ref, halves_ref, starts_ref, basis_out, inverse_out, partner_ref, sum_ref = refs[arrays:]
     count = len(faces)
     packed = []
     done = 0
@@ -307,14 +307,14 @@
         number = face_arrays(lax.axis_size(axis))
         packed += receive(inputs[done : done + number], axis)
         done += number
-    guesses = begin(packed, [own_ref[f] for f in faces], partner_out, sum_ref)
+    guesses = begin(packed, [own_ref[f] for f in faces], partner_ref, sum_ref)
     for sweep in range(NS_ITERS - 1):
         guesses = newton(guesses, sum_ref)
     for i in range(count):
         store(inverse_out, i, guesses[i])
     basis = [starts_ref[f] for f in faces]
     matrices = [
-        [load(partner_out, i) for i in range(count)],
+        [load(partner_ref, i) for i in range(count)],
         [load(inverse_out, i) for i in range(count)],
         [load(halves_ref, f) for f in faces],
     ]
@@ -328,7 +328,7 @@
     arrays = len(refs) - 11
     inputs = refs[:arrays]
     own_ref, halves_ref, upper_ref, starts_ref, resid_ref, early_basis = refs[arrays : arrays + 6]
-    payload_ref, product_ref, partner_out, inverse_out, sum_ref = refs[arrays + 6 :]
+    payload_ref, product_ref, inverse_out, partner_ref, sum_ref = refs[arrays + 6 :]
     ncon, width = starts_ref.shape[1:]
     columns = resid_ref.shape[1]
     sides = {}
@@ -353,7 +353,7 @@
         number = face_arrays(lax.axis_size(axis))
         packed += receive(inputs[done : done + number], axis)
         done += number
-    guesses = begin(packed, [own_ref[f] for f in late], partner_out, sum_ref)
+    guesses = begin(packed, [own_ref[f] for f in late], partner_ref, sum_ref)
     pending = [(f, early_basis[i]) for i, f in enumerate(early)]
     for sweep in range(NS_ITERS - 1):
         guesses = newton(guesses, sum_ref)
@@ -363,7 +363,7 @@
         store(inverse_out, i, guesses[i])
     basis = [starts_ref[f] for f in late]
     matrices = [
-        [load(partner_out, i) for i in range(count)],
+        [load(partner_ref, i) for i in range(count)],
         [load(inverse_out, i) for i in range(count)],
         [load(halves_ref, f) for f in late],
     ]
@@ -435,20 +435,20 @@
     return jnp.where(upward, outer, inner), jnp.where(upward, inner, outer)
 
 
-def spread_kernel(faces, start, unread, product_ref, early_inverse, late_inverse, *refs):
-    out_ref = refs[-1]
+def spread_kernel(faces, start, unread, *refs):
+    product_ref, early_inverse, late_inverse, there_ref, matrix_ref, right_ref, out_ref = refs
     inverses = (early_inverse, late_inverse)
-    ready = refs[:-1]
-    if start:
-        ready, (there_ref, matrix_ref, right_ref) = refs[:-4], refs[-4:-1]
-    theirs = list(receive(ready, AXES[0]))
-    if start:
-        theirs += their_y_products(there_ref, matrix_ref, start)
-        half = product_ref.shape[2] // 2
-        theirs.append(unfold(right_ref[:, right_ref.shape[1] - half :]))
-    for i, product in enumerate(theirs):
-        f = i if i < 4 else FACES - 1
-        out_ref[i] = spread_pair(product_ref[f], product, find(faces, inverses, f))
+    half = product_ref.shape[2] // 2
+    theirs = list(their_y_products(there_ref, matrix_ref, start))
+    theirs.append(unfold(right_ref[:, right_ref.shape[1] - half :]))
+    for i, f in enumerate((2, 3, FACES - 1)):
+        out_ref[i] = spread_pair(product_ref[f], theirs[i], find(faces, inverses, f))
+
+
+def far_spread(faces, product_ref, inverses, inputs, out_ref):
+    theirs = receive(inputs, AXES[0])
+    for f in range(2):
+        out_ref[f] = spread_pair(product_ref[f], theirs[f], find(faces, inverses, f))
 
 
 def choose_kernel(flag_ref, here_ref, there_ref, product_ref, matrix_ref, right_ref, *sent):
@@ -561,7 +561,9 @@
 
 
 def last_plain_kernel(faces, product_ref, early_inverse, late_inverse, answer_ref, *refs):
-    inputs, rest = refs[:-3], refs[-3:]
+    number = face_arrays(lax.axis_size(AXES[0]))
+    inputs, rest = refs[number:-4], (refs[-4], *refs[-2:])
+    far_spread(faces, product_ref, (early_inverse, late_inverse), refs[:number], refs[-3])
     ncon, width = product_ref.shape[1:]
     values = {}
     done = 0
@@ -586,6 +588,8 @@
     faces, flag_ref, product_ref, early_inverse, late_inverse, matrix_ref, spread_ref, *refs
 ):
     here_answer, there_answer = refs[:2]
+    inverses = (early_inverse, late_inverse)
+    far_spread(faces, product_ref, inverses, refs[2:-4], refs[-3])
     ncon, width = product_ref.shape[1:]
     half = width // 2
 
@@ -597,17 +601,17 @@
     values = {}
     for f in (2, 3, 5):
         values[f] = functools.partial(
-            last_product, spread_ref[min(f, 4)], answer(0, f), answer(f, f ^ 1)
+            last_product, spread_ref[min(f - 2, 2)], answer(0, f), answer(f, f ^ 1)
         )
     values[4] = functools.partial(
         through,
-        find(faces, (early_inverse, late_inverse), 4),
+        find(faces, inverses, 4),
         product_ref[4],
         unfold(matrix_ref[:, matrix_ref.shape[1] - half :]),
         answer(0, 4),
         answer(4, 5),
     )
-    last_faces(values, width, *refs[2:])
+    last_faces(values, width, refs[-4], *refs[-2:])
 
 
 def last_far_kernel(ncon, spread_ref, rows_ref, *refs):
@@ -680,51 +684,43 @@
         cost_estimate=cost(2),
     )(matrix, group_of, own)
 
-    early_basis, early_partner, early_inverse = pl.pallas_call(
+    early_basis, early_inverse = pl.pallas_call(
         functools.partial(early_kernel, AXES[1:2], early),
-        out_shape=[shape(len(early), ncon, width)] + [halves(len(early))] * 2,
+        out_shape=[shape(len(early), ncon, width), halves(len(early))],
         in_specs=vmem_specs(len(got[1]) + 3),
-        out_specs=vmem_specs(3),
-        scratch_shapes=[pltpu.VMEM((len(early), 2, width, width), jnp.bfloat16)],
+        out_specs=vmem_specs(2),
+        scratch_shapes=[pltpu.VMEM((len(early), 2, width, width), jnp.bfloat16)] * 2,
         compiler_params=params(16),
         cost_estimate=cost(2),
     )(*got[1], own, own_halves, starts)
 
-    payload, product, late_partner, late_inverse = pl.pallas_call(
+    payload, product, late_inverse = pl.pallas_call(
         functools.partial(main_kernel, (AXES[0], AXES[2]), early, late),
-        out_shape=[shape(size, lanes + right_lanes + 2 * half), shape(FACES, ncon, width)]
-        + [halves(len(late))] * 2,
+        out_shape=[
+            shape(size, lanes + right_lanes + 2 * half),
+            shape(FACES, ncon, width),
+            halves(len(late)),
+        ],
         in_specs=vmem_specs(len(got[0]) + len(got[2]) + 6),
-        out_specs=vmem_specs(4),
-        scratch_shapes=[pltpu.VMEM((len(late), 2, width, width), jnp.bfloat16)],
+        out_specs=vmem_specs(3),
+        scratch_shapes=[pltpu.VMEM((len(late), 2, width, width), jnp.bfloat16)] * 2,
         compiler_params=params(24),
         cost_estimate=cost(8),
     )(*got[0], *got[2], own, own_halves, upper_halves, starts, right, early_basis)
 
     inverses = [early_inverse, late_inverse]
-    def spread_of(token, theirs, start, *more):
-        return pl.pallas_call(
-            functools.partial(spread_kernel, faces, start),
-            out_shape=jax.ShapeDtypeStruct((5 if start else 2, width, 3 * size), jnp.bfloat16),
-            in_specs=[anywhere] + vmem_specs(3 + len(theirs) + len(more)),
-            out_specs=vmem_specs(1)[0],
-            compiler_params=params(16),
-            cost_estimate=cost(3),
-        )(token, product, *inverses, *theirs, *more)
-
     def solve(matrices, rights, unread):
         return pl.pallas_call(
             functools.partial(solve_kernel, size, len(matrices), columns),
             out_shape=shape(coarse, columns),
-            in_specs=vmem_specs(2 * len(matrices)) + [anywhere],
+            in_specs=vmem_specs(2 * len(matrices)) + [anywhere] * len(unread),
             out_specs=vmem_specs(1)[0],
             compiler_params=params(12),
             cost_estimate=cost(7),
-        )(*matrices, *rights, unread)
-
+        )(*matrices, *rights, *unread)
+
+    far_shape = jax.ShapeDtypeStruct((2, width, 3 * size), jnp.bfloat16)
     result = dict(
-        out_shape=shape(order, columns),
-        out_specs=main_memory,
         scratch_shapes=[
             pltpu.VMEM((order, columns), jnp.float32),
             pltpu.SemaphoreType.DMA((FACES,)),
@@ -750,16 +746,21 @@
         left_last, rest_last = pl.pallas_call(
             add_kernel,
             out_shape=[shape(size, lanes + half), shape(size, right_lanes)],
-            in_specs=vmem_specs(5) + [anywhere] * len(theirs),
+            in_specs=vmem_specs(5),
             out_specs=vmem_specs(2),
             compiler_params=params(8),
-        )(left, left_moved, rest, rest_moved, product, *theirs)
+        )(left, left_moved, rest, rest_moved, product)
         left_other = lax.ppermute(left_last, "gz", chip_y)
         rest_other = lax.ppermute(rest_last, "gy", chip_x)
-        spread = spread_of(
-            left_last, theirs, lanes + right_lanes, other, left_moved, rest_moved
-        )
-        answer = solve([left_last, left_other], [rest_last, rest_other], spread)
+        spread = pl.pallas_call(
+            functools.partial(spread_kernel, faces, lanes + right_lanes),
+            out_shape=jax.ShapeDtypeStruct((3, width, 3 * size), jnp.bfloat16),
+            in_specs=[anywhere] + vmem_specs(6),
+            out_specs=vmem_specs(1)[0],
+            compiler_params=params(16),
+            cost_estimate=cost(1),
+        )(left_last, product, *inverses, other, left_moved, rest_moved)
+        answer = solve([left_last, left_other], [rest_last, rest_other], [spread, *theirs])
         there = lax.ppermute(answer, "gy", core_swap)
         *sent, mine = pl.pallas_call(
             functools.partial(rows_kernel, ncon),
@@ -769,11 +770,13 @@
             compiler_params=params(8),
         )(flags, answer, there)
         across = exchange(sent, AXES[0])
-        correction = pl.pallas_call(
+        correction, spread = pl.pallas_call(
             functools.partial(last_near_kernel, faces),
-            in_specs=vmem_specs(8),
+            out_shape=[shape(order, columns), far_shape],
+            in_specs=vmem_specs(8 + len(theirs)),
+            out_specs=[main_memory] + vmem_specs(1),
             **result,
-        )(flags, product, *inverses, left_other, spread, answer, there)
+        )(flags, product, *inverses, left_other, spread, answer, there, *theirs)
     else:
         y, z = lax.axis_index("gy"), lax.axis_index("gz")
         member_of = group_of[y * planes + z]
@@ -781,14 +784,14 @@
         part = payload[:, : lanes + right_lanes]
         total = lax.psum(jnp.where(chosen[:, None, None], part[None], 0.0), ("gy", "gz"))
         total = lax.dynamic_index_in_dim(total, member_of, 0, keepdims=False)
-        answer = solve([total[:, :lanes]], [total[:, lanes:]], product)
+        answer = solve([total[:, :lanes]], [total[:, lanes:]], [])
 
         def from_near(faces_of, axis):
             even, odd = faces_of
             if lax.axis_size(axis) == 2:
                 return exchange([jnp.stack([even, odd])], axis)
             upward = is_even(axis)
-            return exchange([jnp.where(upward, even, odd), jnp.where(upward, odd, even)], axis)
+            return exchange([jnp.where(upward, odd, even), jnp.where(upward, even, odd)], axis)
 
         blocks = answer.reshape(FACES, ncon, columns)
         near = []
@@ -796,14 +799,18 @@
             near += from_near(parts[2:4], AXES[1]) + from_near(parts[4:6], AXES[2])
         mine = answer[:size]
         across = from_near(blocks[:2], AXES[0])
-        spread = spread_of(payload, from_near(product[:2], AXES[0]), 0)
-        correction = pl.pallas_call(
+        theirs = from_near(product[:2], AXES[0])
+        correction, spread = pl.pallas_call(
             functools.partial(last_plain_kernel, faces),
-            in_specs=vmem_specs(4 + len(near)),
+            out_shape=[shape(order, columns), far_shape],
+            in_specs=vmem_specs(4 + len(theirs) + len(near)),
+            out_specs=[main_memory] + vmem_specs(1),
             **result,
-        )(product, *inverses, answer, *near)
+        )(product, *inverses, answer, *theirs, *near)
     correction = pl.pallas_call(
         functools.partial(last_far_kernel, ncon),
+        out_shape=shape(order, columns),
+        out_specs=main_memory,
         in_specs=vmem_specs(2 + len(across)) + [main_memory],
         input_output_aliases={2 + len(across): 0},
         **result,

time: 57.9 us -> 59.1 us (1.021)
  waiting for transfers between devices: 13.1 us -> 15.3 us
  Pallas kernels: 27.5 us -> 26.7 us
    ppermute x1, waiting for transfers between devices: 0.01 us -> 3.49 us  [per_device(): left_moved = lax.ppermute(left, 'gy', chip_x)]
    ppermute x1, waiting for transfers between devices: 1.98 us -> 0.01 us  [per_device(): rest_other = lax.ppermute(rest_last, 'gy', chip_x)]
    ppermute x1, waiting for transfers between devices: 1.79 us -> 0.01 us  [per_device(): left_other = lax.ppermute(left_last, 'gz', chip_y)]
    ppermute x8, waiting for transfers between devices: 5.85 us -> 7.52 us  [the longest x4 4.18 us: exchange(): lax.ppermute(arrays[1], axis, outer_pairs(axis))]
    ppermute x8, starting transfers between devices: 11 us -> 9.78 us  [the longest x4 5.95 us: exchange(): lax.ppermute(arrays[1], axis, outer_pairs(axis))]
    ppermute x1, starting transfers between devices: 0.51 us -> 1.58 us  [per_device(): left_other = lax.ppermute(left_last, 'gz', chip_y)]
    pallas_call x1, Pallas kernels: 3.45 us -> 2.85 us  [per_device(): pl.pallas_call(functools.partial(early_kernel, AXES[1:2], early), out_sha...]
  transfers between devices with their start and end apart: 15 -> 15, of which waited for: 8 -> 9; matrix products, arithmetic and copies ran while one was open for 0% -> 0% of each run, Pallas kernels for 14% -> 13%
where the time goes in v8:
time: 59.1 us; the launch traced here: 58.9 us
  Pallas kernels  26.7 us (45%)
  starting transfers between devices  16.6 us (28%)
  waiting for transfers between devices  15.3 us (26%)
    pallas_call x1, Pallas kernels, per_device(): pl.pallas_call(functools.partial(main_kernel, (AXES[0], AXES[2]), early,...  8.87 us
    pallas_call x1, Pallas kernels, solve(): pl.pallas_call(functools.partial(solve_kernel, size, len(matrices), colum...  7.73 us
    ppermute x4, starting transfers between devices, exchange(): lax.ppermute(arrays[1], axis, outer_pairs(axis))  5.95 us
    ppermute x4, waiting for transfers between devices, exchange(): lax.ppermute(arrays[1], axis, outer_pairs(axis))  4.18 us
    ppermute x4, starting transfers between devices, exchange(): lax.ppermute(arrays[0], axis, flipped(axis, 1))  3.84 us
    ppermute x1, waiting for transfers between devices, per_device(): left_moved = lax.ppermute(left, 'gy', chip_x)  3.49 us
    ppermute x4, waiting for transfers between devices, exchange(): lax.ppermute(arrays[0], axis, flipped(axis, 1))  3.34 us
    pallas_call x1, Pallas kernels, per_device(): pl.pallas_call(functools.partial(early_kernel, AXES[1:2], early), out_sha...  2.85 us
  transfers between devices with their start and end apart: 15, of which 9 were waited for; matrix products, arithmetic and copies ran while one was open for 0% of the time, Pallas kernels for 13%

profile of v8, /device:TPU:0, one launch (start us, length us, event | category | flops | bytes accessed | tf_op | source)
XLA Modules:
  0.0 58.9 jit_solution(13129778796423705198)
XLA Ops:
  0.0 0.0 copy-start
  0.0 1.5 %shard_map.46 = (f32[264,128]{1,0:T(8,128)S(1)}, f32[264,128]{1,0:T(8,128)S(1)}, f32[264,128]{1,0:T(8,128)S(1)}, f32[264,128]{1,0:T(8,128)S(1)}, f32[2,264,128]{2,1,0:T(8,128)S(1)}, /*index=5*/f32[6,256,256]{2,1,0:T(8,128)S(1)}) custom-call(f32[1536,1536]{1,0:T(8,128)} %bitcast.9), custom_call_target="tpu_custom_call" | custom-call | tf_op jit(solution)/shard_map/pallas_call | solution.py:660
  1.5 3.1 %collective-permute-start = (f32[264,128]{1,0:T(8,128)S(1)}, f32[264,128]{1,0:T(8,128)S(1)}, u32[]{:S(2)}, u32[]{:S(2)}) collective-permute-start(f32[264,128]{1,0:T(8,128)S(1)} %get-tuple-element.32), channel_id=1, source_target_pairs={{0,8},{8,0},{16,24},{24,16},{1,9},{9,1},{17,25},{25,17},{2,10},{10... | collective-permute-start | bytes 405512 | tf_op jit(solution)/shard_map/ppermute | solution.py:77
  4.6 2.5 %collective-permute-start.1 = (f32[264,128]{1,0:T(8,128)S(1)}, f32[264,128]{1,0:T(8,128)S(1)}, u32[]{:S(2)}, u32[]{:S(2)}) collective-permute-start(f32[264,128]{1,0:T(8,128)S(1)} %get-tuple-element.33), channel_id=1, source_target_pairs={{0,24},{8,16},{16,8},{24,0},{1,25},{9,17},{17,9},{25,1},{2,26},{10... | collective-permute-start | bytes 405512 | tf_op jit(solution)/shard_map/ppermute | solution.py:78
  7.0 0.0 collective-permute-start.3
  7.0 1.6 %collective-permute-start.4 = (f32[264,128]{1,0:T(8,128)S(1)}, f32[264,128]{1,0:T(8,128)S(1)}, u32[]{:S(2)}, u32[]{:S(2)}) collective-permute-start(f32[264,128]{1,0:T(8,128)S(1)} %get-tuple-element.38), channel_id=1, source_target_pairs={{0,6},{2,4},{4,2},{6,0},{1,7},{3,5},{5,3},{7,1},{8,14},{10,12},{12... | collective-permute-start | bytes 405512 | tf_op jit(solution)/shard_map/ppermute | solution.py:78
  8.6 1.5 %collective-permute-start.2 = (f32[2,264,128]{2,1,0:T(8,128)S(1)}, f32[2,264,128]{2,1,0:T(8,128)S(1)}, u32[]{:S(2)}, u32[]{:S(2)}) collective-permute-start(f32[2,264,128]{2,1,0:T(8,128)S(1)} %get-tuple-element.34), channel_id=1, source_target_pairs={{0,1},{1,0},{2,3},{3,2},{4,5},{5,4},{6,7},{7,6},{8,9},{9,8},{10,11... | collective-permute-start | bytes 811016 | tf_op jit(solution)/shard_map/ppermute | solution.py:75
  10.2 0.0 copy-done
  10.2 0.0 copy-start.2
  10.2 2.7 %shard_map.47 = (bf16[6,2,256,256]{3,2,1,0:T(8,128)(2,1)S(1)}, bf16[15,2,256,256]{3,2,1,0:T(8,128)(2,1)S(1)}, f32[8,128]{1,0:T(8,128)S(1)}) custom-call(f32[1536,1536]{1,0:T(8,128)} %bitcast.10, s32[8]{0:T(128)S(1)} %copy-done, f32[6,256,256]{2,1,0:T(8,128)S(1)} %get-tuple-element.30.own_ref.refs_2_.refs_3_), custom_call_target="tpu_custom_call" | custom-call | flops 2000000000 | bytes 1048576 | tf_op jit(solution)/shard_map/pallas_call | solution.py:674
  12.9 0.0 copy-start.1
  12.9 0.0 collective-permute-done.3.refs_0_
  12.9 0.0 collective-permute-done.4.refs_1_
  12.9 0.0 copy-done.2
  12.9 2.9 %shard_map.48 = (f32[2,32,256]{2,1,0:T(8,128)S(1)}, bf16[2,2,256,256]{3,2,1,0:T(8,128)(2,1)S(1)}) custom-call(f32[264,128]{1,0:T(8,128)S(1)} %collective-permute-done.3.refs_0_, f32[264,128]{1,0:T(8,128)S(1)} %collective-permute-done.4.refs_1_, f32[6,256,256]{2,1,0:T(8,128)S(1)} %get-tuple-element.30.own_ref.refs_2_.refs_3_, ...), custom_call_target="tpu_custom_call" | custom-call | flops 2000000000 | bytes 1048576 | tf_op jit(solution)/shard_map/pallas_call | solution.py:687
  15.8 0.0 collective-permute-done.refs_0_
  15.8 0.0 collective-permute-done.1.refs_1_
  15.8 1.2 %collective-permute-done.2.refs_2_ = f32[2,264,128]{2,1,0:T(8,128)S(1)} collective-permute-done((f32[2,264,128]{2,1,0:T(8,128)S(1)}, f32[2,264,128]{2,1,0:T(8,128)S(1)}, u32[]{:S(2)}, u32[]{:S(2)}) %collective-permute-start.2) | collective-permute-done | bytes 270368 | tf_op jit(solution)/shard_map/ppermute | solution.py:75
  17.0 0.0 copy-done.1
  17.0 8.9 %shard_map.49 = (f32[64,1024]{1,0:T(8,128)S(1)}, f32[6,32,256]{2,1,0:T(8,128)S(1)}, bf16[4,2,256,256]{3,2,1,0:T(8,128)(2,1)S(1)}) custom-call(f32[264,128]{1,0:T(8,128)S(1)} %collective-permute-done.refs_0_, f32[264,128]{1,0:T(8,128)S(1)} %collective-permute-done.1.refs_1_, f32[2,264,128]{2,1,0:T(8,128)S(1)} %collective-permute-done.2.refs_2_, ...), custom_call_target="tpu_custom_call" | custom-call | flops 8000000000 | bytes 1048576 | tf_op jit(solution)/shard_map/pallas_call | solution.py:697
  25.9 0.1 collective-permute-start.5
  26.0 1.5 %collective-permute-done.5.there_ref.refs_3_ = f32[64,1024]{1,0:T(8,128)S(1)} collective-permute-done((f32[64,1024]{1,0:T(8,128)S(1)}, f32[64,1024]{1,0:T(8,128)S(1)}, u32[]{:S(2)}, u32[]{:S(2)}) %collective-permute-start.5) | collective-permute-done | bytes 262176 | tf_op jit(solution)/shard_map/ppermute | solution.py:734
  27.5 0.1 shard_map.50
  27.6 0.6 %collective-permute-start.6 = (f32[64,512]{1,0:T(8,128)S(1)}, f32[64,512]{1,0:T(8,128)S(1)}, u32[]{:S(2)}, u32[]{:S(2)}) collective-permute-start(f32[64,512]{1,0:T(8,128)S(1)} %get-tuple-element.44.first_ref), channel_id=1, source_target_pairs={{0,4},{2,6},{4,0},{6,2},{1,5},{3,7},{5,1},{7,3},{8,12},{10,14},{12... | collective-permute-start | bytes 393224 | tf_op jit(solution)/shard_map/ppermute | solution.py:743
  28.2 1.5 %collective-permute-start.7 = (f32[64,512]{1,0:T(8,128)S(1)}, f32[64,512]{1,0:T(8,128)S(1)}, u32[]{:S(2)}, u32[]{:S(2)}) collective-permute-start(f32[64,512]{1,0:T(8,128)S(1)} %get-tuple-element.45.third_ref), channel_id=1, source_target_pairs={{0,1},{1,0},{2,3},{3,2},{4,5},{5,4},{6,7},{7,6},{8,9},{9,8},{10,11... | collective-permute-start | bytes 393224 | tf_op jit(solution)/shard_map/ppermute | solution.py:744
  29.7 3.5 %collective-permute-done.6.second_ref.refs_4_ = f32[64,512]{1,0:T(8,128)S(1)} collective-permute-done((f32[64,512]{1,0:T(8,128)S(1)}, f32[64,512]{1,0:T(8,128)S(1)}, u32[]{:S(2)}, u32[]{:S(2)}) %collective-permute-start.6) | collective-permute-done | bytes 131104 | tf_op jit(solution)/shard_map/ppermute | solution.py:743
  33.2 0.3 collective-permute-done.7.fourth_ref.refs_5_
  33.5 1.6 %collective-permute-start.8 = (f32[64,512]{1,0:T(8,128)S(1)}, f32[64,512]{1,0:T(8,128)S(1)}, u32[]{:S(2)}, u32[]{:S(2)}) collective-permute-start(f32[64,512]{1,0:T(8,128)S(1)} %get-tuple-element.46.unread.refs_0_), channel_id=1, source_target_pairs={{0,1},{1,0},{2,3},{3,2},{4,5},{5,4},{6,7},{7,6},{8,9},{9,8},{10,11... | collective-permute-start | bytes 393224 | tf_op jit(solution)/shard_map/ppermute | solution.py:753
  35.1 1.5 %collective-permute-start.9 = (f32[64,384]{1,0:T(8,128)S(1)}, f32[64,384]{1,0:T(8,128)S(1)}, u32[]{:S(2)}, u32[]{:S(2)}) collective-permute-start(f32[64,384]{1,0:T(8,128)S(1)} %get-tuple-element.47.refs_2_), channel_id=1, source_target_pairs={{0,4},{2,6},{4,0},{6,2},{1,5},{3,7},{5,1},{7,3},{8,12},{10,14},{12... | collective-permute-start | bytes 294920 | tf_op jit(solution)/shard_map/ppermute | solution.py:754
  36.6 0.7 %collective-permute-start.10 = (f32[32,256]{1,0:T(8,128)S(1)}, f32[32,256]{1,0:T(8,128)S(1)}, u32[]{:S(2)}, u32[]{:S(2)}) collective-permute-start(f32[32,256]{1,0:T(8,128)S(1)} %get-tuple-element.48), channel_id=1, source_target_pairs={{0,8},{8,0},{16,24},{24,16},{1,9},{9,1},{17,25},{25,17},{2,10},{10... | collective-permute-start | bytes 98312 | tf_op jit(solution)/shard_map/ppermute | solution.py:77
  37.2 0.9 %collective-permute-start.11 = (f32[32,256]{1,0:T(8,128)S(1)}, f32[32,256]{1,0:T(8,128)S(1)}, u32[]{:S(2)}, u32[]{:S(2)}) collective-permute-start(f32[32,256]{1,0:T(8,128)S(1)} %get-tuple-element.49), channel_id=1, source_target_pairs={{0,24},{8,16},{16,8},{24,0},{1,25},{9,17},{17,9},{25,1},{2,26},{10... | collective-permute-start | bytes 98312 | tf_op jit(solution)/shard_map/ppermute | solution.py:78
  38.1 0.5 shard_map.52.refs_4_.spread_ref
  38.7 2.0 %collective-permute-done.10.refs_5_.refs_2_ = f32[32,256]{1,0:T(8,128)S(1)} collective-permute-done((f32[32,256]{1,0:T(8,128)S(1)}, f32[32,256]{1,0:T(8,128)S(1)}, u32[]{:S(2)}, u32[]{:S(2)}) %collective-permute-start.10) | collective-permute-done | bytes 32800 | tf_op jit(solution)/shard_map/ppermute | solution.py:77
  40.7 2.3 %collective-permute-done.11.refs_6_.refs_3_ = f32[32,256]{1,0:T(8,128)S(1)} collective-permute-done((f32[32,256]{1,0:T(8,128)S(1)}, f32[32,256]{1,0:T(8,128)S(1)}, u32[]{:S(2)}, u32[]{:S(2)}) %collective-permute-start.11) | collective-permute-done | bytes 32800 | tf_op jit(solution)/shard_map/ppermute | solution.py:78
  43.0 0.0 collective-permute-done.9.refs_3_
  43.0 0.0 collective-permute-done.8.refs_1_.matrix_ref
  43.0 7.7 %shard_map.53.refs_0_.here_ref = f32[192,128]{1,0:T(8,128)S(1)} custom-call(f32[64,512]{1,0:T(8,128)S(1)} %get-tuple-element.46.unread.refs_0_, f32[64,512]{1,0:T(8,128)S(1)} %collective-permute-done.8.refs_1_.matrix_ref, f32[64,384]{1,0:T(8,128)S(1)} %get-tuple-element.47.refs_2_, f32[64,384]{1,0:T(8,128)S(1)} %collective-permute-done.9.refs_3_, ...), custom_call_target="tpu_custom_call" | custom-call | flops 7000000000 | bytes 1048576 | tf_op jit(solution)/shard_map/pallas_call | solution.py:713
  50.7 0.1 collective-permute-start.12
  50.8 1.3 %collective-permute-done.12.refs_1_.there_ref = f32[192,128]{1,0:T(8,128)S(1)} collective-permute-done((f32[192,128]{1,0:T(8,128)S(1)}, f32[192,128]{1,0:T(8,128)S(1)}, u32[]{:S(2)}, u32[]{:S(2)}) %collective-permute-start.12) | collective-permute-done | bytes 98336 | tf_op jit(solution)/shard_map/ppermute | solution.py:764
  52.1 0.1 collective-permute-start.13
  52.2 1.0 %collective-permute-start.14 = (f32[32,128]{1,0:T(8,128)S(1)}, f32[32,128]{1,0:T(8,128)S(1)}, u32[]{:S(2)}, u32[]{:S(2)}) collective-permute-start(f32[32,128]{1,0:T(8,128)S(1)} %get-tuple-element.53), channel_id=1, source_target_pairs={{0,24},{8,16},{16,8},{24,0},{1,25},{9,17},{17,9},{25,1},{2,26},{10... | collective-permute-start | bytes 49160 | tf_op jit(solution)/shard_map/ppermute | solution.py:78
  53.2 1.4 %shard_map.54 = (f32[1536,128]{1,0:T(8,128)}, bf16[2,256,192]{2,1,0:T(8,128)(2,1)S(1)}) custom-call(f32[8,128]{1,0:T(8,128)S(1)} %get-tuple-element.31.flag_ref, f32[6,32,256]{2,1,0:T(8,128)S(1)} %get-tuple-element.40.product_ref.refs_0_, bf16[2,2,256,256]{3,2,1,0:T(8,128)(2,1)S(1)} %get-tuple-element.41.refs_1_.early_inverse, ...), custom_call_target="tpu_custom_call" | custom-call | flops 1000000000 | bytes 1048576 | tf_op jit(solution)/shard_map/pallas_call | solution.py:773
  54.6 1.4 %collective-permute-done.13.refs_0_ = f32[32,128]{1,0:T(8,128)S(1)} collective-permute-done((f32[32,128]{1,0:T(8,128)S(1)}, f32[32,128]{1,0:T(8,128)S(1)}, u32[]{:S(2)}, u32[]{:S(2)}) %collective-permute-start.13) | collective-permute-done | bytes 16416 | tf_op jit(solution)/shard_map/ppermute | solution.py:77
  55.9 1.9 %collective-permute-done.14.refs_1_ = f32[32,128]{1,0:T(8,128)S(1)} collective-permute-done((f32[32,128]{1,0:T(8,128)S(1)}, f32[32,128]{1,0:T(8,128)S(1)}, u32[]{:S(2)}, u32[]{:S(2)}) %collective-permute-start.14) | collective-permute-done | bytes 16416 | tf_op jit(solution)/shard_map/ppermute | solution.py:78
  57.8 1.0 %shard_map.56 = f32[1536,128]{1,0:T(8,128)} custom-call(bf16[2,256,192]{2,1,0:T(8,128)(2,1)S(1)} %get-tuple-element.50.spread_ref, f32[64,128]{1,0:T(8,128)S(1)} %get-tuple-element.51.rows_ref, f32[32,128]{1,0:T(8,128)S(1)} %collective-permute-done.13.refs_0_, f32[32,128]{1,0:T(8,128)S(1)} %collective-permute-done.14.refs_1_, ...), custom_call_target="tpu_custom_call", output_to_operand_aliasing={{}: (4, {})} | custom-call | flops 1000000000 | bytes 1048576 | tf_op jit(solution)/shard_map/pallas_call | solution.py:810
  (2 shorter events, 0.1 us)
Async XLA Ops:
  0.0 10.2 %copy-start = (s32[8]{0:T(128)S(1)}, s32[8]{0:T(128)}, u32[]{:S(2)}) copy-start(s32[8]{0:T(128)} %group_ref.1) | copy-start | bytes 100
  1.5 14.3 %collective-permute-start = (f32[264,128]{1,0:T(8,128)S(1)}, f32[264,128]{1,0:T(8,128)S(1)}, u32[]{:S(2)}, u32[]{:S(2)}) collective-permute-start(f32[264,128]{1,0:T(8,128)S(1)} %get-tuple-element.32), channel_id=1, source_target_pairs={{0,8},{8,0},{16,24},{24,16},{1,9},{9,1},{17,25},{25,17},{2,10},{10... | collective-permute-start | bytes 405512 | tf_op jit(solution)/shard_map/ppermute | solution.py:77
  4.6 11.2 %collective-permute-start.1 = (f32[264,128]{1,0:T(8,128)S(1)}, f32[264,128]{1,0:T(8,128)S(1)}, u32[]{:S(2)}, u32[]{:S(2)}) collective-permute-start(f32[264,128]{1,0:T(8,128)S(1)} %get-tuple-element.33), channel_id=1, source_target_pairs={{0,24},{8,16},{16,8},{24,0},{1,25},{9,17},{17,9},{25,1},{2,26},{10... | collective-permute-start | bytes 405512 | tf_op jit(solution)/shard_map/ppermute | solution.py:78
  7.0 5.8 %collective-permute-start.3 = (f32[264,128]{1,0:T(8,128)S(1)}, f32[264,128]{1,0:T(8,128)S(1)}, u32[]{:S(2)}, u32[]{:S(2)}) collective-permute-start(f32[264,128]{1,0:T(8,128)S(1)} %get-tuple-element.37), channel_id=1, source_target_pairs={{0,2},{2,0},{4,6},{6,4},{1,3},{3,1},{5,7},{7,5},{8,10},{10,8},{12,... | collective-permute-start | bytes 405512 | tf_op jit(solution)/shard_map/ppermute | solution.py:77
  7.0 5.9 %collective-permute-start.4 = (f32[264,128]{1,0:T(8,128)S(1)}, f32[264,128]{1,0:T(8,128)S(1)}, u32[]{:S(2)}, u32[]{:S(2)}) collective-permute-start(f32[264,128]{1,0:T(8,128)S(1)} %get-tuple-element.38), channel_id=1, source_target_pairs={{0,6},{2,4},{4,2},{6,0},{1,7},{3,5},{5,3},{7,1},{8,14},{10,12},{12... | collective-permute-start | bytes 405512 | tf_op jit(solution)/shard_map/ppermute | solution.py:78
  8.6 8.4 %collective-permute-start.2 = (f32[2,264,128]{2,1,0:T(8,128)S(1)}, f32[2,264,128]{2,1,0:T(8,128)S(1)}, u32[]{:S(2)}, u32[]{:S(2)}) collective-permute-start(f32[2,264,128]{2,1,0:T(8,128)S(1)} %get-tuple-element.34), channel_id=1, source_target_pairs={{0,1},{1,0},{2,3},{3,2},{4,5},{5,4},{6,7},{7,6},{8,9},{9,8},{10,11... | collective-permute-start | bytes 811016 | tf_op jit(solution)/shard_map/ppermute | solution.py:75
  10.2 2.7 %copy-start.2 = (f32[1,1,1,6,256,32]{4,5,3,2,1,0:T(8,128)S(1)}, f32[1,1,1,6,256,32]{4,5,3,2,1,0:T(8,128)}, u32[]{:S(2)}) copy-start(f32[1,1,1,6,256,32]{4,5,3,2,1,0:T(8,128)} %param.5) | copy-start | bytes 589828
  12.9 4.2 %copy-start.1 = (f32[1,1,1,1536,128]{4,3,2,1,0:T(8,128)S(1)}, f32[1,1,1,1536,128]{4,3,2,1,0:T(8,128)}, u32[]{:S(2)}) copy-start(f32[1,1,1,1536,128]{4,3,2,1,0:T(8,128)} %param.6) | copy-start | bytes 2359300
  25.9 1.6 %collective-permute-start.5 = (f32[64,1024]{1,0:T(8,128)S(1)}, f32[64,1024]{1,0:T(8,128)S(1)}, u32[]{:S(2)}, u32[]{:S(2)}) collective-permute-start(f32[64,1024]{1,0:T(8,128)S(1)} %get-tuple-element.43.here_ref), channel_id=1, source_target_pairs={{0,2},{2,0},{4,6},{6,4},{1,3},{3,1},{5,7},{7,5},{8,10},{10,8},{12,... | collective-permute-start | bytes 786440 | tf_op jit(solution)/shard_map/ppermute | solution.py:734
  27.6 5.6 %collective-permute-start.6 = (f32[64,512]{1,0:T(8,128)S(1)}, f32[64,512]{1,0:T(8,128)S(1)}, u32[]{:S(2)}, u32[]{:S(2)}) collective-permute-start(f32[64,512]{1,0:T(8,128)S(1)} %get-tuple-element.44.first_ref), channel_id=1, source_target_pairs={{0,4},{2,6},{4,0},{6,2},{1,5},{3,7},{5,1},{7,3},{8,12},{10,14},{12... | collective-permute-start | bytes 393224 | tf_op jit(solution)/shard_map/ppermute | solution.py:743
  28.2 5.3 %collective-permute-start.7 = (f32[64,512]{1,0:T(8,128)S(1)}, f32[64,512]{1,0:T(8,128)S(1)}, u32[]{:S(2)}, u32[]{:S(2)}) collective-permute-start(f32[64,512]{1,0:T(8,128)S(1)} %get-tuple-element.45.third_ref), channel_id=1, source_target_pairs={{0,1},{1,0},{2,3},{3,2},{4,5},{5,4},{6,7},{7,6},{8,9},{9,8},{10,11... | collective-permute-start | bytes 393224 | tf_op jit(solution)/shard_map/ppermute | solution.py:744
  33.5 9.5 %collective-permute-start.8 = (f32[64,512]{1,0:T(8,128)S(1)}, f32[64,512]{1,0:T(8,128)S(1)}, u32[]{:S(2)}, u32[]{:S(2)}) collective-permute-start(f32[64,512]{1,0:T(8,128)S(1)} %get-tuple-element.46.unread.refs_0_), channel_id=1, source_target_pairs={{0,1},{1,0},{2,3},{3,2},{4,5},{5,4},{6,7},{7,6},{8,9},{9,8},{10,11... | collective-permute-start | bytes 393224 | tf_op jit(solution)/shard_map/ppermute | solution.py:753
  35.1 7.9 %collective-permute-start.9 = (f32[64,384]{1,0:T(8,128)S(1)}, f32[64,384]{1,0:T(8,128)S(1)}, u32[]{:S(2)}, u32[]{:S(2)}) collective-permute-start(f32[64,384]{1,0:T(8,128)S(1)} %get-tuple-element.47.refs_2_), channel_id=1, source_target_pairs={{0,4},{2,6},{4,0},{6,2},{1,5},{3,7},{5,1},{7,3},{8,12},{10,14},{12... | collective-permute-start | bytes 294920 | tf_op jit(solution)/shard_map/ppermute | solution.py:754
  36.6 4.1 %collective-permute-start.10 = (f32[32,256]{1,0:T(8,128)S(1)}, f32[32,256]{1,0:T(8,128)S(1)}, u32[]{:S(2)}, u32[]{:S(2)}) collective-permute-start(f32[32,256]{1,0:T(8,128)S(1)} %get-tuple-element.48), channel_id=1, source_target_pairs={{0,8},{8,0},{16,24},{24,16},{1,9},{9,1},{17,25},{25,17},{2,10},{10... | collective-permute-start | bytes 98312 | tf_op jit(solution)/shard_map/ppermute | solution.py:77
  37.2 5.7 %collective-permute-start.11 = (f32[32,256]{1,0:T(8,128)S(1)}, f32[32,256]{1,0:T(8,128)S(1)}, u32[]{:S(2)}, u32[]{:S(2)}) collective-permute-start(f32[32,256]{1,0:T(8,128)S(1)} %get-tuple-element.49), channel_id=1, source_target_pairs={{0,24},{8,16},{16,8},{24,0},{1,25},{9,17},{17,9},{25,1},{2,26},{10... | collective-permute-start | bytes 98312 | tf_op jit(solution)/shard_map/ppermute | solution.py:78
  50.7 1.4 %collective-permute-start.12 = (f32[192,128]{1,0:T(8,128)S(1)}, f32[192,128]{1,0:T(8,128)S(1)}, u32[]{:S(2)}, u32[]{:S(2)}) collective-permute-start(f32[192,128]{1,0:T(8,128)S(1)} %shard_map.53.refs_0_.here_ref), channel_id=1, source_target_pairs={{0,2},{2,0},{4,6},{6,4},{1,3},{3,1},{5,7},{7,5},{8,10},{10,8},{12,... | collective-permute-start | bytes 294920 | tf_op jit(solution)/shard_map/ppermute | solution.py:764
  52.1 3.8 %collective-permute-start.13 = (f32[32,128]{1,0:T(8,128)S(1)}, f32[32,128]{1,0:T(8,128)S(1)}, u32[]{:S(2)}, u32[]{:S(2)}) collective-permute-start(f32[32,128]{1,0:T(8,128)S(1)} %get-tuple-element.52), channel_id=1, source_target_pairs={{0,8},{8,0},{16,24},{24,16},{1,9},{9,1},{17,25},{25,17},{2,10},{10... | collective-permute-start | bytes 49160 | tf_op jit(solution)/shard_map/ppermute | solution.py:77
  52.2 5.6 %collective-permute-start.14 = (f32[32,128]{1,0:T(8,128)S(1)}, f32[32,128]{1,0:T(8,128)S(1)}, u32[]{:S(2)}, u32[]{:S(2)}) collective-permute-start(f32[32,128]{1,0:T(8,128)S(1)} %get-tuple-element.53), channel_id=1, source_target_pairs={{0,24},{8,16},{16,8},{24,0},{1,25},{9,17},{17,9},{25,1},{2,26},{10... | collective-permute-start | bytes 49160 | tf_op jit(solution)/shard_map/ppermute | solution.py:78

commit v9 on v6

--- a/solution.py
+++ b/solution.py
@@ -51,6 +51,17 @@
     )
     half = rows.shape[0] // 2
     return out[:half] + out[half:]
+
+
+def triple(left, right, dims=((1,), (0,))):
+    (left_high, left_low), (right_high, right_low) = split(left), split(right)
+    total = None
+    for one, other in ((left_high, right_high), (left_high, right_low), (left_low, right_high)):
+        part = lax.dot_general(
+            one, other, (dims, ((), ())), preferred_element_type=jnp.float32
+        )
+        total = part if total is None else total + part
+    return total
 
 
 def iota(shape, dim):
@@ -276,17 +287,31 @@
 
 def begin(packed, owns, partner_out, sum_ref):
     width = owns[0].shape[1]
-    eye = iota((width, width), 0) == iota((width, width), 1)
+    half = width // 2
+    eye = iota((half, half), 0) == iota((half, half), 1)
+    zero = jnp.zeros((half, half), jnp.float32)
     guesses = []
     for f in range(len(packed)):
         partner = unpack(packed[f])
         total = owns[f] + partner
         store(partner_out, f, partner)
         store(sum_ref, f, total)
-        diagonal = jnp.where(eye, total, 0.0)
-        across = 1.0 / jnp.sum(diagonal, axis=0, keepdims=True)
-        down = 1.0 / jnp.sum(diagonal, axis=1, keepdims=True)
-        guesses.append(jnp.where(eye, 2.0 * across, 0.0) - down * total * across)
+        across, down, twice = [], [], []
+        for start in (0, half):
+            block = total[start : start + half, start : start + half]
+            diagonal = jnp.where(eye, block, 0.0)
+            across.append(1.0 / jnp.sum(diagonal, axis=0, keepdims=True))
+            down.append(1.0 / jnp.sum(diagonal, axis=1, keepdims=True))
+            twice.append(jnp.where(eye, 2.0 * across[-1], 0.0))
+        start = jnp.concatenate(
+            [
+                jnp.concatenate([twice[0], zero], axis=1),
+                jnp.concatenate([zero, twice[1]], axis=1),
+            ],
+            axis=0,
+        )
+        across, down = jnp.concatenate(across, axis=1), jnp.concatenate(down, axis=0)
+        guesses.append(start - down * total * across)
     return guesses
 
 
@@ -392,14 +417,14 @@
     blocks = []
     for g in range(FACES):
         tall = jnp.concatenate([sides[f][g] for f in range(g + 1)], axis=0)
-        blocks.append(dot(dot(tall, vectors[g], ((1,), (1,))), factors[g], ((1,), (1,))))
+        blocks.append(triple(triple(tall, vectors[g], ((1,), (1,))), factors[g], ((1,), (1,))))
     even, odd, right, products = [], [], [], []
     lows = None
     for f in range(FACES):
-        products.append(dot(factors[f], sides[f][f]))
+        products.append(triple(factors[f], sides[f][f]))
         product_ref[f] = products[f]
         line = [blocks[g][f * ncon : (f + 1) * ncon] for g in range(f, FACES)]
-        line = dot(factors[f], jnp.concatenate([rights[f]] + line, axis=1))
+        line = triple(factors[f], jnp.concatenate([rights[f]] + line, axis=1))
         right.append(line[:, :columns])
         line = line[:, columns:]
         if f % 2 == 0:
@@ -449,7 +474,7 @@
         basis = sweep_basis(*matrices, basis)
     factors = factor_inverses([dot(b, b, ((1,), (1,))) for b in basis])
     for f in range(2):
-        theirs = dot(factors[f], thin(stacked(basis[f]), matrices[2][f]))
+        theirs = triple(factors[f], thin(stacked(basis[f]), matrices[2][f]))
         both = jnp.concatenate([product_ref[f], theirs], axis=0)
         high, low = split(thin(stacked(both), matrices[1][f]).T)
         out_ref[f] = jnp.concatenate([high, high, low], axis=1)
@@ -467,7 +492,7 @@
     right_ref[...] = jnp.concatenate([total[:, lanes:], fold(product_ref[4])], axis=1)
 
 
-def add_kernel(first_ref, second_ref, third_ref, fourth_ref, product_ref, unread, *refs):
+def add_kernel(first_ref, second_ref, third_ref, fourth_ref, product_ref, *refs):
     matrix_ref, right_ref = refs
     half = product_ref.shape[2] // 2
     lanes, right_lanes = matrix_ref.shape[1] - half, right_ref.shape[1]
@@ -506,24 +531,24 @@
     for b in range(BLOCKS):
         (inverse,) = factor_inverses([blocks[b, b]])
         later = range(b + 1, BLOCKS)
-        row = dot(inverse, jnp.concatenate([rights[b]] + [blocks[b, c] for c in later], axis=1))
+        row = triple(inverse, jnp.concatenate([rights[b]] + [blocks[b, c] for c in later], axis=1))
         if later:
             column = jnp.concatenate([blocks[c, b] for c in later], axis=0)
-            change = dot(dot(column, inverse, ((1,), (1,))), row)
+            change = triple(triple(column, inverse, ((1,), (1,))), row)
         for i, c in enumerate(later):
             part = change[i * size : (i + 1) * size]
             rights[c] = rights[c] - part[:, :columns]
             for j, d in enumerate(later):
                 start = columns + j * size
                 blocks[c, d] = blocks[c, d] - part[:, start : start + size]
-        row = dot(inverse, row, ((0,), (0,)))
+        row = triple(inverse, row, ((0,), (0,)))
         rights[b] = row[:, :columns]
         for c in later:
             blocks[b, c] = row[:, columns + (c - b - 1) * size : columns + (c - b) * size]
         for i in range(b):
             for c in later:
-                blocks[i, c] = blocks[i, c] - dot(blocks[i, b], blocks[b, c])
-            rights[i] = rights[i] - dot(blocks[i, b], rights[b])
+                blocks[i, c] = blocks[i, c] - triple(blocks[i, b], blocks[b, c])
+            rights[i] = rights[i] - triple(blocks[i, b], rights[b])
     answer = [downs[b] * rights[b] for b in range(BLOCKS)]
     answer_ref[...] = jnp.concatenate(answer, axis=0)
 
@@ -740,15 +765,15 @@
             cost_estimate=cost(3),
         )(token, *got[0], own_halves, product, *partners, *inverses)
 
-    def solve(matrices, rights):
+    def solve(matrices, rights, unread):
         return pl.pallas_call(
             functools.partial(solve_kernel, size, len(matrices), columns),
             out_shape=shape(coarse, columns),
-            in_specs=vmem_specs(2 * len(matrices)),
+            in_specs=vmem_specs(2 * len(matrices)) + [anywhere] * len(unread),
             out_specs=vmem_specs(1)[0],
             compiler_params=params(12),
             cost_estimate=cost(7),
-        )(*matrices, *rights)
+        )(*matrices, *rights, *unread)
 
     result = dict(
         out_shape=shape(order, columns),
@@ -773,17 +798,17 @@
         )(flags, payload, other, product)
         left_moved = lax.ppermute(left, "gy", chip_x)
         rest_moved = lax.ppermute(rest, "gz", chip_y)
-        spread = spread_of(left)
         left_last, rest_last = pl.pallas_call(
             add_kernel,
             out_shape=[shape(size, lanes + half), shape(size, right_lanes)],
-            in_specs=vmem_specs(5) + [anywhere],
+            in_specs=vmem_specs(5),
             out_specs=vmem_specs(2),
             compiler_params=params(8),
-        )(left, left_moved, rest, rest_moved, product, spread)
+        )(left, left_moved, rest, rest_moved, product)
         left_other = lax.ppermute(left_last, "gz", chip_y)
         rest_other = lax.ppermute(rest_last, "gy", chip_x)
-        answer = solve([left_last, left_other], [rest_last, rest_other])
+        spread = spread_of(left_last)
+        answer = solve([left_last, left_other], [rest_last, rest_other], [spread])
         there = lax.ppermute(answer, "gy", core_swap)
         *sent, mine = pl.pallas_call(
             functools.partial(rows_kernel, ncon),
@@ -808,7 +833,7 @@
         total = lax.psum(jnp.where(chosen[:, None, None], part[None], 0.0), ("gy", "gz"))
         total = lax.dynamic_index_in_dim(total, member_of, 0, keepdims=False)
         spread = spread_of(payload)
-        answer = solve([total[:, :lanes]], [total[:, lanes:]])
+        answer = solve([total[:, :lanes]], [total[:, lanes:]], [])
 
         def from_near(faces_of, axis):
             even, odd = faces_of

time: 54.7 us -> 54.3 us (level)
  waiting for transfers between devices: 8.53 us -> 10.6 us
  starting transfers between devices: 15.5 us -> 13.6 us
  Pallas kernels: 30.2 us -> 29.5 us
    ppermute x1, waiting for transfers between devices: 0.23 us -> 3.54 us  [per_device(): left_moved = lax.ppermute(left, 'gy', chip_x)]
    ppermute x1, waiting for transfers between devices: 3.13 us -> 0.35 us  [per_device(): rest_other = lax.ppermute(rest_last, 'gy', chip_x)]
    ppermute x1, starting transfers between devices: 1.58 us -> 0.5 us  [per_device(): left_other = lax.ppermute(left_last, 'gz', chip_y)]
    ppermute x1, waiting for transfers between devices: 0.01 us -> 0.89 us  [per_device(): left_other = lax.ppermute(left_last, 'gz', chip_y)]
    ppermute x1, starting transfers between devices: 1.49 us -> 0.61 us  [per_device(): rest_other = lax.ppermute(rest_last, 'gy', chip_x)]
    ppermute x1, waiting for transfers between devices: 0.34 us -> 1.2 us  [per_device(): rest_moved = lax.ppermute(rest, 'gz', chip_y)]
  transfers between devices with their start and end apart: 13 -> 13, of which waited for: 8 -> 9; matrix products, arithmetic and copies ran while one was open for 0% -> 0% of each run, Pallas kernels for 20% -> 21%
where the time goes in v9:
time: 54.3 us; the launch traced here: 54.1 us
  Pallas kernels  29.5 us (54%)
  starting transfers between devices  13.6 us (25%)
  waiting for transfers between devices  10.6 us (20%)
    pallas_call x1, Pallas kernels, per_device(): pl.pallas_call(functools.partial(main_kernel, (AXES[0], AXES[1]), early,...  8.39 us
    pallas_call x1, Pallas kernels, solve(): pl.pallas_call(functools.partial(solve_kernel, size, len(matrices), colum...  7.19 us
    ppermute x3, starting transfers between devices, exchange(): lax.ppermute(arrays[0], axis, outer_pairs(axis))  6.06 us
    ppermute x1, waiting for transfers between devices, per_device(): left_moved = lax.ppermute(left, 'gy', chip_x)  3.54 us
    pallas_call x1, Pallas kernels, spread_of(): pl.pallas_call(functools.partial(spread_kernel, faces, ncon), out_shape=j...  3.22 us
    ppermute x1, starting transfers between devices, exchange(): return [lax.ppermute(arrays[0], axis, flipped(axis, 1))]  3.03 us
    pallas_call x1, Pallas kernels, per_device(): pl.pallas_call(functools.partial(early_kernel, AXES[2:3], early), out_sha...  2.97 us
    pallas_call x1, Pallas kernels, per_device(): pl.pallas_call(functools.partial(halves_kernel, planes), out_shape=[halve...  2.7 us
  transfers between devices with their start and end apart: 13, of which 9 were waited for; matrix products, arithmetic and copies ran while one was open for 0% of the time, Pallas kernels for 21%

profile of v9, /device:TPU:0, one launch (start us, length us, event | category | flops | bytes accessed | tf_op | source)
XLA Modules:
  0.0 54.1 jit_solution(15582404113768848934)
XLA Ops:
  0.0 0.0 copy-start.1
  0.0 1.7 %shard_map.46 = (f32[328,128]{1,0:T(8,128)S(1)}, f32[328,128]{1,0:T(8,128)S(1)}, f32[328,128]{1,0:T(8,128)S(1)}, f32[328,128]{1,0:T(8,128)S(1)}, f32[2,264,128]{2,1,0:T(8,128)S(1)}, /*index=5*/f32[6,256,256]{2,1,0:T(8,128)S(1)}) custom-call(f32[1536,1536]{1,0:T(8,128)} %bitcast.10, f32[6,32,256]{2,1,0:T(8,128)} %bitcast.6), custom_call_target="tpu_custom_call" | custom-call | tf_op jit(solution)/shard_map/pallas_call | solution.py:702
  1.7 3.0 %collective-permute-start.4 = (f32[2,264,128]{2,1,0:T(8,128)S(1)}, f32[2,264,128]{2,1,0:T(8,128)S(1)}, u32[]{:S(2)}, u32[]{:S(2)}) collective-permute-start(f32[2,264,128]{2,1,0:T(8,128)S(1)} %get-tuple-element.36), channel_id=1, source_target_pairs={{0,1},{1,0},{2,3},{3,2},{4,5},{5,4},{6,7},{7,6},{8,9},{9,8},{10,11... | collective-permute-start | bytes 811016 | tf_op jit(solution)/shard_map/ppermute | solution.py:86
  4.7 3.6 %collective-permute-start = (f32[328,128]{1,0:T(8,128)S(1)}, f32[328,128]{1,0:T(8,128)S(1)}, u32[]{:S(2)}, u32[]{:S(2)}) collective-permute-start(f32[328,128]{1,0:T(8,128)S(1)} %get-tuple-element.30), channel_id=1, source_target_pairs={{0,24},{8,16},{16,8},{24,0},{1,25},{9,17},{17,9},{25,1},{2,26},{10... | collective-permute-start | bytes 503816 | tf_op jit(solution)/shard_map/ppermute | solution.py:88
  8.3 0.0 collective-permute-start.1
  8.3 0.4 collective-permute-start.2
  8.7 1.2 %collective-permute-start.3 = (f32[328,128]{1,0:T(8,128)S(1)}, f32[328,128]{1,0:T(8,128)S(1)}, u32[]{:S(2)}, u32[]{:S(2)}) collective-permute-start(f32[328,128]{1,0:T(8,128)S(1)} %get-tuple-element.33), channel_id=1, source_target_pairs={{0,2},{2,0},{4,6},{6,4},{1,3},{3,1},{5,7},{7,5},{8,10},{10,8},{12,... | collective-permute-start | bytes 503816 | tf_op jit(solution)/shard_map/ppermute | solution.py:89
  9.9 0.0 copy-done.1
  9.9 0.0 copy-start
  9.9 2.7 %shard_map.47 = (bf16[6,2,256,256]{3,2,1,0:T(8,128)(2,1)S(1)}, bf16[15,2,256,256]{3,2,1,0:T(8,128)(2,1)S(1)}, f32[8,128]{1,0:T(8,128)S(1)}) custom-call(f32[1536,1536]{1,0:T(8,128)} %bitcast.11, s32[8]{0:T(128)S(1)} %copy-done.1, f32[6,256,256]{2,1,0:T(8,128)S(1)} %get-tuple-element.28.own_ref.refs_1_.refs_4_), custom_call_target="tpu_custom_call" | custom-call | flops 2000000000 | bytes 1048576 | tf_op jit(solution)/shard_map/pallas_call | solution.py:722
  12.6 0.0 copy-start.2
  12.7 0.0 collective-permute-done.4.refs_0_
  12.7 0.0 copy-done
  12.7 3.0 %shard_map.48 = (f32[2,32,256]{2,1,0:T(8,128)S(1)}, bf16[2,2,256,256]{3,2,1,0:T(8,128)(2,1)S(1)}, bf16[2,2,256,256]{3,2,1,0:T(8,128)(2,1)S(1)}) custom-call(f32[2,264,128]{2,1,0:T(8,128)S(1)} %collective-permute-done.4.refs_0_, f32[6,256,256]{2,1,0:T(8,128)S(1)} %get-tuple-element.28.own_ref.refs_1_.refs_4_, ...), custom_call_target="tpu_custom_call" | custom-call | flops 2000000000 | bytes 1048576 | tf_op jit(solution)/shard_map/pallas_call | solution.py:735
  15.7 0.0 collective-permute-done.refs_0_
  15.7 0.4 collective-permute-done.1.refs_1_
  16.0 0.0 collective-permute-done.2.refs_2_
  16.0 0.0 collective-permute-done.3.refs_3_
  16.0 0.0 copy-done.2
  16.0 8.4 %shard_map.49 = (f32[64,1024]{1,0:T(8,128)S(1)}, f32[6,32,256]{2,1,0:T(8,128)S(1)}, bf16[4,2,256,256]{3,2,1,0:T(8,128)(2,1)S(1)}, bf16[4,2,256,256]{3,2,1,0:T(8,128)(2,1)S(1)}) custom-call(f32[328,128]{1,0:T(8,128)S(1)} %collective-permute-done.refs_0_, f32[328,128]{1,0:T(8,128)S(1)} %collective-permute-done.1.refs_1_, ...), custom_call_target="tpu_custom_call" | custom-call | flops 8000000000 | bytes 1048576 | tf_op jit(solution)/shard_map/pallas_call | solution.py:745
  24.4 0.1 collective-permute-start.5
  24.5 1.5 %collective-permute-done.5.there_ref = f32[64,1024]{1,0:T(8,128)S(1)} collective-permute-done((f32[64,1024]{1,0:T(8,128)S(1)}, f32[64,1024]{1,0:T(8,128)S(1)}, u32[]{:S(2)}, u32[]{:S(2)}) %collective-permute-start.5) | collective-permute-done | bytes 262176 | tf_op jit(solution)/shard_map/ppermute | solution.py:791
  26.0 0.1 shard_map.50
  26.1 1.5 %collective-permute-start.6 = (f32[64,512]{1,0:T(8,128)S(1)}, f32[64,512]{1,0:T(8,128)S(1)}, u32[]{:S(2)}, u32[]{:S(2)}) collective-permute-start(f32[64,512]{1,0:T(8,128)S(1)} %get-tuple-element.40.first_ref), channel_id=1, source_target_pairs={{0,4},{2,6},{4,0},{6,2},{1,5},{3,7},{5,1},{7,3},{8,12},{10,14},{12... | collective-permute-start | bytes 393224 | tf_op jit(solution)/shard_map/ppermute | solution.py:799
  27.7 0.5 collective-permute-start.7
  28.2 3.5 %collective-permute-done.6.second_ref.matrix_ref = f32[64,512]{1,0:T(8,128)S(1)} collective-permute-done((f32[64,512]{1,0:T(8,128)S(1)}, f32[64,512]{1,0:T(8,128)S(1)}, u32[]{:S(2)}, u32[]{:S(2)}) %collective-permute-start.6) | collective-permute-done | bytes 131104 | tf_op jit(solution)/shard_map/ppermute | solution.py:799
  31.7 1.2 %collective-permute-done.7.fourth_ref.right_ref = f32[64,512]{1,0:T(8,128)S(1)} collective-permute-done((f32[64,512]{1,0:T(8,128)S(1)}, f32[64,512]{1,0:T(8,128)S(1)}, u32[]{:S(2)}, u32[]{:S(2)}) %collective-permute-start.7) | collective-permute-done | bytes 131104 | tf_op jit(solution)/shard_map/ppermute | solution.py:800
  33.0 0.6 %collective-permute-start.9 = (f32[64,384]{1,0:T(8,128)S(1)}, f32[64,384]{1,0:T(8,128)S(1)}, u32[]{:S(2)}, u32[]{:S(2)}) collective-permute-start(f32[64,384]{1,0:T(8,128)S(1)} %get-tuple-element.47.refs_2_), channel_id=1, source_target_pairs={{0,4},{2,6},{4,0},{6,2},{1,5},{3,7},{5,1},{7,3},{8,12},{10,14},{12... | collective-permute-start | bytes 294920 | tf_op jit(solution)/shard_map/ppermute | solution.py:809
  33.6 0.5 collective-permute-start.8
  34.1 3.2 %shard_map.52.refs_4_.spread_ref = bf16[2,256,192]{2,1,0:T(8,128)(2,1)S(1)} custom-call(f32[64,512]{1,0:T(8,128)S(1)} %get-tuple-element.42.unread.refs_0_, f32[328,128]{1,0:T(8,128)S(1)} %collective-permute-done.refs_0_, f32[328,128]{1,0:T(8,128)S(1)} %collective-permute-done.1.refs_1_, bf16[6,2,256,256]{3,2,1,0:T(8,128)(2,1)S(1)} %get-tuple-element.34.refs_2_.refs_5_, ...), custom_call_target="tpu_custom_call" | custom-call | flops 3000000000 | bytes 1048576 | tf_op jit(solution)/shard_map/pallas_call | solution.py:759
  37.3 0.3 collective-permute-done.9.refs_3_
  37.6 0.9 %collective-permute-done.8.refs_1_.matrix_last = f32[64,512]{1,0:T(8,128)S(1)} collective-permute-done((f32[64,512]{1,0:T(8,128)S(1)}, f32[64,512]{1,0:T(8,128)S(1)}, u32[]{:S(2)}, u32[]{:S(2)}) %collective-permute-start.8) | collective-permute-done | bytes 131104 | tf_op jit(solution)/shard_map/ppermute | solution.py:808
  38.5 7.2 %shard_map.53.here_ref.here_answer = f32[192,128]{1,0:T(8,128)S(1)} custom-call(f32[64,512]{1,0:T(8,128)S(1)} %get-tuple-element.42.unread.refs_0_, f32[64,512]{1,0:T(8,128)S(1)} %collective-permute-done.8.refs_1_.matrix_last, f32[64,384]{1,0:T(8,128)S(1)} %get-tuple-element.47.refs_2_, f32[64,384]{1,0:T(8,128)S(1)} %collective-permute-done.9.refs_3_, ...), custom_call_target="tpu_custom_call" | custom-call | flops 7000000000 | bytes 1048576 | tf_op jit(solution)/shard_map/pallas_call | solution.py:769
  45.7 0.1 collective-permute-start.10
  45.8 1.3 %collective-permute-done.10.there_ref.there_answer = f32[192,128]{1,0:T(8,128)S(1)} collective-permute-done((f32[192,128]{1,0:T(8,128)S(1)}, f32[192,128]{1,0:T(8,128)S(1)}, u32[]{:S(2)}, u32[]{:S(2)}) %collective-permute-start.10) | collective-permute-done | bytes 98336 | tf_op jit(solution)/shard_map/ppermute | solution.py:812
  47.2 2.1 %collective-permute-start.11 = (f32[32,128]{1,0:T(8,128)S(1)}, f32[32,128]{1,0:T(8,128)S(1)}, u32[]{:S(2)}, u32[]{:S(2)}) collective-permute-start(f32[32,128]{1,0:T(8,128)S(1)} %get-tuple-element.49), channel_id=1, source_target_pairs={{0,24},{8,16},{16,8},{24,0},{1,25},{9,17},{17,9},{25,1},{2,26},{10... | collective-permute-start | bytes 49160 | tf_op jit(solution)/shard_map/ppermute | solution.py:88
  49.2 0.0 collective-permute-start.12
  49.2 2.3 %shard_map.55.refs_2_ = f32[1536,128]{1,0:T(8,128)} custom-call(f32[8,128]{1,0:T(8,128)S(1)} %get-tuple-element.29.flag_ref, f32[6,32,256]{2,1,0:T(8,128)S(1)} %get-tuple-element.39.product_ref.refs_3_, bf16[2,2,256,256]{3,2,1,0:T(8,128)(2,1)S(1)} %get-tuple-element.45.refs_6_.early_inverse, ...), custom_call_target="tpu_custom_call" | custom-call | flops 1000000000 | bytes 1048576 | tf_op jit(solution)/shard_map/pallas_call | solution.py:821
  51.5 1.2 %collective-permute-done.11.refs_0_ = f32[32,128]{1,0:T(8,128)S(1)} collective-permute-done((f32[32,128]{1,0:T(8,128)S(1)}, f32[32,128]{1,0:T(8,128)S(1)}, u32[]{:S(2)}, u32[]{:S(2)}) %collective-permute-start.11) | collective-permute-done | bytes 16416 | tf_op jit(solution)/shard_map/ppermute | solution.py:88
  52.8 0.2 collective-permute-done.12.refs_1_
  53.0 1.0 %shard_map.56 = f32[1536,128]{1,0:T(8,128)} custom-call(bf16[2,256,192]{2,1,0:T(8,128)(2,1)S(1)} %shard_map.52.refs_4_.spread_ref, f32[64,128]{1,0:T(8,128)S(1)} %get-tuple-element.48.rows_ref, f32[32,128]{1,0:T(8,128)S(1)} %collective-permute-done.11.refs_0_, f32[32,128]{1,0:T(8,128)S(1)} %collective-permute-done.12.refs_1_, ...), custom_call_target="tpu_custom_call", output_to_operand_aliasing={{}: (4, {})} | custom-call | flops 1000000000 | bytes 1048576 | tf_op jit(solution)/shard_map/pallas_call | solution.py:856
  (2 shorter events, 0.1 us)
Async XLA Ops:
  0.0 9.9 %copy-start.1 = (s32[8]{0:T(128)S(1)}, s32[8]{0:T(128)}, u32[]{:S(2)}) copy-start(s32[8]{0:T(128)} %group_ref.1) | copy-start | bytes 100
  1.7 11.0 %collective-permute-start.4 = (f32[2,264,128]{2,1,0:T(8,128)S(1)}, f32[2,264,128]{2,1,0:T(8,128)S(1)}, u32[]{:S(2)}, u32[]{:S(2)}) collective-permute-start(f32[2,264,128]{2,1,0:T(8,128)S(1)} %get-tuple-element.36), channel_id=1, source_target_pairs={{0,1},{1,0},{2,3},{3,2},{4,5},{5,4},{6,7},{7,6},{8,9},{9,8},{10,11... | collective-permute-start | bytes 811016 | tf_op jit(solution)/shard_map/ppermute | solution.py:86
  4.7 10.9 %collective-permute-start = (f32[328,128]{1,0:T(8,128)S(1)}, f32[328,128]{1,0:T(8,128)S(1)}, u32[]{:S(2)}, u32[]{:S(2)}) collective-permute-start(f32[328,128]{1,0:T(8,128)S(1)} %get-tuple-element.30), channel_id=1, source_target_pairs={{0,24},{8,16},{16,8},{24,0},{1,25},{9,17},{17,9},{25,1},{2,26},{10... | collective-permute-start | bytes 503816 | tf_op jit(solution)/shard_map/ppermute | solution.py:88
  8.3 7.7 %collective-permute-start.1 = (f32[328,128]{1,0:T(8,128)S(1)}, f32[328,128]{1,0:T(8,128)S(1)}, u32[]{:S(2)}, u32[]{:S(2)}) collective-permute-start(f32[328,128]{1,0:T(8,128)S(1)} %get-tuple-element.31), channel_id=1, source_target_pairs={{0,8},{8,0},{16,24},{24,16},{1,9},{9,1},{17,25},{25,17},{2,10},{10... | collective-permute-start | bytes 503816 | tf_op jit(solution)/shard_map/ppermute | solution.py:89
  8.3 7.7 %collective-permute-start.2 = (f32[328,128]{1,0:T(8,128)S(1)}, f32[328,128]{1,0:T(8,128)S(1)}, u32[]{:S(2)}, u32[]{:S(2)}) collective-permute-start(f32[328,128]{1,0:T(8,128)S(1)} %get-tuple-element.32), channel_id=1, source_target_pairs={{0,6},{2,4},{4,2},{6,0},{1,7},{3,5},{5,3},{7,1},{8,14},{10,12},{12... | collective-permute-start | bytes 503816 | tf_op jit(solution)/shard_map/ppermute | solution.py:88
  8.7 7.3 %collective-permute-start.3 = (f32[328,128]{1,0:T(8,128)S(1)}, f32[328,128]{1,0:T(8,128)S(1)}, u32[]{:S(2)}, u32[]{:S(2)}) collective-permute-start(f32[328,128]{1,0:T(8,128)S(1)} %get-tuple-element.33), channel_id=1, source_target_pairs={{0,2},{2,0},{4,6},{6,4},{1,3},{3,1},{5,7},{7,5},{8,10},{10,8},{12,... | collective-permute-start | bytes 503816 | tf_op jit(solution)/shard_map/ppermute | solution.py:89
  9.9 2.7 %copy-start = (f32[1,1,1,6,256,32]{4,5,3,2,1,0:T(8,128)S(1)}, f32[1,1,1,6,256,32]{4,5,3,2,1,0:T(8,128)}, u32[]{:S(2)}) copy-start(f32[1,1,1,6,256,32]{4,5,3,2,1,0:T(8,128)} %param.5) | copy-start | bytes 589828
  12.6 3.4 %copy-start.2 = (f32[1,1,1,1536,128]{4,3,2,1,0:T(8,128)S(1)}, f32[1,1,1,1536,128]{4,3,2,1,0:T(8,128)}, u32[]{:S(2)}) copy-start(f32[1,1,1,1536,128]{4,3,2,1,0:T(8,128)} %param.6) | copy-start | bytes 2359300
  24.4 1.6 %collective-permute-start.5 = (f32[64,1024]{1,0:T(8,128)S(1)}, f32[64,1024]{1,0:T(8,128)S(1)}, u32[]{:S(2)}, u32[]{:S(2)}) collective-permute-start(f32[64,1024]{1,0:T(8,128)S(1)} %get-tuple-element.38.here_ref), channel_id=1, source_target_pairs={{0,2},{2,0},{4,6},{6,4},{1,3},{3,1},{5,7},{7,5},{8,10},{10,8},{12,... | collective-permute-start | bytes 786440 | tf_op jit(solution)/shard_map/ppermute | solution.py:791
  26.1 5.6 %collective-permute-start.6 = (f32[64,512]{1,0:T(8,128)S(1)}, f32[64,512]{1,0:T(8,128)S(1)}, u32[]{:S(2)}, u32[]{:S(2)}) collective-permute-start(f32[64,512]{1,0:T(8,128)S(1)} %get-tuple-element.40.first_ref), channel_id=1, source_target_pairs={{0,4},{2,6},{4,0},{6,2},{1,5},{3,7},{5,1},{7,3},{8,12},{10,14},{12... | collective-permute-start | bytes 393224 | tf_op jit(solution)/shard_map/ppermute | solution.py:799
  27.7 5.3 %collective-permute-start.7 = (f32[64,512]{1,0:T(8,128)S(1)}, f32[64,512]{1,0:T(8,128)S(1)}, u32[]{:S(2)}, u32[]{:S(2)}) collective-permute-start(f32[64,512]{1,0:T(8,128)S(1)} %get-tuple-element.41.third_ref), channel_id=1, source_target_pairs={{0,1},{1,0},{2,3},{3,2},{4,5},{5,4},{6,7},{7,6},{8,9},{9,8},{10,11... | collective-permute-start | bytes 393224 | tf_op jit(solution)/shard_map/ppermute | solution.py:800
  33.0 4.7 %collective-permute-start.9 = (f32[64,384]{1,0:T(8,128)S(1)}, f32[64,384]{1,0:T(8,128)S(1)}, u32[]{:S(2)}, u32[]{:S(2)}) collective-permute-start(f32[64,384]{1,0:T(8,128)S(1)} %get-tuple-element.47.refs_2_), channel_id=1, source_target_pairs={{0,4},{2,6},{4,0},{6,2},{1,5},{3,7},{5,1},{7,3},{8,12},{10,14},{12... | collective-permute-start | bytes 294920 | tf_op jit(solution)/shard_map/ppermute | solution.py:809
  33.6 5.0 %collective-permute-start.8 = (f32[64,512]{1,0:T(8,128)S(1)}, f32[64,512]{1,0:T(8,128)S(1)}, u32[]{:S(2)}, u32[]{:S(2)}) collective-permute-start(f32[64,512]{1,0:T(8,128)S(1)} %get-tuple-element.42.unread.refs_0_), channel_id=1, source_target_pairs={{0,1},{1,0},{2,3},{3,2},{4,5},{5,4},{6,7},{7,6},{8,9},{9,8},{10,11... | collective-permute-start | bytes 393224 | tf_op jit(solution)/shard_map/ppermute | solution.py:808
  45.7 1.4 %collective-permute-start.10 = (f32[192,128]{1,0:T(8,128)S(1)}, f32[192,128]{1,0:T(8,128)S(1)}, u32[]{:S(2)}, u32[]{:S(2)}) collective-permute-start(f32[192,128]{1,0:T(8,128)S(1)} %shard_map.53.here_ref.here_answer), channel_id=1, source_target_pairs={{0,2},{2,0},{4,6},{6,4},{1,3},{3,1},{5,7},{7,5},{8,10},{10,8},{12,... | collective-permute-start | bytes 294920 | tf_op jit(solution)/shard_map/ppermute | solution.py:812
  47.2 5.6 %collective-permute-start.11 = (f32[32,128]{1,0:T(8,128)S(1)}, f32[32,128]{1,0:T(8,128)S(1)}, u32[]{:S(2)}, u32[]{:S(2)}) collective-permute-start(f32[32,128]{1,0:T(8,128)S(1)} %get-tuple-element.49), channel_id=1, source_target_pairs={{0,24},{8,16},{16,8},{24,0},{1,25},{9,17},{17,9},{25,1},{2,26},{10... | collective-permute-start | bytes 49160 | tf_op jit(solution)/shard_map/ppermute | solution.py:88
  49.2 3.7 %collective-permute-start.12 = (f32[32,128]{1,0:T(8,128)S(1)}, f32[32,128]{1,0:T(8,128)S(1)}, u32[]{:S(2)}, u32[]{:S(2)}) collective-permute-start(f32[32,128]{1,0:T(8,128)S(1)} %get-tuple-element.50), channel_id=1, source_target_pairs={{0,8},{8,0},{16,24},{24,16},{1,9},{9,1},{17,25},{25,17},{2,10},{10... | collective-permute-start | bytes 49160 | tf_op jit(solution)/shard_map/ppermute | solution.py:89

commit v10 on v9

--- a/solution.py
+++ b/solution.py
@@ -418,11 +418,10 @@
     for g in range(FACES):
         tall = jnp.concatenate([sides[f][g] for f in range(g + 1)], axis=0)
         blocks.append(triple(triple(tall, vectors[g], ((1,), (1,))), factors[g], ((1,), (1,))))
-    even, odd, right, products = [], [], [], []
+    even, odd, right = [], [], []
     lows = None
     for f in range(FACES):
-        products.append(triple(factors[f], sides[f][f]))
-        product_ref[f] = products[f]
+        product_ref[f] = triple(factors[f], sides[f][f])
         line = [blocks[g][f * ncon : (f + 1) * ncon] for g in range(f, FACES)]
         line = triple(factors[f], jnp.concatenate([rights[f]] + line, axis=1))
         right.append(line[:, :columns])
@@ -432,26 +431,13 @@
             lows = line[:, ncon : 2 * ncon].T
         else:
             odd += [lows, line]
-    upward = is_even("gy")
-    inner = jnp.where(upward, products[3], products[2])
-    outer = jnp.where(upward, products[2], products[3])
-    whole = [
-        jnp.concatenate(even + right[0::2], axis=1),
-        jnp.concatenate(odd + right[1::2], axis=1),
-    ]
     payload_ref[...] = jnp.concatenate(
-        [jnp.concatenate(whole, axis=0), fold(inner), fold(outer)], axis=1
+        [
+            jnp.concatenate(even + right[0::2], axis=1),
+            jnp.concatenate(odd + right[1::2], axis=1),
+        ],
+        axis=0,
     )
-
-
-def fold(product):
-    half = product.shape[1] // 2
-    return jnp.concatenate([product[:, :half], product[:, half:]], axis=0)
-
-
-def unfold(rows):
-    half = rows.shape[0] // 2
-    return jnp.concatenate([rows[:half], rows[half:]], axis=1)
 
 
 def find(faces, refs, f):
@@ -460,45 +446,54 @@
             return load(ref, list(group).index(f))
 
 
-def spread_kernel(faces, ncon, unread, *refs):
-    packed = receive(refs[:-7], AXES[0])
-    own_ref, product_ref = refs[-7:-5]
-    partner_refs, inverse_refs, out_ref = refs[-5:-3], refs[-3:-1], refs[-1]
-    basis = [unpack_starts(part, ncon) for part in packed]
+def theirs_kernel(faces, ncon, own_ref, *refs):
+    inputs, partner_refs, inverse_refs = refs[:-6], refs[-6:-4], refs[-4:-2]
+    basis_out, product_out = refs[-2:]
+    basis = []
+    done = 0
+    for axis in AXES[:2]:
+        number = face_arrays(lax.axis_size(axis))
+        packed = receive(inputs[done : done + number], axis)
+        basis += [unpack_starts(part, ncon) for part in packed]
+        done += number
+    count = len(basis)
     matrices = [
-        [load(own_ref, f) for f in range(2)],
-        [find(faces, inverse_refs, f) for f in range(2)],
-        [find(faces, partner_refs, f) for f in range(2)],
+        [load(own_ref, f) for f in range(count)],
+        [find(faces, inverse_refs, f) for f in range(count)],
+        [find(faces, partner_refs, f) for f in range(count)],
     ]
     for sweep in range(SUB_ITERS):
         basis = sweep_basis(*matrices, basis)
+    for f in range(count):
+        basis_out[f] = basis[f]
+        product_out[f] = thin(stacked(basis[f]), matrices[2][f])
+
+
+def spread_kernel(faces, unread, basis_ref, theirs_ref, product_ref, *refs):
+    inverse_refs, out_ref = refs[:2], refs[2]
+    basis = [basis_ref[f] for f in range(basis_ref.shape[0])]
     factors = factor_inverses([dot(b, b, ((1,), (1,))) for b in basis])
-    for f in range(2):
-        theirs = triple(factors[f], thin(stacked(basis[f]), matrices[2][f]))
+    for f in range(len(basis)):
+        theirs = triple(factors[f], theirs_ref[f])
         both = jnp.concatenate([product_ref[f], theirs], axis=0)
-        high, low = split(thin(stacked(both), matrices[1][f]).T)
+        high, low = split(thin(stacked(both), find(faces, inverse_refs, f)).T)
         out_ref[f] = jnp.concatenate([high, high, low], axis=1)
 
 
-def choose_kernel(flag_ref, here_ref, there_ref, product_ref, matrix_ref, right_ref):
+def choose_kernel(flag_ref, here_ref, there_ref, matrix_ref, right_ref):
     mine = flag_ref[0:1, 0:1] > 0.5
     other = flag_ref[1:2, 0:1] > 0.5
-    half = product_ref.shape[2] // 2
-    lanes, wide_lanes = matrix_ref.shape[1] - half, here_ref.shape[1] - 2 * half
-    here, there = here_ref[:, :wide_lanes], there_ref[:, :wide_lanes]
-    total = jnp.where(mine, here, 0.0) + jnp.where(other, there, 0.0)
-    outer = there_ref[:, wide_lanes + half :]
-    matrix_ref[...] = jnp.concatenate([total[:, :lanes], outer], axis=1)
-    right_ref[...] = jnp.concatenate([total[:, lanes:], fold(product_ref[4])], axis=1)
-
-
-def add_kernel(first_ref, second_ref, third_ref, fourth_ref, product_ref, *refs):
-    matrix_ref, right_ref = refs
-    half = product_ref.shape[2] // 2
-    lanes, right_lanes = matrix_ref.shape[1] - half, right_ref.shape[1]
-    total = first_ref[:, :lanes] + second_ref[:, :lanes]
-    matrix_ref[...] = jnp.concatenate([total, fold(product_ref[5])], axis=1)
-    right_ref[...] = third_ref[:, :right_lanes] + fourth_ref[:, :right_lanes]
+    total = jnp.where(mine, here_ref[...], 0.0) + jnp.where(other, there_ref[...], 0.0)
+    lanes = matrix_ref.shape[1]
+    matrix_ref[...] = total[:, :lanes]
+    right_ref[...] = total[:, lanes:]
+
+
+def add_kernel(first_ref, second_ref, third_ref, fourth_ref, product_ref, unread, *refs):
+    matrix_ref, right_ref, *sent = refs
+    matrix_ref[...] = first_ref[...] + second_ref[...]
+    right_ref[...] = third_ref[...] + fourth_ref[...]
+    send(sent, AXES[2], product_ref[4], product_ref[5])
 
 
 def solve_kernel(size, terms, columns, *refs):
@@ -588,72 +583,54 @@
         copy.wait()
 
 
-def last_plain_kernel(faces, product_ref, early_inverse, late_inverse, answer_ref, *refs):
-    inputs, rest = refs[:-3], refs[-3:]
+def last_plain_kernel(faces, product_ref, early_inverse, late_inverse, *refs):
+    spread_ref, answer_ref, *inputs = refs[:-3]
     ncon, width = product_ref.shape[1:]
+    number = face_arrays(lax.axis_size(AXES[2]))
+    theirs = receive(inputs[:number], AXES[2])
+    near = receive(inputs[number:-number], AXES[1]) + receive(inputs[-number:], AXES[2])
     values = {}
-    done = 0
-    near = []
-    for axis in AXES[1:] * 2:
-        number = face_arrays(lax.axis_size(axis))
-        near += receive(inputs[done : done + number], axis)
-        done += number
     for f in range(2, FACES):
+        mine = answer_ref[f * ncon : (f + 1) * ncon]
+        if f < 4:
+            values[f] = functools.partial(last_product, spread_ref[f], mine, near[f - 2])
+        else:
+            values[f] = functools.partial(
+                through,
+                find(faces, (early_inverse, late_inverse), f),
+                product_ref[f],
+                theirs[f - 4],
+                mine,
+                near[f - 2],
+            )
+    last_faces(values, width, *refs[-3:])
+
+
+def last_near_kernel(faces, flag_ref, product_ref, early_inverse, late_inverse, *refs):
+    spread_ref, here_answer, there_answer = refs[:3]
+    theirs = receive(refs[3:-3], AXES[2])
+    ncon, width = product_ref.shape[1:]
+
+    def answer(flag, f):
+        place = slice(f * ncon, (f + 1) * ncon)
+        hit = flag_ref[flag : flag + 1, 0:1] > 0.5
+        return jnp.where(hit, here_answer[place], there_answer[place])
+
+    values = {}
+    for f in (2, 3):
+        values[f] = functools.partial(
+            last_product, spread_ref[f], answer(0, f), answer(f, f ^ 1)
+        )
+    for f in (4, 5):
         values[f] = functools.partial(
             through,
             find(faces, (early_inverse, late_inverse), f),
             product_ref[f],
-            near[f - 2],
-            answer_ref[f * ncon : (f + 1) * ncon],
-            near[f + 2],
-        )
-    last_faces(values, width, *rest)
-
-
-def last_near_kernel(
-    faces,
-    columns,
-    flag_ref,
-    product_ref,
-    early_inverse,
-    late_inverse,
-    there_ref,
-    matrix_ref,
-    right_ref,
-    matrix_last,
-    here_answer,
-    there_answer,
-    *refs,
-):
-    ncon, width = product_ref.shape[1:]
-    half = width // 2
-    lanes = matrix_ref.shape[1] - half
-    inner = unfold(there_ref[:, lanes + BLOCKS * columns : lanes + BLOCKS * columns + half])
-    outer = unfold(matrix_ref[:, lanes:])
-    upward = is_even("gy")
-    theirs = {
-        2: jnp.where(upward, outer, inner),
-        3: jnp.where(upward, inner, outer),
-        4: unfold(matrix_last[:, lanes:]),
-        5: unfold(right_ref[:, BLOCKS * columns :]),
-    }
-
-    def answer(flag, f):
-        place = slice(f * ncon, (f + 1) * ncon)
-        hit = flag_ref[flag : flag + 1, 0:1] > 0.5
-        return jnp.where(hit, here_answer[place], there_answer[place])
-
-    values = {}
-    for f in range(2, FACES):
-        values[f] = functools.partial(
-            through,
-            find(faces, (early_inverse, late_inverse), f),
-            product_ref[f],
-            theirs[f],
+            theirs[f - 4],
             answer(0, f),
             answer(f, f ^ 1),
         )
-    last_faces(values, width, *refs)
+    last_faces(values, width, *refs[-3:])
 
 
 def last_far_kernel(ncon, spread_ref, rows_ref, *refs):
@@ -744,7 +721,7 @@
 
     payload, product, late_partner, late_inverse = pl.pallas_call(
         functools.partial(main_kernel, (AXES[0], AXES[1]), early, late),
-        out_shape=[shape(size, lanes + right_lanes + 2 * half), shape(FACES, ncon, width)]
+        out_shape=[shape(size, lanes + right_lanes), shape(FACES, ncon, width)]
         + [halves(len(late))] * 2,
         in_specs=vmem_specs(len(got[0]) + len(got[1]) + 6),
         out_specs=vmem_specs(4),
@@ -755,15 +732,24 @@
 
     partners = [early_partner, late_partner]
     inverses = [early_inverse, late_inverse]
+    their_basis, their_product = pl.pallas_call(
+        functools.partial(theirs_kernel, faces, ncon),
+        out_shape=[shape(4, ncon, width)] * 2,
+        in_specs=vmem_specs(5 + len(got[0]) + len(got[1])),
+        out_specs=vmem_specs(2),
+        compiler_params=params(16),
+        cost_estimate=cost(2),
+    )(own_halves, *got[0], *got[1], *partners, *inverses)
+
     def spread_of(token):
         return pl.pallas_call(
-            functools.partial(spread_kernel, faces, ncon),
-            out_shape=jax.ShapeDtypeStruct((2, width, 3 * size), jnp.bfloat16),
-            in_specs=[anywhere] + vmem_specs(len(got[0]) + 6),
+            functools.partial(spread_kernel, faces),
+            out_shape=jax.ShapeDtypeStruct((4, width, 3 * size), jnp.bfloat16),
+            in_specs=[anywhere] + vmem_specs(5),
             out_specs=vmem_specs(1)[0],
             compiler_params=params(16),
-            cost_estimate=cost(3),
-        )(token, *got[0], own_halves, product, *partners, *inverses)
+            cost_estimate=cost(2),
+        )(token, their_basis, their_product, product, *inverses)
 
     def solve(matrices, rights, unread):
         return pl.pallas_call(
@@ -791,22 +777,24 @@
         other = lax.ppermute(payload, "gy", core_swap)
         left, rest = pl.pallas_call(
             choose_kernel,
-            out_shape=[shape(size, lanes + half), shape(size, right_lanes + half)],
-            in_specs=vmem_specs(4),
+            out_shape=[shape(size, lanes), shape(size, right_lanes)],
+            in_specs=vmem_specs(3),
             out_specs=vmem_specs(2),
             compiler_params=params(8),
-        )(flags, payload, other, product)
+        )(flags, payload, other)
         left_moved = lax.ppermute(left, "gy", chip_x)
         rest_moved = lax.ppermute(rest, "gz", chip_y)
-        left_last, rest_last = pl.pallas_call(
+        left_last, rest_last, *sent = pl.pallas_call(
             add_kernel,
-            out_shape=[shape(size, lanes + half), shape(size, right_lanes)],
-            in_specs=vmem_specs(5),
-            out_specs=vmem_specs(2),
+            out_shape=[shape(size, lanes), shape(size, right_lanes)]
+            + face_shapes(counts[2], (ncon, width)),
+            in_specs=vmem_specs(5) + [anywhere],
+            out_specs=vmem_specs(2 + face_arrays(counts[2])),
             compiler_params=params(8),
-        )(left, left_moved, rest, rest_moved, product)
+        )(left, left_moved, rest, rest_moved, product, their_basis)
         left_other = lax.ppermute(left_last, "gz", chip_y)
         rest_other = lax.ppermute(rest_last, "gy", chip_x)
+        theirs = exchange(sent, AXES[2])
         spread = spread_of(left_last)
         answer = solve([left_last, left_other], [rest_last, rest_other], [spread])
         there = lax.ppermute(answer, "gy", core_swap)
@@ -819,18 +807,15 @@
         )(flags, answer, there)
         across = exchange(sent, AXES[0])
         correction = pl.pallas_call(
-            functools.partial(last_near_kernel, faces, columns),
-            in_specs=vmem_specs(10),
+            functools.partial(last_near_kernel, faces),
+            in_specs=vmem_specs(7 + len(theirs)),
             **result,
-        )(
-            flags, product, *inverses, other, left_moved, rest_moved, left_other, answer, there
-        )
+        )(flags, product, *inverses, spread, answer, there, *theirs)
     else:
         y, z = lax.axis_index("gy"), lax.axis_index("gz")
         member_of = group_of[y * planes + z]
         chosen = jnp.arange(groups, dtype=jnp.int32) == member_of
-        part = payload[:, : lanes + right_lanes]
-        total = lax.psum(jnp.where(chosen[:, None, None], part[None], 0.0), ("gy", "gz"))
+        total = lax.psum(jnp.where(chosen[:, None, None], payload[None], 0.0), ("gy", "gz"))
         total = lax.dynamic_index_in_dim(total, member_of, 0, keepdims=False)
         spread = spread_of(payload)
         answer = solve([total[:, :lanes]], [total[:, lanes:]], [])
@@ -843,16 +828,18 @@
             return exchange([jnp.where(upward, even, odd), jnp.where(upward, odd, even)], axis)
 
         blocks = answer.reshape(FACES, ncon, columns)
-        near = []
-        for parts in (product, blocks):
-            near += from_near(parts[2:4], AXES[1]) + from_near(parts[4:6], AXES[2])
+        near = [
+            *from_near(product[4:6], AXES[2]),
+            *from_near(blocks[2:4], AXES[1]),
+            *from_near(blocks[4:6], AXES[2]),
+        ]
         mine = answer[:size]
         across = from_near(blocks[:2], AXES[0])
         correction = pl.pallas_call(
             functools.partial(last_plain_kernel, faces),
-            in_specs=vmem_specs(4 + len(near)),
+            in_specs=vmem_specs(5 + len(near)),
             **result,
-        )(product, *inverses, answer, *near)
+        )(product, *inverses, spread, answer, *near)
     correction = pl.pallas_call(
         functools.partial(last_far_kernel, ncon),
         in_specs=vmem_specs(2 + len(across)) + [main_memory],

time: 54.3 us -> 53.5 us (0.985)
  waiting for transfers between devices: 10.6 us -> 8.81 us
  starting transfers between devices: 13.6 us -> 14.5 us
    ppermute x1, waiting for transfers between devices: 3.54 us -> 1.27 us  [per_device(): left_moved = lax.ppermute(left, 'gy', chip_x)]
    ppermute x1 -> x2, waiting for transfers between devices: 0.01 us -> 0.8 us  [exchange(): return [lax.ppermute(arrays[0], axis, flipped(axis, 1))]]
    ppermute x1, waiting for transfers between devices: 0.35 us -> 1.14 us  [per_device(): rest_other = lax.ppermute(rest_last, 'gy', chip_x)]
    ppermute x1, waiting for transfers between devices: 1.29 us -> 0.73 us  [per_device(): there = lax.ppermute(answer, 'gy', core_swap)]
    ppermute x1 -> x2, starting transfers between devices: 3.03 us -> 3.59 us  [exchange(): return [lax.ppermute(arrays[0], axis, flipped(axis, 1))]]
    pallas_call x4 -> x5, Pallas kernels: 5.59 us -> 5.77 us  [the longest x1 2.43 us: spread_of(): pl.pallas_call(functools.partial(spread_kernel, faces), out_shape=jax.Sha...]
  transfers between devices with their start and end apart: 13 -> 14, of which waited for: 9 -> 10; matrix products, arithmetic and copies ran while one was open for 0% -> 0% of each run, Pallas kernels for 21% -> 21%
where the time goes in v10:
time: 53.5 us; the launch traced here: 53.3 us
  Pallas kernels  29.7 us (56%)
  starting transfers between devices  14.5 us (27%)
  waiting for transfers between devices  8.81 us (16%)
    pallas_call x1, Pallas kernels, per_device(): pl.pallas_call(functools.partial(main_kernel, (AXES[0], AXES[1]), early,...  8.39 us
    pallas_call x1, Pallas kernels, solve(): pl.pallas_call(functools.partial(solve_kernel, size, len(matrices), colum...  7.19 us
    ppermute x3, starting transfers between devices, exchange(): lax.ppermute(arrays[0], axis, outer_pairs(axis))  6.34 us
    ppermute x2, starting transfers between devices, exchange(): return [lax.ppermute(arrays[0], axis, flipped(axis, 1))]  3.59 us
    pallas_call x1, Pallas kernels, per_device(): pl.pallas_call(functools.partial(early_kernel, AXES[2:3], early), out_sha...  2.98 us
    pallas_call x1, Pallas kernels, per_device(): pl.pallas_call(functools.partial(halves_kernel, planes), out_shape=[halve...  2.7 us
    pallas_call x1, Pallas kernels, spread_of(): pl.pallas_call(functools.partial(spread_kernel, faces), out_shape=jax.Sha...  2.43 us
    pallas_call x1, Pallas kernels, per_device(): pl.pallas_call(functools.partial(pack_kernel, counts, width), out_shape=f...  1.68 us
  transfers between devices with their start and end apart: 14, of which 10 were waited for; matrix products, arithmetic and copies ran while one was open for 0% of the time, Pallas kernels for 21%

profile of v10, /device:TPU:0, one launch (start us, length us, event | category | flops | bytes accessed | tf_op | source)
XLA Modules:
  0.0 53.3 jit_solution(12523305679391319288)
XLA Ops:
  0.0 0.0 copy-start.1
  0.0 1.7 %shard_map.46 = (f32[328,128]{1,0:T(8,128)S(1)}, f32[328,128]{1,0:T(8,128)S(1)}, f32[328,128]{1,0:T(8,128)S(1)}, f32[328,128]{1,0:T(8,128)S(1)}, f32[2,264,128]{2,1,0:T(8,128)S(1)}, /*index=5*/f32[6,256,256]{2,1,0:T(8,128)S(1)}) custom-call(f32[1536,1536]{1,0:T(8,128)} %bitcast.10, f32[6,32,256]{2,1,0:T(8,128)} %bitcast.6), custom_call_target="tpu_custom_call" | custom-call | tf_op jit(solution)/shard_map/pallas_call | solution.py:679
  1.7 3.0 %collective-permute-start.4 = (f32[2,264,128]{2,1,0:T(8,128)S(1)}, f32[2,264,128]{2,1,0:T(8,128)S(1)}, u32[]{:S(2)}, u32[]{:S(2)}) collective-permute-start(f32[2,264,128]{2,1,0:T(8,128)S(1)} %get-tuple-element.39), channel_id=1, source_target_pairs={{0,1},{1,0},{2,3},{3,2},{4,5},{5,4},{6,7},{7,6},{8,9},{9,8},{10,11... | collective-permute-start | bytes 811016 | tf_op jit(solution)/shard_map/ppermute | solution.py:86
  4.7 3.6 %collective-permute-start = (f32[328,128]{1,0:T(8,128)S(1)}, f32[328,128]{1,0:T(8,128)S(1)}, u32[]{:S(2)}, u32[]{:S(2)}) collective-permute-start(f32[328,128]{1,0:T(8,128)S(1)} %get-tuple-element.33), channel_id=1, source_target_pairs={{0,24},{8,16},{16,8},{24,0},{1,25},{9,17},{17,9},{25,1},{2,26},{10... | collective-permute-start | bytes 503816 | tf_op jit(solution)/shard_map/ppermute | solution.py:88
  8.3 0.0 collective-permute-start.1
  8.3 0.4 collective-permute-start.2
  8.7 1.2 %collective-permute-start.3 = (f32[328,128]{1,0:T(8,128)S(1)}, f32[328,128]{1,0:T(8,128)S(1)}, u32[]{:S(2)}, u32[]{:S(2)}) collective-permute-start(f32[328,128]{1,0:T(8,128)S(1)} %get-tuple-element.36), channel_id=1, source_target_pairs={{0,2},{2,0},{4,6},{6,4},{1,3},{3,1},{5,7},{7,5},{8,10},{10,8},{12,... | collective-permute-start | bytes 503816 | tf_op jit(solution)/shard_map/ppermute | solution.py:89
  9.9 0.0 copy-done.1
  9.9 0.0 copy-start
  9.9 2.7 %shard_map.47 = (bf16[6,2,256,256]{3,2,1,0:T(8,128)(2,1)S(1)}, bf16[15,2,256,256]{3,2,1,0:T(8,128)(2,1)S(1)}, f32[8,128]{1,0:T(8,128)S(1)}) custom-call(f32[1536,1536]{1,0:T(8,128)} %bitcast.11, s32[8]{0:T(128)S(1)} %copy-done.1, f32[6,256,256]{2,1,0:T(8,128)S(1)} %get-tuple-element.31.own_ref.refs_1_.refs_4_), custom_call_target="tpu_custom_call" | custom-call | flops 2000000000 | bytes 1048576 | tf_op jit(solution)/shard_map/pallas_call | solution.py:699
  12.6 0.0 copy-start.2
  12.7 0.0 collective-permute-done.4.refs_0_
  12.7 0.0 copy-done
  12.7 3.0 %shard_map.48 = (f32[2,32,256]{2,1,0:T(8,128)S(1)}, bf16[2,2,256,256]{3,2,1,0:T(8,128)(2,1)S(1)}, bf16[2,2,256,256]{3,2,1,0:T(8,128)(2,1)S(1)}) custom-call(f32[2,264,128]{2,1,0:T(8,128)S(1)} %collective-permute-done.4.refs_0_, f32[6,256,256]{2,1,0:T(8,128)S(1)} %get-tuple-element.31.own_ref.refs_1_.refs_4_, ...), custom_call_target="tpu_custom_call" | custom-call | flops 2000000000 | bytes 1048576 | tf_op jit(solution)/shard_map/pallas_call | solution.py:712
  15.7 0.0 collective-permute-done.refs_0_
  15.7 0.4 collective-permute-done.1.refs_1_
  16.0 0.0 collective-permute-done.2.refs_2_
  16.0 0.0 collective-permute-done.3.refs_3_
  16.0 0.0 copy-done.2
  16.0 8.4 %shard_map.49 = (f32[64,768]{1,0:T(8,128)S(1)}, f32[6,32,256]{2,1,0:T(8,128)S(1)}, bf16[4,2,256,256]{3,2,1,0:T(8,128)(2,1)S(1)}, bf16[4,2,256,256]{3,2,1,0:T(8,128)(2,1)S(1)}) custom-call(f32[328,128]{1,0:T(8,128)S(1)} %collective-permute-done.refs_0_, f32[328,128]{1,0:T(8,128)S(1)} %collective-permute-done.1.refs_1_, ...), custom_call_target="tpu_custom_call" | custom-call | flops 8000000000 | bytes 1048576 | tf_op jit(solution)/shard_map/pallas_call | solution.py:722
  24.4 0.1 collective-permute-start.5
  24.5 1.4 %collective-permute-done.5.there_ref = f32[64,768]{1,0:T(8,128)S(1)} collective-permute-done((f32[64,768]{1,0:T(8,128)S(1)}, f32[64,768]{1,0:T(8,128)S(1)}, u32[]{:S(2)}, u32[]{:S(2)}) %collective-permute-start.5) | collective-permute-done | bytes 196640 | tf_op jit(solution)/shard_map/ppermute | solution.py:777
  25.9 0.1 shard_map.50
  26.0 1.5 %collective-permute-start.6 = (f32[64,384]{1,0:T(8,128)S(1)}, f32[64,384]{1,0:T(8,128)S(1)}, u32[]{:S(2)}, u32[]{:S(2)}) collective-permute-start(f32[64,384]{1,0:T(8,128)S(1)} %get-tuple-element.42.first_ref), channel_id=1, source_target_pairs={{0,4},{2,6},{4,0},{6,2},{1,5},{3,7},{5,1},{7,3},{8,12},{10,14},{12... | collective-permute-start | bytes 294920 | tf_op jit(solution)/shard_map/ppermute | solution.py:785
  27.6 0.5 collective-permute-start.7
  28.1 1.6 %shard_map.51 = (f32[4,32,256]{2,1,0:T(8,128)S(1)}, f32[4,32,256]{2,1,0:T(8,128)S(1)}) custom-call(bf16[6,2,256,256]{3,2,1,0:T(8,128)(2,1)S(1)} %get-tuple-element.37.refs_2_.refs_5_.own_ref, f32[328,128]{1,0:T(8,128)S(1)} %collective-permute-done.refs_0_, f32[328,128]{1,0:T(8,128)S(1)} %collective-permute-done.1.refs_1_, ...), custom_call_target="tpu_custom_call" | custom-call | flops 2000000000 | bytes 1048576 | tf_op jit(solution)/shard_map/pallas_call | solution.py:735
  29.7 1.3 %collective-permute-done.6.second_ref = f32[64,384]{1,0:T(8,128)S(1)} collective-permute-done((f32[64,384]{1,0:T(8,128)S(1)}, f32[64,384]{1,0:T(8,128)S(1)}, u32[]{:S(2)}, u32[]{:S(2)}) %collective-permute-start.6) | collective-permute-done | bytes 98336 | tf_op jit(solution)/shard_map/ppermute | solution.py:785
  30.9 1.3 %collective-permute-done.7.fourth_ref = f32[64,384]{1,0:T(8,128)S(1)} collective-permute-done((f32[64,384]{1,0:T(8,128)S(1)}, f32[64,384]{1,0:T(8,128)S(1)}, u32[]{:S(2)}, u32[]{:S(2)}) %collective-permute-start.7) | collective-permute-done | bytes 98336 | tf_op jit(solution)/shard_map/ppermute | solution.py:786
  32.2 0.6 %collective-permute-start.9 = (f32[64,384]{1,0:T(8,128)S(1)}, f32[64,384]{1,0:T(8,128)S(1)}, u32[]{:S(2)}, u32[]{:S(2)}) collective-permute-start(f32[64,384]{1,0:T(8,128)S(1)} %get-tuple-element.52.refs_2_), channel_id=1, source_target_pairs={{0,4},{2,6},{4,0},{6,2},{1,5},{3,7},{5,1},{7,3},{8,12},{10,14},{12... | collective-permute-start | bytes 294920 | tf_op jit(solution)/shard_map/ppermute | solution.py:796
  32.8 0.5 collective-permute-start.8
  33.3 2.4 %shard_map.53.refs_4_.refs_0_.spread_ref = bf16[4,256,192]{2,1,0:T(8,128)(2,1)S(1)} custom-call(f32[64,384]{1,0:T(8,128)S(1)} %get-tuple-element.50.unread.refs_0_, f32[4,32,256]{2,1,0:T(8,128)S(1)} %get-tuple-element.49.unread.basis_ref, f32[4,32,256]{2,1,0:T(8,128)S(1)} %get-tuple-element.51.theirs_ref, f32[6,32,256]{2,1,0:T(8,128)S(1)} %get-tuple-element.44.product_ref, ...), custom_call_target="tpu_custom_call" | custom-call | flops 2000000000 | bytes 1048576 | tf_op jit(solution)/shard_map/pallas_call | solution.py:745
  35.8 1.1 %collective-permute-done.9.refs_3_ = f32[64,384]{1,0:T(8,128)S(1)} collective-permute-done((f32[64,384]{1,0:T(8,128)S(1)}, f32[64,384]{1,0:T(8,128)S(1)}, u32[]{:S(2)}, u32[]{:S(2)}) %collective-permute-start.9) | collective-permute-done | bytes 98336 | tf_op jit(solution)/shard_map/ppermute | solution.py:796
  36.9 0.6 %collective-permute-done.8.refs_1_ = f32[64,384]{1,0:T(8,128)S(1)} collective-permute-done((f32[64,384]{1,0:T(8,128)S(1)}, f32[64,384]{1,0:T(8,128)S(1)}, u32[]{:S(2)}, u32[]{:S(2)}) %collective-permute-start.8) | collective-permute-done | bytes 98336 | tf_op jit(solution)/shard_map/ppermute | solution.py:795
  37.4 7.2 %shard_map.54.here_ref.refs_1_ = f32[192,128]{1,0:T(8,128)S(1)} custom-call(f32[64,384]{1,0:T(8,128)S(1)} %get-tuple-element.50.unread.refs_0_, f32[64,384]{1,0:T(8,128)S(1)} %collective-permute-done.8.refs_1_, f32[64,384]{1,0:T(8,128)S(1)} %get-tuple-element.52.refs_2_, f32[64,384]{1,0:T(8,128)S(1)} %collective-permute-done.9.refs_3_, ...), custom_call_target="tpu_custom_call" | custom-call | flops 7000000000 | bytes 1048576 | tf_op jit(solution)/shard_map/pallas_call | solution.py:755
  44.7 0.1 collective-permute-start.10
  44.7 0.6 %collective-permute-start.13 = (f32[2,32,256]{2,1,0:T(8,128)S(1)}, f32[2,32,256]{2,1,0:T(8,128)S(1)}, u32[]{:S(2)}, u32[]{:S(2)}) collective-permute-start(f32[2,32,256]{2,1,0:T(8,128)S(1)} %get-tuple-element.56), channel_id=1, source_target_pairs={{0,1},{1,0},{2,3},{3,2},{4,5},{5,4},{6,7},{7,6},{8,9},{9,8},{10,11... | collective-permute-start | bytes 196616 | tf_op jit(solution)/shard_map/ppermute | solution.py:86
  45.3 0.7 %collective-permute-done.10.there_ref.refs_2_ = f32[192,128]{1,0:T(8,128)S(1)} collective-permute-done((f32[192,128]{1,0:T(8,128)S(1)}, f32[192,128]{1,0:T(8,128)S(1)}, u32[]{:S(2)}, u32[]{:S(2)}) %collective-permute-start.10) | collective-permute-done | bytes 98336 | tf_op jit(solution)/shard_map/ppermute | solution.py:800
  46.1 2.4 %collective-permute-start.11 = (f32[32,128]{1,0:T(8,128)S(1)}, f32[32,128]{1,0:T(8,128)S(1)}, u32[]{:S(2)}, u32[]{:S(2)}) collective-permute-start(f32[32,128]{1,0:T(8,128)S(1)} %get-tuple-element.54), channel_id=1, source_target_pairs={{0,24},{8,16},{16,8},{24,0},{1,25},{9,17},{17,9},{25,1},{2,26},{10... | collective-permute-start | bytes 49160 | tf_op jit(solution)/shard_map/ppermute | solution.py:88
  48.4 0.0 collective-permute-start.12
  48.4 0.8 %collective-permute-done.13.refs_3_ = f32[2,32,256]{2,1,0:T(8,128)S(1)} collective-permute-done((f32[2,32,256]{2,1,0:T(8,128)S(1)}, f32[2,32,256]{2,1,0:T(8,128)S(1)}, u32[]{:S(2)}, u32[]{:S(2)}) %collective-permute-start.13) | collective-permute-done | bytes 65568 | tf_op jit(solution)/shard_map/ppermute | solution.py:86
  49.2 1.7 %shard_map.56.refs_2_ = f32[1536,128]{1,0:T(8,128)} custom-call(f32[8,128]{1,0:T(8,128)S(1)} %get-tuple-element.32.flag_ref, f32[6,32,256]{2,1,0:T(8,128)S(1)} %get-tuple-element.44.product_ref, bf16[2,2,256,256]{3,2,1,0:T(8,128)(2,1)S(1)} %get-tuple-element.47.refs_6_.refs_0_.early_inverse, ...), custom_call_target="tpu_custom_call" | custom-call | flops 1000000000 | bytes 1048576 | tf_op jit(solution)/shard_map/pallas_call | solution.py:809
  50.9 0.8 %collective-permute-done.11.refs_0_ = f32[32,128]{1,0:T(8,128)S(1)} collective-permute-done((f32[32,128]{1,0:T(8,128)S(1)}, f32[32,128]{1,0:T(8,128)S(1)}, u32[]{:S(2)}, u32[]{:S(2)}) %collective-permute-start.11) | collective-permute-done | bytes 16416 | tf_op jit(solution)/shard_map/ppermute | solution.py:88
  51.7 0.5 collective-permute-done.12.refs_1_
  52.2 1.0 %shard_map.57 = f32[1536,128]{1,0:T(8,128)} custom-call(bf16[4,256,192]{2,1,0:T(8,128)(2,1)S(1)} %shard_map.53.refs_4_.refs_0_.spread_ref, f32[64,128]{1,0:T(8,128)S(1)} %get-tuple-element.53.rows_ref, f32[32,128]{1,0:T(8,128)S(1)} %collective-permute-done.11.refs_0_, f32[32,128]{1,0:T(8,128)S(1)} %collective-permute-done.12.refs_1_, ...), custom_call_target="tpu_custom_call", output_to_operand_aliasing={{}: (4, {})} | custom-call | flops 1000000000 | bytes 1048576 | tf_op jit(solution)/shard_map/pallas_call | solution.py:843
  (2 shorter events, 0.1 us)
Async XLA Ops:
  0.0 9.9 %copy-start.1 = (s32[8]{0:T(128)S(1)}, s32[8]{0:T(128)}, u32[]{:S(2)}) copy-start(s32[8]{0:T(128)} %group_ref.1) | copy-start | bytes 100
  1.7 11.0 %collective-permute-start.4 = (f32[2,264,128]{2,1,0:T(8,128)S(1)}, f32[2,264,128]{2,1,0:T(8,128)S(1)}, u32[]{:S(2)}, u32[]{:S(2)}) collective-permute-start(f32[2,264,128]{2,1,0:T(8,128)S(1)} %get-tuple-element.39), channel_id=1, source_target_pairs={{0,1},{1,0},{2,3},{3,2},{4,5},{5,4},{6,7},{7,6},{8,9},{9,8},{10,11... | collective-permute-start | bytes 811016 | tf_op jit(solution)/shard_map/ppermute | solution.py:86
  4.7 10.9 %collective-permute-start = (f32[328,128]{1,0:T(8,128)S(1)}, f32[328,128]{1,0:T(8,128)S(1)}, u32[]{:S(2)}, u32[]{:S(2)}) collective-permute-start(f32[328,128]{1,0:T(8,128)S(1)} %get-tuple-element.33), channel_id=1, source_target_pairs={{0,24},{8,16},{16,8},{24,0},{1,25},{9,17},{17,9},{25,1},{2,26},{10... | collective-permute-start | bytes 503816 | tf_op jit(solution)/shard_map/ppermute | solution.py:88
  8.3 7.7 %collective-permute-start.1 = (f32[328,128]{1,0:T(8,128)S(1)}, f32[328,128]{1,0:T(8,128)S(1)}, u32[]{:S(2)}, u32[]{:S(2)}) collective-permute-start(f32[328,128]{1,0:T(8,128)S(1)} %get-tuple-element.34), channel_id=1, source_target_pairs={{0,8},{8,0},{16,24},{24,16},{1,9},{9,1},{17,25},{25,17},{2,10},{10... | collective-permute-start | bytes 503816 | tf_op jit(solution)/shard_map/ppermute | solution.py:89
  8.3 7.7 %collective-permute-start.2 = (f32[328,128]{1,0:T(8,128)S(1)}, f32[328,128]{1,0:T(8,128)S(1)}, u32[]{:S(2)}, u32[]{:S(2)}) collective-permute-start(f32[328,128]{1,0:T(8,128)S(1)} %get-tuple-element.35), channel_id=1, source_target_pairs={{0,6},{2,4},{4,2},{6,0},{1,7},{3,5},{5,3},{7,1},{8,14},{10,12},{12... | collective-permute-start | bytes 503816 | tf_op jit(solution)/shard_map/ppermute | solution.py:88
  8.7 7.3 %collective-permute-start.3 = (f32[328,128]{1,0:T(8,128)S(1)}, f32[328,128]{1,0:T(8,128)S(1)}, u32[]{:S(2)}, u32[]{:S(2)}) collective-permute-start(f32[328,128]{1,0:T(8,128)S(1)} %get-tuple-element.36), channel_id=1, source_target_pairs={{0,2},{2,0},{4,6},{6,4},{1,3},{3,1},{5,7},{7,5},{8,10},{10,8},{12,... | collective-permute-start | bytes 503816 | tf_op jit(solution)/shard_map/ppermute | solution.py:89
  9.9 2.7 %copy-start = (f32[1,1,1,6,256,32]{4,5,3,2,1,0:T(8,128)S(1)}, f32[1,1,1,6,256,32]{4,5,3,2,1,0:T(8,128)}, u32[]{:S(2)}) copy-start(f32[1,1,1,6,256,32]{4,5,3,2,1,0:T(8,128)} %param.5) | copy-start | bytes 589828
  12.6 3.4 %copy-start.2 = (f32[1,1,1,1536,128]{4,3,2,1,0:T(8,128)S(1)}, f32[1,1,1,1536,128]{4,3,2,1,0:T(8,128)}, u32[]{:S(2)}) copy-start(f32[1,1,1,1536,128]{4,3,2,1,0:T(8,128)} %param.6) | copy-start | bytes 2359300
  24.4 1.5 %collective-permute-start.5 = (f32[64,768]{1,0:T(8,128)S(1)}, f32[64,768]{1,0:T(8,128)S(1)}, u32[]{:S(2)}, u32[]{:S(2)}) collective-permute-start(f32[64,768]{1,0:T(8,128)S(1)} %get-tuple-element.41.here_ref), channel_id=1, source_target_pairs={{0,2},{2,0},{4,6},{6,4},{1,3},{3,1},{5,7},{7,5},{8,10},{10,8},{12,... | collective-permute-start | bytes 589832 | tf_op jit(solution)/shard_map/ppermute | solution.py:777
  26.0 4.9 %collective-permute-start.6 = (f32[64,384]{1,0:T(8,128)S(1)}, f32[64,384]{1,0:T(8,128)S(1)}, u32[]{:S(2)}, u32[]{:S(2)}) collective-permute-start(f32[64,384]{1,0:T(8,128)S(1)} %get-tuple-element.42.first_ref), channel_id=1, source_target_pairs={{0,4},{2,6},{4,0},{6,2},{1,5},{3,7},{5,1},{7,3},{8,12},{10,14},{12... | collective-permute-start | bytes 294920 | tf_op jit(solution)/shard_map/ppermute | solution.py:785
  27.6 4.6 %collective-permute-start.7 = (f32[64,384]{1,0:T(8,128)S(1)}, f32[64,384]{1,0:T(8,128)S(1)}, u32[]{:S(2)}, u32[]{:S(2)}) collective-permute-start(f32[64,384]{1,0:T(8,128)S(1)} %get-tuple-element.43.third_ref), channel_id=1, source_target_pairs={{0,1},{1,0},{2,3},{3,2},{4,5},{5,4},{6,7},{7,6},{8,9},{9,8},{10,11... | collective-permute-start | bytes 294920 | tf_op jit(solution)/shard_map/ppermute | solution.py:786
  32.2 4.7 %collective-permute-start.9 = (f32[64,384]{1,0:T(8,128)S(1)}, f32[64,384]{1,0:T(8,128)S(1)}, u32[]{:S(2)}, u32[]{:S(2)}) collective-permute-start(f32[64,384]{1,0:T(8,128)S(1)} %get-tuple-element.52.refs_2_), channel_id=1, source_target_pairs={{0,4},{2,6},{4,0},{6,2},{1,5},{3,7},{5,1},{7,3},{8,12},{10,14},{12... | collective-permute-start | bytes 294920 | tf_op jit(solution)/shard_map/ppermute | solution.py:796
  32.8 4.6 %collective-permute-start.8 = (f32[64,384]{1,0:T(8,128)S(1)}, f32[64,384]{1,0:T(8,128)S(1)}, u32[]{:S(2)}, u32[]{:S(2)}) collective-permute-start(f32[64,384]{1,0:T(8,128)S(1)} %get-tuple-element.50.unread.refs_0_), channel_id=1, source_target_pairs={{0,1},{1,0},{2,3},{3,2},{4,5},{5,4},{6,7},{7,6},{8,9},{9,8},{10,11... | collective-permute-start | bytes 294920 | tf_op jit(solution)/shard_map/ppermute | solution.py:795
  44.7 1.4 %collective-permute-start.10 = (f32[192,128]{1,0:T(8,128)S(1)}, f32[192,128]{1,0:T(8,128)S(1)}, u32[]{:S(2)}, u32[]{:S(2)}) collective-permute-start(f32[192,128]{1,0:T(8,128)S(1)} %shard_map.54.here_ref.refs_1_), channel_id=1, source_target_pairs={{0,2},{2,0},{4,6},{6,4},{1,3},{3,1},{5,7},{7,5},{8,10},{10,8},{12,... | collective-permute-start | bytes 294920 | tf_op jit(solution)/shard_map/ppermute | solution.py:800
  44.7 4.5 %collective-permute-start.13 = (f32[2,32,256]{2,1,0:T(8,128)S(1)}, f32[2,32,256]{2,1,0:T(8,128)S(1)}, u32[]{:S(2)}, u32[]{:S(2)}) collective-permute-start(f32[2,32,256]{2,1,0:T(8,128)S(1)} %get-tuple-element.56), channel_id=1, source_target_pairs={{0,1},{1,0},{2,3},{3,2},{4,5},{5,4},{6,7},{7,6},{8,9},{9,8},{10,11... | collective-permute-start | bytes 196616 | tf_op jit(solution)/shard_map/ppermute | solution.py:86
  46.1 5.6 %collective-permute-start.11 = (f32[32,128]{1,0:T(8,128)S(1)}, f32[32,128]{1,0:T(8,128)S(1)}, u32[]{:S(2)}, u32[]{:S(2)}) collective-permute-start(f32[32,128]{1,0:T(8,128)S(1)} %get-tuple-element.54), channel_id=1, source_target_pairs={{0,24},{8,16},{16,8},{24,0},{1,25},{9,17},{17,9},{25,1},{2,26},{10... | collective-permute-start | bytes 49160 | tf_op jit(solution)/shard_map/ppermute | solution.py:88
  48.4 3.7 %collective-permute-start.12 = (f32[32,128]{1,0:T(8,128)S(1)}, f32[32,128]{1,0:T(8,128)S(1)}, u32[]{:S(2)}, u32[]{:S(2)}) collective-permute-start(f32[32,128]{1,0:T(8,128)S(1)} %get-tuple-element.55), channel_id=1, source_target_pairs={{0,8},{8,0},{16,24},{24,16},{1,9},{9,1},{17,25},{25,17},{2,10},{10... | collective-permute-start | bytes 49160 | tf_op jit(solution)/shard_map/ppermute | solution.py:89

commit v11 on v10

--- a/solution.py
+++ b/solution.py
@@ -62,6 +62,13 @@
         )
         total = part if total is None else total + part
     return total
+
+
+def reciprocal(value):
+    guess = pl.reciprocal(value, approx=True)
+    for correction in range(2):
+        guess = guess * (2.0 - value * guess)
+    return guess
 
 
 def iota(shape, dim):
@@ -218,8 +225,8 @@
                 corner = line_of(cols[j][strip], line)
                 side = line_of(cols[j][strip], line + 1)
                 last = line_of(cols[j + 1][strip], line + 1)
-                inverse = 1.0 / (corner * last - side * side)
-                eliminate(j, 1.0 / corner, block)
+                inverse = reciprocal(corner * last - side * side)
+                eliminate(j, reciprocal(corner), block)
                 eliminate(j + 1, corner * inverse, block)
             for j in range(block):
                 row = line_of(work[strip], first + j)
@@ -285,43 +292,30 @@
             store(upper_out, upper_index(f, g), upper_ref[f, :, g * width : (g + 1) * width])
 
 
-def begin(packed, owns, partner_out, sum_ref):
+def inverses_of(packed, owns, partner_ref):
     width = owns[0].shape[1]
     half = width // 2
     eye = iota((half, half), 0) == iota((half, half), 1)
-    zero = jnp.zeros((half, half), jnp.float32)
-    guesses = []
+    whole_eye = iota((width, width), 0) == iota((width, width), 1)
+    powers, sums, downs = [], [], []
     for f in range(len(packed)):
         partner = unpack(packed[f])
+        store(partner_ref, f, partner)
         total = owns[f] + partner
-        store(partner_out, f, partner)
-        store(sum_ref, f, total)
-        across, down, twice = [], [], []
+        across, down = [], []
         for start in (0, half):
             block = total[start : start + half, start : start + half]
             diagonal = jnp.where(eye, block, 0.0)
             across.append(1.0 / jnp.sum(diagonal, axis=0, keepdims=True))
             down.append(1.0 / jnp.sum(diagonal, axis=1, keepdims=True))
-            twice.append(jnp.where(eye, 2.0 * across[-1], 0.0))
-        start = jnp.concatenate(
-            [
-                jnp.concatenate([twice[0], zero], axis=1),
-                jnp.concatenate([zero, twice[1]], axis=1),
-            ],
-            axis=0,
-        )
-        across, down = jnp.concatenate(across, axis=1), jnp.concatenate(down, axis=0)
-        guesses.append(start - down * total * across)
-    return guesses
-
-
-def newton(guesses, sum_ref):
-    results = []
-    for f, guess in enumerate(guesses):
-        halves = split(guess)
-        product = split(wide(load(sum_ref, f), halves))
-        results.append(2.0 * guess - wide(halves, product))
-    return results
+        downs.append(jnp.concatenate(down, axis=0))
+        power = jnp.where(whole_eye, 0.0, -total * jnp.concatenate(across, axis=1))
+        powers.append(split(power))
+        sums.append(jnp.where(whole_eye, 1.0, power))
+    for step in range(1, NS_ITERS):
+        powers = [split(wide(power, power)) for power in powers]
+        sums = [total + wide(split(total), power) for total, power in zip(sums, powers)]
+    return [down * total for down, total in zip(downs, sums)]
 
 
 def unit_rows(basis):
@@ -335,9 +329,9 @@
 
 
 def early_kernel(axes, faces, *refs):
-    arrays = len(refs) - 7
+    arrays = len(refs) - 6
     inputs = refs[:arrays]
-    own_ref, halves_ref, starts_ref, basis_out, partner_out, inverse_out, sum_ref = refs[arrays:]
+    own_ref, halves_ref, starts_ref, basis_out, partner_out, inverse_out = refs[arrays:]
     count = len(faces)
     packed = []
     done = 0
@@ -345,11 +339,9 @@
         number = face_arrays(lax.axis_size(axis))
         packed += receive(inputs[done : done + number], axis)
         done += number
-    guesses = begin(packed, [own_ref[f] for f in faces], partner_out, sum_ref)
-    for sweep in range(NS_ITERS - 1):
-        guesses = newton(guesses, sum_ref)
+    inverses = inverses_of(packed, [own_ref[f] for f in faces], partner_out)
     for i in range(count):
-        store(inverse_out, i, guesses[i])
+        store(inverse_out, i, inverses[i])
     basis = [starts_ref[f] for f in faces]
     matrices = [
         [load(partner_out, i) for i in range(count)],
@@ -363,10 +355,10 @@
 
 
 def main_kernel(axes, early, late, *refs):
-    arrays = len(refs) - 11
+    arrays = len(refs) - 10
     inputs = refs[:arrays]
     own_ref, halves_ref, upper_ref, starts_ref, resid_ref, early_basis = refs[arrays : arrays + 6]
-    payload_ref, product_ref, partner_out, inverse_out, sum_ref = refs[arrays + 6 :]
+    payload_ref, product_ref, partner_out, inverse_out = refs[arrays + 6 :]
     ncon, width = starts_ref.shape[1:]
     columns = resid_ref.shape[1]
     sides = {}
@@ -391,14 +383,10 @@
         number = face_arrays(lax.axis_size(axis))
         packed += receive(inputs[done : done + number], axis)
         done += number
-    guesses = begin(packed, [own_ref[f] for f in late], partner_out, sum_ref)
+    inverses = inverses_of(packed, [own_ref[f] for f in late], partner_out)
     pending = [(f, early_basis[i]) for i, f in enumerate(early)]
-    for sweep in range(NS_ITERS - 1):
-        guesses = newton(guesses, sum_ref)
-        if pending:
-            project(*pending.pop(0))
     for i in range(count):
-        store(inverse_out, i, guesses[i])
+        store(inverse_out, i, inverses[i])
     basis = [starts_ref[f] for f in late]
     matrices = [
         [load(partner_out, i) for i in range(count)],
@@ -447,8 +435,8 @@
 
 
 def theirs_kernel(faces, ncon, own_ref, *refs):
-    inputs, partner_refs, inverse_refs = refs[:-6], refs[-6:-4], refs[-4:-2]
-    basis_out, product_out = refs[-2:]
+    inputs, partner_refs, inverse_refs = refs[:-5], refs[-5:-3], refs[-3:-1]
+    product_out = refs[-1]
     basis = []
     done = 0
     for axis in AXES[:2]:
@@ -464,18 +452,15 @@
     ]
     for sweep in range(SUB_ITERS):
         basis = sweep_basis(*matrices, basis)
+    factors = factor_inverses([dot(b, b, ((1,), (1,))) for b in basis])
     for f in range(count):
-        basis_out[f] = basis[f]
-        product_out[f] = thin(stacked(basis[f]), matrices[2][f])
-
-
-def spread_kernel(faces, unread, basis_ref, theirs_ref, product_ref, *refs):
+        product_out[f] = triple(factors[f], thin(stacked(basis[f]), matrices[2][f]))
+
+
+def spread_kernel(faces, unread, theirs_ref, product_ref, *refs):
     inverse_refs, out_ref = refs[:2], refs[2]
-    basis = [basis_ref[f] for f in range(basis_ref.shape[0])]
-    factors = factor_inverses([dot(b, b, ((1,), (1,))) for b in basis])
-    for f in range(len(basis)):
-        theirs = triple(factors[f], theirs_ref[f])
-        both = jnp.concatenate([product_ref[f], theirs], axis=0)
+    for f in range(theirs_ref.shape[0]):
+        both = jnp.concatenate([product_ref[f], theirs_ref[f]], axis=0)
         high, low = split(thin(stacked(both), find(faces, inverse_refs, f)).T)
         out_ref[f] = jnp.concatenate([high, high, low], axis=1)
 
@@ -714,7 +699,6 @@
         out_shape=[shape(len(early), ncon, width)] + [halves(len(early))] * 2,
         in_specs=vmem_specs(len(got[2]) + 3),
         out_specs=vmem_specs(3),
-        scratch_shapes=[pltpu.VMEM((len(early), 2, width, width), jnp.bfloat16)],
         compiler_params=params(16),
         cost_estimate=cost(2),
     )(*got[2], own, own_halves, starts)
@@ -725,18 +709,17 @@
         + [halves(len(late))] * 2,
         in_specs=vmem_specs(len(got[0]) + len(got[1]) + 6),
         out_specs=vmem_specs(4),
-        scratch_shapes=[pltpu.VMEM((len(late), 2, width, width), jnp.bfloat16)],
         compiler_params=params(24),
         cost_estimate=cost(8),
     )(*got[0], *got[1], own, own_halves, upper_halves, starts, right, early_basis)
 
     partners = [early_partner, late_partner]
     inverses = [early_inverse, late_inverse]
-    their_basis, their_product = pl.pallas_call(
+    their_product = pl.pallas_call(
         functools.partial(theirs_kernel, faces, ncon),
-        out_shape=[shape(4, ncon, width)] * 2,
+        out_shape=shape(4, ncon, width),
         in_specs=vmem_specs(5 + len(got[0]) + len(got[1])),
-        out_specs=vmem_specs(2),
+        out_specs=vmem_specs(1)[0],
         compiler_params=params(16),
         cost_estimate=cost(2),
     )(own_halves, *got[0], *got[1], *partners, *inverses)
@@ -745,11 +728,11 @@
         return pl.pallas_call(
             functools.partial(spread_kernel, faces),
             out_shape=jax.ShapeDtypeStruct((4, width, 3 * size), jnp.bfloat16),
-            in_specs=[anywhere] + vmem_specs(5),
+            in_specs=[anywhere] + vmem_specs(4),
             out_specs=vmem_specs(1)[0],
             compiler_params=params(16),
             cost_estimate=cost(2),
-        )(token, their_basis, their_product, product, *inverses)
+        )(token, their_product, product, *inverses)
 
     def solve(matrices, rights, unread):
         return pl.pallas_call(
@@ -791,7 +774,7 @@
             in_specs=vmem_specs(5) + [anywhere],
             out_specs=vmem_specs(2 + face_arrays(counts[2])),
             compiler_params=params(8),
-        )(left, left_moved, rest, rest_moved, product, their_basis)
+        )(left, left_moved, rest, rest_moved, product, their_product)
         left_other = lax.ppermute(left_last, "gz", chip_y)
         rest_other = lax.ppermute(rest_last, "gy", chip_x)
         theirs = exchange(sent, AXES[2])

time: 53.5 us -> 53.5 us (level)
  starting transfers between devices: 14.5 us -> 16 us
  waiting for transfers between devices: 8.81 us -> 7.37 us
    pallas_call x1, Pallas kernels: 1.58 us -> 3.79 us  [per_device(): pl.pallas_call(functools.partial(theirs_kernel, faces, ncon), out_shape=s...]
    pallas_call x1, Pallas kernels: 2.43 us -> 0.59 us  [spread_of(): pl.pallas_call(functools.partial(spread_kernel, faces), out_shape=jax.Sha...]
    ppermute x1, waiting for transfers between devices: 1.27 us -> 0.01 us  [per_device(): left_moved = lax.ppermute(left, 'gy', chip_x)]
    ppermute x1, waiting for transfers between devices: 1.14 us -> 2.25 us  [per_device(): rest_other = lax.ppermute(rest_last, 'gy', chip_x)]
    ppermute x1, waiting for transfers between devices: 1.25 us -> 0.32 us  [per_device(): rest_moved = lax.ppermute(rest, 'gz', chip_y)]
    ppermute x1, starting transfers between devices: 0.49 us -> 1.24 us  [per_device(): left_other = lax.ppermute(left_last, 'gz', chip_y)]
    ppermute x2, starting transfers between devices: 3.59 us -> 4.33 us  [exchange(): return [lax.ppermute(arrays[0], axis, flipped(axis, 1))]]
    ppermute x1, waiting for transfers between devices: 0.73 us -> 0.01 us  [per_device(): there = lax.ppermute(answer, 'gy', core_swap)]
  transfers between devices with their start and end apart: 14 -> 14, of which waited for: 10 -> 8; matrix products, arithmetic and copies ran while one was open for 0% -> 0% of each run, Pallas kernels for 21% -> 21%
where the time goes in v11:
time: 53.5 us; the launch traced here: 53.4 us
  Pallas kernels  29.7 us (56%)
  starting transfers between devices  16 us (30%)
  waiting for transfers between devices  7.37 us (14%)
    pallas_call x1, Pallas kernels, per_device(): pl.pallas_call(functools.partial(main_kernel, (AXES[0], AXES[1]), early,...  7.91 us
    pallas_call x1, Pallas kernels, solve(): pl.pallas_call(functools.partial(solve_kernel, size, len(matrices), colum...  7.66 us
    ppermute x3, starting transfers between devices, exchange(): lax.ppermute(arrays[0], axis, outer_pairs(axis))  6.39 us
    ppermute x2, starting transfers between devices, exchange(): return [lax.ppermute(arrays[0], axis, flipped(axis, 1))]  4.33 us
    pallas_call x1, Pallas kernels, per_device(): pl.pallas_call(functools.partial(theirs_kernel, faces, ncon), out_shape=s...  3.79 us
    pallas_call x1, Pallas kernels, per_device(): pl.pallas_call(functools.partial(halves_kernel, planes), out_shape=[halve...  2.7 us
    pallas_call x1, Pallas kernels, per_device(): pl.pallas_call(functools.partial(early_kernel, AXES[2:3], early), out_sha...  2.58 us
    ppermute x1, waiting for transfers between devices, per_device(): rest_other = lax.ppermute(rest_last, 'gy', chip_x)  2.25 us
  transfers between devices with their start and end apart: 14, of which 8 were waited for; matrix products, arithmetic and copies ran while one was open for 0% of the time, Pallas kernels for 21%

profile of v11, /device:TPU:0, one launch (start us, length us, event | category | flops | bytes accessed | tf_op | source)
XLA Modules:
  0.0 53.4 jit_solution(6416457832501241482)
XLA Ops:
  0.0 0.0 copy-start.1
  0.0 1.7 %shard_map.46 = (f32[328,128]{1,0:T(8,128)S(1)}, f32[328,128]{1,0:T(8,128)S(1)}, f32[328,128]{1,0:T(8,128)S(1)}, f32[328,128]{1,0:T(8,128)S(1)}, f32[2,264,128]{2,1,0:T(8,128)S(1)}, /*index=5*/f32[6,256,256]{2,1,0:T(8,128)S(1)}) custom-call(f32[1536,1536]{1,0:T(8,128)} %bitcast.10, f32[6,32,256]{2,1,0:T(8,128)} %bitcast.6), custom_call_target="tpu_custom_call" | custom-call | tf_op jit(solution)/shard_map/pallas_call | solution.py:664
  1.7 3.0 %collective-permute-start.4 = (f32[2,264,128]{2,1,0:T(8,128)S(1)}, f32[2,264,128]{2,1,0:T(8,128)S(1)}, u32[]{:S(2)}, u32[]{:S(2)}) collective-permute-start(f32[2,264,128]{2,1,0:T(8,128)S(1)} %get-tuple-element.37), channel_id=1, source_target_pairs={{0,1},{1,0},{2,3},{3,2},{4,5},{5,4},{6,7},{7,6},{8,9},{9,8},{10,11... | collective-permute-start | bytes 811016 | tf_op jit(solution)/shard_map/ppermute | solution.py:93
  4.7 3.6 %collective-permute-start = (f32[328,128]{1,0:T(8,128)S(1)}, f32[328,128]{1,0:T(8,128)S(1)}, u32[]{:S(2)}, u32[]{:S(2)}) collective-permute-start(f32[328,128]{1,0:T(8,128)S(1)} %get-tuple-element.31), channel_id=1, source_target_pairs={{0,24},{8,16},{16,8},{24,0},{1,25},{9,17},{17,9},{25,1},{2,26},{10... | collective-permute-start | bytes 503816 | tf_op jit(solution)/shard_map/ppermute | solution.py:95
  8.3 0.0 collective-permute-start.1
  8.3 0.4 collective-permute-start.2
  8.7 1.2 %collective-permute-start.3 = (f32[328,128]{1,0:T(8,128)S(1)}, f32[328,128]{1,0:T(8,128)S(1)}, u32[]{:S(2)}, u32[]{:S(2)}) collective-permute-start(f32[328,128]{1,0:T(8,128)S(1)} %get-tuple-element.34), channel_id=1, source_target_pairs={{0,2},{2,0},{4,6},{6,4},{1,3},{3,1},{5,7},{7,5},{8,10},{10,8},{12,... | collective-permute-start | bytes 503816 | tf_op jit(solution)/shard_map/ppermute | solution.py:96
  9.9 0.0 copy-done.1
  9.9 0.0 copy-start
  9.9 2.7 %shard_map.47 = (bf16[6,2,256,256]{3,2,1,0:T(8,128)(2,1)S(1)}, bf16[15,2,256,256]{3,2,1,0:T(8,128)(2,1)S(1)}, f32[8,128]{1,0:T(8,128)S(1)}) custom-call(f32[1536,1536]{1,0:T(8,128)} %bitcast.11, s32[8]{0:T(128)S(1)} %copy-done.1, f32[6,256,256]{2,1,0:T(8,128)S(1)} %get-tuple-element.29.own_ref.refs_1_.refs_4_), custom_call_target="tpu_custom_call" | custom-call | flops 2000000000 | bytes 1048576 | tf_op jit(solution)/shard_map/pallas_call | solution.py:684
  12.6 0.0 copy-start.2
  12.7 0.0 collective-permute-done.4.refs_0_
  12.7 0.0 copy-done
  12.7 2.6 %shard_map.48 = (f32[2,32,256]{2,1,0:T(8,128)S(1)}, bf16[2,2,256,256]{3,2,1,0:T(8,128)(2,1)S(1)}, bf16[2,2,256,256]{3,2,1,0:T(8,128)(2,1)S(1)}) custom-call(f32[2,264,128]{2,1,0:T(8,128)S(1)} %collective-permute-done.4.refs_0_, f32[6,256,256]{2,1,0:T(8,128)S(1)} %get-tuple-element.29.own_ref.refs_1_.refs_4_, ...), custom_call_target="tpu_custom_call" | custom-call | flops 2000000000 | bytes 1048576 | tf_op jit(solution)/shard_map/pallas_call | solution.py:697
  15.3 0.0 collective-permute-done.refs_0_
  15.3 0.8 %collective-permute-done.1.refs_1_ = f32[328,128]{1,0:T(8,128)S(1)} collective-permute-done((f32[328,128]{1,0:T(8,128)S(1)}, f32[328,128]{1,0:T(8,128)S(1)}, u32[]{:S(2)}, u32[]{:S(2)}) %collective-permute-start.1) | collective-permute-done | bytes 167968 | tf_op jit(solution)/shard_map/ppermute | solution.py:96
  16.0 0.0 collective-permute-done.2.refs_2_
  16.0 0.0 collective-permute-done.3.refs_3_
  16.0 0.0 copy-done.2
  16.0 7.9 %shard_map.49 = (f32[64,768]{1,0:T(8,128)S(1)}, f32[6,32,256]{2,1,0:T(8,128)S(1)}, bf16[4,2,256,256]{3,2,1,0:T(8,128)(2,1)S(1)}, bf16[4,2,256,256]{3,2,1,0:T(8,128)(2,1)S(1)}) custom-call(f32[328,128]{1,0:T(8,128)S(1)} %collective-permute-done.refs_0_, f32[328,128]{1,0:T(8,128)S(1)} %collective-permute-done.1.refs_1_, ...), custom_call_target="tpu_custom_call" | custom-call | flops 8000000000 | bytes 1048576 | tf_op jit(solution)/shard_map/pallas_call | solution.py:706
  24.0 0.1 collective-permute-start.5
  24.0 1.4 %collective-permute-done.5.there_ref = f32[64,768]{1,0:T(8,128)S(1)} collective-permute-done((f32[64,768]{1,0:T(8,128)S(1)}, f32[64,768]{1,0:T(8,128)S(1)}, u32[]{:S(2)}, u32[]{:S(2)}) %collective-permute-start.5) | collective-permute-done | bytes 196640 | tf_op jit(solution)/shard_map/ppermute | solution.py:760
  25.5 0.1 shard_map.50
  25.5 1.6 %collective-permute-start.6 = (f32[64,384]{1,0:T(8,128)S(1)}, f32[64,384]{1,0:T(8,128)S(1)}, u32[]{:S(2)}, u32[]{:S(2)}) collective-permute-start(f32[64,384]{1,0:T(8,128)S(1)} %get-tuple-element.40.first_ref), channel_id=1, source_target_pairs={{0,4},{2,6},{4,0},{6,2},{1,5},{3,7},{5,1},{7,3},{8,12},{10,14},{12... | collective-permute-start | bytes 294920 | tf_op jit(solution)/shard_map/ppermute | solution.py:768
  27.1 0.5 collective-permute-start.7
  27.6 3.8 %shard_map.51.unread.theirs_ref = f32[4,32,256]{2,1,0:T(8,128)S(1)} custom-call(bf16[6,2,256,256]{3,2,1,0:T(8,128)(2,1)S(1)} %get-tuple-element.35.refs_2_.refs_5_.own_ref, f32[328,128]{1,0:T(8,128)S(1)} %collective-permute-done.refs_0_, f32[328,128]{1,0:T(8,128)S(1)} %collective-permute-done.1.refs_1_, f32[328,128]{1,0:T(8,128)S(1)} %collective-permute-done.2.refs_2_, ...), custom_call_target="tpu_custom_call" | custom-call | flops 2000000000 | bytes 1048576 | tf_op jit(solution)/shard_map/pallas_call | solution.py:718
  31.4 0.0 collective-permute-done.6.second_ref
  31.4 0.3 collective-permute-done.7.fourth_ref
  31.8 0.6 %collective-permute-start.9 = (f32[64,384]{1,0:T(8,128)S(1)}, f32[64,384]{1,0:T(8,128)S(1)}, u32[]{:S(2)}, u32[]{:S(2)}) collective-permute-start(f32[64,384]{1,0:T(8,128)S(1)} %get-tuple-element.48.refs_2_), channel_id=1, source_target_pairs={{0,4},{2,6},{4,0},{6,2},{1,5},{3,7},{5,1},{7,3},{8,12},{10,14},{12... | collective-permute-start | bytes 294920 | tf_op jit(solution)/shard_map/ppermute | solution.py:779
  32.3 1.2 %collective-permute-start.8 = (f32[64,384]{1,0:T(8,128)S(1)}, f32[64,384]{1,0:T(8,128)S(1)}, u32[]{:S(2)}, u32[]{:S(2)}) collective-permute-start(f32[64,384]{1,0:T(8,128)S(1)} %get-tuple-element.47.unread.refs_0_), channel_id=1, source_target_pairs={{0,1},{1,0},{2,3},{3,2},{4,5},{5,4},{6,7},{7,6},{8,9},{9,8},{10,11... | collective-permute-start | bytes 294920 | tf_op jit(solution)/shard_map/ppermute | solution.py:778
  33.6 0.6 %shard_map.53.refs_4_.refs_0_.spread_ref = bf16[4,256,192]{2,1,0:T(8,128)(2,1)S(1)} custom-call(f32[64,384]{1,0:T(8,128)S(1)} %get-tuple-element.47.unread.refs_0_, f32[4,32,256]{2,1,0:T(8,128)S(1)} %shard_map.51.unread.theirs_ref, f32[6,32,256]{2,1,0:T(8,128)S(1)} %get-tuple-element.42.product_ref, ...), custom_call_target="tpu_custom_call" | custom-call | flops 2000000000 | bytes 1048576 | tf_op jit(solution)/shard_map/pallas_call | solution.py:728
  34.2 2.3 %collective-permute-done.9.refs_3_ = f32[64,384]{1,0:T(8,128)S(1)} collective-permute-done((f32[64,384]{1,0:T(8,128)S(1)}, f32[64,384]{1,0:T(8,128)S(1)}, u32[]{:S(2)}, u32[]{:S(2)}) %collective-permute-start.9) | collective-permute-done | bytes 98336 | tf_op jit(solution)/shard_map/ppermute | solution.py:779
  36.4 0.5 collective-permute-done.8.refs_1_
  37.0 7.7 %shard_map.54.here_ref.refs_1_ = f32[192,128]{1,0:T(8,128)S(1)} custom-call(f32[64,384]{1,0:T(8,128)S(1)} %get-tuple-element.47.unread.refs_0_, f32[64,384]{1,0:T(8,128)S(1)} %collective-permute-done.8.refs_1_, f32[64,384]{1,0:T(8,128)S(1)} %get-tuple-element.48.refs_2_, f32[64,384]{1,0:T(8,128)S(1)} %collective-permute-done.9.refs_3_, ...), custom_call_target="tpu_custom_call" | custom-call | flops 7000000000 | bytes 1048576 | tf_op jit(solution)/shard_map/pallas_call | solution.py:738
  44.6 0.1 collective-permute-start.10
  44.7 1.3 %collective-permute-start.13 = (f32[2,32,256]{2,1,0:T(8,128)S(1)}, f32[2,32,256]{2,1,0:T(8,128)S(1)}, u32[]{:S(2)}, u32[]{:S(2)}) collective-permute-start(f32[2,32,256]{2,1,0:T(8,128)S(1)} %get-tuple-element.52), channel_id=1, source_target_pairs={{0,1},{1,0},{2,3},{3,2},{4,5},{5,4},{6,7},{7,6},{8,9},{9,8},{10,11... | collective-permute-start | bytes 196616 | tf_op jit(solution)/shard_map/ppermute | solution.py:93
  46.0 0.0 collective-permute-done.10.there_ref.refs_2_
  46.1 2.4 %collective-permute-start.11 = (f32[32,128]{1,0:T(8,128)S(1)}, f32[32,128]{1,0:T(8,128)S(1)}, u32[]{:S(2)}, u32[]{:S(2)}) collective-permute-start(f32[32,128]{1,0:T(8,128)S(1)} %get-tuple-element.50), channel_id=1, source_target_pairs={{0,24},{8,16},{16,8},{24,0},{1,25},{9,17},{17,9},{25,1},{2,26},{10... | collective-permute-start | bytes 49160 | tf_op jit(solution)/shard_map/ppermute | solution.py:95
  48.5 0.0 collective-permute-start.12
  48.5 0.7 %collective-permute-done.13.refs_3_ = f32[2,32,256]{2,1,0:T(8,128)S(1)} collective-permute-done((f32[2,32,256]{2,1,0:T(8,128)S(1)}, f32[2,32,256]{2,1,0:T(8,128)S(1)}, u32[]{:S(2)}, u32[]{:S(2)}) %collective-permute-start.13) | collective-permute-done | bytes 65568 | tf_op jit(solution)/shard_map/ppermute | solution.py:93
  49.2 1.7 %shard_map.56.refs_2_ = f32[1536,128]{1,0:T(8,128)} custom-call(f32[8,128]{1,0:T(8,128)S(1)} %get-tuple-element.30.flag_ref, f32[6,32,256]{2,1,0:T(8,128)S(1)} %get-tuple-element.42.product_ref, bf16[2,2,256,256]{3,2,1,0:T(8,128)(2,1)S(1)} %get-tuple-element.45.refs_6_.refs_0_.early_inverse, ...), custom_call_target="tpu_custom_call" | custom-call | flops 1000000000 | bytes 1048576 | tf_op jit(solution)/shard_map/pallas_call | solution.py:792
  50.9 0.8 %collective-permute-done.11.refs_0_ = f32[32,128]{1,0:T(8,128)S(1)} collective-permute-done((f32[32,128]{1,0:T(8,128)S(1)}, f32[32,128]{1,0:T(8,128)S(1)}, u32[]{:S(2)}, u32[]{:S(2)}) %collective-permute-start.11) | collective-permute-done | bytes 16416 | tf_op jit(solution)/shard_map/ppermute | solution.py:95
  51.7 0.6 %collective-permute-done.12.refs_1_ = f32[32,128]{1,0:T(8,128)S(1)} collective-permute-done((f32[32,128]{1,0:T(8,128)S(1)}, f32[32,128]{1,0:T(8,128)S(1)}, u32[]{:S(2)}, u32[]{:S(2)}) %collective-permute-start.12) | collective-permute-done | bytes 16416 | tf_op jit(solution)/shard_map/ppermute | solution.py:96
  52.2 1.0 %shard_map.57 = f32[1536,128]{1,0:T(8,128)} custom-call(bf16[4,256,192]{2,1,0:T(8,128)(2,1)S(1)} %shard_map.53.refs_4_.refs_0_.spread_ref, f32[64,128]{1,0:T(8,128)S(1)} %get-tuple-element.49.rows_ref, f32[32,128]{1,0:T(8,128)S(1)} %collective-permute-done.11.refs_0_, f32[32,128]{1,0:T(8,128)S(1)} %collective-permute-done.12.refs_1_, ...), custom_call_target="tpu_custom_call", output_to_operand_aliasing={{}: (4, {})} | custom-call | flops 1000000000 | bytes 1048576 | tf_op jit(solution)/shard_map/pallas_call | solution.py:826
  (2 shorter events, 0.1 us)
Async XLA Ops:
  0.0 9.9 %copy-start.1 = (s32[8]{0:T(128)S(1)}, s32[8]{0:T(128)}, u32[]{:S(2)}) copy-start(s32[8]{0:T(128)} %group_ref.1) | copy-start | bytes 100
  1.7 11.0 %collective-permute-start.4 = (f32[2,264,128]{2,1,0:T(8,128)S(1)}, f32[2,264,128]{2,1,0:T(8,128)S(1)}, u32[]{:S(2)}, u32[]{:S(2)}) collective-permute-start(f32[2,264,128]{2,1,0:T(8,128)S(1)} %get-tuple-element.37), channel_id=1, source_target_pairs={{0,1},{1,0},{2,3},{3,2},{4,5},{5,4},{6,7},{7,6},{8,9},{9,8},{10,11... | collective-permute-start | bytes 811016 | tf_op jit(solution)/shard_map/ppermute | solution.py:93
  4.7 10.5 %collective-permute-start = (f32[328,128]{1,0:T(8,128)S(1)}, f32[328,128]{1,0:T(8,128)S(1)}, u32[]{:S(2)}, u32[]{:S(2)}) collective-permute-start(f32[328,128]{1,0:T(8,128)S(1)} %get-tuple-element.31), channel_id=1, source_target_pairs={{0,24},{8,16},{16,8},{24,0},{1,25},{9,17},{17,9},{25,1},{2,26},{10... | collective-permute-start | bytes 503816 | tf_op jit(solution)/shard_map/ppermute | solution.py:95
  8.3 7.7 %collective-permute-start.1 = (f32[328,128]{1,0:T(8,128)S(1)}, f32[328,128]{1,0:T(8,128)S(1)}, u32[]{:S(2)}, u32[]{:S(2)}) collective-permute-start(f32[328,128]{1,0:T(8,128)S(1)} %get-tuple-element.32), channel_id=1, source_target_pairs={{0,8},{8,0},{16,24},{24,16},{1,9},{9,1},{17,25},{25,17},{2,10},{10... | collective-permute-start | bytes 503816 | tf_op jit(solution)/shard_map/ppermute | solution.py:96
  8.3 7.7 %collective-permute-start.2 = (f32[328,128]{1,0:T(8,128)S(1)}, f32[328,128]{1,0:T(8,128)S(1)}, u32[]{:S(2)}, u32[]{:S(2)}) collective-permute-start(f32[328,128]{1,0:T(8,128)S(1)} %get-tuple-element.33), channel_id=1, source_target_pairs={{0,6},{2,4},{4,2},{6,0},{1,7},{3,5},{5,3},{7,1},{8,14},{10,12},{12... | collective-permute-start | bytes 503816 | tf_op jit(solution)/shard_map/ppermute | solution.py:95
  8.7 7.3 %collective-permute-start.3 = (f32[328,128]{1,0:T(8,128)S(1)}, f32[328,128]{1,0:T(8,128)S(1)}, u32[]{:S(2)}, u32[]{:S(2)}) collective-permute-start(f32[328,128]{1,0:T(8,128)S(1)} %get-tuple-element.34), channel_id=1, source_target_pairs={{0,2},{2,0},{4,6},{6,4},{1,3},{3,1},{5,7},{7,5},{8,10},{10,8},{12,... | collective-permute-start | bytes 503816 | tf_op jit(solution)/shard_map/ppermute | solution.py:96
  9.9 2.7 %copy-start = (f32[1,1,1,6,256,32]{4,5,3,2,1,0:T(8,128)S(1)}, f32[1,1,1,6,256,32]{4,5,3,2,1,0:T(8,128)}, u32[]{:S(2)}) copy-start(f32[1,1,1,6,256,32]{4,5,3,2,1,0:T(8,128)} %param.5) | copy-start | bytes 589828
  12.6 3.4 %copy-start.2 = (f32[1,1,1,1536,128]{4,3,2,1,0:T(8,128)S(1)}, f32[1,1,1,1536,128]{4,3,2,1,0:T(8,128)}, u32[]{:S(2)}) copy-start(f32[1,1,1,1536,128]{4,3,2,1,0:T(8,128)} %param.6) | copy-start | bytes 2359300
  24.0 1.5 %collective-permute-start.5 = (f32[64,768]{1,0:T(8,128)S(1)}, f32[64,768]{1,0:T(8,128)S(1)}, u32[]{:S(2)}, u32[]{:S(2)}) collective-permute-start(f32[64,768]{1,0:T(8,128)S(1)} %get-tuple-element.39.here_ref), channel_id=1, source_target_pairs={{0,2},{2,0},{4,6},{6,4},{1,3},{3,1},{5,7},{7,5},{8,10},{10,8},{12,... | collective-permute-start | bytes 589832 | tf_op jit(solution)/shard_map/ppermute | solution.py:760
  25.5 5.9 %collective-permute-start.6 = (f32[64,384]{1,0:T(8,128)S(1)}, f32[64,384]{1,0:T(8,128)S(1)}, u32[]{:S(2)}, u32[]{:S(2)}) collective-permute-start(f32[64,384]{1,0:T(8,128)S(1)} %get-tuple-element.40.first_ref), channel_id=1, source_target_pairs={{0,4},{2,6},{4,0},{6,2},{1,5},{3,7},{5,1},{7,3},{8,12},{10,14},{12... | collective-permute-start | bytes 294920 | tf_op jit(solution)/shard_map/ppermute | solution.py:768
  27.1 4.6 %collective-permute-start.7 = (f32[64,384]{1,0:T(8,128)S(1)}, f32[64,384]{1,0:T(8,128)S(1)}, u32[]{:S(2)}, u32[]{:S(2)}) collective-permute-start(f32[64,384]{1,0:T(8,128)S(1)} %get-tuple-element.41.third_ref), channel_id=1, source_target_pairs={{0,1},{1,0},{2,3},{3,2},{4,5},{5,4},{6,7},{7,6},{8,9},{9,8},{10,11... | collective-permute-start | bytes 294920 | tf_op jit(solution)/shard_map/ppermute | solution.py:769
  31.8 4.7 %collective-permute-start.9 = (f32[64,384]{1,0:T(8,128)S(1)}, f32[64,384]{1,0:T(8,128)S(1)}, u32[]{:S(2)}, u32[]{:S(2)}) collective-permute-start(f32[64,384]{1,0:T(8,128)S(1)} %get-tuple-element.48.refs_2_), channel_id=1, source_target_pairs={{0,4},{2,6},{4,0},{6,2},{1,5},{3,7},{5,1},{7,3},{8,12},{10,14},{12... | collective-permute-start | bytes 294920 | tf_op jit(solution)/shard_map/ppermute | solution.py:779
  32.3 4.6 %collective-permute-start.8 = (f32[64,384]{1,0:T(8,128)S(1)}, f32[64,384]{1,0:T(8,128)S(1)}, u32[]{:S(2)}, u32[]{:S(2)}) collective-permute-start(f32[64,384]{1,0:T(8,128)S(1)} %get-tuple-element.47.unread.refs_0_), channel_id=1, source_target_pairs={{0,1},{1,0},{2,3},{3,2},{4,5},{5,4},{6,7},{7,6},{8,9},{9,8},{10,11... | collective-permute-start | bytes 294920 | tf_op jit(solution)/shard_map/ppermute | solution.py:778
  44.6 1.4 %collective-permute-start.10 = (f32[192,128]{1,0:T(8,128)S(1)}, f32[192,128]{1,0:T(8,128)S(1)}, u32[]{:S(2)}, u32[]{:S(2)}) collective-permute-start(f32[192,128]{1,0:T(8,128)S(1)} %shard_map.54.here_ref.refs_1_), channel_id=1, source_target_pairs={{0,2},{2,0},{4,6},{6,4},{1,3},{3,1},{5,7},{7,5},{8,10},{10,8},{12,... | collective-permute-start | bytes 294920 | tf_op jit(solution)/shard_map/ppermute | solution.py:783
  44.7 4.5 %collective-permute-start.13 = (f32[2,32,256]{2,1,0:T(8,128)S(1)}, f32[2,32,256]{2,1,0:T(8,128)S(1)}, u32[]{:S(2)}, u32[]{:S(2)}) collective-permute-start(f32[2,32,256]{2,1,0:T(8,128)S(1)} %get-tuple-element.52), channel_id=1, source_target_pairs={{0,1},{1,0},{2,3},{3,2},{4,5},{5,4},{6,7},{7,6},{8,9},{9,8},{10,11... | collective-permute-start | bytes 196616 | tf_op jit(solution)/shard_map/ppermute | solution.py:93
  46.1 5.6 %collective-permute-start.11 = (f32[32,128]{1,0:T(8,128)S(1)}, f32[32,128]{1,0:T(8,128)S(1)}, u32[]{:S(2)}, u32[]{:S(2)}) collective-permute-start(f32[32,128]{1,0:T(8,128)S(1)} %get-tuple-element.50), channel_id=1, source_target_pairs={{0,24},{8,16},{16,8},{24,0},{1,25},{9,17},{17,9},{25,1},{2,26},{10... | collective-permute-start | bytes 49160 | tf_op jit(solution)/shard_map/ppermute | solution.py:95
  48.5 3.7 %collective-permute-start.12 = (f32[32,128]{1,0:T(8,128)S(1)}, f32[32,128]{1,0:T(8,128)S(1)}, u32[]{:S(2)}, u32[]{:S(2)}) collective-permute-start(f32[32,128]{1,0:T(8,128)S(1)} %get-tuple-element.51), channel_id=1, source_target_pairs={{0,8},{8,0},{16,24},{24,16},{1,9},{9,1},{17,25},{25,17},{2,10},{10... | collective-permute-start | bytes 49160 | tf_op jit(solution)/shard_map/ppermute | solution.py:96

commit v12 on v11

--- a/solution.py
+++ b/solution.py
@@ -62,13 +62,6 @@
         )
         total = part if total is None else total + part
     return total
-
-
-def reciprocal(value):
-    guess = pl.reciprocal(value, approx=True)
-    for correction in range(2):
-        guess = guess * (2.0 - value * guess)
-    return guess
 
 
 def iota(shape, dim):
@@ -183,65 +176,78 @@
     return jnp.concatenate([rows[:ncon], rows[ncon:]], axis=1)
 
 
-def factor_inverses(grams, block=8):
+def factor_inverses(grams):
     size = grams[0].shape[0]
-    strips = size // 8
-    lanes = 128
-    full = (8, lanes)
-    state = []
-    for gram in grams:
-        parts = [gram, jnp.where(iota((size, size), 0) == iota((size, size), 1), 1.0, 0.0)]
-        if 2 * size < lanes:
-            parts.append(jnp.zeros((size, lanes - 2 * size), jnp.float32))
+    strips, block, lanes = size // 8, 8, 128
+    full = (block, lanes)
+    beside = lanes // (2 * size)
+    one = jnp.where(iota((size, size), 0) == iota((size, size), 1), 1.0, 0.0)
+    states = []
+    for first in range(0, len(grams), beside):
+        parts = [part for gram in grams[first : first + beside] for part in (gram, one)]
         whole = jnp.concatenate(parts, axis=1)
-        state.append([whole[8 * s : 8 * s + 8] for s in range(strips)])
+        states.append([whole[8 * s : 8 * s + 8] for s in range(strips)])
     below = iota(full, 0)
-
-    def line_of(strip, line):
-        return jnp.broadcast_to(strip[line : line + 1], full)
-
-    for start in range(0, size, block):
-        strip, first = start // 8, start % 8
-        active = range(strip, strips)
-        for work in state:
-            cols = [
-                {s: jnp.broadcast_to(work[s][:, start + j : start + j + 1], full) for s in active}
-                for j in range(block)
-            ]
-            factors = []
-
-            def eliminate(j, scale, stop):
-                line = first + j
-                factor = {s: cols[j][s] * scale for s in active}
-                factor[strip] = jnp.where(below > line, factor[strip], 0.0)
-                for later in range(j + 1, stop):
-                    head = line_of(cols[later][strip], line)
-                    for s in active:
-                        cols[later][s] = cols[later][s] - factor[s] * head
-                factors.append(factor)
-
-            for j in range(0, block, 2):
-                line = first + j
-                corner = line_of(cols[j][strip], line)
-                side = line_of(cols[j][strip], line + 1)
-                last = line_of(cols[j + 1][strip], line + 1)
-                inverse = reciprocal(corner * last - side * side)
-                eliminate(j, reciprocal(corner), block)
-                eliminate(j + 1, corner * inverse, block)
-            for j in range(block):
-                row = line_of(work[strip], first + j)
-                for s in active:
-                    if s == strip and first + j == 7:
-                        continue
-                    work[s] = work[s] - factors[j][s] * row
+    base = iota(full, 1) // (2 * size) * (2 * size)
+
+    def column(rows, k):
+        if beside == 1:
+            return jnp.broadcast_to(rows[:, k : k + 1], full)
+        return jnp.take_along_axis(rows, base + k, axis=1, mode="promise_in_bounds")
+
+    def line_of(rows, line):
+        return jnp.broadcast_to(rows[line : line + 1], full)
+
+    roots = [[None] * strips for _ in states]
+    for strip in range(strips):
+        start = strip * block
+        columns = [
+            [[column(work[s], start + j) for s in range(strip, strips)] for j in range(block)]
+            for work in states
+        ]
+        heads = [[column_set[0] for column_set in per_state] for per_state in columns]
+        lowers = [work[strip] for work in states]
+        solved = list(lowers)
+        pivots = [jnp.ones(full, jnp.float32) for _ in states]
+        scales = list(pivots)
+
+        def eliminate(i, j, scale, pivot, side):
+            cols = heads[i]
+            factor = jnp.where(below != j, cols[j] * scale, 0.0)
+            for later in range(j + 1, block):
+                use = side if later == j + 1 and side is not None else line_of(cols[later], j)
+                cols[later] = cols[later] - factor * use
+            row = line_of(lowers[i], j)
+            solved[i] = solved[i] - factor * row
+            lowers[i] = lowers[i] - jnp.where(below > j, factor, 0.0) * row
+            pivots[i] = jnp.where(below == j, pivot, pivots[i])
+            scales[i] = jnp.where(below == j, scale, scales[i])
+
+        for j in range(0, block, 2):
+            for i in range(len(states)):
+                cols = heads[i]
+                corner, side = line_of(cols[j], j), line_of(cols[j], j + 1)
+                last = line_of(cols[j + 1], j + 1)
+                minor = corner * last - side * side
+                scale = 1.0 / corner
+                eliminate(i, j, scale, corner, side)
+                eliminate(i, j + 1, corner * (1.0 / minor), minor * scale, None)
+        for i, work in enumerate(states):
+            work[strip] = lowers[i]
+            roots[i][strip] = lax.rsqrt(pivots[i])
+            if strip == strips - 1:
+                continue
+            answer = solved[i] * scales[i]
+            rows = [line_of(answer, j) for j in range(block)]
+            for s in range(strip + 1, strips):
+                for j in range(block):
+                    work[s] = work[s] - columns[i][j][s - strip] * rows[j]
     results = []
-    for work in state:
-        parts = []
-        for s in range(strips):
-            place = iota((8, size), 0) + 8 * s == iota((8, size), 1)
-            pivot = jnp.sum(jnp.where(place, work[s][:, :size], 0.0), axis=1, keepdims=True)
-            parts.append(work[s][:, size : 2 * size] * lax.rsqrt(pivot))
-        results.append(jnp.concatenate(parts, axis=0))
+    for i, work in enumerate(states):
+        scaled = jnp.concatenate([work[s] * roots[i][s] for s in range(strips)], axis=0)
+        for m in range(beside):
+            begin = (2 * m + 1) * size
+            results.append(scaled[:, begin : begin + size])
     return results
 
 

time: 53.5 us -> 52.9 us (0.989)
  waiting for transfers between devices: 7.37 us -> 8.85 us
  starting transfers between devices: 16 us -> 14.6 us
  Pallas kernels: 29.7 us -> 29 us
    pallas_call x1, Pallas kernels: 7.91 us -> 7.14 us  [per_device(): pl.pallas_call(functools.partial(main_kernel, (AXES[0], AXES[1]), early,...]
  transfers between devices with their start and end apart: 14 -> 14, of which waited for: 8 -> 9; matrix products, arithmetic and copies ran while one was open for 0% -> 0% of each run, Pallas kernels for 21% -> 21%
where the time goes in v12:
time: 52.9 us; the launch traced here: 52.7 us
  Pallas kernels  29 us (55%)
  starting transfers between devices  14.6 us (28%)
  waiting for transfers between devices  8.85 us (17%)
    pallas_call x1, Pallas kernels, solve(): pl.pallas_call(functools.partial(solve_kernel, size, len(matrices), colum...  8.19 us
    pallas_call x1, Pallas kernels, per_device(): pl.pallas_call(functools.partial(main_kernel, (AXES[0], AXES[1]), early,...  7.14 us
    ppermute x3, starting transfers between devices, exchange(): lax.ppermute(arrays[0], axis, outer_pairs(axis))  5.97 us
    ppermute x2, starting transfers between devices, exchange(): return [lax.ppermute(arrays[0], axis, flipped(axis, 1))]  3.85 us
    pallas_call x1, Pallas kernels, per_device(): pl.pallas_call(functools.partial(theirs_kernel, faces, ncon), out_shape=s...  3.3 us
    ppermute x1, waiting for transfers between devices, per_device(): rest_other = lax.ppermute(rest_last, 'gy', chip_x)  2.73 us
    pallas_call x1, Pallas kernels, per_device(): pl.pallas_call(functools.partial(halves_kernel, planes), out_shape=[halve...  2.7 us
    pallas_call x1, Pallas kernels, per_device(): pl.pallas_call(functools.partial(early_kernel, AXES[2:3], early), out_sha...  2.58 us
  transfers between devices with their start and end apart: 14, of which 9 were waited for; matrix products, arithmetic and copies ran while one was open for 0% of the time, Pallas kernels for 21%

profile of v12, /device:TPU:0, one launch (start us, length us, event | category | flops | bytes accessed | tf_op | source)
XLA Modules:
  0.0 52.7 jit_solution(3445474858450179074)
XLA Ops:
  0.0 0.0 copy-start.1
  0.0 1.7 %shard_map.46 = (f32[328,128]{1,0:T(8,128)S(1)}, f32[328,128]{1,0:T(8,128)S(1)}, f32[328,128]{1,0:T(8,128)S(1)}, f32[328,128]{1,0:T(8,128)S(1)}, f32[2,264,128]{2,1,0:T(8,128)S(1)}, /*index=5*/f32[6,256,256]{2,1,0:T(8,128)S(1)}) custom-call(f32[1536,1536]{1,0:T(8,128)} %bitcast.10, f32[6,32,256]{2,1,0:T(8,128)} %bitcast.6), custom_call_target="tpu_custom_call" | custom-call | tf_op jit(solution)/shard_map/pallas_call | solution.py:670
  1.7 3.0 %collective-permute-start.4 = (f32[2,264,128]{2,1,0:T(8,128)S(1)}, f32[2,264,128]{2,1,0:T(8,128)S(1)}, u32[]{:S(2)}, u32[]{:S(2)}) collective-permute-start(f32[2,264,128]{2,1,0:T(8,128)S(1)} %get-tuple-element.37), channel_id=1, source_target_pairs={{0,1},{1,0},{2,3},{3,2},{4,5},{5,4},{6,7},{7,6},{8,9},{9,8},{10,11... | collective-permute-start | bytes 811016 | tf_op jit(solution)/shard_map/ppermute | solution.py:86
  4.7 3.6 %collective-permute-start = (f32[328,128]{1,0:T(8,128)S(1)}, f32[328,128]{1,0:T(8,128)S(1)}, u32[]{:S(2)}, u32[]{:S(2)}) collective-permute-start(f32[328,128]{1,0:T(8,128)S(1)} %get-tuple-element.31), channel_id=1, source_target_pairs={{0,24},{8,16},{16,8},{24,0},{1,25},{9,17},{17,9},{25,1},{2,26},{10... | collective-permute-start | bytes 503816 | tf_op jit(solution)/shard_map/ppermute | solution.py:88
  8.3 0.0 collective-permute-start.1
  8.3 0.4 collective-permute-start.2
  8.7 1.2 %collective-permute-start.3 = (f32[328,128]{1,0:T(8,128)S(1)}, f32[328,128]{1,0:T(8,128)S(1)}, u32[]{:S(2)}, u32[]{:S(2)}) collective-permute-start(f32[328,128]{1,0:T(8,128)S(1)} %get-tuple-element.34), channel_id=1, source_target_pairs={{0,2},{2,0},{4,6},{6,4},{1,3},{3,1},{5,7},{7,5},{8,10},{10,8},{12,... | collective-permute-start | bytes 503816 | tf_op jit(solution)/shard_map/ppermute | solution.py:89
  9.9 0.0 copy-done.1
  9.9 0.0 copy-start
  9.9 2.7 %shard_map.47 = (bf16[6,2,256,256]{3,2,1,0:T(8,128)(2,1)S(1)}, bf16[15,2,256,256]{3,2,1,0:T(8,128)(2,1)S(1)}, f32[8,128]{1,0:T(8,128)S(1)}) custom-call(f32[1536,1536]{1,0:T(8,128)} %bitcast.11, s32[8]{0:T(128)S(1)} %copy-done.1, f32[6,256,256]{2,1,0:T(8,128)S(1)} %get-tuple-element.29.own_ref.refs_1_.refs_4_), custom_call_target="tpu_custom_call" | custom-call | flops 2000000000 | bytes 1048576 | tf_op jit(solution)/shard_map/pallas_call | solution.py:690
  12.6 0.0 copy-start.2
  12.7 0.0 collective-permute-done.4.refs_0_
  12.7 0.0 copy-done
  12.7 2.6 %shard_map.48 = (f32[2,32,256]{2,1,0:T(8,128)S(1)}, bf16[2,2,256,256]{3,2,1,0:T(8,128)(2,1)S(1)}, bf16[2,2,256,256]{3,2,1,0:T(8,128)(2,1)S(1)}) custom-call(f32[2,264,128]{2,1,0:T(8,128)S(1)} %collective-permute-done.4.refs_0_, f32[6,256,256]{2,1,0:T(8,128)S(1)} %get-tuple-element.29.own_ref.refs_1_.refs_4_, ...), custom_call_target="tpu_custom_call" | custom-call | flops 2000000000 | bytes 1048576 | tf_op jit(solution)/shard_map/pallas_call | solution.py:703
  15.3 0.0 collective-permute-done.refs_0_
  15.3 0.8 %collective-permute-done.1.refs_1_ = f32[328,128]{1,0:T(8,128)S(1)} collective-permute-done((f32[328,128]{1,0:T(8,128)S(1)}, f32[328,128]{1,0:T(8,128)S(1)}, u32[]{:S(2)}, u32[]{:S(2)}) %collective-permute-start.1) | collective-permute-done | bytes 167968 | tf_op jit(solution)/shard_map/ppermute | solution.py:89
  16.0 0.0 collective-permute-done.2.refs_2_
  16.0 0.0 collective-permute-done.3.refs_3_
  16.0 0.0 copy-done.2
  16.0 7.1 %shard_map.49 = (f32[64,768]{1,0:T(8,128)S(1)}, f32[6,32,256]{2,1,0:T(8,128)S(1)}, bf16[4,2,256,256]{3,2,1,0:T(8,128)(2,1)S(1)}, bf16[4,2,256,256]{3,2,1,0:T(8,128)(2,1)S(1)}) custom-call(f32[328,128]{1,0:T(8,128)S(1)} %collective-permute-done.refs_0_, f32[328,128]{1,0:T(8,128)S(1)} %collective-permute-done.1.refs_1_, ...), custom_call_target="tpu_custom_call" | custom-call | flops 8000000000 | bytes 1048576 | tf_op jit(solution)/shard_map/pallas_call | solution.py:712
  23.2 0.1 collective-permute-start.5
  23.3 1.4 %collective-permute-done.5.there_ref = f32[64,768]{1,0:T(8,128)S(1)} collective-permute-done((f32[64,768]{1,0:T(8,128)S(1)}, f32[64,768]{1,0:T(8,128)S(1)}, u32[]{:S(2)}, u32[]{:S(2)}) %collective-permute-start.5) | collective-permute-done | bytes 196640 | tf_op jit(solution)/shard_map/ppermute | solution.py:766
  24.7 0.1 shard_map.50
  24.8 1.6 %collective-permute-start.6 = (f32[64,384]{1,0:T(8,128)S(1)}, f32[64,384]{1,0:T(8,128)S(1)}, u32[]{:S(2)}, u32[]{:S(2)}) collective-permute-start(f32[64,384]{1,0:T(8,128)S(1)} %get-tuple-element.40.first_ref), channel_id=1, source_target_pairs={{0,4},{2,6},{4,0},{6,2},{1,5},{3,7},{5,1},{7,3},{8,12},{10,14},{12... | collective-permute-start | bytes 294920 | tf_op jit(solution)/shard_map/ppermute | solution.py:774
  26.3 0.5 collective-permute-start.7
  26.8 3.3 %shard_map.51.unread.theirs_ref = f32[4,32,256]{2,1,0:T(8,128)S(1)} custom-call(bf16[6,2,256,256]{3,2,1,0:T(8,128)(2,1)S(1)} %get-tuple-element.35.refs_2_.refs_5_.own_ref, f32[328,128]{1,0:T(8,128)S(1)} %collective-permute-done.refs_0_, f32[328,128]{1,0:T(8,128)S(1)} %collective-permute-done.1.refs_1_, f32[328,128]{1,0:T(8,128)S(1)} %collective-permute-done.2.refs_2_, ...), custom_call_target="tpu_custom_call" | custom-call | flops 2000000000 | bytes 1048576 | tf_op jit(solution)/shard_map/pallas_call | solution.py:724
  30.1 0.0 collective-permute-done.6.second_ref
  30.1 0.8 %collective-permute-done.7.fourth_ref = f32[64,384]{1,0:T(8,128)S(1)} collective-permute-done((f32[64,384]{1,0:T(8,128)S(1)}, f32[64,384]{1,0:T(8,128)S(1)}, u32[]{:S(2)}, u32[]{:S(2)}) %collective-permute-start.7) | collective-permute-done | bytes 98336 | tf_op jit(solution)/shard_map/ppermute | solution.py:775
  31.0 0.6 %collective-permute-start.9 = (f32[64,384]{1,0:T(8,128)S(1)}, f32[64,384]{1,0:T(8,128)S(1)}, u32[]{:S(2)}, u32[]{:S(2)}) collective-permute-start(f32[64,384]{1,0:T(8,128)S(1)} %get-tuple-element.48.refs_2_), channel_id=1, source_target_pairs={{0,4},{2,6},{4,0},{6,2},{1,5},{3,7},{5,1},{7,3},{8,12},{10,14},{12... | collective-permute-start | bytes 294920 | tf_op jit(solution)/shard_map/ppermute | solution.py:785
  31.6 0.7 %collective-permute-start.8 = (f32[64,384]{1,0:T(8,128)S(1)}, f32[64,384]{1,0:T(8,128)S(1)}, u32[]{:S(2)}, u32[]{:S(2)}) collective-permute-start(f32[64,384]{1,0:T(8,128)S(1)} %get-tuple-element.47.unread.refs_0_), channel_id=1, source_target_pairs={{0,1},{1,0},{2,3},{3,2},{4,5},{5,4},{6,7},{7,6},{8,9},{9,8},{10,11... | collective-permute-start | bytes 294920 | tf_op jit(solution)/shard_map/ppermute | solution.py:784
  32.3 0.6 %shard_map.53.refs_4_.refs_0_.spread_ref = bf16[4,256,192]{2,1,0:T(8,128)(2,1)S(1)} custom-call(f32[64,384]{1,0:T(8,128)S(1)} %get-tuple-element.47.unread.refs_0_, f32[4,32,256]{2,1,0:T(8,128)S(1)} %shard_map.51.unread.theirs_ref, f32[6,32,256]{2,1,0:T(8,128)S(1)} %get-tuple-element.42.product_ref, ...), custom_call_target="tpu_custom_call" | custom-call | flops 2000000000 | bytes 1048576 | tf_op jit(solution)/shard_map/pallas_call | solution.py:734
  32.9 2.7 %collective-permute-done.9.refs_3_ = f32[64,384]{1,0:T(8,128)S(1)} collective-permute-done((f32[64,384]{1,0:T(8,128)S(1)}, f32[64,384]{1,0:T(8,128)S(1)}, u32[]{:S(2)}, u32[]{:S(2)}) %collective-permute-start.9) | collective-permute-done | bytes 98336 | tf_op jit(solution)/shard_map/ppermute | solution.py:785
  35.7 0.5 %collective-permute-done.8.refs_1_ = f32[64,384]{1,0:T(8,128)S(1)} collective-permute-done((f32[64,384]{1,0:T(8,128)S(1)}, f32[64,384]{1,0:T(8,128)S(1)}, u32[]{:S(2)}, u32[]{:S(2)}) %collective-permute-start.8) | collective-permute-done | bytes 98336 | tf_op jit(solution)/shard_map/ppermute | solution.py:784
  36.2 8.2 %shard_map.54.here_ref.refs_1_ = f32[192,128]{1,0:T(8,128)S(1)} custom-call(f32[64,384]{1,0:T(8,128)S(1)} %get-tuple-element.47.unread.refs_0_, f32[64,384]{1,0:T(8,128)S(1)} %collective-permute-done.8.refs_1_, f32[64,384]{1,0:T(8,128)S(1)} %get-tuple-element.48.refs_2_, f32[64,384]{1,0:T(8,128)S(1)} %collective-permute-done.9.refs_3_, ...), custom_call_target="tpu_custom_call" | custom-call | flops 7000000000 | bytes 1048576 | tf_op jit(solution)/shard_map/pallas_call | solution.py:744
  44.4 0.1 collective-permute-start.10
  44.5 0.8 %collective-permute-start.13 = (f32[2,32,256]{2,1,0:T(8,128)S(1)}, f32[2,32,256]{2,1,0:T(8,128)S(1)}, u32[]{:S(2)}, u32[]{:S(2)}) collective-permute-start(f32[2,32,256]{2,1,0:T(8,128)S(1)} %get-tuple-element.52), channel_id=1, source_target_pairs={{0,1},{1,0},{2,3},{3,2},{4,5},{5,4},{6,7},{7,6},{8,9},{9,8},{10,11... | collective-permute-start | bytes 196616 | tf_op jit(solution)/shard_map/ppermute | solution.py:86
  45.3 0.5 collective-permute-done.10.there_ref.refs_2_
  45.8 2.0 %collective-permute-start.11 = (f32[32,128]{1,0:T(8,128)S(1)}, f32[32,128]{1,0:T(8,128)S(1)}, u32[]{:S(2)}, u32[]{:S(2)}) collective-permute-start(f32[32,128]{1,0:T(8,128)S(1)} %get-tuple-element.50), channel_id=1, source_target_pairs={{0,24},{8,16},{16,8},{24,0},{1,25},{9,17},{17,9},{25,1},{2,26},{10... | collective-permute-start | bytes 49160 | tf_op jit(solution)/shard_map/ppermute | solution.py:88
  47.8 0.0 collective-permute-start.12
  47.8 1.2 %collective-permute-done.13.refs_3_ = f32[2,32,256]{2,1,0:T(8,128)S(1)} collective-permute-done((f32[2,32,256]{2,1,0:T(8,128)S(1)}, f32[2,32,256]{2,1,0:T(8,128)S(1)}, u32[]{:S(2)}, u32[]{:S(2)}) %collective-permute-start.13) | collective-permute-done | bytes 65568 | tf_op jit(solution)/shard_map/ppermute | solution.py:86
  49.0 1.7 %shard_map.56.refs_2_ = f32[1536,128]{1,0:T(8,128)} custom-call(f32[8,128]{1,0:T(8,128)S(1)} %get-tuple-element.30.flag_ref, f32[6,32,256]{2,1,0:T(8,128)S(1)} %get-tuple-element.42.product_ref, bf16[2,2,256,256]{3,2,1,0:T(8,128)(2,1)S(1)} %get-tuple-element.45.refs_6_.refs_0_.early_inverse, ...), custom_call_target="tpu_custom_call" | custom-call | flops 1000000000 | bytes 1048576 | tf_op jit(solution)/shard_map/pallas_call | solution.py:798
  50.7 0.8 %collective-permute-done.11.refs_0_ = f32[32,128]{1,0:T(8,128)S(1)} collective-permute-done((f32[32,128]{1,0:T(8,128)S(1)}, f32[32,128]{1,0:T(8,128)S(1)}, u32[]{:S(2)}, u32[]{:S(2)}) %collective-permute-start.11) | collective-permute-done | bytes 16416 | tf_op jit(solution)/shard_map/ppermute | solution.py:88
  51.4 0.2 collective-permute-done.12.refs_1_
  51.6 1.0 %shard_map.57 = f32[1536,128]{1,0:T(8,128)} custom-call(bf16[4,256,192]{2,1,0:T(8,128)(2,1)S(1)} %shard_map.53.refs_4_.refs_0_.spread_ref, f32[64,128]{1,0:T(8,128)S(1)} %get-tuple-element.49.rows_ref, f32[32,128]{1,0:T(8,128)S(1)} %collective-permute-done.11.refs_0_, f32[32,128]{1,0:T(8,128)S(1)} %collective-permute-done.12.refs_1_, ...), custom_call_target="tpu_custom_call", output_to_operand_aliasing={{}: (4, {})} | custom-call | flops 1000000000 | bytes 1048576 | tf_op jit(solution)/shard_map/pallas_call | solution.py:832
  (2 shorter events, 0.1 us)
Async XLA Ops:
  0.0 9.9 %copy-start.1 = (s32[8]{0:T(128)S(1)}, s32[8]{0:T(128)}, u32[]{:S(2)}) copy-start(s32[8]{0:T(128)} %group_ref.1) | copy-start | bytes 100
  1.7 11.0 %collective-permute-start.4 = (f32[2,264,128]{2,1,0:T(8,128)S(1)}, f32[2,264,128]{2,1,0:T(8,128)S(1)}, u32[]{:S(2)}, u32[]{:S(2)}) collective-permute-start(f32[2,264,128]{2,1,0:T(8,128)S(1)} %get-tuple-element.37), channel_id=1, source_target_pairs={{0,1},{1,0},{2,3},{3,2},{4,5},{5,4},{6,7},{7,6},{8,9},{9,8},{10,11... | collective-permute-start | bytes 811016 | tf_op jit(solution)/shard_map/ppermute | solution.py:86
  4.7 10.5 %collective-permute-start = (f32[328,128]{1,0:T(8,128)S(1)}, f32[328,128]{1,0:T(8,128)S(1)}, u32[]{:S(2)}, u32[]{:S(2)}) collective-permute-start(f32[328,128]{1,0:T(8,128)S(1)} %get-tuple-element.31), channel_id=1, source_target_pairs={{0,24},{8,16},{16,8},{24,0},{1,25},{9,17},{17,9},{25,1},{2,26},{10... | collective-permute-start | bytes 503816 | tf_op jit(solution)/shard_map/ppermute | solution.py:88
  8.3 7.7 %collective-permute-start.1 = (f32[328,128]{1,0:T(8,128)S(1)}, f32[328,128]{1,0:T(8,128)S(1)}, u32[]{:S(2)}, u32[]{:S(2)}) collective-permute-start(f32[328,128]{1,0:T(8,128)S(1)} %get-tuple-element.32), channel_id=1, source_target_pairs={{0,8},{8,0},{16,24},{24,16},{1,9},{9,1},{17,25},{25,17},{2,10},{10... | collective-permute-start | bytes 503816 | tf_op jit(solution)/shard_map/ppermute | solution.py:89
  8.3 7.7 %collective-permute-start.2 = (f32[328,128]{1,0:T(8,128)S(1)}, f32[328,128]{1,0:T(8,128)S(1)}, u32[]{:S(2)}, u32[]{:S(2)}) collective-permute-start(f32[328,128]{1,0:T(8,128)S(1)} %get-tuple-element.33), channel_id=1, source_target_pairs={{0,6},{2,4},{4,2},{6,0},{1,7},{3,5},{5,3},{7,1},{8,14},{10,12},{12... | collective-permute-start | bytes 503816 | tf_op jit(solution)/shard_map/ppermute | solution.py:88
  8.7 7.3 %collective-permute-start.3 = (f32[328,128]{1,0:T(8,128)S(1)}, f32[328,128]{1,0:T(8,128)S(1)}, u32[]{:S(2)}, u32[]{:S(2)}) collective-permute-start(f32[328,128]{1,0:T(8,128)S(1)} %get-tuple-element.34), channel_id=1, source_target_pairs={{0,2},{2,0},{4,6},{6,4},{1,3},{3,1},{5,7},{7,5},{8,10},{10,8},{12,... | collective-permute-start | bytes 503816 | tf_op jit(solution)/shard_map/ppermute | solution.py:89
  9.9 2.7 %copy-start = (f32[1,1,1,6,256,32]{4,5,3,2,1,0:T(8,128)S(1)}, f32[1,1,1,6,256,32]{4,5,3,2,1,0:T(8,128)}, u32[]{:S(2)}) copy-start(f32[1,1,1,6,256,32]{4,5,3,2,1,0:T(8,128)} %param.5) | copy-start | bytes 589828
  12.6 3.4 %copy-start.2 = (f32[1,1,1,1536,128]{4,3,2,1,0:T(8,128)S(1)}, f32[1,1,1,1536,128]{4,3,2,1,0:T(8,128)}, u32[]{:S(2)}) copy-start(f32[1,1,1,1536,128]{4,3,2,1,0:T(8,128)} %param.6) | copy-start | bytes 2359300
  23.2 1.5 %collective-permute-start.5 = (f32[64,768]{1,0:T(8,128)S(1)}, f32[64,768]{1,0:T(8,128)S(1)}, u32[]{:S(2)}, u32[]{:S(2)}) collective-permute-start(f32[64,768]{1,0:T(8,128)S(1)} %get-tuple-element.39.here_ref), channel_id=1, source_target_pairs={{0,2},{2,0},{4,6},{6,4},{1,3},{3,1},{5,7},{7,5},{8,10},{10,8},{12,... | collective-permute-start | bytes 589832 | tf_op jit(solution)/shard_map/ppermute | solution.py:766
  24.8 5.4 %collective-permute-start.6 = (f32[64,384]{1,0:T(8,128)S(1)}, f32[64,384]{1,0:T(8,128)S(1)}, u32[]{:S(2)}, u32[]{:S(2)}) collective-permute-start(f32[64,384]{1,0:T(8,128)S(1)} %get-tuple-element.40.first_ref), channel_id=1, source_target_pairs={{0,4},{2,6},{4,0},{6,2},{1,5},{3,7},{5,1},{7,3},{8,12},{10,14},{12... | collective-permute-start | bytes 294920 | tf_op jit(solution)/shard_map/ppermute | solution.py:774
  26.3 4.6 %collective-permute-start.7 = (f32[64,384]{1,0:T(8,128)S(1)}, f32[64,384]{1,0:T(8,128)S(1)}, u32[]{:S(2)}, u32[]{:S(2)}) collective-permute-start(f32[64,384]{1,0:T(8,128)S(1)} %get-tuple-element.41.third_ref), channel_id=1, source_target_pairs={{0,1},{1,0},{2,3},{3,2},{4,5},{5,4},{6,7},{7,6},{8,9},{9,8},{10,11... | collective-permute-start | bytes 294920 | tf_op jit(solution)/shard_map/ppermute | solution.py:775
  31.0 4.7 %collective-permute-start.9 = (f32[64,384]{1,0:T(8,128)S(1)}, f32[64,384]{1,0:T(8,128)S(1)}, u32[]{:S(2)}, u32[]{:S(2)}) collective-permute-start(f32[64,384]{1,0:T(8,128)S(1)} %get-tuple-element.48.refs_2_), channel_id=1, source_target_pairs={{0,4},{2,6},{4,0},{6,2},{1,5},{3,7},{5,1},{7,3},{8,12},{10,14},{12... | collective-permute-start | bytes 294920 | tf_op jit(solution)/shard_map/ppermute | solution.py:785
  31.6 4.6 %collective-permute-start.8 = (f32[64,384]{1,0:T(8,128)S(1)}, f32[64,384]{1,0:T(8,128)S(1)}, u32[]{:S(2)}, u32[]{:S(2)}) collective-permute-start(f32[64,384]{1,0:T(8,128)S(1)} %get-tuple-element.47.unread.refs_0_), channel_id=1, source_target_pairs={{0,1},{1,0},{2,3},{3,2},{4,5},{5,4},{6,7},{7,6},{8,9},{9,8},{10,11... | collective-permute-start | bytes 294920 | tf_op jit(solution)/shard_map/ppermute | solution.py:784
  44.4 1.4 %collective-permute-start.10 = (f32[192,128]{1,0:T(8,128)S(1)}, f32[192,128]{1,0:T(8,128)S(1)}, u32[]{:S(2)}, u32[]{:S(2)}) collective-permute-start(f32[192,128]{1,0:T(8,128)S(1)} %shard_map.54.here_ref.refs_1_), channel_id=1, source_target_pairs={{0,2},{2,0},{4,6},{6,4},{1,3},{3,1},{5,7},{7,5},{8,10},{10,8},{12,... | collective-permute-start | bytes 294920 | tf_op jit(solution)/shard_map/ppermute | solution.py:789
  44.5 4.5 %collective-permute-start.13 = (f32[2,32,256]{2,1,0:T(8,128)S(1)}, f32[2,32,256]{2,1,0:T(8,128)S(1)}, u32[]{:S(2)}, u32[]{:S(2)}) collective-permute-start(f32[2,32,256]{2,1,0:T(8,128)S(1)} %get-tuple-element.52), channel_id=1, source_target_pairs={{0,1},{1,0},{2,3},{3,2},{4,5},{5,4},{6,7},{7,6},{8,9},{9,8},{10,11... | collective-permute-start | bytes 196616 | tf_op jit(solution)/shard_map/ppermute | solution.py:86
  45.8 5.6 %collective-permute-start.11 = (f32[32,128]{1,0:T(8,128)S(1)}, f32[32,128]{1,0:T(8,128)S(1)}, u32[]{:S(2)}, u32[]{:S(2)}) collective-permute-start(f32[32,128]{1,0:T(8,128)S(1)} %get-tuple-element.50), channel_id=1, source_target_pairs={{0,24},{8,16},{16,8},{24,0},{1,25},{9,17},{17,9},{25,1},{2,26},{10... | collective-permute-start | bytes 49160 | tf_op jit(solution)/shard_map/ppermute | solution.py:88
  47.8 3.8 %collective-permute-start.12 = (f32[32,128]{1,0:T(8,128)S(1)}, f32[32,128]{1,0:T(8,128)S(1)}, u32[]{:S(2)}, u32[]{:S(2)}) collective-permute-start(f32[32,128]{1,0:T(8,128)S(1)} %get-tuple-element.51), channel_id=1, source_target_pairs={{0,8},{8,0},{16,24},{24,16},{1,9},{9,1},{17,25},{25,17},{2,10},{10... | collective-permute-start | bytes 49160 | tf_op jit(solution)/shard_map/ppermute | solution.py:89

commit v13 on v12

--- a/solution.py
+++ b/solution.py
@@ -249,6 +249,60 @@
             begin = (2 * m + 1) * size
             results.append(scaled[:, begin : begin + size])
     return results
+
+
+def factor_inverse(gram):
+    size = gram.shape[0]
+    strips, block, lanes = size // 8, 8, 128
+    full = (block, lanes)
+    parts = [gram, jnp.where(iota((size, size), 0) == iota((size, size), 1), 1.0, 0.0)]
+    if 2 * size < lanes:
+        parts.append(jnp.zeros((size, lanes - 2 * size), jnp.float32))
+    whole = jnp.concatenate(parts, axis=1)
+    work = [whole[8 * s : 8 * s + 8] for s in range(strips)]
+    below = iota(full, 0)
+
+    def line_of(rows, line):
+        return jnp.broadcast_to(rows[line : line + 1], full)
+
+    for strip in range(strips):
+        start = strip * block
+        active = range(strip, strips)
+        cols = [
+            {s: jnp.broadcast_to(work[s][:, start + j : start + j + 1], full) for s in active}
+            for j in range(block)
+        ]
+        factors = []
+
+        def eliminate(j, scale, side):
+            factor = {s: cols[j][s] * scale for s in active}
+            factor[strip] = jnp.where(below > j, factor[strip], 0.0)
+            for later in range(j + 1, block):
+                use = side if later == j + 1 and side is not None else None
+                head = line_of(cols[later][strip], j) if use is None else use
+                for s in active:
+                    cols[later][s] = cols[later][s] - factor[s] * head
+            factors.append(factor)
+
+        for j in range(0, block, 2):
+            corner = line_of(cols[j][strip], j)
+            side = line_of(cols[j][strip], j + 1)
+            last = line_of(cols[j + 1][strip], j + 1)
+            inverse = 1.0 / (corner * last - side * side)
+            eliminate(j, 1.0 / corner, side)
+            eliminate(j + 1, corner * inverse, None)
+        for j in range(block):
+            row = line_of(work[strip], j)
+            for s in active:
+                if s == strip and j == block - 1:
+                    continue
+                work[s] = work[s] - factors[j][s] * row
+    parts = []
+    for s in range(strips):
+        place = iota((8, size), 0) + 8 * s == iota((8, size), 1)
+        pivot = jnp.sum(jnp.where(place, work[s][:, :size], 0.0), axis=1, keepdims=True)
+        parts.append(work[s][:, size : 2 * size] * lax.rsqrt(pivot))
+    return jnp.concatenate(parts, axis=0)
 
 
 def member(group_ref, planes, dy=0, dz=0):
@@ -407,31 +461,37 @@
         project(*item)
     for i, f in enumerate(late):
         project(f, basis[i])
+    tall = {}
+    for g in range(FACES):
+        column = jnp.concatenate([sides[f][g] for f in range(g + 1)], axis=0)
+        column = triple(column, vectors[g], ((1,), (1,)))
+        for f in range(g + 1):
+            tall[f, g] = column[f * ncon : (f + 1) * ncon]
+    for f in range(0, FACES, 2):
+        tall[f + 1, f] = tall[f, f + 1].T
+    zero = jnp.zeros((ncon, ncon), jnp.float32)
+
+    def square(parts):
+        lines = []
+        for f in range(FACES):
+            line = [parts.get((f, g), zero) for g in range(FACES)]
+            lines.append(jnp.concatenate(line, axis=1))
+        return jnp.concatenate(lines, axis=0)
+
+    coarse = square(tall)
+    right = jnp.concatenate([rights[f] for f in range(FACES)], axis=0)
     factors = factor_inverses([grams[f] for f in range(FACES)])
-    blocks = []
-    for g in range(FACES):
-        tall = jnp.concatenate([sides[f][g] for f in range(g + 1)], axis=0)
-        blocks.append(triple(triple(tall, vectors[g], ((1,), (1,))), factors[g], ((1,), (1,))))
-    even, odd, right = [], [], []
-    lows = None
+    factor = square({(f, f): factors[f] for f in range(FACES)})
+    coarse = triple(factor, triple(coarse, factor, ((1,), (1,))))
+    right = triple(factor, right)
     for f in range(FACES):
         product_ref[f] = triple(factors[f], sides[f][f])
-        line = [blocks[g][f * ncon : (f + 1) * ncon] for g in range(f, FACES)]
-        line = triple(factors[f], jnp.concatenate([rights[f]] + line, axis=1))
-        right.append(line[:, :columns])
-        line = line[:, columns:]
-        if f % 2 == 0:
-            even.append(line)
-            lows = line[:, ncon : 2 * ncon].T
-        else:
-            odd += [lows, line]
-    payload_ref[...] = jnp.concatenate(
-        [
-            jnp.concatenate(even + right[0::2], axis=1),
-            jnp.concatenate(odd + right[1::2], axis=1),
-        ],
-        axis=0,
-    )
+    size = 2 * ncon
+    line = []
+    for b in range(BLOCKS):
+        line.append(coarse[b * size : (b + 1) * size, b * size :])
+    line += [right[b * size : (b + 1) * size] for b in range(BLOCKS)]
+    payload_ref[...] = jnp.concatenate(line, axis=1)
 
 
 def find(faces, refs, f):
@@ -441,8 +501,8 @@
 
 
 def theirs_kernel(faces, ncon, own_ref, *refs):
-    inputs, partner_refs, inverse_refs = refs[:-5], refs[-5:-3], refs[-3:-1]
-    product_out = refs[-1]
+    inputs, partner_refs, inverse_refs = refs[:-6], refs[-6:-4], refs[-4:-2]
+    basis_out, product_out = refs[-2:]
     basis = []
     done = 0
     for axis in AXES[:2]:
@@ -458,15 +518,18 @@
     ]
     for sweep in range(SUB_ITERS):
         basis = sweep_basis(*matrices, basis)
+    for f in range(count):
+        basis_out[f] = basis[f]
+        product_out[f] = thin(stacked(basis[f]), matrices[2][f])
+
+
+def spread_kernel(faces, unread, basis_ref, theirs_ref, product_ref, *refs):
+    inverse_refs, out_ref = refs[:2], refs[2]
+    basis = [basis_ref[f] for f in range(basis_ref.shape[0])]
     factors = factor_inverses([dot(b, b, ((1,), (1,))) for b in basis])
-    for f in range(count):
-        product_out[f] = triple(factors[f], thin(stacked(basis[f]), matrices[2][f]))
-
-
-def spread_kernel(faces, unread, theirs_ref, product_ref, *refs):
-    inverse_refs, out_ref = refs[:2], refs[2]
-    for f in range(theirs_ref.shape[0]):
-        both = jnp.concatenate([product_ref[f], theirs_ref[f]], axis=0)
+    for f in range(len(basis)):
+        theirs = triple(factors[f], theirs_ref[f])
+        both = jnp.concatenate([product_ref[f], theirs], axis=0)
         high, low = split(thin(stacked(both), find(faces, inverse_refs, f)).T)
         out_ref[f] = jnp.concatenate([high, high, low], axis=1)
 
@@ -515,7 +578,7 @@
                 blocks[c, b] = blocks[b, c].T
         rights.append(downs[b] * right[:, b * columns : (b + 1) * columns])
     for b in range(BLOCKS):
-        (inverse,) = factor_inverses([blocks[b, b]])
+        inverse = factor_inverse(blocks[b, b])
         later = range(b + 1, BLOCKS)
         row = triple(inverse, jnp.concatenate([rights[b]] + [blocks[b, c] for c in later], axis=1))
         if later:
@@ -721,11 +784,11 @@
 
     partners = [early_partner, late_partner]
     inverses = [early_inverse, late_inverse]
-    their_product = pl.pallas_call(
+    their_basis, their_product = pl.pallas_call(
         functools.partial(theirs_kernel, faces, ncon),
-        out_shape=shape(4, ncon, width),
+        out_shape=[shape(4, ncon, width)] * 2,
         in_specs=vmem_specs(5 + len(got[0]) + len(got[1])),
-        out_specs=vmem_specs(1)[0],
+        out_specs=vmem_specs(2),
         compiler_params=params(16),
         cost_estimate=cost(2),
     )(own_halves, *got[0], *got[1], *partners, *inverses)
@@ -734,11 +797,11 @@
         return pl.pallas_call(
             functools.partial(spread_kernel, faces),
             out_shape=jax.ShapeDtypeStruct((4, width, 3 * size), jnp.bfloat16),
-            in_specs=[anywhere] + vmem_specs(4),
+            in_specs=[anywhere] + vmem_specs(5),
             out_specs=vmem_specs(1)[0],
             compiler_params=params(16),
             cost_estimate=cost(2),
-        )(token, their_product, product, *inverses)
+        )(token, their_basis, their_product, product, *inverses)
 
     def solve(matrices, rights, unread):
         return pl.pallas_call(
@@ -780,7 +843,7 @@
             in_specs=vmem_specs(5) + [anywhere],
             out_specs=vmem_specs(2 + face_arrays(counts[2])),
             compiler_params=params(8),
-        )(left, left_moved, rest, rest_moved, product, their_product)
+        )(left, left_moved, rest, rest_moved, product, their_basis)
         left_other = lax.ppermute(left_last, "gz", chip_y)
         rest_other = lax.ppermute(rest_last, "gy", chip_x)
         theirs = exchange(sent, AXES[2])

time: 52.9 us -> 51.2 us (0.968)
  Pallas kernels: 29 us -> 27 us
  waiting for transfers between devices: 8.85 us -> 9.7 us
    pallas_call x1, Pallas kernels: 3.3 us -> 1.58 us  [per_device(): pl.pallas_call(functools.partial(theirs_kernel, faces, ncon), out_shape=[...]
    pallas_call x1, Pallas kernels: 0.59 us -> 1.95 us  [spread_of(): pl.pallas_call(functools.partial(spread_kernel, faces), out_shape=jax.Sha...]
    ppermute x1, waiting for transfers between devices: 0.01 us -> 1.26 us  [per_device(): left_moved = lax.ppermute(left, 'gy', chip_x)]
    ppermute x1, waiting for transfers between devices: 2.73 us -> 1.62 us  [per_device(): rest_other = lax.ppermute(rest_last, 'gy', chip_x)]
    pallas_call x1, Pallas kernels: 7.14 us -> 6.29 us  [per_device(): pl.pallas_call(functools.partial(main_kernel, (AXES[0], AXES[1]), early,...]
    pallas_call x1, Pallas kernels: 8.19 us -> 7.41 us  [solve(): pl.pallas_call(functools.partial(solve_kernel, size, len(matrices), colum...]
  transfers between devices with their start and end apart: 14 -> 14, of which waited for: 9 -> 10; matrix products, arithmetic and copies ran while one was open for 0% -> 0% of each run, Pallas kernels for 21% -> 21%
where the time goes in v13:
time: 51.2 us; the launch traced here: 51.1 us
  Pallas kernels  27 us (53%)
  starting transfers between devices  14.1 us (28%)
  waiting for transfers between devices  9.7 us (19%)
    pallas_call x1, Pallas kernels, solve(): pl.pallas_call(functools.partial(solve_kernel, size, len(matrices), colum...  7.41 us
    pallas_call x1, Pallas kernels, per_device(): pl.pallas_call(functools.partial(main_kernel, (AXES[0], AXES[1]), early,...  6.29 us
    ppermute x3, starting transfers between devices, exchange(): lax.ppermute(arrays[0], axis, outer_pairs(axis))  5.97 us
    ppermute x2, starting transfers between devices, exchange(): return [lax.ppermute(arrays[0], axis, flipped(axis, 1))]  3.61 us
    pallas_call x1, Pallas kernels, per_device(): pl.pallas_call(functools.partial(halves_kernel, planes), out_shape=[halve...  2.7 us
    pallas_call x1, Pallas kernels, per_device(): pl.pallas_call(functools.partial(early_kernel, AXES[2:3], early), out_sha...  2.58 us
    pallas_call x1, Pallas kernels, spread_of(): pl.pallas_call(functools.partial(spread_kernel, faces), out_shape=jax.Sha...  1.95 us
    pallas_call x1, Pallas kernels, per_device(): pl.pallas_call(functools.partial(pack_kernel, counts, width), out_shape=f...  1.68 us
  transfers between devices with their start and end apart: 14, of which 10 were waited for; matrix products, arithmetic and copies ran while one was open for 0% of the time, Pallas kernels for 21%

profile of v13, /device:TPU:0, one launch (start us, length us, event | category | flops | bytes accessed | tf_op | source)
XLA Modules:
  0.0 51.1 jit_solution(529486672191479678)
XLA Ops:
  0.0 0.0 copy-start.1
  0.0 1.7 %shard_map.46 = (f32[328,128]{1,0:T(8,128)S(1)}, f32[328,128]{1,0:T(8,128)S(1)}, f32[328,128]{1,0:T(8,128)S(1)}, f32[328,128]{1,0:T(8,128)S(1)}, f32[2,264,128]{2,1,0:T(8,128)S(1)}, /*index=5*/f32[6,256,256]{2,1,0:T(8,128)S(1)}) custom-call(f32[1536,1536]{1,0:T(8,128)} %bitcast.10, f32[6,32,256]{2,1,0:T(8,128)} %bitcast.6), custom_call_target="tpu_custom_call" | custom-call | tf_op jit(solution)/shard_map/pallas_call | solution.py:733
  1.7 3.0 %collective-permute-start.4 = (f32[2,264,128]{2,1,0:T(8,128)S(1)}, f32[2,264,128]{2,1,0:T(8,128)S(1)}, u32[]{:S(2)}, u32[]{:S(2)}) collective-permute-start(f32[2,264,128]{2,1,0:T(8,128)S(1)} %get-tuple-element.39), channel_id=1, source_target_pairs={{0,1},{1,0},{2,3},{3,2},{4,5},{5,4},{6,7},{7,6},{8,9},{9,8},{10,11... | collective-permute-start | bytes 811016 | tf_op jit(solution)/shard_map/ppermute | solution.py:86
  4.7 3.6 %collective-permute-start = (f32[328,128]{1,0:T(8,128)S(1)}, f32[328,128]{1,0:T(8,128)S(1)}, u32[]{:S(2)}, u32[]{:S(2)}) collective-permute-start(f32[328,128]{1,0:T(8,128)S(1)} %get-tuple-element.33), channel_id=1, source_target_pairs={{0,24},{8,16},{16,8},{24,0},{1,25},{9,17},{17,9},{25,1},{2,26},{10... | collective-permute-start | bytes 503816 | tf_op jit(solution)/shard_map/ppermute | solution.py:88
  8.3 0.0 collective-permute-start.1
  8.3 0.4 collective-permute-start.2
  8.7 1.2 %collective-permute-start.3 = (f32[328,128]{1,0:T(8,128)S(1)}, f32[328,128]{1,0:T(8,128)S(1)}, u32[]{:S(2)}, u32[]{:S(2)}) collective-permute-start(f32[328,128]{1,0:T(8,128)S(1)} %get-tuple-element.36), channel_id=1, source_target_pairs={{0,2},{2,0},{4,6},{6,4},{1,3},{3,1},{5,7},{7,5},{8,10},{10,8},{12,... | collective-permute-start | bytes 503816 | tf_op jit(solution)/shard_map/ppermute | solution.py:89
  9.9 0.0 copy-done.1
  9.9 0.0 copy-start
  9.9 2.7 %shard_map.47 = (bf16[6,2,256,256]{3,2,1,0:T(8,128)(2,1)S(1)}, bf16[15,2,256,256]{3,2,1,0:T(8,128)(2,1)S(1)}, f32[8,128]{1,0:T(8,128)S(1)}) custom-call(f32[1536,1536]{1,0:T(8,128)} %bitcast.11, s32[8]{0:T(128)S(1)} %copy-done.1, f32[6,256,256]{2,1,0:T(8,128)S(1)} %get-tuple-element.31.own_ref.refs_1_.refs_4_), custom_call_target="tpu_custom_call" | custom-call | flops 2000000000 | bytes 1048576 | tf_op jit(solution)/shard_map/pallas_call | solution.py:753
  12.6 0.0 copy-start.2
  12.7 0.0 collective-permute-done.4.refs_0_
  12.7 0.0 copy-done
  12.7 2.6 %shard_map.48 = (f32[2,32,256]{2,1,0:T(8,128)S(1)}, bf16[2,2,256,256]{3,2,1,0:T(8,128)(2,1)S(1)}, bf16[2,2,256,256]{3,2,1,0:T(8,128)(2,1)S(1)}) custom-call(f32[2,264,128]{2,1,0:T(8,128)S(1)} %collective-permute-done.4.refs_0_, f32[6,256,256]{2,1,0:T(8,128)S(1)} %get-tuple-element.31.own_ref.refs_1_.refs_4_, ...), custom_call_target="tpu_custom_call" | custom-call | flops 2000000000 | bytes 1048576 | tf_op jit(solution)/shard_map/pallas_call | solution.py:766
  15.3 0.0 collective-permute-done.refs_0_
  15.3 0.8 %collective-permute-done.1.refs_1_ = f32[328,128]{1,0:T(8,128)S(1)} collective-permute-done((f32[328,128]{1,0:T(8,128)S(1)}, f32[328,128]{1,0:T(8,128)S(1)}, u32[]{:S(2)}, u32[]{:S(2)}) %collective-permute-start.1) | collective-permute-done | bytes 167968 | tf_op jit(solution)/shard_map/ppermute | solution.py:89
  16.0 0.0 collective-permute-done.2.refs_2_
  16.0 0.0 collective-permute-done.3.refs_3_
  16.0 0.0 copy-done.2
  16.0 6.3 %shard_map.49 = (f32[64,768]{1,0:T(8,128)S(1)}, f32[6,32,256]{2,1,0:T(8,128)S(1)}, bf16[4,2,256,256]{3,2,1,0:T(8,128)(2,1)S(1)}, bf16[4,2,256,256]{3,2,1,0:T(8,128)(2,1)S(1)}) custom-call(f32[328,128]{1,0:T(8,128)S(1)} %collective-permute-done.refs_0_, f32[328,128]{1,0:T(8,128)S(1)} %collective-permute-done.1.refs_1_, ...), custom_call_target="tpu_custom_call" | custom-call | flops 8000000000 | bytes 1048576 | tf_op jit(solution)/shard_map/pallas_call | solution.py:775
  22.3 0.1 collective-permute-start.5
  22.4 1.4 %collective-permute-done.5.there_ref = f32[64,768]{1,0:T(8,128)S(1)} collective-permute-done((f32[64,768]{1,0:T(8,128)S(1)}, f32[64,768]{1,0:T(8,128)S(1)}, u32[]{:S(2)}, u32[]{:S(2)}) %collective-permute-start.5) | collective-permute-done | bytes 196640 | tf_op jit(solution)/shard_map/ppermute | solution.py:829
  23.8 0.1 shard_map.50
  23.9 1.6 %collective-permute-start.6 = (f32[64,384]{1,0:T(8,128)S(1)}, f32[64,384]{1,0:T(8,128)S(1)}, u32[]{:S(2)}, u32[]{:S(2)}) collective-permute-start(f32[64,384]{1,0:T(8,128)S(1)} %get-tuple-element.42.first_ref), channel_id=1, source_target_pairs={{0,4},{2,6},{4,0},{6,2},{1,5},{3,7},{5,1},{7,3},{8,12},{10,14},{12... | collective-permute-start | bytes 294920 | tf_op jit(solution)/shard_map/ppermute | solution.py:837
  25.5 0.5 collective-permute-start.7
  26.0 1.6 %shard_map.51 = (f32[4,32,256]{2,1,0:T(8,128)S(1)}, f32[4,32,256]{2,1,0:T(8,128)S(1)}) custom-call(bf16[6,2,256,256]{3,2,1,0:T(8,128)(2,1)S(1)} %get-tuple-element.37.refs_2_.refs_5_.own_ref, f32[328,128]{1,0:T(8,128)S(1)} %collective-permute-done.refs_0_, f32[328,128]{1,0:T(8,128)S(1)} %collective-permute-done.1.refs_1_, ...), custom_call_target="tpu_custom_call" | custom-call | flops 2000000000 | bytes 1048576 | tf_op jit(solution)/shard_map/pallas_call | solution.py:787
  27.5 1.3 %collective-permute-done.6.second_ref = f32[64,384]{1,0:T(8,128)S(1)} collective-permute-done((f32[64,384]{1,0:T(8,128)S(1)}, f32[64,384]{1,0:T(8,128)S(1)}, u32[]{:S(2)}, u32[]{:S(2)}) %collective-permute-start.6) | collective-permute-done | bytes 98336 | tf_op jit(solution)/shard_map/ppermute | solution.py:837
  28.8 1.3 %collective-permute-done.7.fourth_ref = f32[64,384]{1,0:T(8,128)S(1)} collective-permute-done((f32[64,384]{1,0:T(8,128)S(1)}, f32[64,384]{1,0:T(8,128)S(1)}, u32[]{:S(2)}, u32[]{:S(2)}) %collective-permute-start.7) | collective-permute-done | bytes 98336 | tf_op jit(solution)/shard_map/ppermute | solution.py:838
  30.1 0.6 %collective-permute-start.9 = (f32[64,384]{1,0:T(8,128)S(1)}, f32[64,384]{1,0:T(8,128)S(1)}, u32[]{:S(2)}, u32[]{:S(2)}) collective-permute-start(f32[64,384]{1,0:T(8,128)S(1)} %get-tuple-element.52.refs_2_), channel_id=1, source_target_pairs={{0,4},{2,6},{4,0},{6,2},{1,5},{3,7},{5,1},{7,3},{8,12},{10,14},{12... | collective-permute-start | bytes 294920 | tf_op jit(solution)/shard_map/ppermute | solution.py:848
  30.7 0.5 collective-permute-start.8
  31.2 1.9 %shard_map.53.refs_4_.refs_0_.spread_ref = bf16[4,256,192]{2,1,0:T(8,128)(2,1)S(1)} custom-call(f32[64,384]{1,0:T(8,128)S(1)} %get-tuple-element.50.unread.refs_0_, f32[4,32,256]{2,1,0:T(8,128)S(1)} %get-tuple-element.49.unread.basis_ref, f32[4,32,256]{2,1,0:T(8,128)S(1)} %get-tuple-element.51.theirs_ref, f32[6,32,256]{2,1,0:T(8,128)S(1)} %get-tuple-element.44.product_ref, ...), custom_call_target="tpu_custom_call" | custom-call | flops 2000000000 | bytes 1048576 | tf_op jit(solution)/shard_map/pallas_call | solution.py:797
  33.2 1.6 %collective-permute-done.9.refs_3_ = f32[64,384]{1,0:T(8,128)S(1)} collective-permute-done((f32[64,384]{1,0:T(8,128)S(1)}, f32[64,384]{1,0:T(8,128)S(1)}, u32[]{:S(2)}, u32[]{:S(2)}) %collective-permute-start.9) | collective-permute-done | bytes 98336 | tf_op jit(solution)/shard_map/ppermute | solution.py:848
  34.8 0.5 %collective-permute-done.8.refs_1_ = f32[64,384]{1,0:T(8,128)S(1)} collective-permute-done((f32[64,384]{1,0:T(8,128)S(1)}, f32[64,384]{1,0:T(8,128)S(1)}, u32[]{:S(2)}, u32[]{:S(2)}) %collective-permute-start.8) | collective-permute-done | bytes 98336 | tf_op jit(solution)/shard_map/ppermute | solution.py:847
  35.3 7.4 %shard_map.54.here_ref.refs_1_ = f32[192,128]{1,0:T(8,128)S(1)} custom-call(f32[64,384]{1,0:T(8,128)S(1)} %get-tuple-element.50.unread.refs_0_, f32[64,384]{1,0:T(8,128)S(1)} %collective-permute-done.8.refs_1_, f32[64,384]{1,0:T(8,128)S(1)} %get-tuple-element.52.refs_2_, f32[64,384]{1,0:T(8,128)S(1)} %collective-permute-done.9.refs_3_, ...), custom_call_target="tpu_custom_call" | custom-call | flops 7000000000 | bytes 1048576 | tf_op jit(solution)/shard_map/pallas_call | solution.py:807
  42.7 0.1 collective-permute-start.10
  42.8 0.6 %collective-permute-start.13 = (f32[2,32,256]{2,1,0:T(8,128)S(1)}, f32[2,32,256]{2,1,0:T(8,128)S(1)}, u32[]{:S(2)}, u32[]{:S(2)}) collective-permute-start(f32[2,32,256]{2,1,0:T(8,128)S(1)} %get-tuple-element.56), channel_id=1, source_target_pairs={{0,1},{1,0},{2,3},{3,2},{4,5},{5,4},{6,7},{7,6},{8,9},{9,8},{10,11... | collective-permute-start | bytes 196616 | tf_op jit(solution)/shard_map/ppermute | solution.py:86
  43.4 0.7 %collective-permute-done.10.there_ref.refs_2_ = f32[192,128]{1,0:T(8,128)S(1)} collective-permute-done((f32[192,128]{1,0:T(8,128)S(1)}, f32[192,128]{1,0:T(8,128)S(1)}, u32[]{:S(2)}, u32[]{:S(2)}) %collective-permute-start.10) | collective-permute-done | bytes 98336 | tf_op jit(solution)/shard_map/ppermute | solution.py:852
  44.2 2.0 %collective-permute-start.11 = (f32[32,128]{1,0:T(8,128)S(1)}, f32[32,128]{1,0:T(8,128)S(1)}, u32[]{:S(2)}, u32[]{:S(2)}) collective-permute-start(f32[32,128]{1,0:T(8,128)S(1)} %get-tuple-element.54), channel_id=1, source_target_pairs={{0,24},{8,16},{16,8},{24,0},{1,25},{9,17},{17,9},{25,1},{2,26},{10... | collective-permute-start | bytes 49160 | tf_op jit(solution)/shard_map/ppermute | solution.py:88
  46.2 0.0 collective-permute-start.12
  46.2 1.2 %collective-permute-done.13.refs_3_ = f32[2,32,256]{2,1,0:T(8,128)S(1)} collective-permute-done((f32[2,32,256]{2,1,0:T(8,128)S(1)}, f32[2,32,256]{2,1,0:T(8,128)S(1)}, u32[]{:S(2)}, u32[]{:S(2)}) %collective-permute-start.13) | collective-permute-done | bytes 65568 | tf_op jit(solution)/shard_map/ppermute | solution.py:86
  47.3 1.7 %shard_map.56.refs_2_ = f32[1536,128]{1,0:T(8,128)} custom-call(f32[8,128]{1,0:T(8,128)S(1)} %get-tuple-element.32.flag_ref, f32[6,32,256]{2,1,0:T(8,128)S(1)} %get-tuple-element.44.product_ref, bf16[2,2,256,256]{3,2,1,0:T(8,128)(2,1)S(1)} %get-tuple-element.47.refs_6_.refs_0_.early_inverse, ...), custom_call_target="tpu_custom_call" | custom-call | flops 1000000000 | bytes 1048576 | tf_op jit(solution)/shard_map/pallas_call | solution.py:861
  49.0 0.8 %collective-permute-done.11.refs_0_ = f32[32,128]{1,0:T(8,128)S(1)} collective-permute-done((f32[32,128]{1,0:T(8,128)S(1)}, f32[32,128]{1,0:T(8,128)S(1)}, u32[]{:S(2)}, u32[]{:S(2)}) %collective-permute-start.11) | collective-permute-done | bytes 16416 | tf_op jit(solution)/shard_map/ppermute | solution.py:88
  49.8 0.2 collective-permute-done.12.refs_1_
  49.9 1.0 %shard_map.57 = f32[1536,128]{1,0:T(8,128)} custom-call(bf16[4,256,192]{2,1,0:T(8,128)(2,1)S(1)} %shard_map.53.refs_4_.refs_0_.spread_ref, f32[64,128]{1,0:T(8,128)S(1)} %get-tuple-element.53.rows_ref, f32[32,128]{1,0:T(8,128)S(1)} %collective-permute-done.11.refs_0_, f32[32,128]{1,0:T(8,128)S(1)} %collective-permute-done.12.refs_1_, ...), custom_call_target="tpu_custom_call", output_to_operand_aliasing={{}: (4, {})} | custom-call | flops 1000000000 | bytes 1048576 | tf_op jit(solution)/shard_map/pallas_call | solution.py:895
  (2 shorter events, 0.1 us)
Async XLA Ops:
  0.0 9.9 %copy-start.1 = (s32[8]{0:T(128)S(1)}, s32[8]{0:T(128)}, u32[]{:S(2)}) copy-start(s32[8]{0:T(128)} %group_ref.1) | copy-start | bytes 100
  1.7 11.0 %collective-permute-start.4 = (f32[2,264,128]{2,1,0:T(8,128)S(1)}, f32[2,264,128]{2,1,0:T(8,128)S(1)}, u32[]{:S(2)}, u32[]{:S(2)}) collective-permute-start(f32[2,264,128]{2,1,0:T(8,128)S(1)} %get-tuple-element.39), channel_id=1, source_target_pairs={{0,1},{1,0},{2,3},{3,2},{4,5},{5,4},{6,7},{7,6},{8,9},{9,8},{10,11... | collective-permute-start | bytes 811016 | tf_op jit(solution)/shard_map/ppermute | solution.py:86
  4.7 10.5 %collective-permute-start = (f32[328,128]{1,0:T(8,128)S(1)}, f32[328,128]{1,0:T(8,128)S(1)}, u32[]{:S(2)}, u32[]{:S(2)}) collective-permute-start(f32[328,128]{1,0:T(8,128)S(1)} %get-tuple-element.33), channel_id=1, source_target_pairs={{0,24},{8,16},{16,8},{24,0},{1,25},{9,17},{17,9},{25,1},{2,26},{10... | collective-permute-start | bytes 503816 | tf_op jit(solution)/shard_map/ppermute | solution.py:88
  8.3 7.7 %collective-permute-start.1 = (f32[328,128]{1,0:T(8,128)S(1)}, f32[328,128]{1,0:T(8,128)S(1)}, u32[]{:S(2)}, u32[]{:S(2)}) collective-permute-start(f32[328,128]{1,0:T(8,128)S(1)} %get-tuple-element.34), channel_id=1, source_target_pairs={{0,8},{8,0},{16,24},{24,16},{1,9},{9,1},{17,25},{25,17},{2,10},{10... | collective-permute-start | bytes 503816 | tf_op jit(solution)/shard_map/ppermute | solution.py:89
  8.3 7.7 %collective-permute-start.2 = (f32[328,128]{1,0:T(8,128)S(1)}, f32[328,128]{1,0:T(8,128)S(1)}, u32[]{:S(2)}, u32[]{:S(2)}) collective-permute-start(f32[328,128]{1,0:T(8,128)S(1)} %get-tuple-element.35), channel_id=1, source_target_pairs={{0,6},{2,4},{4,2},{6,0},{1,7},{3,5},{5,3},{7,1},{8,14},{10,12},{12... | collective-permute-start | bytes 503816 | tf_op jit(solution)/shard_map/ppermute | solution.py:88
  8.7 7.3 %collective-permute-start.3 = (f32[328,128]{1,0:T(8,128)S(1)}, f32[328,128]{1,0:T(8,128)S(1)}, u32[]{:S(2)}, u32[]{:S(2)}) collective-permute-start(f32[328,128]{1,0:T(8,128)S(1)} %get-tuple-element.36), channel_id=1, source_target_pairs={{0,2},{2,0},{4,6},{6,4},{1,3},{3,1},{5,7},{7,5},{8,10},{10,8},{12,... | collective-permute-start | bytes 503816 | tf_op jit(solution)/shard_map/ppermute | solution.py:89
  9.9 2.7 %copy-start = (f32[1,1,1,6,256,32]{4,5,3,2,1,0:T(8,128)S(1)}, f32[1,1,1,6,256,32]{4,5,3,2,1,0:T(8,128)}, u32[]{:S(2)}) copy-start(f32[1,1,1,6,256,32]{4,5,3,2,1,0:T(8,128)} %param.5) | copy-start | bytes 589828
  12.6 3.4 %copy-start.2 = (f32[1,1,1,1536,128]{4,3,2,1,0:T(8,128)S(1)}, f32[1,1,1,1536,128]{4,3,2,1,0:T(8,128)}, u32[]{:S(2)}) copy-start(f32[1,1,1,1536,128]{4,3,2,1,0:T(8,128)} %param.6) | copy-start | bytes 2359300
  22.3 1.5 %collective-permute-start.5 = (f32[64,768]{1,0:T(8,128)S(1)}, f32[64,768]{1,0:T(8,128)S(1)}, u32[]{:S(2)}, u32[]{:S(2)}) collective-permute-start(f32[64,768]{1,0:T(8,128)S(1)} %get-tuple-element.41.here_ref), channel_id=1, source_target_pairs={{0,2},{2,0},{4,6},{6,4},{1,3},{3,1},{5,7},{7,5},{8,10},{10,8},{12,... | collective-permute-start | bytes 589832 | tf_op jit(solution)/shard_map/ppermute | solution.py:829
  23.9 4.9 %collective-permute-start.6 = (f32[64,384]{1,0:T(8,128)S(1)}, f32[64,384]{1,0:T(8,128)S(1)}, u32[]{:S(2)}, u32[]{:S(2)}) collective-permute-start(f32[64,384]{1,0:T(8,128)S(1)} %get-tuple-element.42.first_ref), channel_id=1, source_target_pairs={{0,4},{2,6},{4,0},{6,2},{1,5},{3,7},{5,1},{7,3},{8,12},{10,14},{12... | collective-permute-start | bytes 294920 | tf_op jit(solution)/shard_map/ppermute | solution.py:837
  25.5 4.6 %collective-permute-start.7 = (f32[64,384]{1,0:T(8,128)S(1)}, f32[64,384]{1,0:T(8,128)S(1)}, u32[]{:S(2)}, u32[]{:S(2)}) collective-permute-start(f32[64,384]{1,0:T(8,128)S(1)} %get-tuple-element.43.third_ref), channel_id=1, source_target_pairs={{0,1},{1,0},{2,3},{3,2},{4,5},{5,4},{6,7},{7,6},{8,9},{9,8},{10,11... | collective-permute-start | bytes 294920 | tf_op jit(solution)/shard_map/ppermute | solution.py:838
  30.1 4.7 %collective-permute-start.9 = (f32[64,384]{1,0:T(8,128)S(1)}, f32[64,384]{1,0:T(8,128)S(1)}, u32[]{:S(2)}, u32[]{:S(2)}) collective-permute-start(f32[64,384]{1,0:T(8,128)S(1)} %get-tuple-element.52.refs_2_), channel_id=1, source_target_pairs={{0,4},{2,6},{4,0},{6,2},{1,5},{3,7},{5,1},{7,3},{8,12},{10,14},{12... | collective-permute-start | bytes 294920 | tf_op jit(solution)/shard_map/ppermute | solution.py:848
  30.7 4.6 %collective-permute-start.8 = (f32[64,384]{1,0:T(8,128)S(1)}, f32[64,384]{1,0:T(8,128)S(1)}, u32[]{:S(2)}, u32[]{:S(2)}) collective-permute-start(f32[64,384]{1,0:T(8,128)S(1)} %get-tuple-element.50.unread.refs_0_), channel_id=1, source_target_pairs={{0,1},{1,0},{2,3},{3,2},{4,5},{5,4},{6,7},{7,6},{8,9},{9,8},{10,11... | collective-permute-start | bytes 294920 | tf_op jit(solution)/shard_map/ppermute | solution.py:847
  42.7 1.4 %collective-permute-start.10 = (f32[192,128]{1,0:T(8,128)S(1)}, f32[192,128]{1,0:T(8,128)S(1)}, u32[]{:S(2)}, u32[]{:S(2)}) collective-permute-start(f32[192,128]{1,0:T(8,128)S(1)} %shard_map.54.here_ref.refs_1_), channel_id=1, source_target_pairs={{0,2},{2,0},{4,6},{6,4},{1,3},{3,1},{5,7},{7,5},{8,10},{10,8},{12,... | collective-permute-start | bytes 294920 | tf_op jit(solution)/shard_map/ppermute | solution.py:852
  42.8 4.5 %collective-permute-start.13 = (f32[2,32,256]{2,1,0:T(8,128)S(1)}, f32[2,32,256]{2,1,0:T(8,128)S(1)}, u32[]{:S(2)}, u32[]{:S(2)}) collective-permute-start(f32[2,32,256]{2,1,0:T(8,128)S(1)} %get-tuple-element.56), channel_id=1, source_target_pairs={{0,1},{1,0},{2,3},{3,2},{4,5},{5,4},{6,7},{7,6},{8,9},{9,8},{10,11... | collective-permute-start | bytes 196616 | tf_op jit(solution)/shard_map/ppermute | solution.py:86
  44.2 5.6 %collective-permute-start.11 = (f32[32,128]{1,0:T(8,128)S(1)}, f32[32,128]{1,0:T(8,128)S(1)}, u32[]{:S(2)}, u32[]{:S(2)}) collective-permute-start(f32[32,128]{1,0:T(8,128)S(1)} %get-tuple-element.54), channel_id=1, source_target_pairs={{0,24},{8,16},{16,8},{24,0},{1,25},{9,17},{17,9},{25,1},{2,26},{10... | collective-permute-start | bytes 49160 | tf_op jit(solution)/shard_map/ppermute | solution.py:88
  46.2 3.8 %collective-permute-start.12 = (f32[32,128]{1,0:T(8,128)S(1)}, f32[32,128]{1,0:T(8,128)S(1)}, u32[]{:S(2)}, u32[]{:S(2)}) collective-permute-start(f32[32,128]{1,0:T(8,128)S(1)} %get-tuple-element.55), channel_id=1, source_target_pairs={{0,8},{8,0},{16,24},{24,16},{1,9},{9,1},{17,25},{25,17},{2,10},{10... | collective-permute-start | bytes 49160 | tf_op jit(solution)/shard_map/ppermute | solution.py:89

commit v14 on v13

--- a/solution.py
+++ b/solution.py
@@ -265,44 +265,53 @@
     def line_of(rows, line):
         return jnp.broadcast_to(rows[line : line + 1], full)
 
+    scaled = []
     for strip in range(strips):
         start = strip * block
-        active = range(strip, strips)
+        later_strips = range(strip + 1, strips)
         cols = [
-            {s: jnp.broadcast_to(work[s][:, start + j : start + j + 1], full) for s in active}
+            {
+                s: jnp.broadcast_to(work[s][:, start + j : start + j + 1], full)
+                for s in range(strip, strips)
+            }
             for j in range(block)
         ]
-        factors = []
-
-        def eliminate(j, scale, side):
-            factor = {s: cols[j][s] * scale for s in active}
-            factor[strip] = jnp.where(below > j, factor[strip], 0.0)
-            for later in range(j + 1, block):
-                use = side if later == j + 1 and side is not None else None
-                head = line_of(cols[later][strip], j) if use is None else use
-                for s in active:
-                    cols[later][s] = cols[later][s] - factor[s] * head
-            factors.append(factor)
-
+        value = {
+            (p, q): line_of(cols[q][strip], p) for q in range(block) for p in range(q + 1)
+        }
+        rows = [line_of(work[strip], p) for p in range(block)]
+        own = work[strip]
+        pivots = jnp.ones(full, jnp.float32)
+        solved = []
         for j in range(0, block, 2):
-            corner = line_of(cols[j][strip], j)
-            side = line_of(cols[j][strip], j + 1)
-            last = line_of(cols[j + 1][strip], j + 1)
-            inverse = 1.0 / (corner * last - side * side)
-            eliminate(j, 1.0 / corner, side)
-            eliminate(j + 1, corner * inverse, None)
-        for j in range(block):
-            row = line_of(work[strip], j)
-            for s in active:
-                if s == strip and j == block - 1:
-                    continue
-                work[s] = work[s] - factors[j][s] * row
-    parts = []
-    for s in range(strips):
-        place = iota((8, size), 0) + 8 * s == iota((8, size), 1)
-        pivot = jnp.sum(jnp.where(place, work[s][:, :size], 0.0), axis=1, keepdims=True)
-        parts.append(work[s][:, size : 2 * size] * lax.rsqrt(pivot))
-    return jnp.concatenate(parts, axis=0)
+            a, b, c = value[j, j], value[j, j + 1], value[j + 1, j + 1]
+            minor = a * c - b * b
+            inverse = 1.0 / minor
+            over = 1.0 / a
+            top, bottom = rows[j], rows[j + 1]
+            weights = {}
+            for q in range(j + 2, block):
+                upper, lower = value[j, q], value[j + 1, q]
+                weights[q] = (c * upper - b * lower) * inverse, (a * lower - b * upper) * inverse
+            for q in range(j + 2, block):
+                first, second = weights[q]
+                for p in range(j + 2, q + 1):
+                    value[p, q] = value[p, q] - (value[j, p] * first + value[j + 1, p] * second)
+                rows[q] = rows[q] - (top * first + bottom * second)
+                for s in later_strips:
+                    cols[q][s] = cols[q][s] - (cols[j][s] * first + cols[j + 1][s] * second)
+            solved += [(c * top - b * bottom) * inverse, (a * bottom - b * top) * inverse]
+            own = jnp.where(below == j, top, own)
+            own = jnp.where(below == j + 1, bottom - (b * over) * top, own)
+            pivots = jnp.where(below == j, a, pivots)
+            pivots = jnp.where(below == j + 1, minor * over, pivots)
+        scaled.append(own * lax.rsqrt(pivots))
+        for s in later_strips:
+            terms = [cols[j][s] * solved[j] for j in range(block)]
+            while len(terms) > 1:
+                terms = [terms[i] + terms[i + 1] for i in range(0, len(terms), 2)]
+            work[s] = work[s] - terms[0]
+    return jnp.concatenate(scaled, axis=0)[:, size : 2 * size]
 
 
 def member(group_ref, planes, dy=0, dz=0):

time: 51.2 us -> 51.7 us (level)
  transfers between devices with their start and end apart: 14 -> 14, of which waited for: 10 -> 10; matrix products, arithmetic and copies ran while one was open for 0% -> 0% of each run, Pallas kernels for 21% -> 20%
where the time goes in v14:
time: 51.7 us; the launch traced here: 51.5 us
  Pallas kernels  27.4 us (53%)
  starting transfers between devices  14.1 us (27%)
  waiting for transfers between devices  9.69 us (19%)
    pallas_call x1, Pallas kernels, solve(): pl.pallas_call(functools.partial(solve_kernel, size, len(matrices), colum...  7.88 us
    pallas_call x1, Pallas kernels, per_device(): pl.pallas_call(functools.partial(main_kernel, (AXES[0], AXES[1]), early,...  6.29 us
    ppermute x3, starting transfers between devices, exchange(): lax.ppermute(arrays[0], axis, outer_pairs(axis))  5.97 us
    ppermute x2, starting transfers between devices, exchange(): return [lax.ppermute(arrays[0], axis, flipped(axis, 1))]  3.61 us
    pallas_call x1, Pallas kernels, per_device(): pl.pallas_call(functools.partial(halves_kernel, planes), out_shape=[halve...  2.7 us
    pallas_call x1, Pallas kernels, per_device(): pl.pallas_call(functools.partial(early_kernel, AXES[2:3], early), out_sha...  2.58 us
    pallas_call x1, Pallas kernels, spread_of(): pl.pallas_call(functools.partial(spread_kernel, faces), out_shape=jax.Sha...  1.95 us
    pallas_call x1, Pallas kernels, per_device(): pl.pallas_call(functools.partial(pack_kernel, counts, width), out_shape=f...  1.68 us
  transfers between devices with their start and end apart: 14, of which 10 were waited for; matrix products, arithmetic and copies ran while one was open for 0% of the time, Pallas kernels for 20%

profile of v14, /device:TPU:0, one launch (start us, length us, event | category | flops | bytes accessed | tf_op | source)
XLA Modules:
  0.0 51.5 jit_solution(11043009230307655642)
XLA Ops:
  0.0 0.0 copy-start.1
  0.0 1.7 %shard_map.46 = (f32[328,128]{1,0:T(8,128)S(1)}, f32[328,128]{1,0:T(8,128)S(1)}, f32[328,128]{1,0:T(8,128)S(1)}, f32[328,128]{1,0:T(8,128)S(1)}, f32[2,264,128]{2,1,0:T(8,128)S(1)}, /*index=5*/f32[6,256,256]{2,1,0:T(8,128)S(1)}) custom-call(f32[1536,1536]{1,0:T(8,128)} %bitcast.10, f32[6,32,256]{2,1,0:T(8,128)} %bitcast.6), custom_call_target="tpu_custom_call" | custom-call | tf_op jit(solution)/shard_map/pallas_call | solution.py:742
  1.7 3.0 %collective-permute-start.4 = (f32[2,264,128]{2,1,0:T(8,128)S(1)}, f32[2,264,128]{2,1,0:T(8,128)S(1)}, u32[]{:S(2)}, u32[]{:S(2)}) collective-permute-start(f32[2,264,128]{2,1,0:T(8,128)S(1)} %get-tuple-element.39), channel_id=1, source_target_pairs={{0,1},{1,0},{2,3},{3,2},{4,5},{5,4},{6,7},{7,6},{8,9},{9,8},{10,11... | collective-permute-start | bytes 811016 | tf_op jit(solution)/shard_map/ppermute | solution.py:86
  4.7 3.6 %collective-permute-start = (f32[328,128]{1,0:T(8,128)S(1)}, f32[328,128]{1,0:T(8,128)S(1)}, u32[]{:S(2)}, u32[]{:S(2)}) collective-permute-start(f32[328,128]{1,0:T(8,128)S(1)} %get-tuple-element.33), channel_id=1, source_target_pairs={{0,24},{8,16},{16,8},{24,0},{1,25},{9,17},{17,9},{25,1},{2,26},{10... | collective-permute-start | bytes 503816 | tf_op jit(solution)/shard_map/ppermute | solution.py:88
  8.3 0.0 collective-permute-start.1
  8.3 0.4 collective-permute-start.2
  8.7 1.2 %collective-permute-start.3 = (f32[328,128]{1,0:T(8,128)S(1)}, f32[328,128]{1,0:T(8,128)S(1)}, u32[]{:S(2)}, u32[]{:S(2)}) collective-permute-start(f32[328,128]{1,0:T(8,128)S(1)} %get-tuple-element.36), channel_id=1, source_target_pairs={{0,2},{2,0},{4,6},{6,4},{1,3},{3,1},{5,7},{7,5},{8,10},{10,8},{12,... | collective-permute-start | bytes 503816 | tf_op jit(solution)/shard_map/ppermute | solution.py:89
  9.9 0.0 copy-done.1
  9.9 0.0 copy-start
  9.9 2.7 %shard_map.47 = (bf16[6,2,256,256]{3,2,1,0:T(8,128)(2,1)S(1)}, bf16[15,2,256,256]{3,2,1,0:T(8,128)(2,1)S(1)}, f32[8,128]{1,0:T(8,128)S(1)}) custom-call(f32[1536,1536]{1,0:T(8,128)} %bitcast.11, s32[8]{0:T(128)S(1)} %copy-done.1, f32[6,256,256]{2,1,0:T(8,128)S(1)} %get-tuple-element.31.own_ref.refs_1_.refs_4_), custom_call_target="tpu_custom_call" | custom-call | flops 2000000000 | bytes 1048576 | tf_op jit(solution)/shard_map/pallas_call | solution.py:762
  12.6 0.0 copy-start.2
  12.7 0.0 collective-permute-done.4.refs_0_
  12.7 0.0 copy-done
  12.7 2.6 %shard_map.48 = (f32[2,32,256]{2,1,0:T(8,128)S(1)}, bf16[2,2,256,256]{3,2,1,0:T(8,128)(2,1)S(1)}, bf16[2,2,256,256]{3,2,1,0:T(8,128)(2,1)S(1)}) custom-call(f32[2,264,128]{2,1,0:T(8,128)S(1)} %collective-permute-done.4.refs_0_, f32[6,256,256]{2,1,0:T(8,128)S(1)} %get-tuple-element.31.own_ref.refs_1_.refs_4_, ...), custom_call_target="tpu_custom_call" | custom-call | flops 2000000000 | bytes 1048576 | tf_op jit(solution)/shard_map/pallas_call | solution.py:775
  15.3 0.0 collective-permute-done.refs_0_
  15.3 0.8 %collective-permute-done.1.refs_1_ = f32[328,128]{1,0:T(8,128)S(1)} collective-permute-done((f32[328,128]{1,0:T(8,128)S(1)}, f32[328,128]{1,0:T(8,128)S(1)}, u32[]{:S(2)}, u32[]{:S(2)}) %collective-permute-start.1) | collective-permute-done | bytes 167968 | tf_op jit(solution)/shard_map/ppermute | solution.py:89
  16.0 0.0 collective-permute-done.2.refs_2_
  16.0 0.0 collective-permute-done.3.refs_3_
  16.0 0.0 copy-done.2
  16.0 6.3 %shard_map.49 = (f32[64,768]{1,0:T(8,128)S(1)}, f32[6,32,256]{2,1,0:T(8,128)S(1)}, bf16[4,2,256,256]{3,2,1,0:T(8,128)(2,1)S(1)}, bf16[4,2,256,256]{3,2,1,0:T(8,128)(2,1)S(1)}) custom-call(f32[328,128]{1,0:T(8,128)S(1)} %collective-permute-done.refs_0_, f32[328,128]{1,0:T(8,128)S(1)} %collective-permute-done.1.refs_1_, ...), custom_call_target="tpu_custom_call" | custom-call | flops 8000000000 | bytes 1048576 | tf_op jit(solution)/shard_map/pallas_call | solution.py:784
  22.3 0.1 collective-permute-start.5
  22.4 1.4 %collective-permute-done.5.there_ref = f32[64,768]{1,0:T(8,128)S(1)} collective-permute-done((f32[64,768]{1,0:T(8,128)S(1)}, f32[64,768]{1,0:T(8,128)S(1)}, u32[]{:S(2)}, u32[]{:S(2)}) %collective-permute-start.5) | collective-permute-done | bytes 196640 | tf_op jit(solution)/shard_map/ppermute | solution.py:838
  23.8 0.1 shard_map.50
  23.9 1.6 %collective-permute-start.6 = (f32[64,384]{1,0:T(8,128)S(1)}, f32[64,384]{1,0:T(8,128)S(1)}, u32[]{:S(2)}, u32[]{:S(2)}) collective-permute-start(f32[64,384]{1,0:T(8,128)S(1)} %get-tuple-element.42.first_ref), channel_id=1, source_target_pairs={{0,4},{2,6},{4,0},{6,2},{1,5},{3,7},{5,1},{7,3},{8,12},{10,14},{12... | collective-permute-start | bytes 294920 | tf_op jit(solution)/shard_map/ppermute | solution.py:846
  25.5 0.5 collective-permute-start.7
  26.0 1.6 %shard_map.51 = (f32[4,32,256]{2,1,0:T(8,128)S(1)}, f32[4,32,256]{2,1,0:T(8,128)S(1)}) custom-call(bf16[6,2,256,256]{3,2,1,0:T(8,128)(2,1)S(1)} %get-tuple-element.37.refs_2_.refs_5_.own_ref, f32[328,128]{1,0:T(8,128)S(1)} %collective-permute-done.refs_0_, f32[328,128]{1,0:T(8,128)S(1)} %collective-permute-done.1.refs_1_, ...), custom_call_target="tpu_custom_call" | custom-call | flops 2000000000 | bytes 1048576 | tf_op jit(solution)/shard_map/pallas_call | solution.py:796
  27.5 1.3 %collective-permute-done.6.second_ref = f32[64,384]{1,0:T(8,128)S(1)} collective-permute-done((f32[64,384]{1,0:T(8,128)S(1)}, f32[64,384]{1,0:T(8,128)S(1)}, u32[]{:S(2)}, u32[]{:S(2)}) %collective-permute-start.6) | collective-permute-done | bytes 98336 | tf_op jit(solution)/shard_map/ppermute | solution.py:846
  28.8 1.3 %collective-permute-done.7.fourth_ref = f32[64,384]{1,0:T(8,128)S(1)} collective-permute-done((f32[64,384]{1,0:T(8,128)S(1)}, f32[64,384]{1,0:T(8,128)S(1)}, u32[]{:S(2)}, u32[]{:S(2)}) %collective-permute-start.7) | collective-permute-done | bytes 98336 | tf_op jit(solution)/shard_map/ppermute | solution.py:847
  30.1 0.6 %collective-permute-start.9 = (f32[64,384]{1,0:T(8,128)S(1)}, f32[64,384]{1,0:T(8,128)S(1)}, u32[]{:S(2)}, u32[]{:S(2)}) collective-permute-start(f32[64,384]{1,0:T(8,128)S(1)} %get-tuple-element.52.refs_2_), channel_id=1, source_target_pairs={{0,4},{2,6},{4,0},{6,2},{1,5},{3,7},{5,1},{7,3},{8,12},{10,14},{12... | collective-permute-start | bytes 294920 | tf_op jit(solution)/shard_map/ppermute | solution.py:857
  30.7 0.5 collective-permute-start.8
  31.2 1.9 %shard_map.53.refs_4_.refs_0_.spread_ref = bf16[4,256,192]{2,1,0:T(8,128)(2,1)S(1)} custom-call(f32[64,384]{1,0:T(8,128)S(1)} %get-tuple-element.50.unread.refs_0_, f32[4,32,256]{2,1,0:T(8,128)S(1)} %get-tuple-element.49.unread.basis_ref, f32[4,32,256]{2,1,0:T(8,128)S(1)} %get-tuple-element.51.theirs_ref, f32[6,32,256]{2,1,0:T(8,128)S(1)} %get-tuple-element.44.product_ref, ...), custom_call_target="tpu_custom_call" | custom-call | flops 2000000000 | bytes 1048576 | tf_op jit(solution)/shard_map/pallas_call | solution.py:806
  33.2 1.6 %collective-permute-done.9.refs_3_ = f32[64,384]{1,0:T(8,128)S(1)} collective-permute-done((f32[64,384]{1,0:T(8,128)S(1)}, f32[64,384]{1,0:T(8,128)S(1)}, u32[]{:S(2)}, u32[]{:S(2)}) %collective-permute-start.9) | collective-permute-done | bytes 98336 | tf_op jit(solution)/shard_map/ppermute | solution.py:857
  34.8 0.5 %collective-permute-done.8.refs_1_ = f32[64,384]{1,0:T(8,128)S(1)} collective-permute-done((f32[64,384]{1,0:T(8,128)S(1)}, f32[64,384]{1,0:T(8,128)S(1)}, u32[]{:S(2)}, u32[]{:S(2)}) %collective-permute-start.8) | collective-permute-done | bytes 98336 | tf_op jit(solution)/shard_map/ppermute | solution.py:856
  35.3 7.9 %shard_map.54.here_ref.refs_1_ = f32[192,128]{1,0:T(8,128)S(1)} custom-call(f32[64,384]{1,0:T(8,128)S(1)} %get-tuple-element.50.unread.refs_0_, f32[64,384]{1,0:T(8,128)S(1)} %collective-permute-done.8.refs_1_, f32[64,384]{1,0:T(8,128)S(1)} %get-tuple-element.52.refs_2_, f32[64,384]{1,0:T(8,128)S(1)} %collective-permute-done.9.refs_3_, ...), custom_call_target="tpu_custom_call" | custom-call | flops 7000000000 | bytes 1048576 | tf_op jit(solution)/shard_map/pallas_call | solution.py:816
  43.2 0.1 collective-permute-start.10
  43.3 0.6 %collective-permute-start.13 = (f32[2,32,256]{2,1,0:T(8,128)S(1)}, f32[2,32,256]{2,1,0:T(8,128)S(1)}, u32[]{:S(2)}, u32[]{:S(2)}) collective-permute-start(f32[2,32,256]{2,1,0:T(8,128)S(1)} %get-tuple-element.56), channel_id=1, source_target_pairs={{0,1},{1,0},{2,3},{3,2},{4,5},{5,4},{6,7},{7,6},{8,9},{9,8},{10,11... | collective-permute-start | bytes 196616 | tf_op jit(solution)/shard_map/ppermute | solution.py:86
  43.9 0.7 %collective-permute-done.10.there_ref.refs_2_ = f32[192,128]{1,0:T(8,128)S(1)} collective-permute-done((f32[192,128]{1,0:T(8,128)S(1)}, f32[192,128]{1,0:T(8,128)S(1)}, u32[]{:S(2)}, u32[]{:S(2)}) %collective-permute-start.10) | collective-permute-done | bytes 98336 | tf_op jit(solution)/shard_map/ppermute | solution.py:861
  44.6 2.0 %collective-permute-start.11 = (f32[32,128]{1,0:T(8,128)S(1)}, f32[32,128]{1,0:T(8,128)S(1)}, u32[]{:S(2)}, u32[]{:S(2)}) collective-permute-start(f32[32,128]{1,0:T(8,128)S(1)} %get-tuple-element.54), channel_id=1, source_target_pairs={{0,24},{8,16},{16,8},{24,0},{1,25},{9,17},{17,9},{25,1},{2,26},{10... | collective-permute-start | bytes 49160 | tf_op jit(solution)/shard_map/ppermute | solution.py:88
  46.6 0.0 collective-permute-start.12
  46.6 1.2 %collective-permute-done.13.refs_3_ = f32[2,32,256]{2,1,0:T(8,128)S(1)} collective-permute-done((f32[2,32,256]{2,1,0:T(8,128)S(1)}, f32[2,32,256]{2,1,0:T(8,128)S(1)}, u32[]{:S(2)}, u32[]{:S(2)}) %collective-permute-start.13) | collective-permute-done | bytes 65568 | tf_op jit(solution)/shard_map/ppermute | solution.py:86
  47.8 1.7 %shard_map.56.refs_2_ = f32[1536,128]{1,0:T(8,128)} custom-call(f32[8,128]{1,0:T(8,128)S(1)} %get-tuple-element.32.flag_ref, f32[6,32,256]{2,1,0:T(8,128)S(1)} %get-tuple-element.44.product_ref, bf16[2,2,256,256]{3,2,1,0:T(8,128)(2,1)S(1)} %get-tuple-element.47.refs_6_.refs_0_.early_inverse, ...), custom_call_target="tpu_custom_call" | custom-call | flops 1000000000 | bytes 1048576 | tf_op jit(solution)/shard_map/pallas_call | solution.py:870
  49.5 0.8 %collective-permute-done.11.refs_0_ = f32[32,128]{1,0:T(8,128)S(1)} collective-permute-done((f32[32,128]{1,0:T(8,128)S(1)}, f32[32,128]{1,0:T(8,128)S(1)}, u32[]{:S(2)}, u32[]{:S(2)}) %collective-permute-start.11) | collective-permute-done | bytes 16416 | tf_op jit(solution)/shard_map/ppermute | solution.py:88
  50.2 0.2 collective-permute-done.12.refs_1_
  50.4 1.0 %shard_map.57 = f32[1536,128]{1,0:T(8,128)} custom-call(bf16[4,256,192]{2,1,0:T(8,128)(2,1)S(1)} %shard_map.53.refs_4_.refs_0_.spread_ref, f32[64,128]{1,0:T(8,128)S(1)} %get-tuple-element.53.rows_ref, f32[32,128]{1,0:T(8,128)S(1)} %collective-permute-done.11.refs_0_, f32[32,128]{1,0:T(8,128)S(1)} %collective-permute-done.12.refs_1_, ...), custom_call_target="tpu_custom_call", output_to_operand_aliasing={{}: (4, {})} | custom-call | flops 1000000000 | bytes 1048576 | tf_op jit(solution)/shard_map/pallas_call | solution.py:904
  (2 shorter events, 0.1 us)
Async XLA Ops:
  0.0 9.9 %copy-start.1 = (s32[8]{0:T(128)S(1)}, s32[8]{0:T(128)}, u32[]{:S(2)}) copy-start(s32[8]{0:T(128)} %group_ref.1) | copy-start | bytes 100
  1.7 11.0 %collective-permute-start.4 = (f32[2,264,128]{2,1,0:T(8,128)S(1)}, f32[2,264,128]{2,1,0:T(8,128)S(1)}, u32[]{:S(2)}, u32[]{:S(2)}) collective-permute-start(f32[2,264,128]{2,1,0:T(8,128)S(1)} %get-tuple-element.39), channel_id=1, source_target_pairs={{0,1},{1,0},{2,3},{3,2},{4,5},{5,4},{6,7},{7,6},{8,9},{9,8},{10,11... | collective-permute-start | bytes 811016 | tf_op jit(solution)/shard_map/ppermute | solution.py:86
  4.7 10.5 %collective-permute-start = (f32[328,128]{1,0:T(8,128)S(1)}, f32[328,128]{1,0:T(8,128)S(1)}, u32[]{:S(2)}, u32[]{:S(2)}) collective-permute-start(f32[328,128]{1,0:T(8,128)S(1)} %get-tuple-element.33), channel_id=1, source_target_pairs={{0,24},{8,16},{16,8},{24,0},{1,25},{9,17},{17,9},{25,1},{2,26},{10... | collective-permute-start | bytes 503816 | tf_op jit(solution)/shard_map/ppermute | solution.py:88
  8.3 7.7 %collective-permute-start.1 = (f32[328,128]{1,0:T(8,128)S(1)}, f32[328,128]{1,0:T(8,128)S(1)}, u32[]{:S(2)}, u32[]{:S(2)}) collective-permute-start(f32[328,128]{1,0:T(8,128)S(1)} %get-tuple-element.34), channel_id=1, source_target_pairs={{0,8},{8,0},{16,24},{24,16},{1,9},{9,1},{17,25},{25,17},{2,10},{10... | collective-permute-start | bytes 503816 | tf_op jit(solution)/shard_map/ppermute | solution.py:89
  8.3 7.7 %collective-permute-start.2 = (f32[328,128]{1,0:T(8,128)S(1)}, f32[328,128]{1,0:T(8,128)S(1)}, u32[]{:S(2)}, u32[]{:S(2)}) collective-permute-start(f32[328,128]{1,0:T(8,128)S(1)} %get-tuple-element.35), channel_id=1, source_target_pairs={{0,6},{2,4},{4,2},{6,0},{1,7},{3,5},{5,3},{7,1},{8,14},{10,12},{12... | collective-permute-start | bytes 503816 | tf_op jit(solution)/shard_map/ppermute | solution.py:88
  8.7 7.3 %collective-permute-start.3 = (f32[328,128]{1,0:T(8,128)S(1)}, f32[328,128]{1,0:T(8,128)S(1)}, u32[]{:S(2)}, u32[]{:S(2)}) collective-permute-start(f32[328,128]{1,0:T(8,128)S(1)} %get-tuple-element.36), channel_id=1, source_target_pairs={{0,2},{2,0},{4,6},{6,4},{1,3},{3,1},{5,7},{7,5},{8,10},{10,8},{12,... | collective-permute-start | bytes 503816 | tf_op jit(solution)/shard_map/ppermute | solution.py:89
  9.9 2.7 %copy-start = (f32[1,1,1,6,256,32]{4,5,3,2,1,0:T(8,128)S(1)}, f32[1,1,1,6,256,32]{4,5,3,2,1,0:T(8,128)}, u32[]{:S(2)}) copy-start(f32[1,1,1,6,256,32]{4,5,3,2,1,0:T(8,128)} %param.5) | copy-start | bytes 589828
  12.6 3.4 %copy-start.2 = (f32[1,1,1,1536,128]{4,3,2,1,0:T(8,128)S(1)}, f32[1,1,1,1536,128]{4,3,2,1,0:T(8,128)}, u32[]{:S(2)}) copy-start(f32[1,1,1,1536,128]{4,3,2,1,0:T(8,128)} %param.6) | copy-start | bytes 2359300
  22.3 1.5 %collective-permute-start.5 = (f32[64,768]{1,0:T(8,128)S(1)}, f32[64,768]{1,0:T(8,128)S(1)}, u32[]{:S(2)}, u32[]{:S(2)}) collective-permute-start(f32[64,768]{1,0:T(8,128)S(1)} %get-tuple-element.41.here_ref), channel_id=1, source_target_pairs={{0,2},{2,0},{4,6},{6,4},{1,3},{3,1},{5,7},{7,5},{8,10},{10,8},{12,... | collective-permute-start | bytes 589832 | tf_op jit(solution)/shard_map/ppermute | solution.py:838
  23.9 4.9 %collective-permute-start.6 = (f32[64,384]{1,0:T(8,128)S(1)}, f32[64,384]{1,0:T(8,128)S(1)}, u32[]{:S(2)}, u32[]{:S(2)}) collective-permute-start(f32[64,384]{1,0:T(8,128)S(1)} %get-tuple-element.42.first_ref), channel_id=1, source_target_pairs={{0,4},{2,6},{4,0},{6,2},{1,5},{3,7},{5,1},{7,3},{8,12},{10,14},{12... | collective-permute-start | bytes 294920 | tf_op jit(solution)/shard_map/ppermute | solution.py:846
  25.5 4.6 %collective-permute-start.7 = (f32[64,384]{1,0:T(8,128)S(1)}, f32[64,384]{1,0:T(8,128)S(1)}, u32[]{:S(2)}, u32[]{:S(2)}) collective-permute-start(f32[64,384]{1,0:T(8,128)S(1)} %get-tuple-element.43.third_ref), channel_id=1, source_target_pairs={{0,1},{1,0},{2,3},{3,2},{4,5},{5,4},{6,7},{7,6},{8,9},{9,8},{10,11... | collective-permute-start | bytes 294920 | tf_op jit(solution)/shard_map/ppermute | solution.py:847
  30.1 4.7 %collective-permute-start.9 = (f32[64,384]{1,0:T(8,128)S(1)}, f32[64,384]{1,0:T(8,128)S(1)}, u32[]{:S(2)}, u32[]{:S(2)}) collective-permute-start(f32[64,384]{1,0:T(8,128)S(1)} %get-tuple-element.52.refs_2_), channel_id=1, source_target_pairs={{0,4},{2,6},{4,0},{6,2},{1,5},{3,7},{5,1},{7,3},{8,12},{10,14},{12... | collective-permute-start | bytes 294920 | tf_op jit(solution)/shard_map/ppermute | solution.py:857
  30.7 4.6 %collective-permute-start.8 = (f32[64,384]{1,0:T(8,128)S(1)}, f32[64,384]{1,0:T(8,128)S(1)}, u32[]{:S(2)}, u32[]{:S(2)}) collective-permute-start(f32[64,384]{1,0:T(8,128)S(1)} %get-tuple-element.50.unread.refs_0_), channel_id=1, source_target_pairs={{0,1},{1,0},{2,3},{3,2},{4,5},{5,4},{6,7},{7,6},{8,9},{9,8},{10,11... | collective-permute-start | bytes 294920 | tf_op jit(solution)/shard_map/ppermute | solution.py:856
  43.2 1.4 %collective-permute-start.10 = (f32[192,128]{1,0:T(8,128)S(1)}, f32[192,128]{1,0:T(8,128)S(1)}, u32[]{:S(2)}, u32[]{:S(2)}) collective-permute-start(f32[192,128]{1,0:T(8,128)S(1)} %shard_map.54.here_ref.refs_1_), channel_id=1, source_target_pairs={{0,2},{2,0},{4,6},{6,4},{1,3},{3,1},{5,7},{7,5},{8,10},{10,8},{12,... | collective-permute-start | bytes 294920 | tf_op jit(solution)/shard_map/ppermute | solution.py:861
  43.3 4.5 %collective-permute-start.13 = (f32[2,32,256]{2,1,0:T(8,128)S(1)}, f32[2,32,256]{2,1,0:T(8,128)S(1)}, u32[]{:S(2)}, u32[]{:S(2)}) collective-permute-start(f32[2,32,256]{2,1,0:T(8,128)S(1)} %get-tuple-element.56), channel_id=1, source_target_pairs={{0,1},{1,0},{2,3},{3,2},{4,5},{5,4},{6,7},{7,6},{8,9},{9,8},{10,11... | collective-permute-start | bytes 196616 | tf_op jit(solution)/shard_map/ppermute | solution.py:86
  44.6 5.6 %collective-permute-start.11 = (f32[32,128]{1,0:T(8,128)S(1)}, f32[32,128]{1,0:T(8,128)S(1)}, u32[]{:S(2)}, u32[]{:S(2)}) collective-permute-start(f32[32,128]{1,0:T(8,128)S(1)} %get-tuple-element.54), channel_id=1, source_target_pairs={{0,24},{8,16},{16,8},{24,0},{1,25},{9,17},{17,9},{25,1},{2,26},{10... | collective-permute-start | bytes 49160 | tf_op jit(solution)/shard_map/ppermute | solution.py:88
  46.6 3.8 %collective-permute-start.12 = (f32[32,128]{1,0:T(8,128)S(1)}, f32[32,128]{1,0:T(8,128)S(1)}, u32[]{:S(2)}, u32[]{:S(2)}) collective-permute-start(f32[32,128]{1,0:T(8,128)S(1)} %get-tuple-element.55), channel_id=1, source_target_pairs={{0,8},{8,0},{16,24},{24,16},{1,9},{9,1},{17,25},{25,17},{2,10},{10... | collective-permute-start | bytes 49160 | tf_op jit(solution)/shard_map/ppermute | solution.py:89

commit v15 on v13

--- a/solution.py
+++ b/solution.py
@@ -274,12 +274,11 @@
         ]
         factors = []
 
-        def eliminate(j, scale, side):
+        def eliminate(j, scale):
             factor = {s: cols[j][s] * scale for s in active}
             factor[strip] = jnp.where(below > j, factor[strip], 0.0)
             for later in range(j + 1, block):
-                use = side if later == j + 1 and side is not None else None
-                head = line_of(cols[later][strip], j) if use is None else use
+                head = line_of(cols[later][strip], j)
                 for s in active:
                     cols[later][s] = cols[later][s] - factor[s] * head
             factors.append(factor)
@@ -289,8 +288,8 @@
             side = line_of(cols[j][strip], j + 1)
             last = line_of(cols[j + 1][strip], j + 1)
             inverse = 1.0 / (corner * last - side * side)
-            eliminate(j, 1.0 / corner, side)
-            eliminate(j + 1, corner * inverse, None)
+            eliminate(j, 1.0 / corner)
+            eliminate(j + 1, corner * inverse)
         for j in range(block):
             row = line_of(work[strip], j)
             for s in active:
@@ -487,11 +486,49 @@
     for f in range(FACES):
         product_ref[f] = triple(factors[f], sides[f][f])
     size = 2 * ncon
-    line = []
-    for b in range(BLOCKS):
-        line.append(coarse[b * size : (b + 1) * size, b * size :])
-    line += [right[b * size : (b + 1) * size] for b in range(BLOCKS)]
-    payload_ref[...] = jnp.concatenate(line, axis=1)
+    blocks = {
+        (b, c): coarse[b * size : (b + 1) * size, c * size : (c + 1) * size]
+        for b in range(BLOCKS)
+        for c in range(b, BLOCKS)
+    }
+    payload_ref[...] = jnp.concatenate([pack_coarse(blocks, size), right], axis=0)
+
+
+def pack_coarse(blocks, size):
+    row, col = iota((size, size), 0), iota((size, size), 1)
+    diagonal = jnp.sum(jnp.where(row == col, blocks[1, 1], 0.0), axis=0, keepdims=True)
+    corner = (row == 1) & (col == size - 1)
+    above = jnp.where(row == 0, diagonal, jnp.where(corner, diagonal[:, 0:1], 0.0))
+    shared = jnp.where(row >= col, blocks[0, 0], blocks[1, 1])
+    third = jnp.where(row >= col, blocks[2, 2], above)
+    half = size // 2
+    return jnp.concatenate(
+        [
+            jnp.concatenate([shared, blocks[0, 1]], axis=1),
+            jnp.concatenate([blocks[0, 2], blocks[1, 2]], axis=1),
+            jnp.concatenate([third[:half], third[half:]], axis=1),
+        ],
+        axis=0,
+    )
+
+
+def unpack_coarse(packed, size):
+    row, col = iota((size, size), 0), iota((size, size), 1)
+    shared = packed[:size, :size]
+    flip = shared.T
+    tail = packed[2 * size :]
+    third = jnp.concatenate([tail[:, :size], tail[:, size:]], axis=0)
+    first = jnp.broadcast_to(third[1:2, size - 1 : size], (1, size))
+    diagonal = jnp.where(iota((1, size), 1) == 0, first, third[0:1])
+    second = jnp.where(row < col, shared, jnp.where(row > col, flip, diagonal))
+    return {
+        (0, 0): jnp.where(row >= col, shared, flip),
+        (1, 1): second,
+        (2, 2): jnp.where(row >= col, third, third.T),
+        (0, 1): packed[:size, size:],
+        (0, 2): packed[size : 2 * size, :size],
+        (1, 2): packed[size : 2 * size, size:],
+    }
 
 
 def find(faces, refs, f):
@@ -538,9 +575,9 @@
     mine = flag_ref[0:1, 0:1] > 0.5
     other = flag_ref[1:2, 0:1] > 0.5
     total = jnp.where(mine, here_ref[...], 0.0) + jnp.where(other, there_ref[...], 0.0)
-    lanes = matrix_ref.shape[1]
-    matrix_ref[...] = total[:, :lanes]
-    right_ref[...] = total[:, lanes:]
+    rows = matrix_ref.shape[0]
+    matrix_ref[...] = total[:rows]
+    right_ref[...] = total[rows:]
 
 
 def add_kernel(first_ref, second_ref, third_ref, fourth_ref, product_ref, unread, *refs):
@@ -551,32 +588,26 @@
 
 
 def solve_kernel(size, terms, columns, *refs):
-    lanes = size * BLOCKS * (BLOCKS + 1) // 2
-    matrix, right = refs[0][:, :lanes], refs[terms][...]
+    upper, lower = refs[0][...], refs[terms][...]
     for term in range(1, terms):
-        matrix = matrix + refs[term][:, :lanes]
-        right = right + refs[terms + term][...]
+        upper = upper + refs[term][...]
+        lower = lower + refs[terms + term][...]
     answer_ref = refs[-1]
-    lines = []
-    offset = 0
+    total = jnp.concatenate([upper, lower], axis=0)
+    rows = 2 * size + size // 2
+    blocks, right = unpack_coarse(total[:rows], size), total[rows:]
+    eye = iota((size, size), 0) == iota((size, size), 1)
+    downs, acrosses, rights = [], [], []
     for b in range(BLOCKS):
-        lines.append(matrix[:, offset : offset + (BLOCKS - b) * size])
-        offset += (BLOCKS - b) * size
-    eye = iota((size, size), 0) == iota((size, size), 1)
-    downs, acrosses = [], []
-    for b in range(BLOCKS):
-        diagonal = jnp.where(eye, lines[b][:, :size], 0.0)
+        diagonal = jnp.where(eye, blocks[b, b], 0.0)
         downs.append(lax.rsqrt(jnp.sum(diagonal, axis=1, keepdims=True)))
         acrosses.append(lax.rsqrt(jnp.sum(diagonal, axis=0, keepdims=True)))
-    blocks = {}
-    rights = []
+        rights.append(downs[b] * right[b * size : (b + 1) * size])
     for b in range(BLOCKS):
         for c in range(b, BLOCKS):
-            block = lines[b][:, (c - b) * size : (c - b + 1) * size]
-            blocks[b, c] = downs[b] * block * acrosses[c]
+            blocks[b, c] = downs[b] * blocks[b, c] * acrosses[c]
             if c > b:
                 blocks[c, b] = blocks[b, c].T
-        rights.append(downs[b] * right[:, b * columns : (b + 1) * columns])
     for b in range(BLOCKS):
         inverse = factor_inverse(blocks[b, b])
         later = range(b + 1, BLOCKS)
@@ -708,8 +739,7 @@
     coarse = FACES * ncon
     size = 2 * ncon
     half = width // 2
-    lanes = size * BLOCKS * (BLOCKS + 1) // 2
-    right_lanes = BLOCKS * columns
+    half_rows = (2 * size + ncon + coarse) // 2
     uppers = FACES * (FACES - 1) // 2
     anywhere = pl.BlockSpec(memory_space=pl.ANY)
     main_memory = pl.BlockSpec(memory_space=pltpu.HBM)
@@ -774,7 +804,7 @@
 
     payload, product, late_partner, late_inverse = pl.pallas_call(
         functools.partial(main_kernel, (AXES[0], AXES[1]), early, late),
-        out_shape=[shape(size, lanes + right_lanes), shape(FACES, ncon, width)]
+        out_shape=[shape(2 * half_rows, columns), shape(FACES, ncon, width)]
         + [halves(len(late))] * 2,
         in_specs=vmem_specs(len(got[0]) + len(got[1]) + 6),
         out_specs=vmem_specs(4),
@@ -829,7 +859,7 @@
         other = lax.ppermute(payload, "gy", core_swap)
         left, rest = pl.pallas_call(
             choose_kernel,
-            out_shape=[shape(size, lanes), shape(size, right_lanes)],
+            out_shape=[shape(half_rows, columns)] * 2,
             in_specs=vmem_specs(3),
             out_specs=vmem_specs(2),
             compiler_params=params(8),
@@ -838,7 +868,7 @@
         rest_moved = lax.ppermute(rest, "gz", chip_y)
         left_last, rest_last, *sent = pl.pallas_call(
             add_kernel,
-            out_shape=[shape(size, lanes), shape(size, right_lanes)]
+            out_shape=[shape(half_rows, columns)] * 2
             + face_shapes(counts[2], (ncon, width)),
             in_specs=vmem_specs(5) + [anywhere],
             out_specs=vmem_specs(2 + face_arrays(counts[2])),
@@ -870,7 +900,7 @@
         total = lax.psum(jnp.where(chosen[:, None, None], payload[None], 0.0), ("gy", "gz"))
         total = lax.dynamic_index_in_dim(total, member_of, 0, keepdims=False)
         spread = spread_of(payload)
-        answer = solve([total[:, :lanes]], [total[:, lanes:]], [])
+        answer = solve([total[:half_rows]], [total[half_rows:]], [])
 
         def from_near(faces_of, axis):
             even, odd = faces_of

time: 51.2 us -> 51 us (level)
  no operation moved by 1% of the time
where the time goes in v15:
time: 51 us; the launch traced here: 50.8 us
  Pallas kernels  26.9 us (53%)
  starting transfers between devices  14.1 us (28%)
  waiting for transfers between devices  9.5 us (19%)
    pallas_call x1, Pallas kernels, solve(): pl.pallas_call(functools.partial(solve_kernel, size, len(matrices), colum...  7.35 us
    pallas_call x1, Pallas kernels, per_device(): pl.pallas_call(functools.partial(main_kernel, (AXES[0], AXES[1]), early,...  6.28 us
    ppermute x3, starting transfers between devices, exchange(): lax.ppermute(arrays[0], axis, outer_pairs(axis))  5.96 us
    ppermute x2, starting transfers between devices, exchange(): return [lax.ppermute(arrays[0], axis, flipped(axis, 1))]  3.61 us
    pallas_call x1, Pallas kernels, per_device(): pl.pallas_call(functools.partial(halves_kernel, planes), out_shape=[halve...  2.7 us
    pallas_call x1, Pallas kernels, per_device(): pl.pallas_call(functools.partial(early_kernel, AXES[2:3], early), out_sha...  2.58 us
    pallas_call x1, Pallas kernels, spread_of(): pl.pallas_call(functools.partial(spread_kernel, faces), out_shape=jax.Sha...  1.95 us
    pallas_call x1, Pallas kernels, per_device(): pl.pallas_call(functools.partial(pack_kernel, counts, width), out_shape=f...  1.68 us
  transfers between devices with their start and end apart: 14, of which 10 were waited for; matrix products, arithmetic and copies ran while one was open for 0% of the time, Pallas kernels for 21%

profile of v15, /device:TPU:0, one launch (start us, length us, event | category | flops | bytes accessed | tf_op | source)
XLA Modules:
  0.0 50.8 jit_solution(1142413371347198782)
XLA Ops:
  0.0 0.0 copy-start.1
  0.0 1.7 %shard_map.46 = (f32[328,128]{1,0:T(8,128)S(1)}, f32[328,128]{1,0:T(8,128)S(1)}, f32[328,128]{1,0:T(8,128)S(1)}, f32[328,128]{1,0:T(8,128)S(1)}, f32[2,264,128]{2,1,0:T(8,128)S(1)}, /*index=5*/f32[6,256,256]{2,1,0:T(8,128)S(1)}) custom-call(f32[1536,1536]{1,0:T(8,128)} %bitcast.10, f32[6,32,256]{2,1,0:T(8,128)} %bitcast.6), custom_call_target="tpu_custom_call" | custom-call | tf_op jit(solution)/shard_map/pallas_call | solution.py:763
  1.7 3.0 %collective-permute-start.4 = (f32[2,264,128]{2,1,0:T(8,128)S(1)}, f32[2,264,128]{2,1,0:T(8,128)S(1)}, u32[]{:S(2)}, u32[]{:S(2)}) collective-permute-start(f32[2,264,128]{2,1,0:T(8,128)S(1)} %get-tuple-element.39), channel_id=1, source_target_pairs={{0,1},{1,0},{2,3},{3,2},{4,5},{5,4},{6,7},{7,6},{8,9},{9,8},{10,11... | collective-permute-start | bytes 811016 | tf_op jit(solution)/shard_map/ppermute | solution.py:86
  4.7 3.6 %collective-permute-start = (f32[328,128]{1,0:T(8,128)S(1)}, f32[328,128]{1,0:T(8,128)S(1)}, u32[]{:S(2)}, u32[]{:S(2)}) collective-permute-start(f32[328,128]{1,0:T(8,128)S(1)} %get-tuple-element.33), channel_id=1, source_target_pairs={{0,24},{8,16},{16,8},{24,0},{1,25},{9,17},{17,9},{25,1},{2,26},{10... | collective-permute-start | bytes 503816 | tf_op jit(solution)/shard_map/ppermute | solution.py:88
  8.3 0.0 collective-permute-start.1
  8.3 0.4 collective-permute-start.2
  8.7 1.2 %collective-permute-start.3 = (f32[328,128]{1,0:T(8,128)S(1)}, f32[328,128]{1,0:T(8,128)S(1)}, u32[]{:S(2)}, u32[]{:S(2)}) collective-permute-start(f32[328,128]{1,0:T(8,128)S(1)} %get-tuple-element.36), channel_id=1, source_target_pairs={{0,2},{2,0},{4,6},{6,4},{1,3},{3,1},{5,7},{7,5},{8,10},{10,8},{12,... | collective-permute-start | bytes 503816 | tf_op jit(solution)/shard_map/ppermute | solution.py:89
  9.9 0.0 copy-done.1
  9.9 0.0 copy-start
  9.9 2.7 %shard_map.47 = (bf16[6,2,256,256]{3,2,1,0:T(8,128)(2,1)S(1)}, bf16[15,2,256,256]{3,2,1,0:T(8,128)(2,1)S(1)}, f32[8,128]{1,0:T(8,128)S(1)}) custom-call(f32[1536,1536]{1,0:T(8,128)} %bitcast.11, s32[8]{0:T(128)S(1)} %copy-done.1, f32[6,256,256]{2,1,0:T(8,128)S(1)} %get-tuple-element.31.own_ref.refs_1_.refs_4_), custom_call_target="tpu_custom_call" | custom-call | flops 2000000000 | bytes 1048576 | tf_op jit(solution)/shard_map/pallas_call | solution.py:783
  12.6 0.0 copy-start.2
  12.7 0.0 collective-permute-done.4.refs_0_
  12.7 0.0 copy-done
  12.7 2.6 %shard_map.48 = (f32[2,32,256]{2,1,0:T(8,128)S(1)}, bf16[2,2,256,256]{3,2,1,0:T(8,128)(2,1)S(1)}, bf16[2,2,256,256]{3,2,1,0:T(8,128)(2,1)S(1)}) custom-call(f32[2,264,128]{2,1,0:T(8,128)S(1)} %collective-permute-done.4.refs_0_, f32[6,256,256]{2,1,0:T(8,128)S(1)} %get-tuple-element.31.own_ref.refs_1_.refs_4_, ...), custom_call_target="tpu_custom_call" | custom-call | flops 2000000000 | bytes 1048576 | tf_op jit(solution)/shard_map/pallas_call | solution.py:796
  15.3 0.0 collective-permute-done.refs_0_
  15.3 0.8 %collective-permute-done.1.refs_1_ = f32[328,128]{1,0:T(8,128)S(1)} collective-permute-done((f32[328,128]{1,0:T(8,128)S(1)}, f32[328,128]{1,0:T(8,128)S(1)}, u32[]{:S(2)}, u32[]{:S(2)}) %collective-permute-start.1) | collective-permute-done | bytes 167968 | tf_op jit(solution)/shard_map/ppermute | solution.py:89
  16.0 0.0 collective-permute-done.2.refs_2_
  16.0 0.0 collective-permute-done.3.refs_3_
  16.0 0.0 copy-done.2
  16.0 6.3 %shard_map.49 = (f32[352,128]{1,0:T(8,128)S(1)}, f32[6,32,256]{2,1,0:T(8,128)S(1)}, bf16[4,2,256,256]{3,2,1,0:T(8,128)(2,1)S(1)}, bf16[4,2,256,256]{3,2,1,0:T(8,128)(2,1)S(1)}) custom-call(f32[328,128]{1,0:T(8,128)S(1)} %collective-permute-done.refs_0_, f32[328,128]{1,0:T(8,128)S(1)} %collective-permute-done.1.refs_1_, ...), custom_call_target="tpu_custom_call" | custom-call | flops 8000000000 | bytes 1048576 | tf_op jit(solution)/shard_map/pallas_call | solution.py:805
  22.3 0.1 collective-permute-start.5
  22.4 1.4 %collective-permute-done.5.there_ref = f32[352,128]{1,0:T(8,128)S(1)} collective-permute-done((f32[352,128]{1,0:T(8,128)S(1)}, f32[352,128]{1,0:T(8,128)S(1)}, u32[]{:S(2)}, u32[]{:S(2)}) %collective-permute-start.5) | collective-permute-done | bytes 180256 | tf_op jit(solution)/shard_map/ppermute | solution.py:859
  23.8 0.1 shard_map.50
  23.9 1.6 %collective-permute-start.6 = (f32[176,128]{1,0:T(8,128)S(1)}, f32[176,128]{1,0:T(8,128)S(1)}, u32[]{:S(2)}, u32[]{:S(2)}) collective-permute-start(f32[176,128]{1,0:T(8,128)S(1)} %get-tuple-element.42.first_ref), channel_id=1, source_target_pairs={{0,4},{2,6},{4,0},{6,2},{1,5},{3,7},{5,1},{7,3},{8,12},{10,14},{12... | collective-permute-start | bytes 270344 | tf_op jit(solution)/shard_map/ppermute | solution.py:867
  25.4 0.5 collective-permute-start.7
  25.9 1.6 %shard_map.51 = (f32[4,32,256]{2,1,0:T(8,128)S(1)}, f32[4,32,256]{2,1,0:T(8,128)S(1)}) custom-call(bf16[6,2,256,256]{3,2,1,0:T(8,128)(2,1)S(1)} %get-tuple-element.37.refs_2_.refs_5_.own_ref, f32[328,128]{1,0:T(8,128)S(1)} %collective-permute-done.refs_0_, f32[328,128]{1,0:T(8,128)S(1)} %collective-permute-done.1.refs_1_, ...), custom_call_target="tpu_custom_call" | custom-call | flops 2000000000 | bytes 1048576 | tf_op jit(solution)/shard_map/pallas_call | solution.py:817
  27.5 1.1 %collective-permute-done.6.second_ref = f32[176,128]{1,0:T(8,128)S(1)} collective-permute-done((f32[176,128]{1,0:T(8,128)S(1)}, f32[176,128]{1,0:T(8,128)S(1)}, u32[]{:S(2)}, u32[]{:S(2)}) %collective-permute-start.6) | collective-permute-done | bytes 90144 | tf_op jit(solution)/shard_map/ppermute | solution.py:867
  28.6 1.4 %collective-permute-done.7.fourth_ref = f32[176,128]{1,0:T(8,128)S(1)} collective-permute-done((f32[176,128]{1,0:T(8,128)S(1)}, f32[176,128]{1,0:T(8,128)S(1)}, u32[]{:S(2)}, u32[]{:S(2)}) %collective-permute-start.7) | collective-permute-done | bytes 90144 | tf_op jit(solution)/shard_map/ppermute | solution.py:868
  30.0 0.6 %collective-permute-start.9 = (f32[176,128]{1,0:T(8,128)S(1)}, f32[176,128]{1,0:T(8,128)S(1)}, u32[]{:S(2)}, u32[]{:S(2)}) collective-permute-start(f32[176,128]{1,0:T(8,128)S(1)} %get-tuple-element.52.refs_2_), channel_id=1, source_target_pairs={{0,4},{2,6},{4,0},{6,2},{1,5},{3,7},{5,1},{7,3},{8,12},{10,14},{12... | collective-permute-start | bytes 270344 | tf_op jit(solution)/shard_map/ppermute | solution.py:878
  30.6 0.5 collective-permute-start.8
  31.1 1.9 %shard_map.53.refs_4_.refs_0_.spread_ref = bf16[4,256,192]{2,1,0:T(8,128)(2,1)S(1)} custom-call(f32[176,128]{1,0:T(8,128)S(1)} %get-tuple-element.50.unread.refs_0_, f32[4,32,256]{2,1,0:T(8,128)S(1)} %get-tuple-element.49.unread.basis_ref, f32[4,32,256]{2,1,0:T(8,128)S(1)} %get-tuple-element.51.theirs_ref, f32[6,32,256]{2,1,0:T(8,128)S(1)} %get-tuple-element.44.product_ref, ...), custom_call_target="tpu_custom_call" | custom-call | flops 2000000000 | bytes 1048576 | tf_op jit(solution)/shard_map/pallas_call | solution.py:827
  33.0 1.5 %collective-permute-done.9.refs_3_ = f32[176,128]{1,0:T(8,128)S(1)} collective-permute-done((f32[176,128]{1,0:T(8,128)S(1)}, f32[176,128]{1,0:T(8,128)S(1)}, u32[]{:S(2)}, u32[]{:S(2)}) %collective-permute-start.9) | collective-permute-done | bytes 90144 | tf_op jit(solution)/shard_map/ppermute | solution.py:878
  34.6 0.5 %collective-permute-done.8.refs_1_ = f32[176,128]{1,0:T(8,128)S(1)} collective-permute-done((f32[176,128]{1,0:T(8,128)S(1)}, f32[176,128]{1,0:T(8,128)S(1)}, u32[]{:S(2)}, u32[]{:S(2)}) %collective-permute-start.8) | collective-permute-done | bytes 90144 | tf_op jit(solution)/shard_map/ppermute | solution.py:877
  35.1 7.4 %shard_map.54.here_ref.refs_1_ = f32[192,128]{1,0:T(8,128)S(1)} custom-call(f32[176,128]{1,0:T(8,128)S(1)} %get-tuple-element.50.unread.refs_0_, f32[176,128]{1,0:T(8,128)S(1)} %collective-permute-done.8.refs_1_, f32[176,128]{1,0:T(8,128)S(1)} %get-tuple-element.52.refs_2_, f32[176,128]{1,0:T(8,128)S(1)} %collective-permute-done.9.refs_3_, ...), custom_call_target="tpu_custom_call" | custom-call | flops 7000000000 | bytes 1048576 | tf_op jit(solution)/shard_map/pallas_call | solution.py:837
  42.5 0.1 collective-permute-start.10
  42.6 0.6 %collective-permute-start.13 = (f32[2,32,256]{2,1,0:T(8,128)S(1)}, f32[2,32,256]{2,1,0:T(8,128)S(1)}, u32[]{:S(2)}, u32[]{:S(2)}) collective-permute-start(f32[2,32,256]{2,1,0:T(8,128)S(1)} %get-tuple-element.56), channel_id=1, source_target_pairs={{0,1},{1,0},{2,3},{3,2},{4,5},{5,4},{6,7},{7,6},{8,9},{9,8},{10,11... | collective-permute-start | bytes 196616 | tf_op jit(solution)/shard_map/ppermute | solution.py:86
  43.1 0.7 %collective-permute-done.10.there_ref.refs_2_ = f32[192,128]{1,0:T(8,128)S(1)} collective-permute-done((f32[192,128]{1,0:T(8,128)S(1)}, f32[192,128]{1,0:T(8,128)S(1)}, u32[]{:S(2)}, u32[]{:S(2)}) %collective-permute-start.10) | collective-permute-done | bytes 98336 | tf_op jit(solution)/shard_map/ppermute | solution.py:882
  43.9 2.0 %collective-permute-start.11 = (f32[32,128]{1,0:T(8,128)S(1)}, f32[32,128]{1,0:T(8,128)S(1)}, u32[]{:S(2)}, u32[]{:S(2)}) collective-permute-start(f32[32,128]{1,0:T(8,128)S(1)} %get-tuple-element.54), channel_id=1, source_target_pairs={{0,24},{8,16},{16,8},{24,0},{1,25},{9,17},{17,9},{25,1},{2,26},{10... | collective-permute-start | bytes 49160 | tf_op jit(solution)/shard_map/ppermute | solution.py:88
  45.9 0.0 collective-permute-start.12
  45.9 1.2 %collective-permute-done.13.refs_3_ = f32[2,32,256]{2,1,0:T(8,128)S(1)} collective-permute-done((f32[2,32,256]{2,1,0:T(8,128)S(1)}, f32[2,32,256]{2,1,0:T(8,128)S(1)}, u32[]{:S(2)}, u32[]{:S(2)}) %collective-permute-start.13) | collective-permute-done | bytes 65568 | tf_op jit(solution)/shard_map/ppermute | solution.py:86
  47.1 1.7 %shard_map.56.refs_2_ = f32[1536,128]{1,0:T(8,128)} custom-call(f32[8,128]{1,0:T(8,128)S(1)} %get-tuple-element.32.flag_ref, f32[6,32,256]{2,1,0:T(8,128)S(1)} %get-tuple-element.44.product_ref, bf16[2,2,256,256]{3,2,1,0:T(8,128)(2,1)S(1)} %get-tuple-element.47.refs_6_.refs_0_.early_inverse, ...), custom_call_target="tpu_custom_call" | custom-call | flops 1000000000 | bytes 1048576 | tf_op jit(solution)/shard_map/pallas_call | solution.py:891
  48.7 0.8 %collective-permute-done.11.refs_0_ = f32[32,128]{1,0:T(8,128)S(1)} collective-permute-done((f32[32,128]{1,0:T(8,128)S(1)}, f32[32,128]{1,0:T(8,128)S(1)}, u32[]{:S(2)}, u32[]{:S(2)}) %collective-permute-start.11) | collective-permute-done | bytes 16416 | tf_op jit(solution)/shard_map/ppermute | solution.py:88
  49.5 0.2 collective-permute-done.12.refs_1_
  49.7 1.0 %shard_map.57 = f32[1536,128]{1,0:T(8,128)} custom-call(bf16[4,256,192]{2,1,0:T(8,128)(2,1)S(1)} %shard_map.53.refs_4_.refs_0_.spread_ref, f32[64,128]{1,0:T(8,128)S(1)} %get-tuple-element.53.rows_ref, f32[32,128]{1,0:T(8,128)S(1)} %collective-permute-done.11.refs_0_, f32[32,128]{1,0:T(8,128)S(1)} %collective-permute-done.12.refs_1_, ...), custom_call_target="tpu_custom_call", output_to_operand_aliasing={{}: (4, {})} | custom-call | flops 1000000000 | bytes 1048576 | tf_op jit(solution)/shard_map/pallas_call | solution.py:925
  (2 shorter events, 0.1 us)
Async XLA Ops:
  0.0 9.9 %copy-start.1 = (s32[8]{0:T(128)S(1)}, s32[8]{0:T(128)}, u32[]{:S(2)}) copy-start(s32[8]{0:T(128)} %group_ref.1) | copy-start | bytes 100
  1.7 11.0 %collective-permute-start.4 = (f32[2,264,128]{2,1,0:T(8,128)S(1)}, f32[2,264,128]{2,1,0:T(8,128)S(1)}, u32[]{:S(2)}, u32[]{:S(2)}) collective-permute-start(f32[2,264,128]{2,1,0:T(8,128)S(1)} %get-tuple-element.39), channel_id=1, source_target_pairs={{0,1},{1,0},{2,3},{3,2},{4,5},{5,4},{6,7},{7,6},{8,9},{9,8},{10,11... | collective-permute-start | bytes 811016 | tf_op jit(solution)/shard_map/ppermute | solution.py:86
  4.7 10.5 %collective-permute-start = (f32[328,128]{1,0:T(8,128)S(1)}, f32[328,128]{1,0:T(8,128)S(1)}, u32[]{:S(2)}, u32[]{:S(2)}) collective-permute-start(f32[328,128]{1,0:T(8,128)S(1)} %get-tuple-element.33), channel_id=1, source_target_pairs={{0,24},{8,16},{16,8},{24,0},{1,25},{9,17},{17,9},{25,1},{2,26},{10... | collective-permute-start | bytes 503816 | tf_op jit(solution)/shard_map/ppermute | solution.py:88
  8.3 7.7 %collective-permute-start.1 = (f32[328,128]{1,0:T(8,128)S(1)}, f32[328,128]{1,0:T(8,128)S(1)}, u32[]{:S(2)}, u32[]{:S(2)}) collective-permute-start(f32[328,128]{1,0:T(8,128)S(1)} %get-tuple-element.34), channel_id=1, source_target_pairs={{0,8},{8,0},{16,24},{24,16},{1,9},{9,1},{17,25},{25,17},{2,10},{10... | collective-permute-start | bytes 503816 | tf_op jit(solution)/shard_map/ppermute | solution.py:89
  8.3 7.7 %collective-permute-start.2 = (f32[328,128]{1,0:T(8,128)S(1)}, f32[328,128]{1,0:T(8,128)S(1)}, u32[]{:S(2)}, u32[]{:S(2)}) collective-permute-start(f32[328,128]{1,0:T(8,128)S(1)} %get-tuple-element.35), channel_id=1, source_target_pairs={{0,6},{2,4},{4,2},{6,0},{1,7},{3,5},{5,3},{7,1},{8,14},{10,12},{12... | collective-permute-start | bytes 503816 | tf_op jit(solution)/shard_map/ppermute | solution.py:88
  8.7 7.3 %collective-permute-start.3 = (f32[328,128]{1,0:T(8,128)S(1)}, f32[328,128]{1,0:T(8,128)S(1)}, u32[]{:S(2)}, u32[]{:S(2)}) collective-permute-start(f32[328,128]{1,0:T(8,128)S(1)} %get-tuple-element.36), channel_id=1, source_target_pairs={{0,2},{2,0},{4,6},{6,4},{1,3},{3,1},{5,7},{7,5},{8,10},{10,8},{12,... | collective-permute-start | bytes 503816 | tf_op jit(solution)/shard_map/ppermute | solution.py:89
  9.9 2.7 %copy-start = (f32[1,1,1,6,256,32]{4,5,3,2,1,0:T(8,128)S(1)}, f32[1,1,1,6,256,32]{4,5,3,2,1,0:T(8,128)}, u32[]{:S(2)}) copy-start(f32[1,1,1,6,256,32]{4,5,3,2,1,0:T(8,128)} %param.5) | copy-start | bytes 589828
  12.6 3.4 %copy-start.2 = (f32[1,1,1,1536,128]{4,3,2,1,0:T(8,128)S(1)}, f32[1,1,1,1536,128]{4,3,2,1,0:T(8,128)}, u32[]{:S(2)}) copy-start(f32[1,1,1,1536,128]{4,3,2,1,0:T(8,128)} %param.6) | copy-start | bytes 2359300
  22.3 1.5 %collective-permute-start.5 = (f32[352,128]{1,0:T(8,128)S(1)}, f32[352,128]{1,0:T(8,128)S(1)}, u32[]{:S(2)}, u32[]{:S(2)}) collective-permute-start(f32[352,128]{1,0:T(8,128)S(1)} %get-tuple-element.41.here_ref), channel_id=1, source_target_pairs={{0,2},{2,0},{4,6},{6,4},{1,3},{3,1},{5,7},{7,5},{8,10},{10,8},{12,... | collective-permute-start | bytes 540680 | tf_op jit(solution)/shard_map/ppermute | solution.py:859
  23.9 4.7 %collective-permute-start.6 = (f32[176,128]{1,0:T(8,128)S(1)}, f32[176,128]{1,0:T(8,128)S(1)}, u32[]{:S(2)}, u32[]{:S(2)}) collective-permute-start(f32[176,128]{1,0:T(8,128)S(1)} %get-tuple-element.42.first_ref), channel_id=1, source_target_pairs={{0,4},{2,6},{4,0},{6,2},{1,5},{3,7},{5,1},{7,3},{8,12},{10,14},{12... | collective-permute-start | bytes 270344 | tf_op jit(solution)/shard_map/ppermute | solution.py:867
  25.4 4.5 %collective-permute-start.7 = (f32[176,128]{1,0:T(8,128)S(1)}, f32[176,128]{1,0:T(8,128)S(1)}, u32[]{:S(2)}, u32[]{:S(2)}) collective-permute-start(f32[176,128]{1,0:T(8,128)S(1)} %get-tuple-element.43.third_ref), channel_id=1, source_target_pairs={{0,1},{1,0},{2,3},{3,2},{4,5},{5,4},{6,7},{7,6},{8,9},{9,8},{10,11... | collective-permute-start | bytes 270344 | tf_op jit(solution)/shard_map/ppermute | solution.py:868
  30.0 4.6 %collective-permute-start.9 = (f32[176,128]{1,0:T(8,128)S(1)}, f32[176,128]{1,0:T(8,128)S(1)}, u32[]{:S(2)}, u32[]{:S(2)}) collective-permute-start(f32[176,128]{1,0:T(8,128)S(1)} %get-tuple-element.52.refs_2_), channel_id=1, source_target_pairs={{0,4},{2,6},{4,0},{6,2},{1,5},{3,7},{5,1},{7,3},{8,12},{10,14},{12... | collective-permute-start | bytes 270344 | tf_op jit(solution)/shard_map/ppermute | solution.py:878
  30.6 4.5 %collective-permute-start.8 = (f32[176,128]{1,0:T(8,128)S(1)}, f32[176,128]{1,0:T(8,128)S(1)}, u32[]{:S(2)}, u32[]{:S(2)}) collective-permute-start(f32[176,128]{1,0:T(8,128)S(1)} %get-tuple-element.50.unread.refs_0_), channel_id=1, source_target_pairs={{0,1},{1,0},{2,3},{3,2},{4,5},{5,4},{6,7},{7,6},{8,9},{9,8},{10,11... | collective-permute-start | bytes 270344 | tf_op jit(solution)/shard_map/ppermute | solution.py:877
  42.5 1.4 %collective-permute-start.10 = (f32[192,128]{1,0:T(8,128)S(1)}, f32[192,128]{1,0:T(8,128)S(1)}, u32[]{:S(2)}, u32[]{:S(2)}) collective-permute-start(f32[192,128]{1,0:T(8,128)S(1)} %shard_map.54.here_ref.refs_1_), channel_id=1, source_target_pairs={{0,2},{2,0},{4,6},{6,4},{1,3},{3,1},{5,7},{7,5},{8,10},{10,8},{12,... | collective-permute-start | bytes 294920 | tf_op jit(solution)/shard_map/ppermute | solution.py:882
  42.6 4.5 %collective-permute-start.13 = (f32[2,32,256]{2,1,0:T(8,128)S(1)}, f32[2,32,256]{2,1,0:T(8,128)S(1)}, u32[]{:S(2)}, u32[]{:S(2)}) collective-permute-start(f32[2,32,256]{2,1,0:T(8,128)S(1)} %get-tuple-element.56), channel_id=1, source_target_pairs={{0,1},{1,0},{2,3},{3,2},{4,5},{5,4},{6,7},{7,6},{8,9},{9,8},{10,11... | collective-permute-start | bytes 196616 | tf_op jit(solution)/shard_map/ppermute | solution.py:86
  43.9 5.6 %collective-permute-start.11 = (f32[32,128]{1,0:T(8,128)S(1)}, f32[32,128]{1,0:T(8,128)S(1)}, u32[]{:S(2)}, u32[]{:S(2)}) collective-permute-start(f32[32,128]{1,0:T(8,128)S(1)} %get-tuple-element.54), channel_id=1, source_target_pairs={{0,24},{8,16},{16,8},{24,0},{1,25},{9,17},{17,9},{25,1},{2,26},{10... | collective-permute-start | bytes 49160 | tf_op jit(solution)/shard_map/ppermute | solution.py:88
  45.9 3.8 %collective-permute-start.12 = (f32[32,128]{1,0:T(8,128)S(1)}, f32[32,128]{1,0:T(8,128)S(1)}, u32[]{:S(2)}, u32[]{:S(2)}) collective-permute-start(f32[32,128]{1,0:T(8,128)S(1)} %get-tuple-element.55), channel_id=1, source_target_pairs={{0,8},{8,0},{16,24},{24,16},{1,9},{9,1},{17,25},{25,17},{2,10},{10... | collective-permute-start | bytes 49160 | tf_op jit(solution)/shard_map/ppermute | solution.py:89

commit v16 on v15

--- a/solution.py
+++ b/solution.py
@@ -496,17 +496,16 @@
 
 def pack_coarse(blocks, size):
     row, col = iota((size, size), 0), iota((size, size), 1)
-    diagonal = jnp.sum(jnp.where(row == col, blocks[1, 1], 0.0), axis=0, keepdims=True)
-    corner = (row == 1) & (col == size - 1)
-    above = jnp.where(row == 0, diagonal, jnp.where(corner, diagonal[:, 0:1], 0.0))
-    shared = jnp.where(row >= col, blocks[0, 0], blocks[1, 1])
-    third = jnp.where(row >= col, blocks[2, 2], above)
+    diagonal = jnp.sum(jnp.where(row == col, blocks[2, 2], 0.0), axis=0, keepdims=True)
+    tail = jnp.broadcast_to(jnp.concatenate([diagonal, diagonal], axis=1), (8, 2 * size))
+    shared = jnp.where(row >= col, blocks[1, 1], blocks[2, 2])
     half = size // 2
     return jnp.concatenate(
         [
+            jnp.concatenate([blocks[0, 0][:half], blocks[0, 0][half:]], axis=1),
             jnp.concatenate([shared, blocks[0, 1]], axis=1),
             jnp.concatenate([blocks[0, 2], blocks[1, 2]], axis=1),
-            jnp.concatenate([third[:half], third[half:]], axis=1),
+            tail,
         ],
         axis=0,
     )
@@ -516,15 +515,10 @@
     row, col = iota((size, size), 0), iota((size, size), 1)
     shared = packed[:size, :size]
     flip = shared.T
-    tail = packed[2 * size :]
-    third = jnp.concatenate([tail[:, :size], tail[:, size:]], axis=0)
-    first = jnp.broadcast_to(third[1:2, size - 1 : size], (1, size))
-    diagonal = jnp.where(iota((1, size), 1) == 0, first, third[0:1])
-    second = jnp.where(row < col, shared, jnp.where(row > col, flip, diagonal))
+    diagonal = packed[2 * size : 2 * size + 1, :size]
     return {
-        (0, 0): jnp.where(row >= col, shared, flip),
-        (1, 1): second,
-        (2, 2): jnp.where(row >= col, third, third.T),
+        (1, 1): jnp.where(row >= col, shared, flip),
+        (2, 2): jnp.where(row < col, shared, jnp.where(row > col, flip, diagonal)),
         (0, 1): packed[:size, size:],
         (0, 2): packed[size : 2 * size, :size],
         (1, 2): packed[size : 2 * size, size:],
@@ -538,8 +532,8 @@
 
 
 def theirs_kernel(faces, ncon, own_ref, *refs):
-    inputs, partner_refs, inverse_refs = refs[:-6], refs[-6:-4], refs[-4:-2]
-    basis_out, product_out = refs[-2:]
+    inputs, partner_refs, inverse_refs = refs[:-5], refs[-5:-3], refs[-3:-1]
+    product_out = refs[-1]
     basis = []
     done = 0
     for axis in AXES[:2]:
@@ -555,18 +549,15 @@
     ]
     for sweep in range(SUB_ITERS):
         basis = sweep_basis(*matrices, basis)
+    factors = factor_inverses([dot(b, b, ((1,), (1,))) for b in basis])
     for f in range(count):
-        basis_out[f] = basis[f]
-        product_out[f] = thin(stacked(basis[f]), matrices[2][f])
-
-
-def spread_kernel(faces, unread, basis_ref, theirs_ref, product_ref, *refs):
+        product_out[f] = triple(factors[f], thin(stacked(basis[f]), matrices[2][f]))
+
+
+def spread_kernel(faces, unread, theirs_ref, product_ref, *refs):
     inverse_refs, out_ref = refs[:2], refs[2]
-    basis = [basis_ref[f] for f in range(basis_ref.shape[0])]
-    factors = factor_inverses([dot(b, b, ((1,), (1,))) for b in basis])
-    for f in range(len(basis)):
-        theirs = triple(factors[f], theirs_ref[f])
-        both = jnp.concatenate([product_ref[f], theirs], axis=0)
+    for f in range(theirs_ref.shape[0]):
+        both = jnp.concatenate([product_ref[f], theirs_ref[f]], axis=0)
         high, low = split(thin(stacked(both), find(faces, inverse_refs, f)).T)
         out_ref[f] = jnp.concatenate([high, high, low], axis=1)
 
@@ -581,35 +572,55 @@
 
 
 def add_kernel(first_ref, second_ref, third_ref, fourth_ref, product_ref, unread, *refs):
-    matrix_ref, right_ref, *sent = refs
-    matrix_ref[...] = first_ref[...] + second_ref[...]
+    first_out, matrix_ref, right_ref, *sent = refs
+    total = first_ref[...] + second_ref[...]
+    rows = first_out.shape[0]
+    first_out[...] = total[:rows]
+    matrix_ref[...] = total[rows:]
     right_ref[...] = third_ref[...] + fourth_ref[...]
     send(sent, AXES[2], product_ref[4], product_ref[5])
 
 
-def solve_kernel(size, terms, columns, *refs):
+def first_kernel(*refs):
+    total = refs[0][...]
+    for ref in refs[1:-1]:
+        total = total + ref[...]
+    size = total.shape[1] // 2
+    block = jnp.concatenate([total[:, :size], total[:, size:]], axis=0)
+    eye = iota((size, size), 0) == iota((size, size), 1)
+    diagonal = jnp.where(eye, block, 0.0)
+    down = lax.rsqrt(jnp.sum(diagonal, axis=1, keepdims=True))
+    across = lax.rsqrt(jnp.sum(diagonal, axis=0, keepdims=True))
+    refs[-1][...] = factor_inverse(down * block * across) * across
+
+
+def solve_kernel(size, terms, columns, first_ref, *refs):
     upper, lower = refs[0][...], refs[terms][...]
     for term in range(1, terms):
         upper = upper + refs[term][...]
         lower = lower + refs[terms + term][...]
     answer_ref = refs[-1]
     total = jnp.concatenate([upper, lower], axis=0)
-    rows = 2 * size + size // 2
+    rows = 2 * size + 8
     blocks, right = unpack_coarse(total[:rows], size), total[rows:]
     eye = iota((size, size), 0) == iota((size, size), 1)
     downs, acrosses, rights = [], [], []
     for b in range(BLOCKS):
-        diagonal = jnp.where(eye, blocks[b, b], 0.0)
-        downs.append(lax.rsqrt(jnp.sum(diagonal, axis=1, keepdims=True)))
-        acrosses.append(lax.rsqrt(jnp.sum(diagonal, axis=0, keepdims=True)))
+        if b == 0:
+            downs.append(jnp.ones((size, 1), jnp.float32))
+            acrosses.append(jnp.ones((1, size), jnp.float32))
+        else:
+            diagonal = jnp.where(eye, blocks[b, b], 0.0)
+            downs.append(lax.rsqrt(jnp.sum(diagonal, axis=1, keepdims=True)))
+            acrosses.append(lax.rsqrt(jnp.sum(diagonal, axis=0, keepdims=True)))
         rights.append(downs[b] * right[b * size : (b + 1) * size])
     for b in range(BLOCKS):
-        for c in range(b, BLOCKS):
+        for c in range(max(b, 1), BLOCKS):
             blocks[b, c] = downs[b] * blocks[b, c] * acrosses[c]
             if c > b:
                 blocks[c, b] = blocks[b, c].T
     for b in range(BLOCKS):
-        inverse = factor_inverse(blocks[b, b])
+        inverse = factor_inverse(blocks[b, b]) if b else first_ref[...]
         later = range(b + 1, BLOCKS)
         row = triple(inverse, jnp.concatenate([rights[b]] + [blocks[b, c] for c in later], axis=1))
         if later:
@@ -739,7 +750,8 @@
     coarse = FACES * ncon
     size = 2 * ncon
     half = width // 2
-    half_rows = (2 * size + ncon + coarse) // 2
+    first_rows, message_rows = ncon, (2 * size + ncon + 8 + coarse + 8) // 2
+    rest_rows = 2 * size + ncon + 8 + coarse - message_rows
     uppers = FACES * (FACES - 1) // 2
     anywhere = pl.BlockSpec(memory_space=pl.ANY)
     main_memory = pl.BlockSpec(memory_space=pltpu.HBM)
@@ -804,7 +816,7 @@
 
     payload, product, late_partner, late_inverse = pl.pallas_call(
         functools.partial(main_kernel, (AXES[0], AXES[1]), early, late),
-        out_shape=[shape(2 * half_rows, columns), shape(FACES, ncon, width)]
+        out_shape=[shape(message_rows + rest_rows, columns), shape(FACES, ncon, width)]
         + [halves(len(late))] * 2,
         in_specs=vmem_specs(len(got[0]) + len(got[1]) + 6),
         out_specs=vmem_specs(4),
@@ -814,11 +826,11 @@
 
     partners = [early_partner, late_partner]
     inverses = [early_inverse, late_inverse]
-    their_basis, their_product = pl.pallas_call(
+    their_product = pl.pallas_call(
         functools.partial(theirs_kernel, faces, ncon),
-        out_shape=[shape(4, ncon, width)] * 2,
+        out_shape=shape(4, ncon, width),
         in_specs=vmem_specs(5 + len(got[0]) + len(got[1])),
-        out_specs=vmem_specs(2),
+        out_specs=vmem_specs(1)[0],
         compiler_params=params(16),
         cost_estimate=cost(2),
     )(own_halves, *got[0], *got[1], *partners, *inverses)
@@ -827,21 +839,29 @@
         return pl.pallas_call(
             functools.partial(spread_kernel, faces),
             out_shape=jax.ShapeDtypeStruct((4, width, 3 * size), jnp.bfloat16),
-            in_specs=[anywhere] + vmem_specs(5),
+            in_specs=[anywhere] + vmem_specs(4),
             out_specs=vmem_specs(1)[0],
             compiler_params=params(16),
             cost_estimate=cost(2),
-        )(token, their_basis, their_product, product, *inverses)
-
-    def solve(matrices, rights, unread):
+        )(token, their_product, product, *inverses)
+
+    def solve(firsts, matrices, rights, unread):
+        first = pl.pallas_call(
+            first_kernel,
+            out_shape=shape(size, size),
+            in_specs=vmem_specs(len(firsts)),
+            out_specs=vmem_specs(1)[0],
+            compiler_params=params(8),
+            cost_estimate=cost(2),
+        )(*firsts)
         return pl.pallas_call(
             functools.partial(solve_kernel, size, len(matrices), columns),
             out_shape=shape(coarse, columns),
-            in_specs=vmem_specs(2 * len(matrices)) + [anywhere] * len(unread),
+            in_specs=vmem_specs(1 + 2 * len(matrices)) + [anywhere] * len(unread),
             out_specs=vmem_specs(1)[0],
             compiler_params=params(12),
             cost_estimate=cost(7),
-        )(*matrices, *rights, *unread)
+        )(first, *matrices, *rights, *unread)
 
     result = dict(
         out_shape=shape(order, columns),
@@ -859,26 +879,33 @@
         other = lax.ppermute(payload, "gy", core_swap)
         left, rest = pl.pallas_call(
             choose_kernel,
-            out_shape=[shape(half_rows, columns)] * 2,
+            out_shape=[shape(message_rows, columns), shape(rest_rows, columns)],
             in_specs=vmem_specs(3),
             out_specs=vmem_specs(2),
             compiler_params=params(8),
         )(flags, payload, other)
         left_moved = lax.ppermute(left, "gy", chip_x)
         rest_moved = lax.ppermute(rest, "gz", chip_y)
-        left_last, rest_last, *sent = pl.pallas_call(
+        first_last, left_last, rest_last, *sent = pl.pallas_call(
             add_kernel,
-            out_shape=[shape(half_rows, columns)] * 2
+            out_shape=[
+                shape(first_rows, columns),
+                shape(message_rows - first_rows, columns),
+                shape(rest_rows, columns),
+            ]
             + face_shapes(counts[2], (ncon, width)),
             in_specs=vmem_specs(5) + [anywhere],
-            out_specs=vmem_specs(2 + face_arrays(counts[2])),
+            out_specs=vmem_specs(3 + face_arrays(counts[2])),
             compiler_params=params(8),
-        )(left, left_moved, rest, rest_moved, product, their_basis)
+        )(left, left_moved, rest, rest_moved, product, their_product)
+        first_other = lax.ppermute(first_last, "gz", chip_y)
         left_other = lax.ppermute(left_last, "gz", chip_y)
         rest_other = lax.ppermute(rest_last, "gy", chip_x)
         theirs = exchange(sent, AXES[2])
-        spread = spread_of(left_last)
-        answer = solve([left_last, left_other], [rest_last, rest_other], [spread])
+        spread = spread_of(first_other)
+        answer = solve(
+            [first_last, first_other], [left_last, left_other], [rest_last, rest_other], [spread]
+        )
         there = lax.ppermute(answer, "gy", core_swap)
         *sent, mine = pl.pallas_call(
             functools.partial(rows_kernel, ncon),
@@ -900,7 +927,9 @@
         total = lax.psum(jnp.where(chosen[:, None, None], payload[None], 0.0), ("gy", "gz"))
         total = lax.dynamic_index_in_dim(total, member_of, 0, keepdims=False)
         spread = spread_of(payload)
-        answer = solve([total[:half_rows]], [total[half_rows:]], [])
+        answer = solve(
+            [total[:first_rows]], [total[first_rows:message_rows]], [total[message_rows:]], []
+        )
 
         def from_near(faces_of, axis):
             even, odd = faces_of

time: 51 us -> 50.4 us (0.988)
  waiting for transfers between devices: 9.5 us -> 4.9 us
  starting transfers between devices: 14.1 us -> 17.6 us
    pallas_call x3 -> x4, Pallas kernels: 1.68 us -> 5.59 us  [the longest x1 3.3 us: per_device(): pl.pallas_call(functools.partial(theirs_kernel, faces, ncon), out_shape=s...]
    pallas_call x1, Pallas kernels: 7.35 us -> 5.23 us  [solve(): pl.pallas_call(functools.partial(solve_kernel, size, len(matrices), colum...]
    ppermute x0 -> x1, starting transfers between devices: none -> 1.58 us  [per_device(): first_other = lax.ppermute(first_last, 'gz', chip_y)]
    ppermute x1, waiting for transfers between devices: 1.53 us -> 0.01 us  [per_device(): rest_other = lax.ppermute(rest_last, 'gy', chip_x)]
    ppermute x1, waiting for transfers between devices: 1.35 us -> 0.01 us  [per_device(): rest_moved = lax.ppermute(rest, 'gz', chip_y)]
    pallas_call x1, Pallas kernels: 1.95 us -> 0.61 us  [spread_of(): pl.pallas_call(functools.partial(spread_kernel, faces), out_shape=jax.Sha...]
    ppermute x1, waiting for transfers between devices: 1.09 us -> 0.02 us  [per_device(): left_moved = lax.ppermute(left, 'gy', chip_x)]
    ppermute x2, starting transfers between devices: 3.61 us -> 4.44 us  [exchange(): return [lax.ppermute(arrays[0], axis, flipped(axis, 1))]]
  transfers between devices with their start and end apart: 14 -> 15, of which waited for: 10 -> 6; matrix products, arithmetic and copies ran while one was open for 0% -> 0% of each run, Pallas kernels for 21% -> 26%
where the time goes in v16:
time: 50.4 us; the launch traced here: 50.3 us
  Pallas kernels  27.4 us (54%)
  starting transfers between devices  17.6 us (35%)
  waiting for transfers between devices  4.9 us (10%)
    ppermute x3, starting transfers between devices, exchange(): lax.ppermute(arrays[0], axis, outer_pairs(axis))  6.39 us
    pallas_call x1, Pallas kernels, per_device(): pl.pallas_call(functools.partial(main_kernel, (AXES[0], AXES[1]), early,...  6.34 us
    pallas_call x1, Pallas kernels, solve(): pl.pallas_call(functools.partial(solve_kernel, size, len(matrices), colum...  5.23 us
    ppermute x2, starting transfers between devices, exchange(): return [lax.ppermute(arrays[0], axis, flipped(axis, 1))]  4.44 us
    pallas_call x1, Pallas kernels, per_device(): pl.pallas_call(functools.partial(theirs_kernel, faces, ncon), out_shape=s...  3.3 us
    pallas_call x1, Pallas kernels, per_device(): pl.pallas_call(functools.partial(halves_kernel, planes), out_shape=[halve...  2.7 us
    pallas_call x1, Pallas kernels, per_device(): pl.pallas_call(functools.partial(early_kernel, AXES[2:3], early), out_sha...  2.59 us
    pallas_call x1, Pallas kernels, solve(): pl.pallas_call(first_kernel, out_shape=shape(size, size), in_specs=vmem_s...  2.18 us
  transfers between devices with their start and end apart: 15, of which 6 were waited for; matrix products, arithmetic and copies ran while one was open for 0% of the time, Pallas kernels for 26%

profile of v16, /device:TPU:0, one launch (start us, length us, event | category | flops | bytes accessed | tf_op | source)
XLA Modules:
  0.0 50.3 jit_solution(13358110635104701760)
XLA Ops:
  0.0 0.0 copy-start.1
  0.0 1.7 %shard_map.46 = (f32[328,128]{1,0:T(8,128)S(1)}, f32[328,128]{1,0:T(8,128)S(1)}, f32[328,128]{1,0:T(8,128)S(1)}, f32[328,128]{1,0:T(8,128)S(1)}, f32[2,264,128]{2,1,0:T(8,128)S(1)}, /*index=5*/f32[6,256,256]{2,1,0:T(8,128)S(1)}) custom-call(f32[1536,1536]{1,0:T(8,128)} %bitcast.10, f32[6,32,256]{2,1,0:T(8,128)} %bitcast.6), custom_call_target="tpu_custom_call" | custom-call | tf_op jit(solution)/shard_map/pallas_call | solution.py:775
  1.7 3.0 %collective-permute-start.4 = (f32[2,264,128]{2,1,0:T(8,128)S(1)}, f32[2,264,128]{2,1,0:T(8,128)S(1)}, u32[]{:S(2)}, u32[]{:S(2)}) collective-permute-start(f32[2,264,128]{2,1,0:T(8,128)S(1)} %get-tuple-element.38), channel_id=1, source_target_pairs={{0,1},{1,0},{2,3},{3,2},{4,5},{5,4},{6,7},{7,6},{8,9},{9,8},{10,11... | collective-permute-start | bytes 811016 | tf_op jit(solution)/shard_map/ppermute | solution.py:86
  4.7 3.6 %collective-permute-start = (f32[328,128]{1,0:T(8,128)S(1)}, f32[328,128]{1,0:T(8,128)S(1)}, u32[]{:S(2)}, u32[]{:S(2)}) collective-permute-start(f32[328,128]{1,0:T(8,128)S(1)} %get-tuple-element.32), channel_id=1, source_target_pairs={{0,24},{8,16},{16,8},{24,0},{1,25},{9,17},{17,9},{25,1},{2,26},{10... | collective-permute-start | bytes 503816 | tf_op jit(solution)/shard_map/ppermute | solution.py:88
  8.3 0.0 collective-permute-start.1
  8.3 0.4 collective-permute-start.2
  8.7 1.2 %collective-permute-start.3 = (f32[328,128]{1,0:T(8,128)S(1)}, f32[328,128]{1,0:T(8,128)S(1)}, u32[]{:S(2)}, u32[]{:S(2)}) collective-permute-start(f32[328,128]{1,0:T(8,128)S(1)} %get-tuple-element.35), channel_id=1, source_target_pairs={{0,2},{2,0},{4,6},{6,4},{1,3},{3,1},{5,7},{7,5},{8,10},{10,8},{12,... | collective-permute-start | bytes 503816 | tf_op jit(solution)/shard_map/ppermute | solution.py:89
  9.9 0.0 copy-done.1
  9.9 0.0 copy-start
  10.0 2.7 %shard_map.47 = (bf16[6,2,256,256]{3,2,1,0:T(8,128)(2,1)S(1)}, bf16[15,2,256,256]{3,2,1,0:T(8,128)(2,1)S(1)}, f32[8,128]{1,0:T(8,128)S(1)}) custom-call(f32[1536,1536]{1,0:T(8,128)} %bitcast.11, s32[8]{0:T(128)S(1)} %copy-done.1, f32[6,256,256]{2,1,0:T(8,128)S(1)} %get-tuple-element.30.own_ref.refs_1_.refs_4_), custom_call_target="tpu_custom_call" | custom-call | flops 2000000000 | bytes 1048576 | tf_op jit(solution)/shard_map/pallas_call | solution.py:795
  12.7 0.0 copy-start.2
  12.7 0.0 collective-permute-done.4.refs_0_
  12.7 0.0 copy-done
  12.7 2.6 %shard_map.48 = (f32[2,32,256]{2,1,0:T(8,128)S(1)}, bf16[2,2,256,256]{3,2,1,0:T(8,128)(2,1)S(1)}, bf16[2,2,256,256]{3,2,1,0:T(8,128)(2,1)S(1)}) custom-call(f32[2,264,128]{2,1,0:T(8,128)S(1)} %collective-permute-done.4.refs_0_, f32[6,256,256]{2,1,0:T(8,128)S(1)} %get-tuple-element.30.own_ref.refs_1_.refs_4_, ...), custom_call_target="tpu_custom_call" | custom-call | flops 2000000000 | bytes 1048576 | tf_op jit(solution)/shard_map/pallas_call | solution.py:808
  15.3 0.0 collective-permute-done.refs_0_
  15.3 0.7 %collective-permute-done.1.refs_1_ = f32[328,128]{1,0:T(8,128)S(1)} collective-permute-done((f32[328,128]{1,0:T(8,128)S(1)}, f32[328,128]{1,0:T(8,128)S(1)}, u32[]{:S(2)}, u32[]{:S(2)}) %collective-permute-start.1) | collective-permute-done | bytes 167968 | tf_op jit(solution)/shard_map/ppermute | solution.py:89
  16.0 0.0 collective-permute-done.2.refs_2_
  16.0 0.0 collective-permute-done.3.refs_3_
  16.0 0.0 copy-done.2
  16.1 6.3 %shard_map.49 = (f32[360,128]{1,0:T(8,128)S(1)}, f32[6,32,256]{2,1,0:T(8,128)S(1)}, bf16[4,2,256,256]{3,2,1,0:T(8,128)(2,1)S(1)}, bf16[4,2,256,256]{3,2,1,0:T(8,128)(2,1)S(1)}) custom-call(f32[328,128]{1,0:T(8,128)S(1)} %collective-permute-done.refs_0_, f32[328,128]{1,0:T(8,128)S(1)} %collective-permute-done.1.refs_1_, ...), custom_call_target="tpu_custom_call" | custom-call | flops 8000000000 | bytes 1048576 | tf_op jit(solution)/shard_map/pallas_call | solution.py:817
  22.4 0.1 collective-permute-start.5
  22.5 1.4 %collective-permute-done.5.there_ref = f32[360,128]{1,0:T(8,128)S(1)} collective-permute-done((f32[360,128]{1,0:T(8,128)S(1)}, f32[360,128]{1,0:T(8,128)S(1)}, u32[]{:S(2)}, u32[]{:S(2)}) %collective-permute-start.5) | collective-permute-done | bytes 184352 | tf_op jit(solution)/shard_map/ppermute | solution.py:879
  23.9 0.1 shard_map.50
  23.9 0.6 %collective-permute-start.7 = (f32[176,128]{1,0:T(8,128)S(1)}, f32[176,128]{1,0:T(8,128)S(1)}, u32[]{:S(2)}, u32[]{:S(2)}) collective-permute-start(f32[176,128]{1,0:T(8,128)S(1)} %get-tuple-element.42.third_ref), channel_id=1, source_target_pairs={{0,1},{1,0},{2,3},{3,2},{4,5},{5,4},{6,7},{7,6},{8,9},{9,8},{10,11... | collective-permute-start | bytes 270344 | tf_op jit(solution)/shard_map/ppermute | solution.py:888
  24.5 1.5 %collective-permute-start.6 = (f32[184,128]{1,0:T(8,128)S(1)}, f32[184,128]{1,0:T(8,128)S(1)}, u32[]{:S(2)}, u32[]{:S(2)}) collective-permute-start(f32[184,128]{1,0:T(8,128)S(1)} %get-tuple-element.41.first_ref), channel_id=1, source_target_pairs={{0,4},{2,6},{4,0},{6,2},{1,5},{3,7},{5,1},{7,3},{8,12},{10,14},{12... | collective-permute-start | bytes 282632 | tf_op jit(solution)/shard_map/ppermute | solution.py:887
  26.0 3.3 %shard_map.51.unread.theirs_ref = f32[4,32,256]{2,1,0:T(8,128)S(1)} custom-call(bf16[6,2,256,256]{3,2,1,0:T(8,128)(2,1)S(1)} %get-tuple-element.36.refs_2_.refs_5_.own_ref, f32[328,128]{1,0:T(8,128)S(1)} %collective-permute-done.refs_0_, f32[328,128]{1,0:T(8,128)S(1)} %collective-permute-done.1.refs_1_, f32[328,128]{1,0:T(8,128)S(1)} %collective-permute-done.2.refs_2_, ...), custom_call_target="tpu_custom_call" | custom-call | flops 2000000000 | bytes 1048576 | tf_op jit(solution)/shard_map/pallas_call | solution.py:829
  29.3 0.0 collective-permute-done.7.fourth_ref
  29.3 0.0 collective-permute-done.6.second_ref
  29.4 1.6 %collective-permute-start.8 = (f32[32,128]{1,0:T(8,128)S(1)}, f32[32,128]{1,0:T(8,128)S(1)}, u32[]{:S(2)}, u32[]{:S(2)}) collective-permute-start(f32[32,128]{1,0:T(8,128)S(1)} %get-tuple-element.48.refs_0_), channel_id=1, source_target_pairs={{0,1},{1,0},{2,3},{3,2},{4,5},{5,4},{6,7},{7,6},{8,9},{9,8},{10,11... | collective-permute-start | bytes 49160 | tf_op jit(solution)/shard_map/ppermute | solution.py:901
  31.0 0.5 %collective-permute-start.9 = (f32[152,128]{1,0:T(8,128)S(1)}, f32[152,128]{1,0:T(8,128)S(1)}, u32[]{:S(2)}, u32[]{:S(2)}) collective-permute-start(f32[152,128]{1,0:T(8,128)S(1)} %get-tuple-element.49.refs_0_), channel_id=1, source_target_pairs={{0,1},{1,0},{2,3},{3,2},{4,5},{5,4},{6,7},{7,6},{8,9},{9,8},{10,11... | collective-permute-start | bytes 233480 | tf_op jit(solution)/shard_map/ppermute | solution.py:902
  31.5 1.2 %collective-permute-start.10 = (f32[176,128]{1,0:T(8,128)S(1)}, f32[176,128]{1,0:T(8,128)S(1)}, u32[]{:S(2)}, u32[]{:S(2)}) collective-permute-start(f32[176,128]{1,0:T(8,128)S(1)} %get-tuple-element.50.refs_2_), channel_id=1, source_target_pairs={{0,4},{2,6},{4,0},{6,2},{1,5},{3,7},{5,1},{7,3},{8,12},{10,14},{12... | collective-permute-start | bytes 270344 | tf_op jit(solution)/shard_map/ppermute | solution.py:903
  32.7 0.6 %collective-permute-done.8.unread.refs_1_ = f32[32,128]{1,0:T(8,128)S(1)} collective-permute-done((f32[32,128]{1,0:T(8,128)S(1)}, f32[32,128]{1,0:T(8,128)S(1)}, u32[]{:S(2)}, u32[]{:S(2)}) %collective-permute-start.8) | collective-permute-done | bytes 16416 | tf_op jit(solution)/shard_map/ppermute | solution.py:901
  33.4 2.2 %shard_map.54.first_ref = f32[64,64]{1,0:T(8,128)S(1)} custom-call(f32[32,128]{1,0:T(8,128)S(1)} %get-tuple-element.48.refs_0_, f32[32,128]{1,0:T(8,128)S(1)} %collective-permute-done.8.unread.refs_1_), custom_call_target="tpu_custom_call" | custom-call | flops 2000000000 | bytes 1048576 | tf_op jit(solution)/shard_map/pallas_call | solution.py:849
  35.5 0.6 %shard_map.53.refs_4_.refs_0_.spread_ref = bf16[4,256,192]{2,1,0:T(8,128)(2,1)S(1)} custom-call(f32[32,128]{1,0:T(8,128)S(1)} %collective-permute-done.8.unread.refs_1_, f32[4,32,256]{2,1,0:T(8,128)S(1)} %shard_map.51.unread.theirs_ref, f32[6,32,256]{2,1,0:T(8,128)S(1)} %get-tuple-element.43.product_ref, ...), custom_call_target="tpu_custom_call" | custom-call | flops 2000000000 | bytes 1048576 | tf_op jit(solution)/shard_map/pallas_call | solution.py:839
  36.2 0.0 collective-permute-done.9.refs_1_
  36.2 0.0 collective-permute-done.10.refs_3_
  36.2 5.2 %shard_map.55.here_ref.refs_1_ = f32[192,128]{1,0:T(8,128)S(1)} custom-call(f32[64,64]{1,0:T(8,128)S(1)} %shard_map.54.first_ref, f32[152,128]{1,0:T(8,128)S(1)} %get-tuple-element.49.refs_0_, f32[152,128]{1,0:T(8,128)S(1)} %collective-permute-done.9.refs_1_, f32[176,128]{1,0:T(8,128)S(1)} %get-tuple-element.50.refs_2_, ...), custom_call_target="tpu_custom_call" | custom-call | flops 7000000000 | bytes 1048576 | tf_op jit(solution)/shard_map/pallas_call | solution.py:857
  41.4 0.1 collective-permute-start.11
  41.5 1.4 %collective-permute-start.14 = (f32[2,32,256]{2,1,0:T(8,128)S(1)}, f32[2,32,256]{2,1,0:T(8,128)S(1)}, u32[]{:S(2)}, u32[]{:S(2)}) collective-permute-start(f32[2,32,256]{2,1,0:T(8,128)S(1)} %get-tuple-element.54), channel_id=1, source_target_pairs={{0,1},{1,0},{2,3},{3,2},{4,5},{5,4},{6,7},{7,6},{8,9},{9,8},{10,11... | collective-permute-start | bytes 196616 | tf_op jit(solution)/shard_map/ppermute | solution.py:86
  42.9 0.0 collective-permute-done.11.there_ref.refs_2_
  43.0 2.4 %collective-permute-start.12 = (f32[32,128]{1,0:T(8,128)S(1)}, f32[32,128]{1,0:T(8,128)S(1)}, u32[]{:S(2)}, u32[]{:S(2)}) collective-permute-start(f32[32,128]{1,0:T(8,128)S(1)} %get-tuple-element.52), channel_id=1, source_target_pairs={{0,24},{8,16},{16,8},{24,0},{1,25},{9,17},{17,9},{25,1},{2,26},{10... | collective-permute-start | bytes 49160 | tf_op jit(solution)/shard_map/ppermute | solution.py:88
  45.4 0.0 collective-permute-start.13
  45.4 0.6 %collective-permute-done.14.refs_3_ = f32[2,32,256]{2,1,0:T(8,128)S(1)} collective-permute-done((f32[2,32,256]{2,1,0:T(8,128)S(1)}, f32[2,32,256]{2,1,0:T(8,128)S(1)}, u32[]{:S(2)}, u32[]{:S(2)}) %collective-permute-start.14) | collective-permute-done | bytes 65568 | tf_op jit(solution)/shard_map/ppermute | solution.py:86
  46.0 1.7 %shard_map.57.refs_2_ = f32[1536,128]{1,0:T(8,128)} custom-call(f32[8,128]{1,0:T(8,128)S(1)} %get-tuple-element.31.flag_ref, f32[6,32,256]{2,1,0:T(8,128)S(1)} %get-tuple-element.43.product_ref, bf16[2,2,256,256]{3,2,1,0:T(8,128)(2,1)S(1)} %get-tuple-element.46.refs_6_.refs_0_.early_inverse, ...), custom_call_target="tpu_custom_call" | custom-call | flops 1000000000 | bytes 1048576 | tf_op jit(solution)/shard_map/pallas_call | solution.py:918
  47.7 0.9 %collective-permute-done.12.refs_0_ = f32[32,128]{1,0:T(8,128)S(1)} collective-permute-done((f32[32,128]{1,0:T(8,128)S(1)}, f32[32,128]{1,0:T(8,128)S(1)}, u32[]{:S(2)}, u32[]{:S(2)}) %collective-permute-start.12) | collective-permute-done | bytes 16416 | tf_op jit(solution)/shard_map/ppermute | solution.py:88
  48.6 0.6 %collective-permute-done.13.refs_1_ = f32[32,128]{1,0:T(8,128)S(1)} collective-permute-done((f32[32,128]{1,0:T(8,128)S(1)}, f32[32,128]{1,0:T(8,128)S(1)}, u32[]{:S(2)}, u32[]{:S(2)}) %collective-permute-start.13) | collective-permute-done | bytes 16416 | tf_op jit(solution)/shard_map/ppermute | solution.py:89
  49.1 1.0 %shard_map.58 = f32[1536,128]{1,0:T(8,128)} custom-call(bf16[4,256,192]{2,1,0:T(8,128)(2,1)S(1)} %shard_map.53.refs_4_.refs_0_.spread_ref, f32[64,128]{1,0:T(8,128)S(1)} %get-tuple-element.51.rows_ref, f32[32,128]{1,0:T(8,128)S(1)} %collective-permute-done.12.refs_0_, f32[32,128]{1,0:T(8,128)S(1)} %collective-permute-done.13.refs_1_, ...), custom_call_target="tpu_custom_call", output_to_operand_aliasing={{}: (4, {})} | custom-call | flops 1000000000 | bytes 1048576 | tf_op jit(solution)/shard_map/pallas_call | solution.py:954
  (2 shorter events, 0.1 us)
Async XLA Ops:
  0.0 9.9 %copy-start.1 = (s32[8]{0:T(128)S(1)}, s32[8]{0:T(128)}, u32[]{:S(2)}) copy-start(s32[8]{0:T(128)} %group_ref.1) | copy-start | bytes 100
  1.7 11.0 %collective-permute-start.4 = (f32[2,264,128]{2,1,0:T(8,128)S(1)}, f32[2,264,128]{2,1,0:T(8,128)S(1)}, u32[]{:S(2)}, u32[]{:S(2)}) collective-permute-start(f32[2,264,128]{2,1,0:T(8,128)S(1)} %get-tuple-element.38), channel_id=1, source_target_pairs={{0,1},{1,0},{2,3},{3,2},{4,5},{5,4},{6,7},{7,6},{8,9},{9,8},{10,11... | collective-permute-start | bytes 811016 | tf_op jit(solution)/shard_map/ppermute | solution.py:86
  4.7 10.6 %collective-permute-start = (f32[328,128]{1,0:T(8,128)S(1)}, f32[328,128]{1,0:T(8,128)S(1)}, u32[]{:S(2)}, u32[]{:S(2)}) collective-permute-start(f32[328,128]{1,0:T(8,128)S(1)} %get-tuple-element.32), channel_id=1, source_target_pairs={{0,24},{8,16},{16,8},{24,0},{1,25},{9,17},{17,9},{25,1},{2,26},{10... | collective-permute-start | bytes 503816 | tf_op jit(solution)/shard_map/ppermute | solution.py:88
  8.3 7.7 %collective-permute-start.1 = (f32[328,128]{1,0:T(8,128)S(1)}, f32[328,128]{1,0:T(8,128)S(1)}, u32[]{:S(2)}, u32[]{:S(2)}) collective-permute-start(f32[328,128]{1,0:T(8,128)S(1)} %get-tuple-element.33), channel_id=1, source_target_pairs={{0,8},{8,0},{16,24},{24,16},{1,9},{9,1},{17,25},{25,17},{2,10},{10... | collective-permute-start | bytes 503816 | tf_op jit(solution)/shard_map/ppermute | solution.py:89
  8.3 7.7 %collective-permute-start.2 = (f32[328,128]{1,0:T(8,128)S(1)}, f32[328,128]{1,0:T(8,128)S(1)}, u32[]{:S(2)}, u32[]{:S(2)}) collective-permute-start(f32[328,128]{1,0:T(8,128)S(1)} %get-tuple-element.34), channel_id=1, source_target_pairs={{0,6},{2,4},{4,2},{6,0},{1,7},{3,5},{5,3},{7,1},{8,14},{10,12},{12... | collective-permute-start | bytes 503816 | tf_op jit(solution)/shard_map/ppermute | solution.py:88
  8.7 7.3 %collective-permute-start.3 = (f32[328,128]{1,0:T(8,128)S(1)}, f32[328,128]{1,0:T(8,128)S(1)}, u32[]{:S(2)}, u32[]{:S(2)}) collective-permute-start(f32[328,128]{1,0:T(8,128)S(1)} %get-tuple-element.35), channel_id=1, source_target_pairs={{0,2},{2,0},{4,6},{6,4},{1,3},{3,1},{5,7},{7,5},{8,10},{10,8},{12,... | collective-permute-start | bytes 503816 | tf_op jit(solution)/shard_map/ppermute | solution.py:89
  9.9 2.7 %copy-start = (f32[1,1,1,6,256,32]{4,5,3,2,1,0:T(8,128)S(1)}, f32[1,1,1,6,256,32]{4,5,3,2,1,0:T(8,128)}, u32[]{:S(2)}) copy-start(f32[1,1,1,6,256,32]{4,5,3,2,1,0:T(8,128)} %param.5) | copy-start | bytes 589828
  12.7 3.4 %copy-start.2 = (f32[1,1,1,1536,128]{4,3,2,1,0:T(8,128)S(1)}, f32[1,1,1,1536,128]{4,3,2,1,0:T(8,128)}, u32[]{:S(2)}) copy-start(f32[1,1,1,1536,128]{4,3,2,1,0:T(8,128)} %param.6) | copy-start | bytes 2359300
  22.4 1.5 %collective-permute-start.5 = (f32[360,128]{1,0:T(8,128)S(1)}, f32[360,128]{1,0:T(8,128)S(1)}, u32[]{:S(2)}, u32[]{:S(2)}) collective-permute-start(f32[360,128]{1,0:T(8,128)S(1)} %get-tuple-element.40.here_ref), channel_id=1, source_target_pairs={{0,2},{2,0},{4,6},{6,4},{1,3},{3,1},{5,7},{7,5},{8,10},{10,8},{12,... | collective-permute-start | bytes 552968 | tf_op jit(solution)/shard_map/ppermute | solution.py:879
  23.9 5.4 %collective-permute-start.7 = (f32[176,128]{1,0:T(8,128)S(1)}, f32[176,128]{1,0:T(8,128)S(1)}, u32[]{:S(2)}, u32[]{:S(2)}) collective-permute-start(f32[176,128]{1,0:T(8,128)S(1)} %get-tuple-element.42.third_ref), channel_id=1, source_target_pairs={{0,1},{1,0},{2,3},{3,2},{4,5},{5,4},{6,7},{7,6},{8,9},{9,8},{10,11... | collective-permute-start | bytes 270344 | tf_op jit(solution)/shard_map/ppermute | solution.py:888
  24.5 4.8 %collective-permute-start.6 = (f32[184,128]{1,0:T(8,128)S(1)}, f32[184,128]{1,0:T(8,128)S(1)}, u32[]{:S(2)}, u32[]{:S(2)}) collective-permute-start(f32[184,128]{1,0:T(8,128)S(1)} %get-tuple-element.41.first_ref), channel_id=1, source_target_pairs={{0,4},{2,6},{4,0},{6,2},{1,5},{3,7},{5,1},{7,3},{8,12},{10,14},{12... | collective-permute-start | bytes 282632 | tf_op jit(solution)/shard_map/ppermute | solution.py:887
  29.4 4.0 %collective-permute-start.8 = (f32[32,128]{1,0:T(8,128)S(1)}, f32[32,128]{1,0:T(8,128)S(1)}, u32[]{:S(2)}, u32[]{:S(2)}) collective-permute-start(f32[32,128]{1,0:T(8,128)S(1)} %get-tuple-element.48.refs_0_), channel_id=1, source_target_pairs={{0,1},{1,0},{2,3},{3,2},{4,5},{5,4},{6,7},{7,6},{8,9},{9,8},{10,11... | collective-permute-start | bytes 49160 | tf_op jit(solution)/shard_map/ppermute | solution.py:901
  31.0 5.2 %collective-permute-start.9 = (f32[152,128]{1,0:T(8,128)S(1)}, f32[152,128]{1,0:T(8,128)S(1)}, u32[]{:S(2)}, u32[]{:S(2)}) collective-permute-start(f32[152,128]{1,0:T(8,128)S(1)} %get-tuple-element.49.refs_0_), channel_id=1, source_target_pairs={{0,1},{1,0},{2,3},{3,2},{4,5},{5,4},{6,7},{7,6},{8,9},{9,8},{10,11... | collective-permute-start | bytes 233480 | tf_op jit(solution)/shard_map/ppermute | solution.py:902
  31.5 4.7 %collective-permute-start.10 = (f32[176,128]{1,0:T(8,128)S(1)}, f32[176,128]{1,0:T(8,128)S(1)}, u32[]{:S(2)}, u32[]{:S(2)}) collective-permute-start(f32[176,128]{1,0:T(8,128)S(1)} %get-tuple-element.50.refs_2_), channel_id=1, source_target_pairs={{0,4},{2,6},{4,0},{6,2},{1,5},{3,7},{5,1},{7,3},{8,12},{10,14},{12... | collective-permute-start | bytes 270344 | tf_op jit(solution)/shard_map/ppermute | solution.py:903
  41.4 1.5 %collective-permute-start.11 = (f32[192,128]{1,0:T(8,128)S(1)}, f32[192,128]{1,0:T(8,128)S(1)}, u32[]{:S(2)}, u32[]{:S(2)}) collective-permute-start(f32[192,128]{1,0:T(8,128)S(1)} %shard_map.55.here_ref.refs_1_), channel_id=1, source_target_pairs={{0,2},{2,0},{4,6},{6,4},{1,3},{3,1},{5,7},{7,5},{8,10},{10,8},{12,... | collective-permute-start | bytes 294920 | tf_op jit(solution)/shard_map/ppermute | solution.py:909
  41.5 4.5 %collective-permute-start.14 = (f32[2,32,256]{2,1,0:T(8,128)S(1)}, f32[2,32,256]{2,1,0:T(8,128)S(1)}, u32[]{:S(2)}, u32[]{:S(2)}) collective-permute-start(f32[2,32,256]{2,1,0:T(8,128)S(1)} %get-tuple-element.54), channel_id=1, source_target_pairs={{0,1},{1,0},{2,3},{3,2},{4,5},{5,4},{6,7},{7,6},{8,9},{9,8},{10,11... | collective-permute-start | bytes 196616 | tf_op jit(solution)/shard_map/ppermute | solution.py:86
  43.0 5.6 %collective-permute-start.12 = (f32[32,128]{1,0:T(8,128)S(1)}, f32[32,128]{1,0:T(8,128)S(1)}, u32[]{:S(2)}, u32[]{:S(2)}) collective-permute-start(f32[32,128]{1,0:T(8,128)S(1)} %get-tuple-element.52), channel_id=1, source_target_pairs={{0,24},{8,16},{16,8},{24,0},{1,25},{9,17},{17,9},{25,1},{2,26},{10... | collective-permute-start | bytes 49160 | tf_op jit(solution)/shard_map/ppermute | solution.py:88
  45.4 3.7 %collective-permute-start.13 = (f32[32,128]{1,0:T(8,128)S(1)}, f32[32,128]{1,0:T(8,128)S(1)}, u32[]{:S(2)}, u32[]{:S(2)}) collective-permute-start(f32[32,128]{1,0:T(8,128)S(1)} %get-tuple-element.53), channel_id=1, source_target_pairs={{0,8},{8,0},{16,24},{24,16},{1,9},{9,1},{17,25},{25,17},{2,10},{10... | collective-permute-start | bytes 49160 | tf_op jit(solution)/shard_map/ppermute | solution.py:89

commit v17 on v16

--- a/solution.py
+++ b/solution.py
@@ -126,14 +126,14 @@
     outs, blocks = refs[:-4], refs[-4]
     starts, sems, start_sem = refs[-3:]
     half = width // 2
+    start_copy = pltpu.make_async_copy(starts_ref.at[pl.ds(0, 4)], starts, start_sem)
+    start_copy.start()
     copies = []
     for f in range(FACES):
         place = pl.ds(f * width, width)
         copy = pltpu.make_async_copy(schur_ref.at[place, place], blocks.at[f], sems.at[f])
         copy.start()
         copies.append(copy)
-    start_copy = pltpu.make_async_copy(starts_ref.at[pl.ds(0, 4)], starts, start_sem)
-    start_copy.start()
     row, col = iota((half, half), 0), iota((half, half), 1)
     start_copy.wait()
 
@@ -532,8 +532,8 @@
 
 
 def theirs_kernel(faces, ncon, own_ref, *refs):
-    inputs, partner_refs, inverse_refs = refs[:-5], refs[-5:-3], refs[-3:-1]
-    product_out = refs[-1]
+    inputs, partner_refs, inverse_refs = refs[:-6], refs[-6:-4], refs[-4:-2]
+    basis_out, product_out = refs[-2:]
     basis = []
     done = 0
     for axis in AXES[:2]:
@@ -549,20 +549,23 @@
     ]
     for sweep in range(SUB_ITERS):
         basis = sweep_basis(*matrices, basis)
+    for f in range(count):
+        basis_out[f] = basis[f]
+        product_out[f] = thin(stacked(basis[f]), matrices[2][f])
+
+
+def spread_kernel(faces, unread, basis_ref, theirs_ref, product_ref, *refs):
+    inverse_refs, out_ref = refs[:2], refs[2]
+    basis = [basis_ref[f] for f in range(basis_ref.shape[0])]
     factors = factor_inverses([dot(b, b, ((1,), (1,))) for b in basis])
-    for f in range(count):
-        product_out[f] = triple(factors[f], thin(stacked(basis[f]), matrices[2][f]))
-
-
-def spread_kernel(faces, unread, theirs_ref, product_ref, *refs):
-    inverse_refs, out_ref = refs[:2], refs[2]
-    for f in range(theirs_ref.shape[0]):
-        both = jnp.concatenate([product_ref[f], theirs_ref[f]], axis=0)
+    for f in range(len(basis)):
+        theirs = triple(factors[f], theirs_ref[f])
+        both = jnp.concatenate([product_ref[f], theirs], axis=0)
         high, low = split(thin(stacked(both), find(faces, inverse_refs, f)).T)
         out_ref[f] = jnp.concatenate([high, high, low], axis=1)
 
 
-def choose_kernel(flag_ref, here_ref, there_ref, matrix_ref, right_ref):
+def choose_kernel(flag_ref, here_ref, there_ref, unread, matrix_ref, right_ref):
     mine = flag_ref[0:1, 0:1] > 0.5
     other = flag_ref[1:2, 0:1] > 0.5
     total = jnp.where(mine, here_ref[...], 0.0) + jnp.where(other, there_ref[...], 0.0)
@@ -826,11 +829,11 @@
 
     partners = [early_partner, late_partner]
     inverses = [early_inverse, late_inverse]
-    their_product = pl.pallas_call(
+    their_basis, their_product = pl.pallas_call(
         functools.partial(theirs_kernel, faces, ncon),
-        out_shape=shape(4, ncon, width),
+        out_shape=[shape(4, ncon, width)] * 2,
         in_specs=vmem_specs(5 + len(got[0]) + len(got[1])),
-        out_specs=vmem_specs(1)[0],
+        out_specs=vmem_specs(2),
         compiler_params=params(16),
         cost_estimate=cost(2),
     )(own_halves, *got[0], *got[1], *partners, *inverses)
@@ -839,11 +842,11 @@
         return pl.pallas_call(
             functools.partial(spread_kernel, faces),
             out_shape=jax.ShapeDtypeStruct((4, width, 3 * size), jnp.bfloat16),
-            in_specs=[anywhere] + vmem_specs(4),
+            in_specs=[anywhere] + vmem_specs(5),
             out_specs=vmem_specs(1)[0],
             compiler_params=params(16),
             cost_estimate=cost(2),
-        )(token, their_product, product, *inverses)
+        )(token, their_basis, their_product, product, *inverses)
 
     def solve(firsts, matrices, rights, unread):
         first = pl.pallas_call(
@@ -880,12 +883,13 @@
         left, rest = pl.pallas_call(
             choose_kernel,
             out_shape=[shape(message_rows, columns), shape(rest_rows, columns)],
-            in_specs=vmem_specs(3),
+            in_specs=vmem_specs(3) + [anywhere],
             out_specs=vmem_specs(2),
             compiler_params=params(8),
-        )(flags, payload, other)
+        )(flags, payload, other, their_basis)
         left_moved = lax.ppermute(left, "gy", chip_x)
         rest_moved = lax.ppermute(rest, "gz", chip_y)
+        spread = spread_of(left)
         first_last, left_last, rest_last, *sent = pl.pallas_call(
             add_kernel,
             out_shape=[
@@ -897,14 +901,13 @@
             in_specs=vmem_specs(5) + [anywhere],
             out_specs=vmem_specs(3 + face_arrays(counts[2])),
             compiler_params=params(8),
-        )(left, left_moved, rest, rest_moved, product, their_product)
+        )(left, left_moved, rest, rest_moved, product, spread)
         first_other = lax.ppermute(first_last, "gz", chip_y)
         left_other = lax.ppermute(left_last, "gz", chip_y)
         rest_other = lax.ppermute(rest_last, "gy", chip_x)
         theirs = exchange(sent, AXES[2])
-        spread = spread_of(first_other)
         answer = solve(
-            [first_last, first_other], [left_last, left_other], [rest_last, rest_other], [spread]
+            [first_last, first_other], [left_last, left_other], [rest_last, rest_other], []
         )
         there = lax.ppermute(answer, "gy", core_swap)
         *sent, mine = pl.pallas_call(

time: 50.4 us -> 50.5 us (level)
    pallas_call x1, Pallas kernels: 3.3 us -> 1.58 us  [per_device(): pl.pallas_call(functools.partial(theirs_kernel, faces, ncon), out_shape=[...]
    ppermute x1, waiting for transfers between devices: 1.41 us -> 0.02 us  [per_device(): other = lax.ppermute(payload, 'gy', core_swap)]
    pallas_call x1, Pallas kernels: 0.61 us -> 1.95 us  [spread_of(): pl.pallas_call(functools.partial(spread_kernel, faces), out_shape=jax.Sha...]
    ppermute x1, waiting for transfers between devices: 0.01 us -> 1.06 us  [per_device(): rest_moved = lax.ppermute(rest, 'gz', chip_y)]
  transfers between devices with their start and end apart: 15 -> 15, of which waited for: 6 -> 8; matrix products, arithmetic and copies ran while one was open for 0% -> 0% of each run, Pallas kernels for 26% -> 25%
where the time goes in v17:
time: 50.5 us; the launch traced here: 50.4 us
  Pallas kernels  27 us (53%)
  starting transfers between devices  18 us (36%)
  waiting for transfers between devices  5.08 us (10%)
    ppermute x3, starting transfers between devices, exchange(): lax.ppermute(arrays[0], axis, outer_pairs(axis))  6.39 us
    pallas_call x1, Pallas kernels, per_device(): pl.pallas_call(functools.partial(main_kernel, (AXES[0], AXES[1]), early,...  6.33 us
    pallas_call x1, Pallas kernels, solve(): pl.pallas_call(functools.partial(solve_kernel, size, len(matrices), colum...  5.23 us
    ppermute x2, starting transfers between devices, exchange(): return [lax.ppermute(arrays[0], axis, flipped(axis, 1))]  4.61 us
    pallas_call x1, Pallas kernels, per_device(): pl.pallas_call(functools.partial(halves_kernel, planes), out_shape=[halve...  2.7 us
    pallas_call x1, Pallas kernels, per_device(): pl.pallas_call(functools.partial(early_kernel, AXES[2:3], early), out_sha...  2.6 us
    pallas_call x1, Pallas kernels, solve(): pl.pallas_call(first_kernel, out_shape=shape(size, size), in_specs=vmem_s...  2.18 us
    pallas_call x1, Pallas kernels, spread_of(): pl.pallas_call(functools.partial(spread_kernel, faces), out_shape=jax.Sha...  1.95 us
  transfers between devices with their start and end apart: 15, of which 8 were waited for; matrix products, arithmetic and copies ran while one was open for 0% of the time, Pallas kernels for 25%

profile of v17, /device:TPU:0, one launch (start us, length us, event | category | flops | bytes accessed | tf_op | source)
XLA Modules:
  0.0 50.4 jit_solution(12973508021610976455)
XLA Ops:
  0.0 0.0 copy-start.1
  0.0 1.6 %shard_map.46 = (f32[328,128]{1,0:T(8,128)S(1)}, f32[328,128]{1,0:T(8,128)S(1)}, f32[328,128]{1,0:T(8,128)S(1)}, f32[328,128]{1,0:T(8,128)S(1)}, f32[2,264,128]{2,1,0:T(8,128)S(1)}, /*index=5*/f32[6,256,256]{2,1,0:T(8,128)S(1)}) custom-call(f32[1536,1536]{1,0:T(8,128)} %bitcast.10, f32[6,32,256]{2,1,0:T(8,128)} %bitcast.6), custom_call_target="tpu_custom_call" | custom-call | tf_op jit(solution)/shard_map/pallas_call | solution.py:778
  1.6 3.0 %collective-permute-start.4 = (f32[2,264,128]{2,1,0:T(8,128)S(1)}, f32[2,264,128]{2,1,0:T(8,128)S(1)}, u32[]{:S(2)}, u32[]{:S(2)}) collective-permute-start(f32[2,264,128]{2,1,0:T(8,128)S(1)} %get-tuple-element.40), channel_id=1, source_target_pairs={{0,1},{1,0},{2,3},{3,2},{4,5},{5,4},{6,7},{7,6},{8,9},{9,8},{10,11... | collective-permute-start | bytes 811016 | tf_op jit(solution)/shard_map/ppermute | solution.py:86
  4.7 3.6 %collective-permute-start = (f32[328,128]{1,0:T(8,128)S(1)}, f32[328,128]{1,0:T(8,128)S(1)}, u32[]{:S(2)}, u32[]{:S(2)}) collective-permute-start(f32[328,128]{1,0:T(8,128)S(1)} %get-tuple-element.34), channel_id=1, source_target_pairs={{0,24},{8,16},{16,8},{24,0},{1,25},{9,17},{17,9},{25,1},{2,26},{10... | collective-permute-start | bytes 503816 | tf_op jit(solution)/shard_map/ppermute | solution.py:88
  8.3 0.0 collective-permute-start.1
  8.3 0.4 collective-permute-start.2
  8.6 1.2 %collective-permute-start.3 = (f32[328,128]{1,0:T(8,128)S(1)}, f32[328,128]{1,0:T(8,128)S(1)}, u32[]{:S(2)}, u32[]{:S(2)}) collective-permute-start(f32[328,128]{1,0:T(8,128)S(1)} %get-tuple-element.37), channel_id=1, source_target_pairs={{0,2},{2,0},{4,6},{6,4},{1,3},{3,1},{5,7},{7,5},{8,10},{10,8},{12,... | collective-permute-start | bytes 503816 | tf_op jit(solution)/shard_map/ppermute | solution.py:89
  9.9 0.0 copy-done.1
  9.9 0.0 copy-start
  9.9 2.7 %shard_map.47 = (bf16[6,2,256,256]{3,2,1,0:T(8,128)(2,1)S(1)}, bf16[15,2,256,256]{3,2,1,0:T(8,128)(2,1)S(1)}, f32[8,128]{1,0:T(8,128)S(1)}) custom-call(f32[1536,1536]{1,0:T(8,128)} %bitcast.11, s32[8]{0:T(128)S(1)} %copy-done.1, f32[6,256,256]{2,1,0:T(8,128)S(1)} %get-tuple-element.32.own_ref.refs_1_.refs_4_), custom_call_target="tpu_custom_call" | custom-call | flops 2000000000 | bytes 1048576 | tf_op jit(solution)/shard_map/pallas_call | solution.py:798
  12.6 0.0 copy-start.2
  12.6 0.0 collective-permute-done.4.refs_0_
  12.6 0.0 copy-done
  12.6 2.6 %shard_map.48 = (f32[2,32,256]{2,1,0:T(8,128)S(1)}, bf16[2,2,256,256]{3,2,1,0:T(8,128)(2,1)S(1)}, bf16[2,2,256,256]{3,2,1,0:T(8,128)(2,1)S(1)}) custom-call(f32[2,264,128]{2,1,0:T(8,128)S(1)} %collective-permute-done.4.refs_0_, f32[6,256,256]{2,1,0:T(8,128)S(1)} %get-tuple-element.32.own_ref.refs_1_.refs_4_, ...), custom_call_target="tpu_custom_call" | custom-call | flops 2000000000 | bytes 1048576 | tf_op jit(solution)/shard_map/pallas_call | solution.py:811
  15.2 0.0 collective-permute-done.refs_0_
  15.2 0.7 %collective-permute-done.1.refs_1_ = f32[328,128]{1,0:T(8,128)S(1)} collective-permute-done((f32[328,128]{1,0:T(8,128)S(1)}, f32[328,128]{1,0:T(8,128)S(1)}, u32[]{:S(2)}, u32[]{:S(2)}) %collective-permute-start.1) | collective-permute-done | bytes 167968 | tf_op jit(solution)/shard_map/ppermute | solution.py:89
  16.0 0.0 collective-permute-done.2.refs_2_
  16.0 0.0 collective-permute-done.3.refs_3_
  16.0 0.0 copy-done.2
  16.0 6.3 %shard_map.49 = (f32[360,128]{1,0:T(8,128)S(1)}, f32[6,32,256]{2,1,0:T(8,128)S(1)}, bf16[4,2,256,256]{3,2,1,0:T(8,128)(2,1)S(1)}, bf16[4,2,256,256]{3,2,1,0:T(8,128)(2,1)S(1)}) custom-call(f32[328,128]{1,0:T(8,128)S(1)} %collective-permute-done.refs_0_, f32[328,128]{1,0:T(8,128)S(1)} %collective-permute-done.1.refs_1_, ...), custom_call_target="tpu_custom_call" | custom-call | flops 8000000000 | bytes 1048576 | tf_op jit(solution)/shard_map/pallas_call | solution.py:820
  22.3 0.1 collective-permute-start.5
  22.4 1.6 %shard_map.50 = (f32[4,32,256]{2,1,0:T(8,128)S(1)}, f32[4,32,256]{2,1,0:T(8,128)S(1)}) custom-call(bf16[6,2,256,256]{3,2,1,0:T(8,128)(2,1)S(1)} %get-tuple-element.38.refs_2_.refs_5_.own_ref, f32[328,128]{1,0:T(8,128)S(1)} %collective-permute-done.refs_0_, f32[328,128]{1,0:T(8,128)S(1)} %collective-permute-done.1.refs_1_, ...), custom_call_target="tpu_custom_call" | custom-call | flops 2000000000 | bytes 1048576 | tf_op jit(solution)/shard_map/pallas_call | solution.py:832
  24.0 0.0 collective-permute-done.5.there_ref
  24.0 0.1 shard_map.51
  24.1 0.6 %collective-permute-start.7 = (f32[176,128]{1,0:T(8,128)S(1)}, f32[176,128]{1,0:T(8,128)S(1)}, u32[]{:S(2)}, u32[]{:S(2)}) collective-permute-start(f32[176,128]{1,0:T(8,128)S(1)} %get-tuple-element.51.third_ref), channel_id=1, source_target_pairs={{0,1},{1,0},{2,3},{3,2},{4,5},{5,4},{6,7},{7,6},{8,9},{9,8},{10,11... | collective-permute-start | bytes 270344 | tf_op jit(solution)/shard_map/ppermute | solution.py:891
  24.6 1.5 %collective-permute-start.6 = (f32[184,128]{1,0:T(8,128)S(1)}, f32[184,128]{1,0:T(8,128)S(1)}, u32[]{:S(2)}, u32[]{:S(2)}) collective-permute-start(f32[184,128]{1,0:T(8,128)S(1)} %get-tuple-element.48.unread.first_ref), channel_id=1, source_target_pairs={{0,4},{2,6},{4,0},{6,2},{1,5},{3,7},{5,1},{7,3},{8,12},{10,14},{12... | collective-permute-start | bytes 282632 | tf_op jit(solution)/shard_map/ppermute | solution.py:890
  26.1 1.9 %shard_map.52.unread.refs_0_.spread_ref = bf16[4,256,192]{2,1,0:T(8,128)(2,1)S(1)} custom-call(f32[184,128]{1,0:T(8,128)S(1)} %get-tuple-element.48.unread.first_ref, f32[4,32,256]{2,1,0:T(8,128)S(1)} %get-tuple-element.47.unread.basis_ref, f32[4,32,256]{2,1,0:T(8,128)S(1)} %get-tuple-element.49.theirs_ref, f32[6,32,256]{2,1,0:T(8,128)S(1)} %get-tuple-element.50.product_ref, ...), custom_call_target="tpu_custom_call" | custom-call | flops 2000000000 | bytes 1048576 | tf_op jit(solution)/shard_map/pallas_call | solution.py:842
  28.1 1.1 %collective-permute-done.7.fourth_ref = f32[176,128]{1,0:T(8,128)S(1)} collective-permute-done((f32[176,128]{1,0:T(8,128)S(1)}, f32[176,128]{1,0:T(8,128)S(1)}, u32[]{:S(2)}, u32[]{:S(2)}) %collective-permute-start.7) | collective-permute-done | bytes 90144 | tf_op jit(solution)/shard_map/ppermute | solution.py:891
  29.1 0.3 collective-permute-done.6.second_ref
  29.5 1.6 %collective-permute-start.8 = (f32[32,128]{1,0:T(8,128)S(1)}, f32[32,128]{1,0:T(8,128)S(1)}, u32[]{:S(2)}, u32[]{:S(2)}) collective-permute-start(f32[32,128]{1,0:T(8,128)S(1)} %get-tuple-element.52.refs_0_), channel_id=1, source_target_pairs={{0,1},{1,0},{2,3},{3,2},{4,5},{5,4},{6,7},{7,6},{8,9},{9,8},{10,11... | collective-permute-start | bytes 49160 | tf_op jit(solution)/shard_map/ppermute | solution.py:905
  31.1 0.5 %collective-permute-start.9 = (f32[152,128]{1,0:T(8,128)S(1)}, f32[152,128]{1,0:T(8,128)S(1)}, u32[]{:S(2)}, u32[]{:S(2)}) collective-permute-start(f32[152,128]{1,0:T(8,128)S(1)} %get-tuple-element.53.refs_0_), channel_id=1, source_target_pairs={{0,1},{1,0},{2,3},{3,2},{4,5},{5,4},{6,7},{7,6},{8,9},{9,8},{10,11... | collective-permute-start | bytes 233480 | tf_op jit(solution)/shard_map/ppermute | solution.py:906
  31.6 1.5 %collective-permute-start.10 = (f32[176,128]{1,0:T(8,128)S(1)}, f32[176,128]{1,0:T(8,128)S(1)}, u32[]{:S(2)}, u32[]{:S(2)}) collective-permute-start(f32[176,128]{1,0:T(8,128)S(1)} %get-tuple-element.54.refs_2_), channel_id=1, source_target_pairs={{0,4},{2,6},{4,0},{6,2},{1,5},{3,7},{5,1},{7,3},{8,12},{10,14},{12... | collective-permute-start | bytes 270344 | tf_op jit(solution)/shard_map/ppermute | solution.py:907
  33.1 0.4 collective-permute-done.8.refs_1_
  33.5 2.2 %shard_map.54.first_ref = f32[64,64]{1,0:T(8,128)S(1)} custom-call(f32[32,128]{1,0:T(8,128)S(1)} %get-tuple-element.52.refs_0_, f32[32,128]{1,0:T(8,128)S(1)} %collective-permute-done.8.refs_1_), custom_call_target="tpu_custom_call" | custom-call | flops 2000000000 | bytes 1048576 | tf_op jit(solution)/shard_map/pallas_call | solution.py:852
  35.7 0.0 collective-permute-done.9.refs_1_
  35.7 0.5 collective-permute-done.10.refs_3_
  36.1 5.2 %shard_map.55.here_ref.refs_1_ = f32[192,128]{1,0:T(8,128)S(1)} custom-call(f32[64,64]{1,0:T(8,128)S(1)} %shard_map.54.first_ref, f32[152,128]{1,0:T(8,128)S(1)} %get-tuple-element.53.refs_0_, f32[152,128]{1,0:T(8,128)S(1)} %collective-permute-done.9.refs_1_, f32[176,128]{1,0:T(8,128)S(1)} %get-tuple-element.54.refs_2_, ...), custom_call_target="tpu_custom_call" | custom-call | flops 7000000000 | bytes 1048576 | tf_op jit(solution)/shard_map/pallas_call | solution.py:860
  41.4 0.1 collective-permute-start.11
  41.4 1.6 %collective-permute-start.14 = (f32[2,32,256]{2,1,0:T(8,128)S(1)}, f32[2,32,256]{2,1,0:T(8,128)S(1)}, u32[]{:S(2)}, u32[]{:S(2)}) collective-permute-start(f32[2,32,256]{2,1,0:T(8,128)S(1)} %get-tuple-element.58), channel_id=1, source_target_pairs={{0,1},{1,0},{2,3},{3,2},{4,5},{5,4},{6,7},{7,6},{8,9},{9,8},{10,11... | collective-permute-start | bytes 196616 | tf_op jit(solution)/shard_map/ppermute | solution.py:86
  43.0 0.0 collective-permute-done.11.there_ref.refs_2_
  43.1 2.4 %collective-permute-start.12 = (f32[32,128]{1,0:T(8,128)S(1)}, f32[32,128]{1,0:T(8,128)S(1)}, u32[]{:S(2)}, u32[]{:S(2)}) collective-permute-start(f32[32,128]{1,0:T(8,128)S(1)} %get-tuple-element.56), channel_id=1, source_target_pairs={{0,24},{8,16},{16,8},{24,0},{1,25},{9,17},{17,9},{25,1},{2,26},{10... | collective-permute-start | bytes 49160 | tf_op jit(solution)/shard_map/ppermute | solution.py:88
  45.5 0.0 collective-permute-start.13
  45.5 0.5 collective-permute-done.14.refs_3_
  46.0 1.7 %shard_map.57.refs_2_ = f32[1536,128]{1,0:T(8,128)} custom-call(f32[8,128]{1,0:T(8,128)S(1)} %get-tuple-element.33.flag_ref, f32[6,32,256]{2,1,0:T(8,128)S(1)} %get-tuple-element.50.product_ref, bf16[2,2,256,256]{3,2,1,0:T(8,128)(2,1)S(1)} %get-tuple-element.45.refs_6_.refs_0_.early_inverse, ...), custom_call_target="tpu_custom_call" | custom-call | flops 1000000000 | bytes 1048576 | tf_op jit(solution)/shard_map/pallas_call | solution.py:921
  47.6 1.0 %collective-permute-done.12.refs_0_ = f32[32,128]{1,0:T(8,128)S(1)} collective-permute-done((f32[32,128]{1,0:T(8,128)S(1)}, f32[32,128]{1,0:T(8,128)S(1)}, u32[]{:S(2)}, u32[]{:S(2)}) %collective-permute-start.12) | collective-permute-done | bytes 16416 | tf_op jit(solution)/shard_map/ppermute | solution.py:88
  48.7 0.6 %collective-permute-done.13.refs_1_ = f32[32,128]{1,0:T(8,128)S(1)} collective-permute-done((f32[32,128]{1,0:T(8,128)S(1)}, f32[32,128]{1,0:T(8,128)S(1)}, u32[]{:S(2)}, u32[]{:S(2)}) %collective-permute-start.13) | collective-permute-done | bytes 16416 | tf_op jit(solution)/shard_map/ppermute | solution.py:89
  49.2 1.0 %shard_map.58 = f32[1536,128]{1,0:T(8,128)} custom-call(bf16[4,256,192]{2,1,0:T(8,128)(2,1)S(1)} %shard_map.52.unread.refs_0_.spread_ref, f32[64,128]{1,0:T(8,128)S(1)} %get-tuple-element.55.rows_ref, f32[32,128]{1,0:T(8,128)S(1)} %collective-permute-done.12.refs_0_, f32[32,128]{1,0:T(8,128)S(1)} %collective-permute-done.13.refs_1_, ...), custom_call_target="tpu_custom_call", output_to_operand_aliasing={{}: (4, {})} | custom-call | flops 1000000000 | bytes 1048576 | tf_op jit(solution)/shard_map/pallas_call | solution.py:957
  (2 shorter events, 0.1 us)
Async XLA Ops:
  0.0 9.9 %copy-start.1 = (s32[8]{0:T(128)S(1)}, s32[8]{0:T(128)}, u32[]{:S(2)}) copy-start(s32[8]{0:T(128)} %group_ref.1) | copy-start | bytes 100
  1.6 11.0 %collective-permute-start.4 = (f32[2,264,128]{2,1,0:T(8,128)S(1)}, f32[2,264,128]{2,1,0:T(8,128)S(1)}, u32[]{:S(2)}, u32[]{:S(2)}) collective-permute-start(f32[2,264,128]{2,1,0:T(8,128)S(1)} %get-tuple-element.40), channel_id=1, source_target_pairs={{0,1},{1,0},{2,3},{3,2},{4,5},{5,4},{6,7},{7,6},{8,9},{9,8},{10,11... | collective-permute-start | bytes 811016 | tf_op jit(solution)/shard_map/ppermute | solution.py:86
  4.7 10.6 %collective-permute-start = (f32[328,128]{1,0:T(8,128)S(1)}, f32[328,128]{1,0:T(8,128)S(1)}, u32[]{:S(2)}, u32[]{:S(2)}) collective-permute-start(f32[328,128]{1,0:T(8,128)S(1)} %get-tuple-element.34), channel_id=1, source_target_pairs={{0,24},{8,16},{16,8},{24,0},{1,25},{9,17},{17,9},{25,1},{2,26},{10... | collective-permute-start | bytes 503816 | tf_op jit(solution)/shard_map/ppermute | solution.py:88
  8.3 7.7 %collective-permute-start.1 = (f32[328,128]{1,0:T(8,128)S(1)}, f32[328,128]{1,0:T(8,128)S(1)}, u32[]{:S(2)}, u32[]{:S(2)}) collective-permute-start(f32[328,128]{1,0:T(8,128)S(1)} %get-tuple-element.35), channel_id=1, source_target_pairs={{0,8},{8,0},{16,24},{24,16},{1,9},{9,1},{17,25},{25,17},{2,10},{10... | collective-permute-start | bytes 503816 | tf_op jit(solution)/shard_map/ppermute | solution.py:89
  8.3 7.7 %collective-permute-start.2 = (f32[328,128]{1,0:T(8,128)S(1)}, f32[328,128]{1,0:T(8,128)S(1)}, u32[]{:S(2)}, u32[]{:S(2)}) collective-permute-start(f32[328,128]{1,0:T(8,128)S(1)} %get-tuple-element.36), channel_id=1, source_target_pairs={{0,6},{2,4},{4,2},{6,0},{1,7},{3,5},{5,3},{7,1},{8,14},{10,12},{12... | collective-permute-start | bytes 503816 | tf_op jit(solution)/shard_map/ppermute | solution.py:88
  8.6 7.3 %collective-permute-start.3 = (f32[328,128]{1,0:T(8,128)S(1)}, f32[328,128]{1,0:T(8,128)S(1)}, u32[]{:S(2)}, u32[]{:S(2)}) collective-permute-start(f32[328,128]{1,0:T(8,128)S(1)} %get-tuple-element.37), channel_id=1, source_target_pairs={{0,2},{2,0},{4,6},{6,4},{1,3},{3,1},{5,7},{7,5},{8,10},{10,8},{12,... | collective-permute-start | bytes 503816 | tf_op jit(solution)/shard_map/ppermute | solution.py:89
  9.9 2.7 %copy-start = (f32[1,1,1,6,256,32]{4,5,3,2,1,0:T(8,128)S(1)}, f32[1,1,1,6,256,32]{4,5,3,2,1,0:T(8,128)}, u32[]{:S(2)}) copy-start(f32[1,1,1,6,256,32]{4,5,3,2,1,0:T(8,128)} %param.5) | copy-start | bytes 589828
  12.6 3.4 %copy-start.2 = (f32[1,1,1,1536,128]{4,3,2,1,0:T(8,128)S(1)}, f32[1,1,1,1536,128]{4,3,2,1,0:T(8,128)}, u32[]{:S(2)}) copy-start(f32[1,1,1,1536,128]{4,3,2,1,0:T(8,128)} %param.6) | copy-start | bytes 2359300
  22.3 1.7 %collective-permute-start.5 = (f32[360,128]{1,0:T(8,128)S(1)}, f32[360,128]{1,0:T(8,128)S(1)}, u32[]{:S(2)}, u32[]{:S(2)}) collective-permute-start(f32[360,128]{1,0:T(8,128)S(1)} %get-tuple-element.42.here_ref), channel_id=1, source_target_pairs={{0,2},{2,0},{4,6},{6,4},{1,3},{3,1},{5,7},{7,5},{8,10},{10,8},{12,... | collective-permute-start | bytes 552968 | tf_op jit(solution)/shard_map/ppermute | solution.py:882
  24.1 5.1 %collective-permute-start.7 = (f32[176,128]{1,0:T(8,128)S(1)}, f32[176,128]{1,0:T(8,128)S(1)}, u32[]{:S(2)}, u32[]{:S(2)}) collective-permute-start(f32[176,128]{1,0:T(8,128)S(1)} %get-tuple-element.51.third_ref), channel_id=1, source_target_pairs={{0,1},{1,0},{2,3},{3,2},{4,5},{5,4},{6,7},{7,6},{8,9},{9,8},{10,11... | collective-permute-start | bytes 270344 | tf_op jit(solution)/shard_map/ppermute | solution.py:891
  24.6 4.8 %collective-permute-start.6 = (f32[184,128]{1,0:T(8,128)S(1)}, f32[184,128]{1,0:T(8,128)S(1)}, u32[]{:S(2)}, u32[]{:S(2)}) collective-permute-start(f32[184,128]{1,0:T(8,128)S(1)} %get-tuple-element.48.unread.first_ref), channel_id=1, source_target_pairs={{0,4},{2,6},{4,0},{6,2},{1,5},{3,7},{5,1},{7,3},{8,12},{10,14},{12... | collective-permute-start | bytes 282632 | tf_op jit(solution)/shard_map/ppermute | solution.py:890
  29.5 4.0 %collective-permute-start.8 = (f32[32,128]{1,0:T(8,128)S(1)}, f32[32,128]{1,0:T(8,128)S(1)}, u32[]{:S(2)}, u32[]{:S(2)}) collective-permute-start(f32[32,128]{1,0:T(8,128)S(1)} %get-tuple-element.52.refs_0_), channel_id=1, source_target_pairs={{0,1},{1,0},{2,3},{3,2},{4,5},{5,4},{6,7},{7,6},{8,9},{9,8},{10,11... | collective-permute-start | bytes 49160 | tf_op jit(solution)/shard_map/ppermute | solution.py:905
  31.1 4.6 %collective-permute-start.9 = (f32[152,128]{1,0:T(8,128)S(1)}, f32[152,128]{1,0:T(8,128)S(1)}, u32[]{:S(2)}, u32[]{:S(2)}) collective-permute-start(f32[152,128]{1,0:T(8,128)S(1)} %get-tuple-element.53.refs_0_), channel_id=1, source_target_pairs={{0,1},{1,0},{2,3},{3,2},{4,5},{5,4},{6,7},{7,6},{8,9},{9,8},{10,11... | collective-permute-start | bytes 233480 | tf_op jit(solution)/shard_map/ppermute | solution.py:906
  31.6 4.5 %collective-permute-start.10 = (f32[176,128]{1,0:T(8,128)S(1)}, f32[176,128]{1,0:T(8,128)S(1)}, u32[]{:S(2)}, u32[]{:S(2)}) collective-permute-start(f32[176,128]{1,0:T(8,128)S(1)} %get-tuple-element.54.refs_2_), channel_id=1, source_target_pairs={{0,4},{2,6},{4,0},{6,2},{1,5},{3,7},{5,1},{7,3},{8,12},{10,14},{12... | collective-permute-start | bytes 270344 | tf_op jit(solution)/shard_map/ppermute | solution.py:907
  41.4 1.7 %collective-permute-start.11 = (f32[192,128]{1,0:T(8,128)S(1)}, f32[192,128]{1,0:T(8,128)S(1)}, u32[]{:S(2)}, u32[]{:S(2)}) collective-permute-start(f32[192,128]{1,0:T(8,128)S(1)} %shard_map.55.here_ref.refs_1_), channel_id=1, source_target_pairs={{0,2},{2,0},{4,6},{6,4},{1,3},{3,1},{5,7},{7,5},{8,10},{10,8},{12,... | collective-permute-start | bytes 294920 | tf_op jit(solution)/shard_map/ppermute | solution.py:912
  41.4 4.5 %collective-permute-start.14 = (f32[2,32,256]{2,1,0:T(8,128)S(1)}, f32[2,32,256]{2,1,0:T(8,128)S(1)}, u32[]{:S(2)}, u32[]{:S(2)}) collective-permute-start(f32[2,32,256]{2,1,0:T(8,128)S(1)} %get-tuple-element.58), channel_id=1, source_target_pairs={{0,1},{1,0},{2,3},{3,2},{4,5},{5,4},{6,7},{7,6},{8,9},{9,8},{10,11... | collective-permute-start | bytes 196616 | tf_op jit(solution)/shard_map/ppermute | solution.py:86
  43.1 5.6 %collective-permute-start.12 = (f32[32,128]{1,0:T(8,128)S(1)}, f32[32,128]{1,0:T(8,128)S(1)}, u32[]{:S(2)}, u32[]{:S(2)}) collective-permute-start(f32[32,128]{1,0:T(8,128)S(1)} %get-tuple-element.56), channel_id=1, source_target_pairs={{0,24},{8,16},{16,8},{24,0},{1,25},{9,17},{17,9},{25,1},{2,26},{10... | collective-permute-start | bytes 49160 | tf_op jit(solution)/shard_map/ppermute | solution.py:88
  45.5 3.7 %collective-permute-start.13 = (f32[32,128]{1,0:T(8,128)S(1)}, f32[32,128]{1,0:T(8,128)S(1)}, u32[]{:S(2)}, u32[]{:S(2)}) collective-permute-start(f32[32,128]{1,0:T(8,128)S(1)} %get-tuple-element.57), channel_id=1, source_target_pairs={{0,8},{8,0},{16,24},{24,16},{1,9},{9,1},{17,25},{25,17},{2,10},{10... | collective-permute-start | bytes 49160 | tf_op jit(solution)/shard_map/ppermute | solution.py:89

commit v18 on v16

--- a/solution.py
+++ b/solution.py
@@ -126,14 +126,14 @@
     outs, blocks = refs[:-4], refs[-4]
     starts, sems, start_sem = refs[-3:]
     half = width // 2
+    start_copy = pltpu.make_async_copy(starts_ref.at[pl.ds(0, 4)], starts, start_sem)
+    start_copy.start()
     copies = []
     for f in range(FACES):
         place = pl.ds(f * width, width)
         copy = pltpu.make_async_copy(schur_ref.at[place, place], blocks.at[f], sems.at[f])
         copy.start()
         copies.append(copy)
-    start_copy = pltpu.make_async_copy(starts_ref.at[pl.ds(0, 4)], starts, start_sem)
-    start_copy.start()
     row, col = iota((half, half), 0), iota((half, half), 1)
     start_copy.wait()
 

time: 50.4 us -> 50.3 us (level)
  no operation moved by 1% of the time
where the time goes in v18:
time: 50.3 us; the launch traced here: 50.2 us
  Pallas kernels  27.4 us (54%)
  starting transfers between devices  17.6 us (35%)
  waiting for transfers between devices  4.9 us (10%)
    ppermute x3, starting transfers between devices, exchange(): lax.ppermute(arrays[0], axis, outer_pairs(axis))  6.39 us
    pallas_call x1, Pallas kernels, per_device(): pl.pallas_call(functools.partial(main_kernel, (AXES[0], AXES[1]), early,...  6.33 us
    pallas_call x1, Pallas kernels, solve(): pl.pallas_call(functools.partial(solve_kernel, size, len(matrices), colum...  5.23 us
    ppermute x2, starting transfers between devices, exchange(): return [lax.ppermute(arrays[0], axis, flipped(axis, 1))]  4.44 us
    pallas_call x1, Pallas kernels, per_device(): pl.pallas_call(functools.partial(theirs_kernel, faces, ncon), out_shape=s...  3.3 us
    pallas_call x1, Pallas kernels, per_device(): pl.pallas_call(functools.partial(halves_kernel, planes), out_shape=[halve...  2.7 us
    pallas_call x1, Pallas kernels, per_device(): pl.pallas_call(functools.partial(early_kernel, AXES[2:3], early), out_sha...  2.6 us
    pallas_call x1, Pallas kernels, solve(): pl.pallas_call(first_kernel, out_shape=shape(size, size), in_specs=vmem_s...  2.18 us
  transfers between devices with their start and end apart: 15, of which 6 were waited for; matrix products, arithmetic and copies ran while one was open for 0% of the time, Pallas kernels for 26%

profile of v18, /device:TPU:0, one launch (start us, length us, event | category | flops | bytes accessed | tf_op | source)
XLA Modules:
  0.0 50.2 jit_solution(4202689896715787641)
XLA Ops:
  0.0 0.0 copy-start.1
  0.0 1.6 %shard_map.46 = (f32[328,128]{1,0:T(8,128)S(1)}, f32[328,128]{1,0:T(8,128)S(1)}, f32[328,128]{1,0:T(8,128)S(1)}, f32[328,128]{1,0:T(8,128)S(1)}, f32[2,264,128]{2,1,0:T(8,128)S(1)}, /*index=5*/f32[6,256,256]{2,1,0:T(8,128)S(1)}) custom-call(f32[1536,1536]{1,0:T(8,128)} %bitcast.10, f32[6,32,256]{2,1,0:T(8,128)} %bitcast.6), custom_call_target="tpu_custom_call" | custom-call | tf_op jit(solution)/shard_map/pallas_call | solution.py:775
  1.6 3.0 %collective-permute-start.4 = (f32[2,264,128]{2,1,0:T(8,128)S(1)}, f32[2,264,128]{2,1,0:T(8,128)S(1)}, u32[]{:S(2)}, u32[]{:S(2)}) collective-permute-start(f32[2,264,128]{2,1,0:T(8,128)S(1)} %get-tuple-element.38), channel_id=1, source_target_pairs={{0,1},{1,0},{2,3},{3,2},{4,5},{5,4},{6,7},{7,6},{8,9},{9,8},{10,11... | collective-permute-start | bytes 811016 | tf_op jit(solution)/shard_map/ppermute | solution.py:86
  4.7 3.6 %collective-permute-start = (f32[328,128]{1,0:T(8,128)S(1)}, f32[328,128]{1,0:T(8,128)S(1)}, u32[]{:S(2)}, u32[]{:S(2)}) collective-permute-start(f32[328,128]{1,0:T(8,128)S(1)} %get-tuple-element.32), channel_id=1, source_target_pairs={{0,24},{8,16},{16,8},{24,0},{1,25},{9,17},{17,9},{25,1},{2,26},{10... | collective-permute-start | bytes 503816 | tf_op jit(solution)/shard_map/ppermute | solution.py:88
  8.3 0.0 collective-permute-start.1
  8.3 0.4 collective-permute-start.2
  8.6 1.2 %collective-permute-start.3 = (f32[328,128]{1,0:T(8,128)S(1)}, f32[328,128]{1,0:T(8,128)S(1)}, u32[]{:S(2)}, u32[]{:S(2)}) collective-permute-start(f32[328,128]{1,0:T(8,128)S(1)} %get-tuple-element.35), channel_id=1, source_target_pairs={{0,2},{2,0},{4,6},{6,4},{1,3},{3,1},{5,7},{7,5},{8,10},{10,8},{12,... | collective-permute-start | bytes 503816 | tf_op jit(solution)/shard_map/ppermute | solution.py:89
  9.9 0.0 copy-done.1
  9.9 0.0 copy-start
  9.9 2.7 %shard_map.47 = (bf16[6,2,256,256]{3,2,1,0:T(8,128)(2,1)S(1)}, bf16[15,2,256,256]{3,2,1,0:T(8,128)(2,1)S(1)}, f32[8,128]{1,0:T(8,128)S(1)}) custom-call(f32[1536,1536]{1,0:T(8,128)} %bitcast.11, s32[8]{0:T(128)S(1)} %copy-done.1, f32[6,256,256]{2,1,0:T(8,128)S(1)} %get-tuple-element.30.own_ref.refs_1_.refs_4_), custom_call_target="tpu_custom_call" | custom-call | flops 2000000000 | bytes 1048576 | tf_op jit(solution)/shard_map/pallas_call | solution.py:795
  12.6 0.0 copy-start.2
  12.6 0.0 collective-permute-done.4.refs_0_
  12.6 0.0 copy-done
  12.6 2.6 %shard_map.48 = (f32[2,32,256]{2,1,0:T(8,128)S(1)}, bf16[2,2,256,256]{3,2,1,0:T(8,128)(2,1)S(1)}, bf16[2,2,256,256]{3,2,1,0:T(8,128)(2,1)S(1)}) custom-call(f32[2,264,128]{2,1,0:T(8,128)S(1)} %collective-permute-done.4.refs_0_, f32[6,256,256]{2,1,0:T(8,128)S(1)} %get-tuple-element.30.own_ref.refs_1_.refs_4_, ...), custom_call_target="tpu_custom_call" | custom-call | flops 2000000000 | bytes 1048576 | tf_op jit(solution)/shard_map/pallas_call | solution.py:808
  15.2 0.0 collective-permute-done.refs_0_
  15.2 0.7 %collective-permute-done.1.refs_1_ = f32[328,128]{1,0:T(8,128)S(1)} collective-permute-done((f32[328,128]{1,0:T(8,128)S(1)}, f32[328,128]{1,0:T(8,128)S(1)}, u32[]{:S(2)}, u32[]{:S(2)}) %collective-permute-start.1) | collective-permute-done | bytes 167968 | tf_op jit(solution)/shard_map/ppermute | solution.py:89
  16.0 0.0 collective-permute-done.2.refs_2_
  16.0 0.0 collective-permute-done.3.refs_3_
  16.0 0.0 copy-done.2
  16.0 6.3 %shard_map.49 = (f32[360,128]{1,0:T(8,128)S(1)}, f32[6,32,256]{2,1,0:T(8,128)S(1)}, bf16[4,2,256,256]{3,2,1,0:T(8,128)(2,1)S(1)}, bf16[4,2,256,256]{3,2,1,0:T(8,128)(2,1)S(1)}) custom-call(f32[328,128]{1,0:T(8,128)S(1)} %collective-permute-done.refs_0_, f32[328,128]{1,0:T(8,128)S(1)} %collective-permute-done.1.refs_1_, ...), custom_call_target="tpu_custom_call" | custom-call | flops 8000000000 | bytes 1048576 | tf_op jit(solution)/shard_map/pallas_call | solution.py:817
  22.3 0.1 collective-permute-start.5
  22.4 1.4 %collective-permute-done.5.there_ref = f32[360,128]{1,0:T(8,128)S(1)} collective-permute-done((f32[360,128]{1,0:T(8,128)S(1)}, f32[360,128]{1,0:T(8,128)S(1)}, u32[]{:S(2)}, u32[]{:S(2)}) %collective-permute-start.5) | collective-permute-done | bytes 184352 | tf_op jit(solution)/shard_map/ppermute | solution.py:879
  23.8 0.1 shard_map.50
  23.9 0.6 %collective-permute-start.7 = (f32[176,128]{1,0:T(8,128)S(1)}, f32[176,128]{1,0:T(8,128)S(1)}, u32[]{:S(2)}, u32[]{:S(2)}) collective-permute-start(f32[176,128]{1,0:T(8,128)S(1)} %get-tuple-element.42.third_ref), channel_id=1, source_target_pairs={{0,1},{1,0},{2,3},{3,2},{4,5},{5,4},{6,7},{7,6},{8,9},{9,8},{10,11... | collective-permute-start | bytes 270344 | tf_op jit(solution)/shard_map/ppermute | solution.py:888
  24.4 1.5 %collective-permute-start.6 = (f32[184,128]{1,0:T(8,128)S(1)}, f32[184,128]{1,0:T(8,128)S(1)}, u32[]{:S(2)}, u32[]{:S(2)}) collective-permute-start(f32[184,128]{1,0:T(8,128)S(1)} %get-tuple-element.41.first_ref), channel_id=1, source_target_pairs={{0,4},{2,6},{4,0},{6,2},{1,5},{3,7},{5,1},{7,3},{8,12},{10,14},{12... | collective-permute-start | bytes 282632 | tf_op jit(solution)/shard_map/ppermute | solution.py:887
  25.9 3.3 %shard_map.51.unread.theirs_ref = f32[4,32,256]{2,1,0:T(8,128)S(1)} custom-call(bf16[6,2,256,256]{3,2,1,0:T(8,128)(2,1)S(1)} %get-tuple-element.36.refs_2_.refs_5_.own_ref, f32[328,128]{1,0:T(8,128)S(1)} %collective-permute-done.refs_0_, f32[328,128]{1,0:T(8,128)S(1)} %collective-permute-done.1.refs_1_, f32[328,128]{1,0:T(8,128)S(1)} %collective-permute-done.2.refs_2_, ...), custom_call_target="tpu_custom_call" | custom-call | flops 2000000000 | bytes 1048576 | tf_op jit(solution)/shard_map/pallas_call | solution.py:829
  29.2 0.0 collective-permute-done.7.fourth_ref
  29.2 0.0 collective-permute-done.6.second_ref
  29.3 1.6 %collective-permute-start.8 = (f32[32,128]{1,0:T(8,128)S(1)}, f32[32,128]{1,0:T(8,128)S(1)}, u32[]{:S(2)}, u32[]{:S(2)}) collective-permute-start(f32[32,128]{1,0:T(8,128)S(1)} %get-tuple-element.48.refs_0_), channel_id=1, source_target_pairs={{0,1},{1,0},{2,3},{3,2},{4,5},{5,4},{6,7},{7,6},{8,9},{9,8},{10,11... | collective-permute-start | bytes 49160 | tf_op jit(solution)/shard_map/ppermute | solution.py:901
  30.9 0.5 %collective-permute-start.9 = (f32[152,128]{1,0:T(8,128)S(1)}, f32[152,128]{1,0:T(8,128)S(1)}, u32[]{:S(2)}, u32[]{:S(2)}) collective-permute-start(f32[152,128]{1,0:T(8,128)S(1)} %get-tuple-element.49.refs_0_), channel_id=1, source_target_pairs={{0,1},{1,0},{2,3},{3,2},{4,5},{5,4},{6,7},{7,6},{8,9},{9,8},{10,11... | collective-permute-start | bytes 233480 | tf_op jit(solution)/shard_map/ppermute | solution.py:902
  31.4 1.2 %collective-permute-start.10 = (f32[176,128]{1,0:T(8,128)S(1)}, f32[176,128]{1,0:T(8,128)S(1)}, u32[]{:S(2)}, u32[]{:S(2)}) collective-permute-start(f32[176,128]{1,0:T(8,128)S(1)} %get-tuple-element.50.refs_2_), channel_id=1, source_target_pairs={{0,4},{2,6},{4,0},{6,2},{1,5},{3,7},{5,1},{7,3},{8,12},{10,14},{12... | collective-permute-start | bytes 270344 | tf_op jit(solution)/shard_map/ppermute | solution.py:903
  32.6 0.6 %collective-permute-done.8.unread.refs_1_ = f32[32,128]{1,0:T(8,128)S(1)} collective-permute-done((f32[32,128]{1,0:T(8,128)S(1)}, f32[32,128]{1,0:T(8,128)S(1)}, u32[]{:S(2)}, u32[]{:S(2)}) %collective-permute-start.8) | collective-permute-done | bytes 16416 | tf_op jit(solution)/shard_map/ppermute | solution.py:901
  33.3 2.2 %shard_map.54.first_ref = f32[64,64]{1,0:T(8,128)S(1)} custom-call(f32[32,128]{1,0:T(8,128)S(1)} %get-tuple-element.48.refs_0_, f32[32,128]{1,0:T(8,128)S(1)} %collective-permute-done.8.unread.refs_1_), custom_call_target="tpu_custom_call" | custom-call | flops 2000000000 | bytes 1048576 | tf_op jit(solution)/shard_map/pallas_call | solution.py:849
  35.5 0.6 %shard_map.53.refs_4_.refs_0_.spread_ref = bf16[4,256,192]{2,1,0:T(8,128)(2,1)S(1)} custom-call(f32[32,128]{1,0:T(8,128)S(1)} %collective-permute-done.8.unread.refs_1_, f32[4,32,256]{2,1,0:T(8,128)S(1)} %shard_map.51.unread.theirs_ref, f32[6,32,256]{2,1,0:T(8,128)S(1)} %get-tuple-element.43.product_ref, ...), custom_call_target="tpu_custom_call" | custom-call | flops 2000000000 | bytes 1048576 | tf_op jit(solution)/shard_map/pallas_call | solution.py:839
  36.1 0.0 collective-permute-done.9.refs_1_
  36.1 0.0 collective-permute-done.10.refs_3_
  36.1 5.2 %shard_map.55.here_ref.refs_1_ = f32[192,128]{1,0:T(8,128)S(1)} custom-call(f32[64,64]{1,0:T(8,128)S(1)} %shard_map.54.first_ref, f32[152,128]{1,0:T(8,128)S(1)} %get-tuple-element.49.refs_0_, f32[152,128]{1,0:T(8,128)S(1)} %collective-permute-done.9.refs_1_, f32[176,128]{1,0:T(8,128)S(1)} %get-tuple-element.50.refs_2_, ...), custom_call_target="tpu_custom_call" | custom-call | flops 7000000000 | bytes 1048576 | tf_op jit(solution)/shard_map/pallas_call | solution.py:857
  41.3 0.1 collective-permute-start.11
  41.4 1.4 %collective-permute-start.14 = (f32[2,32,256]{2,1,0:T(8,128)S(1)}, f32[2,32,256]{2,1,0:T(8,128)S(1)}, u32[]{:S(2)}, u32[]{:S(2)}) collective-permute-start(f32[2,32,256]{2,1,0:T(8,128)S(1)} %get-tuple-element.54), channel_id=1, source_target_pairs={{0,1},{1,0},{2,3},{3,2},{4,5},{5,4},{6,7},{7,6},{8,9},{9,8},{10,11... | collective-permute-start | bytes 196616 | tf_op jit(solution)/shard_map/ppermute | solution.py:86
  42.8 0.0 collective-permute-done.11.there_ref.refs_2_
  42.9 2.4 %collective-permute-start.12 = (f32[32,128]{1,0:T(8,128)S(1)}, f32[32,128]{1,0:T(8,128)S(1)}, u32[]{:S(2)}, u32[]{:S(2)}) collective-permute-start(f32[32,128]{1,0:T(8,128)S(1)} %get-tuple-element.52), channel_id=1, source_target_pairs={{0,24},{8,16},{16,8},{24,0},{1,25},{9,17},{17,9},{25,1},{2,26},{10... | collective-permute-start | bytes 49160 | tf_op jit(solution)/shard_map/ppermute | solution.py:88
  45.3 0.0 collective-permute-start.13
  45.3 0.6 %collective-permute-done.14.refs_3_ = f32[2,32,256]{2,1,0:T(8,128)S(1)} collective-permute-done((f32[2,32,256]{2,1,0:T(8,128)S(1)}, f32[2,32,256]{2,1,0:T(8,128)S(1)}, u32[]{:S(2)}, u32[]{:S(2)}) %collective-permute-start.14) | collective-permute-done | bytes 65568 | tf_op jit(solution)/shard_map/ppermute | solution.py:86
  45.9 1.7 %shard_map.57.refs_2_ = f32[1536,128]{1,0:T(8,128)} custom-call(f32[8,128]{1,0:T(8,128)S(1)} %get-tuple-element.31.flag_ref, f32[6,32,256]{2,1,0:T(8,128)S(1)} %get-tuple-element.43.product_ref, bf16[2,2,256,256]{3,2,1,0:T(8,128)(2,1)S(1)} %get-tuple-element.46.refs_6_.refs_0_.early_inverse, ...), custom_call_target="tpu_custom_call" | custom-call | flops 1000000000 | bytes 1048576 | tf_op jit(solution)/shard_map/pallas_call | solution.py:918
  47.6 0.9 %collective-permute-done.12.refs_0_ = f32[32,128]{1,0:T(8,128)S(1)} collective-permute-done((f32[32,128]{1,0:T(8,128)S(1)}, f32[32,128]{1,0:T(8,128)S(1)}, u32[]{:S(2)}, u32[]{:S(2)}) %collective-permute-start.12) | collective-permute-done | bytes 16416 | tf_op jit(solution)/shard_map/ppermute | solution.py:88
  48.5 0.6 %collective-permute-done.13.refs_1_ = f32[32,128]{1,0:T(8,128)S(1)} collective-permute-done((f32[32,128]{1,0:T(8,128)S(1)}, f32[32,128]{1,0:T(8,128)S(1)}, u32[]{:S(2)}, u32[]{:S(2)}) %collective-permute-start.13) | collective-permute-done | bytes 16416 | tf_op jit(solution)/shard_map/ppermute | solution.py:89
  49.0 1.0 %shard_map.58 = f32[1536,128]{1,0:T(8,128)} custom-call(bf16[4,256,192]{2,1,0:T(8,128)(2,1)S(1)} %shard_map.53.refs_4_.refs_0_.spread_ref, f32[64,128]{1,0:T(8,128)S(1)} %get-tuple-element.51.rows_ref, f32[32,128]{1,0:T(8,128)S(1)} %collective-permute-done.12.refs_0_, f32[32,128]{1,0:T(8,128)S(1)} %collective-permute-done.13.refs_1_, ...), custom_call_target="tpu_custom_call", output_to_operand_aliasing={{}: (4, {})} | custom-call | flops 1000000000 | bytes 1048576 | tf_op jit(solution)/shard_map/pallas_call | solution.py:954
  (2 shorter events, 0.1 us)
Async XLA Ops:
  0.0 9.9 %copy-start.1 = (s32[8]{0:T(128)S(1)}, s32[8]{0:T(128)}, u32[]{:S(2)}) copy-start(s32[8]{0:T(128)} %group_ref.1) | copy-start | bytes 100
  1.6 11.0 %collective-permute-start.4 = (f32[2,264,128]{2,1,0:T(8,128)S(1)}, f32[2,264,128]{2,1,0:T(8,128)S(1)}, u32[]{:S(2)}, u32[]{:S(2)}) collective-permute-start(f32[2,264,128]{2,1,0:T(8,128)S(1)} %get-tuple-element.38), channel_id=1, source_target_pairs={{0,1},{1,0},{2,3},{3,2},{4,5},{5,4},{6,7},{7,6},{8,9},{9,8},{10,11... | collective-permute-start | bytes 811016 | tf_op jit(solution)/shard_map/ppermute | solution.py:86
  4.7 10.6 %collective-permute-start = (f32[328,128]{1,0:T(8,128)S(1)}, f32[328,128]{1,0:T(8,128)S(1)}, u32[]{:S(2)}, u32[]{:S(2)}) collective-permute-start(f32[328,128]{1,0:T(8,128)S(1)} %get-tuple-element.32), channel_id=1, source_target_pairs={{0,24},{8,16},{16,8},{24,0},{1,25},{9,17},{17,9},{25,1},{2,26},{10... | collective-permute-start | bytes 503816 | tf_op jit(solution)/shard_map/ppermute | solution.py:88
  8.3 7.7 %collective-permute-start.1 = (f32[328,128]{1,0:T(8,128)S(1)}, f32[328,128]{1,0:T(8,128)S(1)}, u32[]{:S(2)}, u32[]{:S(2)}) collective-permute-start(f32[328,128]{1,0:T(8,128)S(1)} %get-tuple-element.33), channel_id=1, source_target_pairs={{0,8},{8,0},{16,24},{24,16},{1,9},{9,1},{17,25},{25,17},{2,10},{10... | collective-permute-start | bytes 503816 | tf_op jit(solution)/shard_map/ppermute | solution.py:89
  8.3 7.7 %collective-permute-start.2 = (f32[328,128]{1,0:T(8,128)S(1)}, f32[328,128]{1,0:T(8,128)S(1)}, u32[]{:S(2)}, u32[]{:S(2)}) collective-permute-start(f32[328,128]{1,0:T(8,128)S(1)} %get-tuple-element.34), channel_id=1, source_target_pairs={{0,6},{2,4},{4,2},{6,0},{1,7},{3,5},{5,3},{7,1},{8,14},{10,12},{12... | collective-permute-start | bytes 503816 | tf_op jit(solution)/shard_map/ppermute | solution.py:88
  8.6 7.3 %collective-permute-start.3 = (f32[328,128]{1,0:T(8,128)S(1)}, f32[328,128]{1,0:T(8,128)S(1)}, u32[]{:S(2)}, u32[]{:S(2)}) collective-permute-start(f32[328,128]{1,0:T(8,128)S(1)} %get-tuple-element.35), channel_id=1, source_target_pairs={{0,2},{2,0},{4,6},{6,4},{1,3},{3,1},{5,7},{7,5},{8,10},{10,8},{12,... | collective-permute-start | bytes 503816 | tf_op jit(solution)/shard_map/ppermute | solution.py:89
  9.9 2.7 %copy-start = (f32[1,1,1,6,256,32]{4,5,3,2,1,0:T(8,128)S(1)}, f32[1,1,1,6,256,32]{4,5,3,2,1,0:T(8,128)}, u32[]{:S(2)}) copy-start(f32[1,1,1,6,256,32]{4,5,3,2,1,0:T(8,128)} %param.5) | copy-start | bytes 589828
  12.6 3.4 %copy-start.2 = (f32[1,1,1,1536,128]{4,3,2,1,0:T(8,128)S(1)}, f32[1,1,1,1536,128]{4,3,2,1,0:T(8,128)}, u32[]{:S(2)}) copy-start(f32[1,1,1,1536,128]{4,3,2,1,0:T(8,128)} %param.6) | copy-start | bytes 2359300
  22.3 1.5 %collective-permute-start.5 = (f32[360,128]{1,0:T(8,128)S(1)}, f32[360,128]{1,0:T(8,128)S(1)}, u32[]{:S(2)}, u32[]{:S(2)}) collective-permute-start(f32[360,128]{1,0:T(8,128)S(1)} %get-tuple-element.40.here_ref), channel_id=1, source_target_pairs={{0,2},{2,0},{4,6},{6,4},{1,3},{3,1},{5,7},{7,5},{8,10},{10,8},{12,... | collective-permute-start | bytes 552968 | tf_op jit(solution)/shard_map/ppermute | solution.py:879
  23.9 5.4 %collective-permute-start.7 = (f32[176,128]{1,0:T(8,128)S(1)}, f32[176,128]{1,0:T(8,128)S(1)}, u32[]{:S(2)}, u32[]{:S(2)}) collective-permute-start(f32[176,128]{1,0:T(8,128)S(1)} %get-tuple-element.42.third_ref), channel_id=1, source_target_pairs={{0,1},{1,0},{2,3},{3,2},{4,5},{5,4},{6,7},{7,6},{8,9},{9,8},{10,11... | collective-permute-start | bytes 270344 | tf_op jit(solution)/shard_map/ppermute | solution.py:888
  24.4 4.8 %collective-permute-start.6 = (f32[184,128]{1,0:T(8,128)S(1)}, f32[184,128]{1,0:T(8,128)S(1)}, u32[]{:S(2)}, u32[]{:S(2)}) collective-permute-start(f32[184,128]{1,0:T(8,128)S(1)} %get-tuple-element.41.first_ref), channel_id=1, source_target_pairs={{0,4},{2,6},{4,0},{6,2},{1,5},{3,7},{5,1},{7,3},{8,12},{10,14},{12... | collective-permute-start | bytes 282632 | tf_op jit(solution)/shard_map/ppermute | solution.py:887
  29.3 4.0 %collective-permute-start.8 = (f32[32,128]{1,0:T(8,128)S(1)}, f32[32,128]{1,0:T(8,128)S(1)}, u32[]{:S(2)}, u32[]{:S(2)}) collective-permute-start(f32[32,128]{1,0:T(8,128)S(1)} %get-tuple-element.48.refs_0_), channel_id=1, source_target_pairs={{0,1},{1,0},{2,3},{3,2},{4,5},{5,4},{6,7},{7,6},{8,9},{9,8},{10,11... | collective-permute-start | bytes 49160 | tf_op jit(solution)/shard_map/ppermute | solution.py:901
  30.9 5.2 %collective-permute-start.9 = (f32[152,128]{1,0:T(8,128)S(1)}, f32[152,128]{1,0:T(8,128)S(1)}, u32[]{:S(2)}, u32[]{:S(2)}) collective-permute-start(f32[152,128]{1,0:T(8,128)S(1)} %get-tuple-element.49.refs_0_), channel_id=1, source_target_pairs={{0,1},{1,0},{2,3},{3,2},{4,5},{5,4},{6,7},{7,6},{8,9},{9,8},{10,11... | collective-permute-start | bytes 233480 | tf_op jit(solution)/shard_map/ppermute | solution.py:902
  31.4 4.7 %collective-permute-start.10 = (f32[176,128]{1,0:T(8,128)S(1)}, f32[176,128]{1,0:T(8,128)S(1)}, u32[]{:S(2)}, u32[]{:S(2)}) collective-permute-start(f32[176,128]{1,0:T(8,128)S(1)} %get-tuple-element.50.refs_2_), channel_id=1, source_target_pairs={{0,4},{2,6},{4,0},{6,2},{1,5},{3,7},{5,1},{7,3},{8,12},{10,14},{12... | collective-permute-start | bytes 270344 | tf_op jit(solution)/shard_map/ppermute | solution.py:903
  41.3 1.5 %collective-permute-start.11 = (f32[192,128]{1,0:T(8,128)S(1)}, f32[192,128]{1,0:T(8,128)S(1)}, u32[]{:S(2)}, u32[]{:S(2)}) collective-permute-start(f32[192,128]{1,0:T(8,128)S(1)} %shard_map.55.here_ref.refs_1_), channel_id=1, source_target_pairs={{0,2},{2,0},{4,6},{6,4},{1,3},{3,1},{5,7},{7,5},{8,10},{10,8},{12,... | collective-permute-start | bytes 294920 | tf_op jit(solution)/shard_map/ppermute | solution.py:909
  41.4 4.5 %collective-permute-start.14 = (f32[2,32,256]{2,1,0:T(8,128)S(1)}, f32[2,32,256]{2,1,0:T(8,128)S(1)}, u32[]{:S(2)}, u32[]{:S(2)}) collective-permute-start(f32[2,32,256]{2,1,0:T(8,128)S(1)} %get-tuple-element.54), channel_id=1, source_target_pairs={{0,1},{1,0},{2,3},{3,2},{4,5},{5,4},{6,7},{7,6},{8,9},{9,8},{10,11... | collective-permute-start | bytes 196616 | tf_op jit(solution)/shard_map/ppermute | solution.py:86
  42.9 5.6 %collective-permute-start.12 = (f32[32,128]{1,0:T(8,128)S(1)}, f32[32,128]{1,0:T(8,128)S(1)}, u32[]{:S(2)}, u32[]{:S(2)}) collective-permute-start(f32[32,128]{1,0:T(8,128)S(1)} %get-tuple-element.52), channel_id=1, source_target_pairs={{0,24},{8,16},{16,8},{24,0},{1,25},{9,17},{17,9},{25,1},{2,26},{10... | collective-permute-start | bytes 49160 | tf_op jit(solution)/shard_map/ppermute | solution.py:88
  45.3 3.7 %collective-permute-start.13 = (f32[32,128]{1,0:T(8,128)S(1)}, f32[32,128]{1,0:T(8,128)S(1)}, u32[]{:S(2)}, u32[]{:S(2)}) collective-permute-start(f32[32,128]{1,0:T(8,128)S(1)} %get-tuple-element.53), channel_id=1, source_target_pairs={{0,8},{8,0},{16,24},{24,16},{1,9},{9,1},{17,25},{25,17},{2,10},{10... | collective-permute-start | bytes 49160 | tf_op jit(solution)/shard_map/ppermute | solution.py:89
